TPU v7x, 256 devices: a whole 4x4x8 slice. The times are simulated.
256 devices in a mesh: row: 8 (over z), col: 32 (over y, x, core).
Axes of the slice: x: 4, y: 4, z: 8, core: 2. Of those that a mesh axis runs over, the one named last changes fastest.
Arguments:
- diag_factor: float32 [512, 512], P('row', 'col'), as said below
- panel_factor: float32 [16384, 512], P('row', 'col'), may hold values from -0.046875 to 0.046875
- row_factor: float32 [512, 12288], P('row', 'col'), may hold values from -0.25 to 0.25
- trailing_factor: float32 [16384, 12288], P('row', 'col'), may hold values from -0.046875 to 0.046875
- panel_grad: float32 [16384, 512], P('row', 'col'), may hold values from -6 to 6
- diag_grad: float32 [512, 512], P('row', 'col'), may hold values from -6 to 6
- row_grad: float32 [512, 12288], P('row', 'col'), may hold values from -6 to 6
- trailing_grad: float32 [16384, 12288], P('row', 'col'), may hold values from -6 to 6
Outputs:
- panel_adjoint: float32 [16384, 512], P('row', 'col')
- trailing_out: float32 [16384, 12288], P('row', 'col')
- row_out: float32 [512, 12288], P('row', 'col')
- diag_out: float32 [512, 512], P('row', 'col')
Inputs may be any that keep to these rules, and one draw needn't show every extreme that they name: diag_factor is zero above its diagonal; its diagonal entries lie between 1 and 2.
All inputs are finite; a program needn't handle non-finite values.
Results may differ from a plain program's by a relative error of at most 0.00011.
Values sent between devices are 32-bit elements; how exact they have to be, the bound alone decides.
No kernel may reach another device: no remote copies, remote signals or barrier semaphores. Data moves between devices by JAX's collectives and lax.ppermute only.
A program may use at most 64 MiB of HBM per device.

v0:
```python
import jax
import jax.numpy as jnp
from jax import lax
from jax.sharding import PartitionSpec as P


def in_order(pieces, dim):
    pieces = jnp.moveaxis(pieces, 0, dim)
    dims = pieces.shape
    return pieces.reshape(*dims[:dim], dims[dim] * dims[dim + 1], *dims[dim + 2 :])


def copy_for_each(x, axis):
    devices = lax.axis_size(axis)
    return lax.all_to_all(jnp.broadcast_to(x[None], (devices, *x.shape)), axis, 0, 0, tiled=True)


def gather_directly(x, axis, dim):
    return in_order(copy_for_each(x, axis), dim)


def split_up(x, dim, devices):
    before, after = (x.shape[:dim], x.shape[dim + 1 :])
    return jnp.moveaxis(x.reshape(*before, devices, -1, *after), dim, 0)


def sent_and_summed(x, axis, dim):
    pieces = split_up(x, dim, lax.axis_size(axis))
    arrived = lax.all_to_all(pieces, axis, split_axis=0, concat_axis=0, tiled=True)
    return arrived.sum(axis=0)


def side_by_side(arrays, axis, dim, along):
    widths = [a.shape[along] for a in arrays]
    both = jnp.concatenate(arrays, axis=along)
    filled = sent_and_summed(both, axis, dim)
    return tuple(jnp.split(filled, [sum(widths[:k]) for k in range(1, len(widths))], axis=along))


def on_device(
    diag_factor,
    panel_factor,
    row_factor,
    trailing_factor,
    panel_grad,
    diag_grad,
    row_grad,
    trailing_grad,
):
    high = lax.Precision.HIGHEST
    tile_rows = gather_directly(diag_factor, "row", 0)
    whole_diag = gather_directly(tile_rows, "col", 1)
    width = panel_grad.shape[1]
    start_col = lax.axis_index("col") * width
    full_grad = lax.all_gather(panel_grad, "col", axis=1, tiled=True)
    solved = jax.scipy.linalg.solve_triangular(whole_diag, full_grad.T, lower=True, trans=1).T
    panel_adjoint = lax.dynamic_slice_in_dim(solved, start_col, width, 1)
    trailing_out = trailing_grad - jnp.dot(
        solved,
        gather_directly(row_factor, "row", 0),
        precision=high,
        preferred_element_type=jnp.float32,
    )
    contract = (((0,), (0,)), ((), ()))
    row_term = lax.dot_general(
        solved, trailing_factor, contract, precision=high, preferred_element_type=jnp.float32
    )
    diag_term = lax.dot_general(
        solved, panel_factor, contract, precision=high, preferred_element_type=jnp.float32
    )
    row_sum, diag_sum = side_by_side((row_term, diag_term), "row", 0, 1)
    row_out = row_grad - row_sum
    height = diag_grad.shape[0]
    global_rows = lax.axis_index("row") * height + jnp.arange(height)[:, None]
    global_cols = start_col + jnp.arange(width)[None, :]
    diag_out = jnp.where(global_rows >= global_cols, diag_grad - diag_sum, jnp.float32(0.0))
    return (panel_adjoint, trailing_out, row_out, diag_out)


def solution(mesh):
    placed = (
        P("row", "col"),
        P("row", "col"),
        P("row", "col"),
        P("row", "col"),
        P("row", "col"),
        P("row", "col"),
        P("row", "col"),
        P("row", "col"),
    )
    return jax.shard_map(
        on_device,
        mesh=mesh,
        in_specs=placed,
        out_specs=(P("row", "col"), P("row", "col"), P("row", "col"), P("row", "col")),
        check_vma=False,
    )
```

profile of v0, /device:TPU:1, one launch (start us, length us, event | category | flops | bytes accessed | tf_op | source)
XLA Modules:
  0.0 188.5 jit_solution(10915436247498761391)
XLA Ops:
  7.2 0.7 all-gather.2.cloned.1.call-update
  7.9 0.9 broadcast_bitcast_fusion
  8.9 15.7 %all_to_all.20 = f32[8,1,1024]{2,1,0:T(1,128)S(1)} all-to-all(f32[8,1,1024]{2,1,0:T(1,128)S(1)} %reshape.64), channel_id=1, replica_groups=mesh['row'=8,'col'=32] {'row'}, dimensions={0} | all-to-all | bytes 65536 | tf_op jit(solution)/shard_map/all_to_all | solution.py:15
  25.1 0.7 reduce
  26.0 1.1 broadcast_in_dim.13
  27.1 9.2 %all-to-all-start.1 = ((f32[32,512,16]{1,2,0:T(8,128)}), f32[32,512,16]{1,2,0:T(8,128)}, u32[]{:S(2)}, u32[]{:S(2)}) async-start(f32[32,512,16]{1,2,0:T(8,128)} %broadcast_in_dim.13), calls=%async_computation.1 | async-start | bytes 2097152 | tf_op jit(solution)/shard_map/all_to_all | solution.py:15
  36.4 17.2 %all-to-all-done.1 = f32[32,512,16]{1,2,0:T(8,128)} async-done(((f32[32,512,16]{1,2,0:T(8,128)}), f32[32,512,16]{1,2,0:T(8,128)}, u32[]{:S(2)}, u32[]{:S(2)}) %all-to-all-start.1) | async-done | bytes 1048608 | tf_op jit(solution)/shard_map/all_to_all | solution.py:15
  53.6 1.9 broadcast_in_dim.28
  55.5 4.2 %all-to-all-start.2 = ((f32[8,64,384]{2,1,0:T(8,128)}), f32[8,64,384]{2,1,0:T(8,128)}, u32[]{:S(2)}, u32[]{:S(2)}) async-start(f32[8,64,384]{2,1,0:T(8,128)} %broadcast_in_dim.28), calls=%async_computation.2 | async-start | bytes 1572864 | tf_op jit(solution)/shard_map/all_to_all | solution.py:15
  59.7 2.3 %bitcast_select_fusion = f32[512,512]{0,1:T(8,128)} fusion(f32[32,512,16]{1,2,0:T(8,128)} %all-to-all-done.1), kind=kLoop, calls=%fused_computation.18 | loop fusion | flops 524288 | bytes 2097152 | tf_op jit(solution)/shard_map/jit(_solve_triangular)/triangular_solve | solution.py:56
  62.0 14.4 %while.1 = (s32[]{:T(128)}, f32[512,512]{0,1:T(8,128)}, s32[4,2]{0,1:T(2,128)S(1)}, f32[4,128,128]{2,1,0:T(8,128)}, s32[]{:T(128)}) while((s32[]{:T(128)}, f32[512,512]{0,1:T(8,128)}, s32[4,2]{0,1:T(2,128)S(1)}, f32[4,128,128]{2,1,0:T(8,128)}, s32[]{:T(128)}) %tuple.30), condition=%wide.while_cond, body=%wide.while_body.sunk | while | flops 2 | bytes 393829 | solution.py:56
  62.6 2.3 %dynamic-slice.12 = f32[128,128]{0,1:T(8,128)S(1)} dynamic-slice(f32[512,512]{0,1:T(8,128)} %get-tuple-element.90, s32[]{:T(128)} %bitcast.44, s32[]{:T(128)} %bitcast.45), dynamic_slice_sizes={128,128} | dynamic-slice | bytes 131076 | tf_op jit(solution)/shard_map/jit(_solve_triangular)/triangular_solve
  66.2 2.3 %dynamic-slice.12 = f32[128,128]{0,1:T(8,128)S(1)} dynamic-slice(f32[512,512]{0,1:T(8,128)} %get-tuple-element.90, s32[]{:T(128)} %bitcast.44, s32[]{:T(128)} %bitcast.45), dynamic_slice_sizes={128,128} | dynamic-slice | bytes 131076 | tf_op jit(solution)/shard_map/jit(_solve_triangular)/triangular_solve
  69.9 2.3 %dynamic-slice.12 = f32[128,128]{0,1:T(8,128)S(1)} dynamic-slice(f32[512,512]{0,1:T(8,128)} %get-tuple-element.90, s32[]{:T(128)} %bitcast.44, s32[]{:T(128)} %bitcast.45), dynamic_slice_sizes={128,128} | dynamic-slice | bytes 131076 | tf_op jit(solution)/shard_map/jit(_solve_triangular)/triangular_solve
  73.5 2.2 %dynamic-slice.12 = f32[128,128]{0,1:T(8,128)S(1)} dynamic-slice(f32[512,512]{0,1:T(8,128)} %get-tuple-element.90, s32[]{:T(128)} %bitcast.44, s32[]{:T(128)} %bitcast.45), dynamic_slice_sizes={128,128} | dynamic-slice | bytes 131076 | tf_op jit(solution)/shard_map/jit(_solve_triangular)/triangular_solve
  76.4 40.3 %custom-call.4 = f32[4,128,128]{1,2,0:T(8,128)S(1)} custom-call(f32[4,128,128]{2,1,0:T(8,128)} %get-tuple-element.11), custom_call_target="InvertDiagBlocksLowerTriangular" | custom-call | tf_op jit(solution)/shard_map/jit(_solve_triangular)/triangular_solve | solution.py:56
  116.8 2.4 %fusion.12 = f32[128,2048]{1,0:T(8,128)S(1)} fusion(f32[512,2048]{1,0:T(8,128)} %bitcast.47, f32[4,128,128]{1,2,0:T(8,128)S(1)} %custom-call.4), kind=kOutput, calls=%fused_computation.16 | convolution fusion | flops 402653184 | bytes 2162688 | tf_op jit(solution)/shard_map/jit(_solve_triangular)/triangular_solve | solution.py:56
  119.2 2.3 %convolution_subtract_fusion.2 = f32[128,2048]{1,0:T(8,128)S(1)} fusion(f32[128,2048]{1,0:T(8,128)S(1)} %fusion.12, f32[512,2048]{1,0:T(8,128)} %bitcast.48, f32[512,512]{0,1:T(8,128)} %get-tuple-element.102), kind=kOutput, calls=%fused_computation.12 | convolution fusion | flops 402915328 | bytes 3211264 | tf_op jit(solution)/shard_map/jit(_solve_triangular)/triangular_solve | solution.py:56
  121.4 1.0 fusion.17
  122.5 2.1 %convolution_subtract_fusion.1 = f32[128,2048]{1,0:T(8,128)S(1)} fusion(f32[128,2048]{1,0:T(8,128)S(1)} %fusion.12, f32[128,2048]{1,0:T(8,128)S(1)} %fusion.17, f32[512,2048]{1,0:T(8,128)S(1)} %bitcast.49, f32[512,512]{0,1:T(8,128)} %get-tuple-element.102), kind=kOutput, calls=%fused_computation.11 | convolution fusion | flops 806092800 | bytes 4325376 | tf_op jit(solution)/shard_map/jit(_solve_triangular)/triangular_solve | solution.py:56
  124.6 1.0 fusion.18
  125.7 3.0 %fusion.6 = f32[128,2048]{1,0:T(8,128)S(1)} fusion(f32[128,2048]{1,0:T(8,128)S(1)} %fusion.12, f32[128,2048]{1,0:T(8,128)S(1)} %fusion.17, f32[128,2048]{1,0:T(8,128)S(1)} %fusion.18, f32[512,2048]{1,0:T(8,128)S(1)} %bitcast.50, f32[512,512]{0,1:T(8,128)} %get-tuple-element.102), kind=kOutput, calls=%fused_computation.10 | convolution fusion | flops 1209794560 | bytes 5439488 | tf_op jit(solution)/shard_map/jit(_solve_triangular)/triangular_solve | solution.py:56
  128.6 1.0 fusion.19
  130.6 3.6 %fusion.25 = f32[512,16]{0,1:T(8,128)S(1)} fusion(f32[512,2048]{1,0:T(8,128)S(1)} %pad_maximum_fusion, f32[2048,16]{0,1:T(8,128)S(1)} %copy-done.3), kind=kOutput, calls=%fused_computation.43 | convolution fusion | flops 201326592 | bytes 4358144 | tf_op jit(solution)/shard_map/dot_general | solution.py:68
  134.2 5.5 %fusion.24 = f32[512,384]{0,1:T(8,128)S(1)} fusion(f32[512,2048]{1,0:T(8,128)S(1)} %pad_maximum_fusion, f32[2048,384]{1,0:T(8,128)S(1)} %copy-done), kind=kOutput, calls=%fused_computation.42 | convolution fusion | flops 4831838208 | bytes 8126464 | tf_op jit(solution)/shard_map/dot_general | solution.py:65
  139.7 0.9 pad_maximum_fusion.1
  140.7 2.5 %copy.25 = f32[512,400]{1,0:T(8,128)} copy(f32[512,400]{0,1:T(8,128)} %pad_maximum_fusion.1) | data formatting | bytes 1638400 | tf_op jit(solution)/shard_map/concatenate | solution.py:35
  143.1 6.5 %all-to-all-start.3 = ((f32[8,64,400]{2,1,0:T(8,128)}), f32[8,64,400]{2,1,0:T(8,128)}, u32[]{:S(2)}, u32[]{:S(2)}) async-start(f32[8,64,400]{2,1,0:T(8,128)} %bitcast.46), calls=%async_computation.3 | async-start | bytes 2097152 | tf_op jit(solution)/shard_map/all_to_all | solution.py:29
  149.7 1.6 dynamic-slice_bitcast_fusion
  151.3 10.4 %convolution_subtract_fusion = f32[2048,384]{1,0:T(8,128)} fusion(f32[2048,384]{1,0:T(8,128)} %param.15, f32[512,2048]{1,0:T(8,128)} %copy-done.1, f32[512,384]{1,0:T(8,128)} %bitcast.8), kind=kOutput, calls=%fused_computation.9 | convolution fusion | flops 4832624640 | bytes 11272192 | tf_op jit(solution)/shard_map/dot_general | solution.py:58
  161.7 17.3 %all-to-all-done.3 = f32[8,64,400]{2,1,0:T(8,128)} async-done(((f32[8,64,400]{2,1,0:T(8,128)}), f32[8,64,400]{2,1,0:T(8,128)}, u32[]{:S(2)}, u32[]{:S(2)}) %all-to-all-start.3) | async-done | bytes 819232 | tf_op jit(solution)/shard_map/all_to_all | solution.py:29
  178.9 1.3 reduce_sum.9
  (46 shorter events, 8.5 us)
Async XLA Ops:
  7.2 127.0 %copy-start = (f32[2048,384]{1,0:T(8,128)S(1)}, f32[2048,384]{1,0:T(8,128)}, u32[]{:S(2)}) copy-start(f32[2048,384]{1,0:T(8,128)} %param.11) | copy-start | bytes 9437188
  7.2 109.6 %all-gather.2.cloned.1.call-start = ((), (), s32[]{:S(2)}) async-start(), calls=%async_computation.4 | async-start | bytes 4325376 | tf_op jit(solution)/shard_map/all_gather | solution.py:55
  27.1 26.5 %all-to-all-start.1 = ((f32[32,512,16]{1,2,0:T(8,128)}), f32[32,512,16]{1,2,0:T(8,128)}, u32[]{:S(2)}, u32[]{:S(2)}) async-start(f32[32,512,16]{1,2,0:T(8,128)} %broadcast_in_dim.13), calls=%async_computation.1 | async-start | bytes 2097152 | tf_op jit(solution)/shard_map/all_to_all | solution.py:15
  55.5 87.6 %all-to-all-start.2 = ((f32[8,64,384]{2,1,0:T(8,128)}), f32[8,64,384]{2,1,0:T(8,128)}, u32[]{:S(2)}, u32[]{:S(2)}) async-start(f32[8,64,384]{2,1,0:T(8,128)} %broadcast_in_dim.28), calls=%async_computation.2 | async-start | bytes 1572864 | tf_op jit(solution)/shard_map/all_to_all | solution.py:15
  116.8 5.7 %copy-start.2 = (f32[2048,512]{0,1:T(8,128)S(1)}, f32[2048,512]{0,1:T(8,128)}, u32[]{:S(2)}) copy-start(f32[2048,512]{0,1:T(8,128)} %all-gather.2.cloned.1.call-done) | copy-start | bytes 12582916
  129.7 0.9 copy-start.3
  130.6 9.1 %copy-start.1 = (f32[512,2048]{1,0:T(8,128)}, f32[512,2048]{1,0:T(8,128)S(1)}, u32[]{:S(2)}) copy-start(f32[512,2048]{1,0:T(8,128)S(1)} %pad_maximum_fusion) | copy-start | bytes 12582916
  139.7 9.9 %copy-start.5 = (f32[64,16]{0,1:T(8,128)S(1)}, f32[64,16]{0,1:T(8,128)}, u32[]{:S(2)}) copy-start(f32[64,16]{0,1:T(8,128)} %param.13) | copy-start | bytes 12292
  143.1 35.8 %all-to-all-start.3 = ((f32[8,64,400]{2,1,0:T(8,128)}), f32[8,64,400]{2,1,0:T(8,128)}, u32[]{:S(2)}, u32[]{:S(2)}) async-start(f32[8,64,400]{2,1,0:T(8,128)} %bitcast.46), calls=%async_computation.3 | async-start | bytes 2097152 | tf_op jit(solution)/shard_map/all_to_all | solution.py:29
  151.3 28.9 %copy-start.4 = (f32[64,384]{1,0:T(8,128)S(1)}, f32[64,384]{1,0:T(8,128)}, u32[]{:S(2)}) copy-start(f32[64,384]{1,0:T(8,128)} %param.14) | copy-start | bytes 294916
Sparse Core Ops, SparseCore 0:
  10.6 62.5 all-gather.1
where the time goes:
time: 189 us
  other arithmetic  46.8 us (25%)
  waiting for transfers between devices  35.2 us (19%)
  matrix products  32.3 us (17%)
  local copies, waits for them, and re-layouts  24.3 us (13%)
  starting transfers between devices  20 us (11%)
  blocking collectives  15.7 us (8%)
  between operations  14.2 us (8%)
    another operation x4, other arithmetic, on_device(): jax.scipy.linalg.solve_triangular(whole_diag, full_grad.T, lower=True, tr...  43.1 us
    all_to_all x1, waiting for transfers between devices, sent_and_summed(): lax.all_to_all(pieces, axis, split_axis=0, concat_axis=0, tiled=True)  17.3 us
    all_to_all x2, waiting for transfers between devices, copy_for_each(): lax.all_to_all(jnp.broadcast_to(x[None], (devices, *x.shape)), axis, 0, 0...  17.2 us
    all_to_all x1, blocking collectives, copy_for_each(): lax.all_to_all(jnp.broadcast_to(x[None], (devices, *x.shape)), axis, 0, 0...  15.7 us
    another operation x20, local copies, waits for them, and re-layouts  14.4 us
    all_to_all x2, starting transfers between devices, copy_for_each(): lax.all_to_all(jnp.broadcast_to(x[None], (devices, *x.shape)), axis, 0, 0...  13.5 us
    another operation x7, matrix products, on_device(): jax.scipy.linalg.solve_triangular(whole_diag, full_grad.T, lower=True, tr...  12.8 us
    dot_general x1, matrix products, on_device(): jnp.dot(solved, gather_directly(row_factor, 'row', 0), precision=high, pr...  10.4 us
  transfers between devices with their start and end apart: 4, of which 2 were waited for; matrix products, arithmetic and copies ran while one was open for 53% of the time, Pallas kernels for 0%

commit v1 on v0

v1 whole, which is shorter than its diff:
```python
import jax
import jax.numpy as jnp
from jax import lax
from jax.experimental import pallas as pl
from jax.experimental.pallas import tpu as pltpu
from jax.sharding import PartitionSpec as P

F32 = jnp.float32
BF16 = jnp.bfloat16
ROWS = 8
COLS = 32
B = 512
MIB = 1 << 20


def with_row_partner(v, k):
    return lax.ppermute(v, "row", [(i, i ^ k) for i in range(ROWS)])


def with_sibling(v):
    return lax.ppermute(v, "col", [(i, i ^ 1) for i in range(COLS)])


def with_col_partner(v, phase, k):
    shift = {0: 1, 1: 3}
    perm = [(i, i ^ (k << shift[phase ^ (i & 1)])) for i in range(COLS)]
    return lax.ppermute(v, "col", perm)


def gather_cols(chunk, core):
    half = chunk.shape[1] // 2
    low, high = chunk[:, :half], chunk[:, half:]
    kept = jnp.where(core == 0, low, high)
    given = jnp.where(core == 0, high, low)
    pair = jnp.concatenate([kept, with_sibling(given)], axis=0)
    quad = jnp.concatenate([pair] + [with_col_partner(pair, 0, k) for k in (1, 2, 3)], axis=0)
    blocks = [quad] + [with_col_partner(quad, 1, k) for k in (2, 1, 3)]
    blocks = [blocks[0], blocks[2], blocks[1], blocks[3]]
    return blocks, [with_sibling(b) for b in blocks]


def place(ids, mine, theirs, store):
    y, x, core = ids[1], ids[2], ids[3]
    for other, blocks in ((0, mine), (1, theirs)):
        half = core ^ other
        for k, block in enumerate(blocks):
            for j in range(4):
                along_x = jnp.where(half == 0, x ^ j, x ^ k)
                along_y = jnp.where(half == 0, y ^ k, y ^ j)
                for r in range(2):
                    row = (along_y * 8 + along_x * 2 + (half ^ r)) * 16
                    at = (j * 2 + r) * 16
                    store(half, pl.multiple_of(row, 16), block[at : at + 16, :])


def split(v):
    high = v.astype(BF16)
    return high, (v - high.astype(F32)).astype(BF16)


def dot3(a, b, contract=((1,), (0,))):
    dims = (contract, ((), ()))
    (ah, al), (bh, bl) = a, b

    def one(p, q):
        return lax.dot_general(p, q, dims, preferred_element_type=F32)

    return one(ah, bh) + (one(ah, bl) + one(al, bh))


def dot_full(a, b):
    return lax.dot_general(
        a, b, (((1,), (0,)), ((), ())), precision=lax.Precision.HIGHEST, preferred_element_type=F32
    )


def invert_kernel(ids, *refs):
    mine, theirs = refs[:4], refs[4:8]
    high_out, low_out, held = refs[8:]

    odd = jnp.broadcast_to(ids[0] % 2, (16, 128)) == 1

    def store(half, row, piece):
        for q in range(2):
            lanes = piece[:, 128 * q : 128 * q + 128]
            swapped = jnp.concatenate([lanes[:, 64:], lanes[:, :64]], axis=1)
            held[(half * 2 + q) ^ (ids[0] // 2), pl.ds(row, 16), :] = jnp.where(odd, swapped, lanes)

    place(ids, mine, theirs, store)

    def part(r, c, n):
        return jnp.concatenate([held[c // 128 + q, r : r + n, :] for q in range(n // 128)], axis=1)

    n = 128
    rows = lax.broadcasted_iota(jnp.int32, (n, n), 0)
    cols = lax.broadcasted_iota(jnp.int32, (n, n), 1)
    in_block = rows // 16 == cols // 16
    diag = [part(n * g, n * g, n) for g in range(4)]
    packed = []
    for d in diag:
        kept = jnp.where(in_block, d, 0.0)
        packed.append(sum(kept[16 * b : 16 * b + 16, :] for b in range(1, 8)) + kept[0:16, :])
    packed = jnp.concatenate(packed, axis=0)
    sub = lax.broadcasted_iota(jnp.int32, (64, n), 0) % 16
    lane = lax.broadcasted_iota(jnp.int32, (64, n), 1) % 16
    inverse = jnp.where(sub == lane, 1.0, 0.0).astype(F32)
    spread = []
    for k in range(16):
        pick = jnp.where(in_block & (rows % 16 == k), 1.0, 0.0).astype(F32)
        spread.append(dot_full(packed, pick))
    for k in range(15, -1, -1):
        factor = spread[k]
        pivot = []
        for g in range(4):
            at = 16 * g + k
            row = inverse[at : at + 1, :] / factor[at : at + 1, :]
            pivot.append(jnp.broadcast_to(row, (16, n)))
        pivot = jnp.concatenate(pivot, axis=0)
        inverse = jnp.where(sub == k, pivot, inverse - jnp.where(sub < k, factor, 0.0) * pivot)
    blocks = []
    for g in range(4):
        tall = jnp.concatenate([inverse[16 * g : 16 * g + 16, :]] * 8, axis=0)
        blocks.append(jnp.where(in_block, tall, 0.0))
    for b in (16, 32, 64):
        off = (rows // (2 * b) == cols // (2 * b)) & (rows // b < cols // b)
        lefts = [dot_full(blocks[g], jnp.where(off, diag[g], 0.0)) for g in range(4)]
        blocks = [blocks[g] - dot_full(lefts[g], blocks[g]) for g in range(4)]
    pairs = []
    for g in (0, 2):
        corner = -dot_full(dot_full(blocks[g], part(n * g, n * g + n, n)), blocks[g + 1])
        top = jnp.concatenate([blocks[g], corner], axis=1)
        low = jnp.concatenate([jnp.zeros_like(corner), blocks[g + 1]], axis=1)
        pairs.append(jnp.concatenate([top, low], axis=0))
    corner = -dot_full(dot_full(pairs[0], part(0, 256, 256)), pairs[1])
    zero = jnp.zeros((256, 256), BF16)
    for out, which in ((high_out, 0), (low_out, 1)):
        out[0:256, 0:256] = split(pairs[0])[which]
        out[0:256, 256:512] = split(corner)[which]
        out[256:512, 0:256] = zero
        out[256:512, 256:512] = split(pairs[1])[which]


def solve_kernel(ids, *refs):
    mine, theirs = refs[:4], refs[4:8]
    inv_high, inv_low, trailing, panel = refs[8:12]
    solved_out, own_out = refs[12:14]
    sends = refs[14:22]
    g_high, g_low, total, corner = refs[22:]

    def store(half, row, piece):
        high, low = split(piece)
        g_high[half, pl.ds(row, 16), :] = high
        g_low[half, pl.ds(row, 16), :] = low

    place(ids, mine, theirs, store)
    total[...] = jnp.zeros_like(total)
    corner[...] = jnp.zeros_like(corner)
    tile = 256
    for half in range(2):

        @pl.loop(0, 1024 // tile)
        def _(step):
            here = pl.ds(pl.multiple_of(step * tile, tile), tile)
            there = pl.ds(pl.multiple_of(half * 1024 + step * tile, tile), tile)
            g = (g_high[half, :, here], g_low[half, :, here])
            g_end = (g[0][256:, :], g[1][256:, :])
            top = dot3((inv_high[0:256, :], inv_low[0:256, :]), g)
            low = dot3((inv_high[256:512, 256:512], inv_low[256:512, 256:512]), g_end)
            x = jnp.concatenate([top, low], axis=0)
            solved_out[:, there] = x
            xs = split(x)
            total[0:512, :] += dot3(xs, split(trailing[there, :]))
            corner[...] += dot3(split(panel[:, there]), xs, ((1,), (1,)))

    own = pl.ds(pl.multiple_of(ids[4] * 16, 16), 16)
    own_out[...] = solved_out[own, :]
    summed = corner[...]
    zero = jnp.zeros((8, 384), F32)
    for t in range(ROWS):
        part = summed[:, 64 * t : 64 * t + 64]
        total[512 + 8 * t : 520 + 8 * t, :] = zero
        total[512 + 8 * t : 520 + 8 * t, 0:64] = part[0:8, :]
        total[512 + 8 * t : 520 + 8 * t, 64:128] = part[8:16, :]
    for k in range(ROWS):
        target = ids[0] ^ k
        sends[k][0:64, :] = total[pl.ds(pl.multiple_of(target * 64, 64), 64), :]
        sends[k][64:72, :] = total[pl.ds(pl.multiple_of(512 + target * 8, 8), 8), :]


def trailing_kernel(ids, *refs):
    pieces = refs[:8]
    solved, grad, out, r_high, r_low = refs[8:]

    @pl.when(pl.program_id(0) == 0)
    def _():
        for k in range(ROWS):
            at = pl.ds(pl.multiple_of((ids[0] ^ k) * 64, 64), 64)
            r_high[at, :], r_low[at, :] = split(pieces[k][...])

    x = split(solved[...].T)
    out[...] = grad[...] - dot3(x, (r_high[...], r_low[...]))


SMEM = pl.BlockSpec(memory_space=pltpu.SMEM)
VMEM = pl.BlockSpec(memory_space=pltpu.VMEM)


def shape(dims, dtype=F32):
    return jax.ShapeDtypeStruct(dims, dtype)


def invert(ids, mine, theirs):
    return pl.pallas_call(
        invert_kernel,
        out_shape=[shape((B, B), BF16)] * 2,
        in_specs=[SMEM] + [VMEM] * 8,
        out_specs=[VMEM] * 2,
        scratch_shapes=[pltpu.VMEM((4, B, 128), F32)],
        compiler_params=pltpu.CompilerParams(vmem_limit_bytes=16 * MIB),
        cost_estimate=pl.CostEstimate(flops=4_000_000_000, bytes_accessed=2 * MIB, transcendentals=0),
        name="invert",
    )(ids, *mine, *theirs)


def solve(ids, mine, theirs, inverse, trailing, panel):
    return pl.pallas_call(
        solve_kernel,
        out_shape=[shape((B, 2048)), shape((16, 2048))] + [shape((72, 384))] * 8,
        in_specs=[SMEM] + [VMEM] * 12,
        out_specs=[VMEM] * 10,
        scratch_shapes=[
            pltpu.VMEM((2, B, 1024), BF16),
            pltpu.VMEM((2, B, 1024), BF16),
            pltpu.VMEM((B + 64, 384), F32),
            pltpu.VMEM((16, B), F32),
        ],
        compiler_params=pltpu.CompilerParams(vmem_limit_bytes=40 * MIB),
        cost_estimate=pl.CostEstimate(flops=5_000_000_000, bytes_accessed=12 * MIB, transcendentals=0),
        name="solve",
    )(ids, *mine, *theirs, *inverse, trailing, panel)


def trailing_update(ids, pieces, solved, grad):
    tile = 256
    return pl.pallas_call(
        trailing_kernel,
        grid=(2048 // tile,),
        out_shape=shape((2048, 384)),
        in_specs=[SMEM]
        + [pl.BlockSpec((64, 384), lambda i: (0, 0))] * 8
        + [pl.BlockSpec((B, tile), lambda i: (0, i)), pl.BlockSpec((tile, 384), lambda i: (i, 0))],
        out_specs=pl.BlockSpec((tile, 384), lambda i: (i, 0)),
        scratch_shapes=[pltpu.VMEM((B, 384), BF16), pltpu.VMEM((B, 384), BF16)],
        compiler_params=pltpu.CompilerParams(vmem_limit_bytes=16 * MIB),
        cost_estimate=pl.CostEstimate(flops=4_000_000_000, bytes_accessed=11 * MIB, transcendentals=0),
        name="trailing",
    )(ids, *pieces, solved, grad)


def on_device(
    diag_factor,
    panel_factor,
    row_factor,
    trailing_factor,
    panel_grad,
    diag_grad,
    row_grad,
    trailing_grad,
):
    z = lax.axis_index("row")
    col = lax.axis_index("col")
    core = col % 2
    ids = jnp.stack([z, col // 8, (col // 2) % 4, core, col]).astype(jnp.int32)

    tile = diag_factor.T
    tiles = [tile] + [with_row_partner(tile, k) for k in range(1, ROWS)]
    diag_chunk = jnp.concatenate(tiles, axis=1)

    diag_mine, diag_theirs = gather_cols(diag_chunk, core)
    grad_mine, grad_theirs = gather_cols(panel_grad.T, core)
    row_pieces = [row_factor] + [with_row_partner(row_factor, k) for k in range(1, ROWS)]

    inverse = invert(ids, diag_mine, diag_theirs)
    solved, own, *sends = solve(ids, grad_mine, grad_theirs, inverse, trailing_factor, panel_factor.T)
    came = [with_row_partner(sends[k], k) for k in range(1, ROWS)]
    trailing_out = trailing_update(ids, row_pieces, solved, trailing_grad)

    total = sends[0]
    for term in came:
        total = total + term
    row_out = row_grad - total[0:64, :]
    diag_sum = jnp.concatenate([total[64:72, 0:64], total[64:72, 64:128]], axis=0)
    global_rows = z * 64 + jnp.arange(64)[None, :]
    global_cols = col * 16 + jnp.arange(16)[:, None]
    diag_out = jnp.where(global_rows >= global_cols, diag_grad.T - diag_sum, jnp.float32(0.0))
    return (own.T, trailing_out, row_out, diag_out.T)


def solution(mesh):
    both = P("row", "col")
    return jax.shard_map(
        on_device,
        mesh=mesh,
        in_specs=(both,) * 8,
        out_specs=(both,) * 4,
        check_vma=False,
    )
```

time: 189 us -> 136 us (0.72)
  starting transfers between devices: 20 us -> 66.9 us
  other arithmetic: 46.8 us -> 3.08 us
  matrix products: 32.3 us -> 0 us
  Pallas kernels: 0 us -> 25.5 us
  local copies, waits for them, and re-layouts: 24.3 us -> 4.91 us
  blocking collectives: 15.7 us -> 0 us
  between operations: 14.2 us -> 0.82 us
    ppermute x0 -> x43, starting transfers between devices: none -> 66.9 us  [the longest x21 37.5 us: with_row_partner(): return lax.ppermute(v, 'row', [(i, i ^ k) for i in range(ROWS)])]
    another operation x4 -> x0, other arithmetic: 43.1 us -> none  [on_device(): jax.scipy.linalg.solve_triangular(whole_diag, full_grad.T, lower=True, tr...]
    ppermute x0 -> x43, waiting for transfers between devices: none -> 34.8 us  [the longest x12 16.7 us: with_col_partner(): return lax.ppermute(v, 'col', perm)]
    all_to_all x3 -> x0, waiting for transfers between devices: 34.5 us -> none  [the longest x1 17.3 us: sent_and_summed(): lax.all_to_all(pieces, axis, split_axis=0, concat_axis=0, tiled=True)]
    pallas_call x0 -> x3, Pallas kernels: none -> 25.5 us  [the longest x1 13.2 us: solve(): pl.pallas_call(solve_kernel, out_shape=[shape((B, 2048)), shape((16, 2048...]
    all_to_all x3 -> x0, starting transfers between devices: 20 us -> none  [the longest x2 13.5 us: copy_for_each(): lax.all_to_all(jnp.broadcast_to(x[None], (devices, *x.shape)), axis, 0, 0...]
    dot_general x3 -> x0, matrix products: 19.4 us -> none  [the longest x1 10.4 us: on_device(): jnp.dot(solved, gather_directly(row_factor, 'row', 0), precision=high, pr...]
    all_to_all x1 -> x0, blocking collectives: 15.7 us -> none  [copy_for_each(): lax.all_to_all(jnp.broadcast_to(x[None], (devices, *x.shape)), axis, 0, 0...]
  transfers between devices with their start and end apart: 4 -> 43, of which waited for: 2 -> 12; matrix products, arithmetic and copies ran while one was open for 53% -> 1% of each run, Pallas kernels for 0% -> 19%
where the time goes in v1:
time: 136 us
  starting transfers between devices  66.9 us (49%)
  waiting for transfers between devices  34.8 us (26%)
  Pallas kernels  25.5 us (19%)
  local copies, waits for them, and re-layouts  4.91 us (4%)
  other arithmetic  3.08 us (2%)
    ppermute x21, starting transfers between devices, with_row_partner(): return lax.ppermute(v, 'row', [(i, i ^ k) for i in range(ROWS)])  37.5 us
    ppermute x12, waiting for transfers between devices, with_col_partner(): return lax.ppermute(v, 'col', perm)  16.7 us
    ppermute x12, starting transfers between devices, with_col_partner(): return lax.ppermute(v, 'col', perm)  15.8 us
    ppermute x21, waiting for transfers between devices, with_row_partner(): return lax.ppermute(v, 'row', [(i, i ^ k) for i in range(ROWS)])  15.8 us
    ppermute x10, starting transfers between devices, with_sibling(): return lax.ppermute(v, 'col', [(i, i ^ 1) for i in range(COLS)])  13.7 us
    pallas_call x1, Pallas kernels, solve(): pl.pallas_call(solve_kernel, out_shape=[shape((B, 2048)), shape((16, 2048...  13.2 us
    pallas_call x1, Pallas kernels, trailing_update(): pl.pallas_call(trailing_kernel, grid=(2048 // tile,), out_shape=shape((20...  7.01 us
    pallas_call x1, Pallas kernels, invert(): pl.pallas_call(invert_kernel, out_shape=[shape((B, B), BF16)] * 2, in_spe...  5.26 us
  transfers between devices with their start and end apart: 43, of which 12 were waited for; matrix products, arithmetic and copies ran while one was open for 1% of the time, Pallas kernels for 19%

profile of v1, /device:TPU:1, one launch (start us, length us, event | category | flops | bytes accessed | tf_op | source)
XLA Modules:
  0.0 136.0 jit_solution(18060423191360432206)
XLA Ops:
  0.6 2.6 %collective-permute-start.11 = (f32[16,64]{1,0:T(8,128)}, f32[16,64]{1,0:T(8,128)S(1)}, u32[]{:S(2)}, u32[]{:S(2)}) collective-permute-start(f32[16,64]{1,0:T(8,128)} %bitcast.15), channel_id=1, source_target_pairs={{0,32},{32,0},{64,96},{96,64},{128,160},{160,128},{192,224},{224,1... | collective-permute-start | bytes 12296 | tf_op jit(solution)/shard_map/ppermute | solution.py:17
  3.2 3.0 %collective-permute-start.12 = (f32[16,64]{1,0:T(8,128)}, f32[16,64]{1,0:T(8,128)S(1)}, u32[]{:S(2)}, u32[]{:S(2)}) collective-permute-start(f32[16,64]{1,0:T(8,128)} %bitcast.16), channel_id=1, source_target_pairs={{0,64},{32,96},{64,0},{96,32},{128,192},{160,224},{192,128},{224,1... | collective-permute-start | bytes 12296 | tf_op jit(solution)/shard_map/ppermute | solution.py:17
  6.2 5.8 %collective-permute-start.14 = (f32[16,64]{1,0:T(8,128)}, f32[16,64]{1,0:T(8,128)S(1)}, u32[]{:S(2)}, u32[]{:S(2)}) collective-permute-start(f32[16,64]{1,0:T(8,128)} %bitcast.18), channel_id=1, source_target_pairs={{0,128},{32,160},{64,192},{96,224},{128,0},{160,32},{192,64},{224,... | collective-permute-start | bytes 12296 | tf_op jit(solution)/shard_map/ppermute | solution.py:17
  12.0 4.0 %collective-permute-start.16 = (f32[16,64]{1,0:T(8,128)}, f32[16,64]{1,0:T(8,128)S(1)}, u32[]{:S(2)}, u32[]{:S(2)}) collective-permute-start(f32[16,64]{1,0:T(8,128)} %bitcast.20), channel_id=1, source_target_pairs={{0,192},{32,224},{64,128},{96,160},{128,64},{160,96},{192,0},{224,... | collective-permute-start | bytes 12296 | tf_op jit(solution)/shard_map/ppermute | solution.py:17
  16.1 1.7 %collective-permute-done.15 = f32[16,64]{1,0:T(8,128)S(1)} collective-permute-done((f32[16,64]{1,0:T(8,128)}, f32[16,64]{1,0:T(8,128)S(1)}, u32[]{:S(2)}, u32[]{:S(2)}) %collective-permute-start.15) | collective-permute-done | bytes 4128 | tf_op jit(solution)/shard_map/ppermute | solution.py:17
  17.7 2.5 %collective-permute-done.17 = f32[16,64]{1,0:T(8,128)S(1)} collective-permute-done((f32[16,64]{1,0:T(8,128)}, f32[16,64]{1,0:T(8,128)S(1)}, u32[]{:S(2)}, u32[]{:S(2)}) %collective-permute-start.17) | collective-permute-done | bytes 4128 | tf_op jit(solution)/shard_map/ppermute | solution.py:17
  21.1 3.3 %collective-permute-start.18 = (f32[16,256]{1,0:T(8,128)S(1)}, f32[16,256]{1,0:T(8,128)S(1)}, u32[]{:S(2)}, u32[]{:S(2)}) collective-permute-start(f32[16,256]{1,0:T(8,128)S(1)} %get-tuple-element.35), channel_id=1, source_target_pairs={{0,1},{1,0},{2,3},{3,2},{4,5},{5,4},{6,7},{7,6},{8,9},{9,8},{10,11... | collective-permute-start | bytes 49160 | tf_op jit(solution)/shard_map/ppermute | solution.py:21
  26.7 2.6 %collective-permute-start.20 = (f32[32,256]{1,0:T(8,128)S(1)}, f32[32,256]{1,0:T(8,128)S(1)}, u32[]{:S(2)}, u32[]{:S(2)}) collective-permute-start(f32[32,256]{1,0:T(8,128)S(1)} %pad_maximum_fusion.1), channel_id=1, source_target_pairs={{0,4},{1,17},{2,6},{3,19},{4,0},{5,21},{6,2},{7,23},{8,12},{9,25},... | collective-permute-start | bytes 98312 | tf_op jit(solution)/shard_map/ppermute | solution.py:27
  29.5 3.8 %collective-permute-start.2 = (f32[32,1024]{1,0:T(8,128)S(1)}, f32[32,1024]{1,0:T(8,128)S(1)}, u32[]{:S(2)}, u32[]{:S(2)}) collective-permute-start(f32[32,1024]{1,0:T(8,128)S(1)} %pad_maximum_fusion), channel_id=1, source_target_pairs={{0,4},{1,17},{2,6},{3,19},{4,0},{5,21},{6,2},{7,23},{8,12},{9,25},... | collective-permute-start | bytes 393224 | tf_op jit(solution)/shard_map/ppermute | solution.py:27
  33.4 3.7 %collective-permute-done.2 = f32[32,1024]{1,0:T(8,128)S(1)} collective-permute-done((f32[32,1024]{1,0:T(8,128)S(1)}, f32[32,1024]{1,0:T(8,128)S(1)}, u32[]{:S(2)}, u32[]{:S(2)}) %collective-permute-start.2) | collective-permute-done | bytes 131104 | tf_op jit(solution)/shard_map/ppermute | solution.py:27
  37.1 1.7 %collective-permute-done.3 = f32[32,1024]{1,0:T(8,128)S(1)} collective-permute-done((f32[32,1024]{1,0:T(8,128)S(1)}, f32[32,1024]{1,0:T(8,128)S(1)}, u32[]{:S(2)}, u32[]{:S(2)}) %collective-permute-start.3) | collective-permute-done | bytes 131104 | tf_op jit(solution)/shard_map/ppermute | solution.py:27
  38.8 2.3 %collective-permute-start.6 = (f32[128,1024]{1,0:T(8,128)S(1)}, f32[128,1024]{1,0:T(8,128)S(1)}, u32[]{:S(2)}, u32[]{:S(2)}) collective-permute-start(f32[128,1024]{1,0:T(8,128)S(1)} %constant_dynamic-update-slice_fusion.refs_0_), channel_id=1, source_target_pairs={{0,24},{1,7},{2,26},{3,5},{4,28},{5,3},{6,30},{7,1},{8,16},{9,15},... | collective-permute-start | bytes 1572872 | tf_op jit(solution)/shard_map/ppermute | solution.py:27
  41.1 1.7 %collective-permute-start.5 = (f32[128,1024]{1,0:T(8,128)S(1)}, f32[128,1024]{1,0:T(8,128)S(1)}, u32[]{:S(2)}, u32[]{:S(2)}) collective-permute-start(f32[128,1024]{1,0:T(8,128)S(1)} %constant_dynamic-update-slice_fusion.refs_0_), channel_id=1, source_target_pairs={{0,16},{1,5},{2,18},{3,7},{4,20},{5,1},{6,22},{7,3},{8,24},{9,13},... | collective-permute-start | bytes 1572872 | tf_op jit(solution)/shard_map/ppermute | solution.py:27
  42.9 3.4 %collective-permute-start.23 = (f32[128,256]{1,0:T(8,128)S(1)}, f32[128,256]{1,0:T(8,128)S(1)}, u32[]{:S(2)}, u32[]{:S(2)}) collective-permute-start(f32[128,256]{1,0:T(8,128)S(1)} %constant_dynamic-update-slice_fusion.5.refs_0_), channel_id=1, source_target_pairs={{0,16},{1,5},{2,18},{3,7},{4,20},{5,1},{6,22},{7,3},{8,24},{9,13},... | collective-permute-start | bytes 393224 | tf_op jit(solution)/shard_map/ppermute | solution.py:27
  46.2 10.2 %collective-permute-done.22.refs_1_ = f32[128,256]{1,0:T(8,128)S(1)} collective-permute-done((f32[128,256]{1,0:T(8,128)S(1)}, f32[128,256]{1,0:T(8,128)S(1)}, u32[]{:S(2)}, u32[]{:S(2)}) %collective-permute-start.22) | collective-permute-done | bytes 131104 | tf_op jit(solution)/shard_map/ppermute | solution.py:27
  58.0 3.5 %collective-permute-start.25 = (f32[128,256]{1,0:T(8,128)S(1)}, f32[128,256]{1,0:T(8,128)S(1)}, u32[]{:S(2)}, u32[]{:S(2)}) collective-permute-start(f32[128,256]{1,0:T(8,128)S(1)} %constant_dynamic-update-slice_fusion.5.refs_0_), channel_id=1, source_target_pairs={{0,1},{1,0},{2,3},{3,2},{4,5},{5,4},{6,7},{7,6},{8,9},{9,8},{10,11... | collective-permute-start | bytes 393224 | tf_op jit(solution)/shard_map/ppermute | solution.py:21
  61.6 5.3 %collective-permute-start.26 = (f32[128,256]{1,0:T(8,128)S(1)}, f32[128,256]{1,0:T(8,128)S(1)}, u32[]{:S(2)}, u32[]{:S(2)}) collective-permute-start(f32[128,256]{1,0:T(8,128)S(1)} %collective-permute-done.22.refs_1_), channel_id=1, source_target_pairs={{0,1},{1,0},{2,3},{3,2},{4,5},{5,4},{6,7},{7,6},{8,9},{9,8},{10,11... | collective-permute-start | bytes 393224 | tf_op jit(solution)/shard_map/ppermute | solution.py:21
  70.7 2.0 %collective-permute-done.28.refs_7_ = f32[128,256]{1,0:T(8,128)} collective-permute-done((f32[128,256]{1,0:T(8,128)}, f32[128,256]{1,0:T(8,128)}, u32[]{:S(2)}, u32[]{:S(2)}) %collective-permute-start.28) | collective-permute-done | bytes 131104 | tf_op jit(solution)/shard_map/ppermute | solution.py:21
  77.0 5.3 %invert.1 = (bf16[512,512]{1,0:T(8,128)(2,1)S(1)}, bf16[512,512]{1,0:T(8,128)(2,1)S(1)}) custom-call(s32[5]{0:T(128)S(1)} %stack.23.ids, f32[128,256]{1,0:T(8,128)S(1)} %constant_dynamic-update-slice_fusion.5.refs_0_, f32[128,256]{1,0:T(8,128)S(1)} %collective-permute-done.22.refs_1_, f32[128,256]{1,0:T(8,128)S(1)} %collective-permute-done.23.refs_2_, ...), custom_call_target="tpu_custom_call" | custom-call | flops 4000000000 | bytes 2097152 | tf_op jit(solution)/shard_map/invert/pallas_call | solution.py:213
  82.9 1.6 %collective-permute-start.31 = (f32[64,384]{1,0:T(8,128)S(1)}, f32[64,384]{1,0:T(8,128)S(1)}, u32[]{:S(2)}, u32[]{:S(2)}) collective-permute-start(f32[64,384]{1,0:T(8,128)S(1)} %copy-done.9), channel_id=1, source_target_pairs={{0,96},{32,64},{64,32},{96,0},{128,224},{160,192},{192,160},{224,1... | collective-permute-start | bytes 294920 | tf_op jit(solution)/shard_map/ppermute | solution.py:17
  86.1 3.2 %collective-permute-start.33 = (f32[64,384]{1,0:T(8,128)S(1)}, f32[64,384]{1,0:T(8,128)S(1)}, u32[]{:S(2)}, u32[]{:S(2)}) collective-permute-start(f32[64,384]{1,0:T(8,128)S(1)} %copy-done.9), channel_id=1, source_target_pairs={{0,160},{32,128},{64,224},{96,192},{128,32},{160,0},{192,96},{224,... | collective-permute-start | bytes 294920 | tf_op jit(solution)/shard_map/ppermute | solution.py:17
  89.3 13.2 %solve.1 = (f32[512,2048]{1,0:T(8,128)S(1)}, f32[16,2048]{1,0:T(8,128)}, f32[72,384]{1,0:T(8,128)S(1)}, f32[72,384]{1,0:T(8,128)S(1)}, f32[72,384]{1,0:T(8,128)S...) custom-call(s32[5]{0:T(128)S(1)} %stack.23.ids, ...), custom_call_target="tpu_custom_call" | custom-call | flops 5000000000 | bytes 12582912 | tf_op jit(solution)/shard_map/solve/pallas_call | solution.py:226
  103.4 2.4 %collective-permute-start.35 = (f32[64,384]{1,0:T(8,128)S(1)}, f32[64,384]{1,0:T(8,128)S(1)}, u32[]{:S(2)}, u32[]{:S(2)}) collective-permute-start(f32[64,384]{1,0:T(8,128)S(1)} %copy-done.9), channel_id=1, source_target_pairs={{0,224},{32,192},{64,160},{96,128},{128,96},{160,64},{192,32},{224... | collective-permute-start | bytes 294920 | tf_op jit(solution)/shard_map/ppermute | solution.py:17
  107.8 1.6 %collective-permute-start.38 = (f32[72,384]{1,0:T(8,128)S(1)}, f32[72,384]{1,0:T(8,128)S(1)}, u32[]{:S(2)}, u32[]{:S(2)}) collective-permute-start(f32[72,384]{1,0:T(8,128)S(1)} %get-tuple-element.23), channel_id=1, source_target_pairs={{0,96},{32,64},{64,32},{96,0},{128,224},{160,192},{192,160},{224,1... | collective-permute-start | bytes 331784 | tf_op jit(solution)/shard_map/ppermute | solution.py:17
  109.4 2.5 %collective-permute-start.39 = (f32[72,384]{1,0:T(8,128)S(1)}, f32[72,384]{1,0:T(8,128)S(1)}, u32[]{:S(2)}, u32[]{:S(2)}) collective-permute-start(f32[72,384]{1,0:T(8,128)S(1)} %get-tuple-element.24), channel_id=1, source_target_pairs={{0,128},{32,160},{64,192},{96,224},{128,0},{160,32},{192,64},{224,... | collective-permute-start | bytes 331784 | tf_op jit(solution)/shard_map/ppermute | solution.py:17
  111.9 3.0 %collective-permute-done.35.refs_7_ = f32[64,384]{1,0:T(8,128)S(1)} collective-permute-done((f32[64,384]{1,0:T(8,128)S(1)}, f32[64,384]{1,0:T(8,128)S(1)}, u32[]{:S(2)}, u32[]{:S(2)}) %collective-permute-start.35) | collective-permute-done | bytes 98336 | tf_op jit(solution)/shard_map/ppermute | solution.py:17
  115.0 1.9 %collective-permute-start.40 = (f32[72,384]{1,0:T(8,128)S(1)}, f32[72,384]{1,0:T(8,128)S(1)}, u32[]{:S(2)}, u32[]{:S(2)}) collective-permute-start(f32[72,384]{1,0:T(8,128)S(1)} %get-tuple-element.25), channel_id=1, source_target_pairs={{0,160},{32,128},{64,224},{96,192},{128,32},{160,0},{192,96},{224,... | collective-permute-start | bytes 331784 | tf_op jit(solution)/shard_map/ppermute | solution.py:17
  116.9 2.2 %collective-permute-start.41 = (f32[72,384]{1,0:T(8,128)S(1)}, f32[72,384]{1,0:T(8,128)S(1)}, u32[]{:S(2)}, u32[]{:S(2)}) collective-permute-start(f32[72,384]{1,0:T(8,128)S(1)} %get-tuple-element.26), channel_id=1, source_target_pairs={{0,192},{32,224},{64,128},{96,160},{128,64},{160,96},{192,0},{224,... | collective-permute-start | bytes 331784 | tf_op jit(solution)/shard_map/ppermute | solution.py:17
  119.0 7.0 %trailing.1 = f32[2048,384]{1,0:T(8,128)} custom-call(s32[5]{0:T(128)S(1)} %stack.23.ids, f32[64,384]{1,0:T(8,128)S(1)} %copy-done.9, f32[64,384]{1,0:T(8,128)S(1)} %collective-permute-done.29.refs_1_, f32[64,384]{1,0:T(8,128)S(1)} %collective-permute-done.30.refs_2_, f32[64,384]{1,0:T(8,128)S(1)} %collective-permute-done.31.refs_3_, ...), custom_call_target="tpu_custom_call" | custom-call | flops 4000000000 | bytes 11534336 | tf_op jit(solution)/shard_map/trailing/pallas_call | solution.py:245
  126.1 4.1 %collective-permute-done.40 = f32[72,384]{1,0:T(8,128)S(1)} collective-permute-done((f32[72,384]{1,0:T(8,128)S(1)}, f32[72,384]{1,0:T(8,128)S(1)}, u32[]{:S(2)}, u32[]{:S(2)}) %collective-permute-start.40) | collective-permute-done | bytes 110624 | tf_op jit(solution)/shard_map/ppermute | solution.py:17
  130.2 1.9 %collective-permute-done.41 = f32[72,384]{1,0:T(8,128)S(1)} collective-permute-done((f32[72,384]{1,0:T(8,128)S(1)}, f32[72,384]{1,0:T(8,128)S(1)}, u32[]{:S(2)}, u32[]{:S(2)}) %collective-permute-start.41) | collective-permute-done | bytes 110624 | tf_op jit(solution)/shard_map/ppermute | solution.py:17
  132.1 2.5 %collective-permute-done.42 = f32[72,384]{1,0:T(8,128)S(1)} collective-permute-done((f32[72,384]{1,0:T(8,128)S(1)}, f32[72,384]{1,0:T(8,128)S(1)}, u32[]{:S(2)}, u32[]{:S(2)}) %collective-permute-start.42) | collective-permute-done | bytes 110624 | tf_op jit(solution)/shard_map/ppermute | solution.py:17
  (100 shorter events, 19.7 us)
Async XLA Ops:
  0.6 11.4 %collective-permute-start.11 = (f32[16,64]{1,0:T(8,128)}, f32[16,64]{1,0:T(8,128)S(1)}, u32[]{:S(2)}, u32[]{:S(2)}) collective-permute-start(f32[16,64]{1,0:T(8,128)} %bitcast.15), channel_id=1, source_target_pairs={{0,32},{32,0},{64,96},{96,64},{128,160},{160,128},{192,224},{224,1... | collective-permute-start | bytes 12296 | tf_op jit(solution)/shard_map/ppermute | solution.py:17
  3.2 12.9 %collective-permute-start.12 = (f32[16,64]{1,0:T(8,128)}, f32[16,64]{1,0:T(8,128)S(1)}, u32[]{:S(2)}, u32[]{:S(2)}) collective-permute-start(f32[16,64]{1,0:T(8,128)} %bitcast.16), channel_id=1, source_target_pairs={{0,64},{32,96},{64,0},{96,32},{128,192},{160,224},{192,128},{224,1... | collective-permute-start | bytes 12296 | tf_op jit(solution)/shard_map/ppermute | solution.py:17
  6.2 9.9 %collective-permute-start.13 = (f32[16,64]{1,0:T(8,128)}, f32[16,64]{1,0:T(8,128)S(1)}, u32[]{:S(2)}, u32[]{:S(2)}) collective-permute-start(f32[16,64]{1,0:T(8,128)} %bitcast.17), channel_id=1, source_target_pairs={{0,96},{32,64},{64,32},{96,0},{128,224},{160,192},{192,160},{224,1... | collective-permute-start | bytes 12296 | tf_op jit(solution)/shard_map/ppermute | solution.py:17
  6.2 9.9 %collective-permute-start.14 = (f32[16,64]{1,0:T(8,128)}, f32[16,64]{1,0:T(8,128)S(1)}, u32[]{:S(2)}, u32[]{:S(2)}) collective-permute-start(f32[16,64]{1,0:T(8,128)} %bitcast.18), channel_id=1, source_target_pairs={{0,128},{32,160},{64,192},{96,224},{128,0},{160,32},{192,64},{224,... | collective-permute-start | bytes 12296 | tf_op jit(solution)/shard_map/ppermute | solution.py:17
  26.7 16.0 %collective-permute-start.20 = (f32[32,256]{1,0:T(8,128)S(1)}, f32[32,256]{1,0:T(8,128)S(1)}, u32[]{:S(2)}, u32[]{:S(2)}) collective-permute-start(f32[32,256]{1,0:T(8,128)S(1)} %pad_maximum_fusion.1), channel_id=1, source_target_pairs={{0,4},{1,17},{2,6},{3,19},{4,0},{5,21},{6,2},{7,23},{8,12},{9,25},... | collective-permute-start | bytes 98312 | tf_op jit(solution)/shard_map/ppermute | solution.py:27
  29.4 13.4 %collective-permute-start.21 = (f32[32,256]{1,0:T(8,128)S(1)}, f32[32,256]{1,0:T(8,128)S(1)}, u32[]{:S(2)}, u32[]{:S(2)}) collective-permute-start(f32[32,256]{1,0:T(8,128)S(1)} %pad_maximum_fusion.1), channel_id=1, source_target_pairs={{0,6},{1,25},{2,4},{3,27},{4,2},{5,29},{6,0},{7,31},{8,14},{9,17},... | collective-permute-start | bytes 98312 | tf_op jit(solution)/shard_map/ppermute | solution.py:27
  29.5 7.6 %collective-permute-start.2 = (f32[32,1024]{1,0:T(8,128)S(1)}, f32[32,1024]{1,0:T(8,128)S(1)}, u32[]{:S(2)}, u32[]{:S(2)}) collective-permute-start(f32[32,1024]{1,0:T(8,128)S(1)} %pad_maximum_fusion), channel_id=1, source_target_pairs={{0,4},{1,17},{2,6},{3,19},{4,0},{5,21},{6,2},{7,23},{8,12},{9,25},... | collective-permute-start | bytes 393224 | tf_op jit(solution)/shard_map/ppermute | solution.py:27
  38.8 30.1 %collective-permute-start.6 = (f32[128,1024]{1,0:T(8,128)S(1)}, f32[128,1024]{1,0:T(8,128)S(1)}, u32[]{:S(2)}, u32[]{:S(2)}) collective-permute-start(f32[128,1024]{1,0:T(8,128)S(1)} %constant_dynamic-update-slice_fusion.refs_0_), channel_id=1, source_target_pairs={{0,24},{1,7},{2,26},{3,5},{4,28},{5,3},{6,30},{7,1},{8,16},{9,15},... | collective-permute-start | bytes 1572872 | tf_op jit(solution)/shard_map/ppermute | solution.py:27
  41.1 28.0 %collective-permute-start.4 = (f32[128,1024]{1,0:T(8,128)S(1)}, f32[128,1024]{1,0:T(8,128)S(1)}, u32[]{:S(2)}, u32[]{:S(2)}) collective-permute-start(f32[128,1024]{1,0:T(8,128)S(1)} %constant_dynamic-update-slice_fusion.refs_0_), channel_id=1, source_target_pairs={{0,8},{1,3},{2,10},{3,1},{4,12},{5,7},{6,14},{7,5},{8,0},{9,11},{1... | collective-permute-start | bytes 1572872 | tf_op jit(solution)/shard_map/ppermute | solution.py:27
  41.1 28.4 %collective-permute-start.5 = (f32[128,1024]{1,0:T(8,128)S(1)}, f32[128,1024]{1,0:T(8,128)S(1)}, u32[]{:S(2)}, u32[]{:S(2)}) collective-permute-start(f32[128,1024]{1,0:T(8,128)S(1)} %constant_dynamic-update-slice_fusion.refs_0_), channel_id=1, source_target_pairs={{0,16},{1,5},{2,18},{3,7},{4,20},{5,1},{6,22},{7,3},{8,24},{9,13},... | collective-permute-start | bytes 1572872 | tf_op jit(solution)/shard_map/ppermute | solution.py:27
  42.8 13.6 %collective-permute-start.22 = (f32[128,256]{1,0:T(8,128)S(1)}, f32[128,256]{1,0:T(8,128)S(1)}, u32[]{:S(2)}, u32[]{:S(2)}) collective-permute-start(f32[128,256]{1,0:T(8,128)S(1)} %constant_dynamic-update-slice_fusion.5.refs_0_), channel_id=1, source_target_pairs={{0,8},{1,3},{2,10},{3,1},{4,12},{5,7},{6,14},{7,5},{8,0},{9,11},{1... | collective-permute-start | bytes 393224 | tf_op jit(solution)/shard_map/ppermute | solution.py:27
  42.9 15.2 %collective-permute-start.23 = (f32[128,256]{1,0:T(8,128)S(1)}, f32[128,256]{1,0:T(8,128)S(1)}, u32[]{:S(2)}, u32[]{:S(2)}) collective-permute-start(f32[128,256]{1,0:T(8,128)S(1)} %constant_dynamic-update-slice_fusion.5.refs_0_), channel_id=1, source_target_pairs={{0,16},{1,5},{2,18},{3,7},{4,20},{5,1},{6,22},{7,3},{8,24},{9,13},... | collective-permute-start | bytes 393224 | tf_op jit(solution)/shard_map/ppermute | solution.py:27
  58.0 8.9 %collective-permute-start.25 = (f32[128,256]{1,0:T(8,128)S(1)}, f32[128,256]{1,0:T(8,128)S(1)}, u32[]{:S(2)}, u32[]{:S(2)}) collective-permute-start(f32[128,256]{1,0:T(8,128)S(1)} %constant_dynamic-update-slice_fusion.5.refs_0_), channel_id=1, source_target_pairs={{0,1},{1,0},{2,3},{3,2},{4,5},{5,4},{6,7},{7,6},{8,9},{9,8},{10,11... | collective-permute-start | bytes 393224 | tf_op jit(solution)/shard_map/ppermute | solution.py:21
  61.6 6.3 %collective-permute-start.26 = (f32[128,256]{1,0:T(8,128)S(1)}, f32[128,256]{1,0:T(8,128)S(1)}, u32[]{:S(2)}, u32[]{:S(2)}) collective-permute-start(f32[128,256]{1,0:T(8,128)S(1)} %collective-permute-done.22.refs_1_), channel_id=1, source_target_pairs={{0,1},{1,0},{2,3},{3,2},{4,5},{5,4},{6,7},{7,6},{8,9},{9,8},{10,11... | collective-permute-start | bytes 393224 | tf_op jit(solution)/shard_map/ppermute | solution.py:21
  68.6 13.7 %collective-permute-start.7 = (f32[128,1024]{1,0:T(8,128)S(1)}, f32[128,1024]{1,0:T(8,128)S(1)}, u32[]{:S(2)}, u32[]{:S(2)}) collective-permute-start(f32[128,1024]{1,0:T(8,128)S(1)} %constant_dynamic-update-slice_fusion.refs_0_), channel_id=1, source_target_pairs={{0,1},{1,0},{2,3},{3,2},{4,5},{5,4},{6,7},{7,6},{8,9},{9,8},{10,11... | collective-permute-start | bytes 1572872 | tf_op jit(solution)/shard_map/ppermute | solution.py:21
  68.9 13.9 %collective-permute-start.10 = (f32[128,1024]{1,0:T(8,128)S(1)}, f32[128,1024]{1,0:T(8,128)S(1)}, u32[]{:S(2)}, u32[]{:S(2)}) collective-permute-start(f32[128,1024]{1,0:T(8,128)S(1)} %collective-permute-done.6.refs_3_), channel_id=1, source_target_pairs={{0,1},{1,0},{2,3},{3,2},{4,5},{5,4},{6,7},{7,6},{8,9},{9,8},{10,11... | collective-permute-start | bytes 1572872 | tf_op jit(solution)/shard_map/ppermute | solution.py:21
  69.1 15.4 %collective-permute-start.8 = (f32[128,1024]{1,0:T(8,128)S(1)}, f32[128,1024]{1,0:T(8,128)}, u32[]{:S(2)}, u32[]{:S(2)}) collective-permute-start(f32[128,1024]{1,0:T(8,128)S(1)} %collective-permute-done.4.refs_1_), channel_id=1, source_target_pairs={{0,1},{1,0},{2,3},{3,2},{4,5},{5,4},{6,7},{7,6},{8,9},{9,8},{10,11... | collective-permute-start | bytes 1572872 | tf_op jit(solution)/shard_map/ppermute | solution.py:21
  69.4 16.7 %collective-permute-start.9 = (f32[128,1024]{1,0:T(8,128)S(1)}, f32[128,1024]{1,0:T(8,128)}, u32[]{:S(2)}, u32[]{:S(2)}) collective-permute-start(f32[128,1024]{1,0:T(8,128)S(1)} %collective-permute-done.5.refs_2_), channel_id=1, source_target_pairs={{0,1},{1,0},{2,3},{3,2},{4,5},{5,4},{6,7},{7,6},{8,9},{9,8},{10,11... | collective-permute-start | bytes 1572872 | tf_op jit(solution)/shard_map/ppermute | solution.py:21
  72.7 29.8 %collective-permute-start.29 = (f32[64,384]{1,0:T(8,128)}, f32[64,384]{1,0:T(8,128)S(1)}, u32[]{:S(2)}, u32[]{:S(2)}) collective-permute-start(f32[64,384]{1,0:T(8,128)} %refs_0_.1), channel_id=1, source_target_pairs={{0,32},{32,0},{64,96},{96,64},{128,160},{160,128},{192,224},{224,1... | collective-permute-start | bytes 294920 | tf_op jit(solution)/shard_map/ppermute | solution.py:17
  82.3 21.0 %collective-permute-start.30 = (f32[64,384]{1,0:T(8,128)S(1)}, f32[64,384]{1,0:T(8,128)S(1)}, u32[]{:S(2)}, u32[]{:S(2)}) collective-permute-start(f32[64,384]{1,0:T(8,128)S(1)} %copy-done.9), channel_id=1, source_target_pairs={{0,64},{32,96},{64,0},{96,32},{128,192},{160,224},{192,128},{224,1... | collective-permute-start | bytes 294920 | tf_op jit(solution)/shard_map/ppermute | solution.py:17
  82.9 22.9 %collective-permute-start.31 = (f32[64,384]{1,0:T(8,128)S(1)}, f32[64,384]{1,0:T(8,128)S(1)}, u32[]{:S(2)}, u32[]{:S(2)}) collective-permute-start(f32[64,384]{1,0:T(8,128)S(1)} %copy-done.9), channel_id=1, source_target_pairs={{0,96},{32,64},{64,32},{96,0},{128,224},{160,192},{192,160},{224,1... | collective-permute-start | bytes 294920 | tf_op jit(solution)/shard_map/ppermute | solution.py:17
  84.5 22.7 %collective-permute-start.32 = (f32[64,384]{1,0:T(8,128)S(1)}, f32[64,384]{1,0:T(8,128)S(1)}, u32[]{:S(2)}, u32[]{:S(2)}) collective-permute-start(f32[64,384]{1,0:T(8,128)S(1)} %copy-done.9), channel_id=1, source_target_pairs={{0,128},{32,160},{64,192},{96,224},{128,0},{160,32},{192,64},{224,... | collective-permute-start | bytes 294920 | tf_op jit(solution)/shard_map/ppermute | solution.py:17
  86.1 21.7 %collective-permute-start.33 = (f32[64,384]{1,0:T(8,128)S(1)}, f32[64,384]{1,0:T(8,128)S(1)}, u32[]{:S(2)}, u32[]{:S(2)}) collective-permute-start(f32[64,384]{1,0:T(8,128)S(1)} %copy-done.9), channel_id=1, source_target_pairs={{0,160},{32,128},{64,224},{96,192},{128,32},{160,0},{192,96},{224,... | collective-permute-start | bytes 294920 | tf_op jit(solution)/shard_map/ppermute | solution.py:17
  102.5 7.0 %collective-permute-start.34 = (f32[64,384]{1,0:T(8,128)S(1)}, f32[64,384]{1,0:T(8,128)S(1)}, u32[]{:S(2)}, u32[]{:S(2)}) collective-permute-start(f32[64,384]{1,0:T(8,128)S(1)} %copy-done.9), channel_id=1, source_target_pairs={{0,192},{32,224},{64,128},{96,160},{128,64},{160,96},{192,0},{224,... | collective-permute-start | bytes 294920 | tf_op jit(solution)/shard_map/ppermute | solution.py:17
  103.4 11.6 %collective-permute-start.35 = (f32[64,384]{1,0:T(8,128)S(1)}, f32[64,384]{1,0:T(8,128)S(1)}, u32[]{:S(2)}, u32[]{:S(2)}) collective-permute-start(f32[64,384]{1,0:T(8,128)S(1)} %copy-done.9), channel_id=1, source_target_pairs={{0,224},{32,192},{64,160},{96,128},{128,96},{160,64},{192,32},{224... | collective-permute-start | bytes 294920 | tf_op jit(solution)/shard_map/ppermute | solution.py:17
  105.8 11.1 %collective-permute-start.36 = (f32[72,384]{1,0:T(8,128)S(1)}, f32[72,384]{1,0:T(8,128)S(1)}, u32[]{:S(2)}, u32[]{:S(2)}) collective-permute-start(f32[72,384]{1,0:T(8,128)S(1)} %get-tuple-element.21), channel_id=1, source_target_pairs={{0,32},{32,0},{64,96},{96,64},{128,160},{160,128},{192,224},{224,1... | collective-permute-start | bytes 331784 | tf_op jit(solution)/shard_map/ppermute | solution.py:17
  107.2 11.8 %collective-permute-start.37 = (f32[72,384]{1,0:T(8,128)S(1)}, f32[72,384]{1,0:T(8,128)S(1)}, u32[]{:S(2)}, u32[]{:S(2)}) collective-permute-start(f32[72,384]{1,0:T(8,128)S(1)} %get-tuple-element.22), channel_id=1, source_target_pairs={{0,64},{32,96},{64,0},{96,32},{128,192},{160,224},{192,128},{224,1... | collective-permute-start | bytes 331784 | tf_op jit(solution)/shard_map/ppermute | solution.py:17
  107.8 18.3 %collective-permute-start.38 = (f32[72,384]{1,0:T(8,128)S(1)}, f32[72,384]{1,0:T(8,128)S(1)}, u32[]{:S(2)}, u32[]{:S(2)}) collective-permute-start(f32[72,384]{1,0:T(8,128)S(1)} %get-tuple-element.23), channel_id=1, source_target_pairs={{0,96},{32,64},{64,32},{96,0},{128,224},{160,192},{192,160},{224,1... | collective-permute-start | bytes 331784 | tf_op jit(solution)/shard_map/ppermute | solution.py:17
  109.4 16.6 %collective-permute-start.39 = (f32[72,384]{1,0:T(8,128)S(1)}, f32[72,384]{1,0:T(8,128)S(1)}, u32[]{:S(2)}, u32[]{:S(2)}) collective-permute-start(f32[72,384]{1,0:T(8,128)S(1)} %get-tuple-element.24), channel_id=1, source_target_pairs={{0,128},{32,160},{64,192},{96,224},{128,0},{160,32},{192,64},{224,... | collective-permute-start | bytes 331784 | tf_op jit(solution)/shard_map/ppermute | solution.py:17
  115.0 15.2 %collective-permute-start.40 = (f32[72,384]{1,0:T(8,128)S(1)}, f32[72,384]{1,0:T(8,128)S(1)}, u32[]{:S(2)}, u32[]{:S(2)}) collective-permute-start(f32[72,384]{1,0:T(8,128)S(1)} %get-tuple-element.25), channel_id=1, source_target_pairs={{0,160},{32,128},{64,224},{96,192},{128,32},{160,0},{192,96},{224,... | collective-permute-start | bytes 331784 | tf_op jit(solution)/shard_map/ppermute | solution.py:17
  116.9 15.2 %collective-permute-start.41 = (f32[72,384]{1,0:T(8,128)S(1)}, f32[72,384]{1,0:T(8,128)S(1)}, u32[]{:S(2)}, u32[]{:S(2)}) collective-permute-start(f32[72,384]{1,0:T(8,128)S(1)} %get-tuple-element.26), channel_id=1, source_target_pairs={{0,192},{32,224},{64,128},{96,160},{128,64},{160,96},{192,0},{224,... | collective-permute-start | bytes 331784 | tf_op jit(solution)/shard_map/ppermute | solution.py:17
  119.0 15.6 %collective-permute-start.42 = (f32[72,384]{1,0:T(8,128)S(1)}, f32[72,384]{1,0:T(8,128)S(1)}, u32[]{:S(2)}, u32[]{:S(2)}) collective-permute-start(f32[72,384]{1,0:T(8,128)S(1)} %get-tuple-element.27), channel_id=1, source_target_pairs={{0,224},{32,192},{64,160},{96,128},{128,96},{160,64},{192,32},{224... | collective-permute-start | bytes 331784 | tf_op jit(solution)/shard_map/ppermute | solution.py:17
  (23 other events, 156.1 us)

commit v2 on v1

v2 whole, which is shorter than its diff:
```python
import jax
import jax.numpy as jnp
from jax import lax
from jax.experimental import pallas as pl
from jax.experimental.pallas import tpu as pltpu
from jax.sharding import PartitionSpec as P

F32 = jnp.float32
BF16 = jnp.bfloat16
ROWS = 8
COLS = 32
B = 512
MIB = 1 << 20


def with_row_partner(v, k):
    return lax.ppermute(v, "row", [(i, i ^ k) for i in range(ROWS)])


def with_sibling(v):
    return lax.ppermute(v, "col", [(i, i ^ 1) for i in range(COLS)])


def with_neighbour(v):
    perm = []
    for r in range(ROWS):
        for c in range(COLS):
            to = r ^ 1 if c % 2 == 0 else (r - 1 + 2 * (r % 2)) % ROWS
            perm.append((r * COLS + c, to * COLS + c))
    return lax.ppermute(v, ("row", "col"), perm)


def with_col_partner(v, phase, k):
    shift = {0: 1, 1: 3}
    perm = [(i, i ^ (k << shift[phase ^ (i & 1)])) for i in range(COLS)]
    return lax.ppermute(v, "col", perm)


def gather_cols(diag, grad, core):
    wide, narrow = grad.shape[1] // 2, diag.shape[1] // 2
    low = jnp.concatenate([grad[:, :wide], diag[:, :narrow]], axis=1)
    high = jnp.concatenate([grad[:, wide:], diag[:, narrow:]], axis=1)
    kept = jnp.where(core == 0, low, high)
    given = jnp.where(core == 0, high, low)
    pair = jnp.concatenate([kept, with_sibling(given)], axis=0)
    pairs = [pair] + [with_col_partner(pair, 0, k) for k in (1, 2, 3)]
    diag_quad = jnp.concatenate([p[:, wide:] for p in pairs], axis=0)
    grad_quad = jnp.concatenate([p[:, :wide] for p in pairs], axis=0)
    diag_blocks = [diag_quad] + [with_col_partner(diag_quad, 1, k) for k in (1, 2, 3)]
    grad_quad, diag_blocks = lax.optimization_barrier((grad_quad, diag_blocks))
    diag_blocks = diag_blocks + [with_sibling(b) for b in diag_blocks]
    return diag_blocks, grad_quad, [with_col_partner(grad_quad, 1, k) for k in (1, 2, 3)]


def place(ids, blocks, store):
    y, x, core = ids[1], ids[2], ids[3]
    for other in range(2):
        half = core ^ other
        for k, block in enumerate(blocks[4 * other : 4 * other + 4]):
            for j in range(4):
                along_x = jnp.where(half == 0, x ^ j, x ^ k)
                along_y = jnp.where(half == 0, y ^ k, y ^ j)
                for r in range(2):
                    row = (along_y * 8 + along_x * 2 + (half ^ r)) * 16
                    at = (j * 2 + r) * 16
                    store(half, pl.multiple_of(row, 16), block[at : at + 16, :])


def split(v):
    high = v.astype(BF16)
    return high, (v - high.astype(F32)).astype(BF16)


def dot(a, b):
    return lax.dot_general(a, b, (((1,), (0,)), ((), ())), preferred_element_type=F32)


def dot_full(a, b):
    return lax.dot_general(
        a, b, (((1,), (0,)), ((), ())), precision=lax.Precision.HIGHEST, preferred_element_type=F32
    )


def invert_kernel(ids, *refs):
    blocks = refs[:8]
    top_out, low_out, held = refs[8:]

    odd = jnp.broadcast_to(ids[0] % 2, (16, 128)) == 1

    def store(half, row, piece):
        for q in range(2):
            lanes = piece[:, 128 * q : 128 * q + 128]
            swapped = jnp.concatenate([lanes[:, 64:], lanes[:, :64]], axis=1)
            held[(half * 2 + q) ^ (ids[0] // 2), pl.ds(row, 16), :] = jnp.where(odd, swapped, lanes)

    place(ids, blocks, store)

    def part(r, c, n):
        return jnp.concatenate([held[c // 128 + q, r : r + n, :] for q in range(n // 128)], axis=1)

    n = 128
    rows = lax.broadcasted_iota(jnp.int32, (n, n), 0)
    cols = lax.broadcasted_iota(jnp.int32, (n, n), 1)
    in_block = rows // 16 == cols // 16
    diag = [part(n * g, n * g, n) for g in range(4)]
    packed = []
    for d in diag:
        kept = jnp.where(in_block, d, 0.0)
        packed.append(sum(kept[16 * b : 16 * b + 16, :] for b in range(1, 8)) + kept[0:16, :])
    packed = jnp.concatenate(packed, axis=0)
    sub = lax.broadcasted_iota(jnp.int32, (64, n), 0) % 16
    lane = lax.broadcasted_iota(jnp.int32, (64, n), 1) % 16
    inverse = jnp.where(sub == lane, 1.0, 0.0).astype(F32)
    spread = []
    for k in range(16):
        pick = jnp.where(in_block & (rows % 16 == k), 1.0, 0.0).astype(F32)
        spread.append(dot_full(packed, pick))
    for k in range(15, -1, -1):
        factor = spread[k]
        pivot = []
        for g in range(4):
            at = 16 * g + k
            row = inverse[at : at + 1, :] / factor[at : at + 1, :]
            pivot.append(jnp.broadcast_to(row, (16, n)))
        pivot = jnp.concatenate(pivot, axis=0)
        inverse = jnp.where(sub == k, pivot, inverse - jnp.where(sub < k, factor, 0.0) * pivot)
    blocks = []
    for g in range(4):
        tall = jnp.concatenate([inverse[16 * g : 16 * g + 16, :]] * 8, axis=0)
        blocks.append(jnp.where(in_block, tall, 0.0))
    for b in (16, 32, 64):
        off = (rows // (2 * b) == cols // (2 * b)) & (rows // b < cols // b)
        lefts = [dot_full(blocks[g], jnp.where(off, diag[g], 0.0)) for g in range(4)]
        blocks = [blocks[g] - dot_full(lefts[g], blocks[g]) for g in range(4)]
    pairs = []
    for g in (0, 2):
        corner = -dot_full(dot_full(blocks[g], part(n * g, n * g + n, n)), blocks[g + 1])
        top = jnp.concatenate([blocks[g], corner], axis=1)
        low = jnp.concatenate([jnp.zeros_like(corner), blocks[g + 1]], axis=1)
        pairs.append(jnp.concatenate([top, low], axis=0))
    corner = -dot_full(dot_full(pairs[0], part(0, 256, 256)), pairs[1])
    for at, out, m in ((0, top_out, pairs[0]), (768, top_out, corner), (0, low_out, pairs[1])):
        high, low = split(m)
        out[:, at : at + 256] = high
        out[:, at + 256 : at + 512] = high
        out[:, at + 512 : at + 768] = low


def split_kernel(trailing, panel, out):
    n = trailing.shape[0]
    side = jnp.concatenate([panel[...], jnp.zeros((112, n), F32)], axis=0).T
    for v, lanes in ((trailing[...], slice(0, 384)), (side, slice(384, 512))):
        high, low = split(v)
        out[0:n, lanes] = high
        out[n : 2 * n, lanes] = low
        out[2 * n : 3 * n, lanes] = high


def solve_kernel(ids, *refs):
    blocks = refs[:8]
    inv_top, inv_low, tall = refs[8:11]
    solved_out, own_out, given_out = refs[11:14]
    kept_outs = refs[14:18]
    g, xs, total, corner = refs[18:]

    def store(half, row, piece):
        high, low = split(piece)
        row = pl.multiple_of(jnp.where(row < 256, row, row + 512), 16)
        g[half, pl.ds(row, 16), :] = high
        g[half, pl.ds(row + 256, 16), :] = low
        g[half, pl.ds(row + 512, 16), :] = high

    place(ids, blocks, store)
    n = TILE
    for t in range(2048 // n):
        half, lane = divmod(t * n, 1024)
        slot = t % 2
        rhs = g[half, :, lane : lane + n]
        for rows, lhs, k in ((slice(0, 256), inv_top, 0), (slice(256, 512), inv_low, 768)):
            x = dot(lhs[...], g[half, k:, lane : lane + n])
            solved_out[rows, t * n : t * n + n] = x
            high, low = split(x)
            xs[slot, rows, 0:n] = high
            xs[slot, rows, n : 2 * n] = high
            xs[slot, rows, 2 * n : 3 * n] = low
        term = dot(xs[slot], tall[3 * n * t : 3 * n * t + 3 * n, :])
        if t == 0:
            total[...] = term
        else:
            total[...] += term

    own = pl.ds(pl.multiple_of(ids[4] * 16, 16), 16)
    own_out[...] = solved_out[own, :]
    corner[...] = jnp.zeros_like(corner)
    summed = total[:, 384:512].T
    for t in range(ROWS):
        corner[t, :, 0:64] = summed[0:8, 64 * t : 64 * t + 64]
        corner[t, :, 64:128] = summed[8:16, 64 * t : 64 * t + 64]
    for j in range(4):
        for first, out, at in ((ids[5], given_out, 72 * j), (ids[0], kept_outs[j], 0)):
            target = first ^ (2 * j)
            out[at : at + 64, :] = total[pl.ds(pl.multiple_of(target * 64, 64), 64), 0:384]
            out[at + 64 : at + 72, :] = corner[target]


def trailing_kernel(ids, *refs):
    own_parity, other_parity = refs[:4], refs[4]
    solved, grad, out, rs = refs[5:]

    @pl.when(pl.program_id(0) == 0)
    def _():
        for j in range(4):
            for first, piece in ((ids[0], own_parity[j][...]), (ids[5], other_parity[64 * j : 64 * j + 64, :])):
                high, low = split(piece)
                row = (first ^ (2 * j)) * 64
                rs[pl.ds(pl.multiple_of(row, 64), 64), :] = high
                rs[pl.ds(pl.multiple_of(row + 512, 64), 64), :] = low
                rs[pl.ds(pl.multiple_of(row + 1024, 64), 64), :] = high

    high, low = split(solved[...].T)
    out[...] = grad[...] - dot(jnp.concatenate([high, high, low], axis=1), rs[...])


TILE = 512
SMEM = pl.BlockSpec(memory_space=pltpu.SMEM)
VMEM = pl.BlockSpec(memory_space=pltpu.VMEM)


def shape(dims, dtype=F32):
    return jax.ShapeDtypeStruct(dims, dtype)


def invert(ids, blocks):
    return pl.pallas_call(
        invert_kernel,
        out_shape=[shape((256, 1536), BF16), shape((256, 768), BF16)],
        in_specs=[SMEM] + [VMEM] * 8,
        out_specs=[VMEM] * 2,
        scratch_shapes=[pltpu.VMEM((4, B, 128), F32)],
        compiler_params=pltpu.CompilerParams(vmem_limit_bytes=10 * MIB),
        cost_estimate=pl.CostEstimate(flops=4_000_000_000, bytes_accessed=2 * MIB, transcendentals=0),
        name="invert",
    )(ids, *blocks)


def split_tall(trailing, panel):
    n = TILE
    return pl.pallas_call(
        split_kernel,
        grid=(2048 // n,),
        out_shape=shape((3 * 2048, 512), BF16),
        in_specs=[pl.BlockSpec((n, 384), lambda i: (i, 0)), pl.BlockSpec((16, n), lambda i: (0, i))],
        out_specs=pl.BlockSpec((3 * n, 512), lambda i: (i, 0)),
        compiler_params=pltpu.CompilerParams(vmem_limit_bytes=10 * MIB),
        cost_estimate=pl.CostEstimate(flops=3_000_000_000, bytes_accessed=9 * MIB, transcendentals=0),
        name="split_tall",
    )(trailing, panel)


def solve(ids, blocks, inverse, tall):
    return pl.pallas_call(
        solve_kernel,
        out_shape=[shape((B, 2048)), shape((16, 2048)), shape((288, 384))] + [shape((72, 384))] * 4,
        in_specs=[SMEM] + [VMEM] * 11,
        out_specs=[VMEM] * 7,
        scratch_shapes=[
            pltpu.VMEM((2, 3 * B, 1024), BF16),
            pltpu.VMEM((2, B, 3 * TILE), BF16),
            pltpu.VMEM((B, 512), F32),
            pltpu.VMEM((ROWS, 8, 384), F32),
        ],
        compiler_params=pltpu.CompilerParams(vmem_limit_bytes=24 * MIB),
        cost_estimate=pl.CostEstimate(flops=6_000_000_000, bytes_accessed=12 * MIB, transcendentals=0),
        name="solve",
    )(ids, *blocks, *inverse, tall)


def trailing_update(ids, pieces, solved, grad):
    tile = 256
    return pl.pallas_call(
        trailing_kernel,
        grid=(2048 // tile,),
        out_shape=shape((2048, 384)),
        in_specs=[SMEM]
        + [pl.BlockSpec((64, 384), lambda i: (0, 0))] * 4
        + [pl.BlockSpec((256, 384), lambda i: (0, 0))]
        + [pl.BlockSpec((B, tile), lambda i: (0, i)), pl.BlockSpec((tile, 384), lambda i: (i, 0))],
        out_specs=pl.BlockSpec((tile, 384), lambda i: (i, 0)),
        scratch_shapes=[pltpu.VMEM((3 * B, 384), BF16)],
        compiler_params=pltpu.CompilerParams(vmem_limit_bytes=10 * MIB),
        cost_estimate=pl.CostEstimate(flops=4_000_000_000, bytes_accessed=11 * MIB, transcendentals=0),
        name="trailing",
    )(ids, *pieces, solved, grad)


def on_device(
    diag_factor,
    panel_factor,
    row_factor,
    trailing_factor,
    panel_grad,
    diag_grad,
    row_grad,
    trailing_grad,
):
    z = lax.axis_index("row")
    col = lax.axis_index("col")
    core = col % 2
    neighbour = jnp.where(core == 0, z ^ 1, (z - 1 + 2 * (z % 2)) % ROWS)
    ids = jnp.stack([z, col // 8, (col // 2) % 4, core, col, neighbour]).astype(jnp.int32)

    tile = diag_factor.T
    even = [tile] + [with_row_partner(tile, k) for k in (2, 4, 6)]
    odd = with_row_partner(jnp.concatenate(even, axis=1), 1)
    tiles = [t for j in range(4) for t in (even[j], odd[:, 64 * j : 64 * j + 64])]
    diag_chunk = jnp.concatenate(tiles, axis=1)
    diag_blocks, grad_quad, grad_far = gather_cols(diag_chunk, panel_grad.T, core)
    quad_swapped = with_sibling(grad_quad)

    row_factor, diag_blocks = lax.optimization_barrier((row_factor, diag_blocks))
    row_pieces = [row_factor] + [with_row_partner(row_factor, k) for k in (2, 4, 6)]
    inverse = invert(ids, diag_blocks)
    tall = split_tall(trailing_factor, panel_factor.T)
    grad_far, row_pieces, inverse, tall = lax.optimization_barrier((grad_far, row_pieces, inverse, tall))
    row_pieces = row_pieces + [with_neighbour(jnp.concatenate(row_pieces, axis=0))]
    grad_blocks = [grad_quad] + grad_far + [quad_swapped] + [with_sibling(b) for b in grad_far]
    solved, own, given, *kept = solve(ids, grad_blocks, inverse, tall)
    taken = with_neighbour(given)
    sums = [kept[j] + taken[72 * j : 72 * j + 72] for j in range(4)]
    came = [with_row_partner(sums[j], 2 * j) for j in range(1, 4)]
    trailing_out = trailing_update(ids, row_pieces, solved, trailing_grad)

    total = sums[0] + (came[0] + came[1] + came[2])
    row_out = row_grad - total[0:64, :]
    diag_sum = jnp.concatenate([total[64:72, 0:64], total[64:72, 64:128]], axis=0)
    global_rows = z * 64 + jnp.arange(64)[None, :]
    global_cols = col * 16 + jnp.arange(16)[:, None]
    diag_out = jnp.where(global_rows >= global_cols, diag_grad.T - diag_sum, jnp.float32(0.0))
    return (own.T, trailing_out, row_out, diag_out.T)


def solution(mesh):
    both = P("row", "col")
    return jax.shard_map(
        on_device,
        mesh=mesh,
        in_specs=(both,) * 8,
        out_specs=(both,) * 4,
        check_vma=False,
    )
```

time: 136 us -> 109 us (0.80)
  starting transfers between devices: 66.9 us -> 45.6 us
  waiting for transfers between devices: 34.8 us -> 26 us
  local copies, waits for them, and re-layouts: 4.91 us -> 12.3 us
  Pallas kernels: 25.5 us -> 21 us
    ppermute x21 -> x10, starting transfers between devices: 37.5 us -> 21.2 us  [with_row_partner(): return lax.ppermute(v, 'row', [(i, i ^ k) for i in range(ROWS)])]
    ppermute x21 -> x10, waiting for transfers between devices: 15.8 us -> 5.78 us  [with_row_partner(): return lax.ppermute(v, 'row', [(i, i ^ k) for i in range(ROWS)])]
    ppermute x12 -> x9, waiting for transfers between devices: 16.7 us -> 10.1 us  [with_col_partner(): return lax.ppermute(v, 'col', perm)]
    ppermute x0 -> x2, waiting for transfers between devices: none -> 5.57 us  [with_neighbour(): return lax.ppermute(v, ('row', 'col'), perm)]
    unnamed x30 -> x24, local copies, waits for them, and re-layouts: 4.74 us -> 10.3 us
    pallas_call x1, Pallas kernels: 13.2 us -> 7.68 us  [solve(): pl.pallas_call(solve_kernel, out_shape=[shape((B, 2048)), shape((16, 2048...]
    ppermute x12 -> x9, starting transfers between devices: 15.8 us -> 11.3 us  [with_col_partner(): return lax.ppermute(v, 'col', perm)]
    ppermute x10 -> x9, starting transfers between devices: 13.7 us -> 10.3 us  [with_sibling(): return lax.ppermute(v, 'col', [(i, i ^ 1) for i in range(COLS)])]
  transfers between devices with their start and end apart: 43 -> 30, of which waited for: 12 -> 16; matrix products, arithmetic and copies ran while one was open for 1% -> 1% of each run, Pallas kernels for 19% -> 12%
where the time goes in v2:
time: 109 us; the launch traced here: 108 us
  starting transfers between devices  45.6 us (42%)
  waiting for transfers between devices  26 us (24%)
  Pallas kernels  21 us (19%)
  local copies, waits for them, and re-layouts  12.3 us (11%)
  other arithmetic  2.3 us (2%)
    ppermute x10, starting transfers between devices, with_row_partner(): return lax.ppermute(v, 'row', [(i, i ^ k) for i in range(ROWS)])  21.2 us
    ppermute x9, starting transfers between devices, with_col_partner(): return lax.ppermute(v, 'col', perm)  11.3 us
    unnamed x24, local copies, waits for them, and re-layouts  10.3 us
    ppermute x9, starting transfers between devices, with_sibling(): return lax.ppermute(v, 'col', [(i, i ^ 1) for i in range(COLS)])  10.3 us
    ppermute x9, waiting for transfers between devices, with_col_partner(): return lax.ppermute(v, 'col', perm)  10.1 us
    pallas_call x1, Pallas kernels, solve(): pl.pallas_call(solve_kernel, out_shape=[shape((B, 2048)), shape((16, 2048...  7.68 us
    pallas_call x1, Pallas kernels, trailing_update(): pl.pallas_call(trailing_kernel, grid=(2048 // tile,), out_shape=shape((20...  7 us
    ppermute x10, waiting for transfers between devices, with_row_partner(): return lax.ppermute(v, 'row', [(i, i ^ k) for i in range(ROWS)])  5.78 us
  transfers between devices with their start and end apart: 30, of which 16 were waited for; matrix products, arithmetic and copies ran while one was open for 1% of the time, Pallas kernels for 12%

profile of v2, /device:TPU:1, one launch (start us, length us, event | category | flops | bytes accessed | tf_op | source)
XLA Modules:
  0.0 107.9 jit_solution(1092491539409067608)
XLA Ops:
  0.7 3.9 %collective-permute-start = (f32[16,64]{1,0:T(8,128)}, f32[16,64]{1,0:T(8,128)S(1)}, u32[]{:S(2)}, u32[]{:S(2)}) collective-permute-start(f32[16,64]{1,0:T(8,128)} %bitcast.16), channel_id=1, source_target_pairs={{0,64},{32,96},{64,0},{96,32},{128,192},{160,224},{192,128},{224,1... | collective-permute-start | bytes 12296 | tf_op jit(solution)/shard_map/ppermute | solution.py:17
  4.6 5.1 %collective-permute-start.1 = (f32[16,64]{1,0:T(8,128)}, f32[16,64]{1,0:T(8,128)S(1)}, u32[]{:S(2)}, u32[]{:S(2)}) collective-permute-start(f32[16,64]{1,0:T(8,128)} %bitcast.17), channel_id=1, source_target_pairs={{0,128},{32,160},{64,192},{96,224},{128,0},{160,32},{192,64},{224,... | collective-permute-start | bytes 12296 | tf_op jit(solution)/shard_map/ppermute | solution.py:17
  9.7 1.5 %collective-permute-done.1 = f32[16,64]{1,0:T(8,128)S(1)} collective-permute-done((f32[16,64]{1,0:T(8,128)}, f32[16,64]{1,0:T(8,128)S(1)}, u32[]{:S(2)}, u32[]{:S(2)}) %collective-permute-start.1) | collective-permute-done | bytes 4128 | tf_op jit(solution)/shard_map/ppermute | solution.py:17
  11.2 3.3 %collective-permute-done.2 = f32[16,64]{1,0:T(8,128)S(1)} collective-permute-done((f32[16,64]{1,0:T(8,128)}, f32[16,64]{1,0:T(8,128)S(1)}, u32[]{:S(2)}, u32[]{:S(2)}) %collective-permute-start.2) | collective-permute-done | bytes 4128 | tf_op jit(solution)/shard_map/ppermute | solution.py:17
  18.8 3.6 %collective-permute-start.4 = (f32[16,1280]{1,0:T(8,128)S(1)}, f32[16,1280]{1,0:T(8,128)S(1)}, u32[]{:S(2)}, u32[]{:S(2)}) collective-permute-start(f32[16,1280]{1,0:T(8,128)S(1)} %get-tuple-element.74), channel_id=1, source_target_pairs={{0,1},{1,0},{2,3},{3,2},{4,5},{5,4},{6,7},{7,6},{8,9},{9,8},{10,11... | collective-permute-start | bytes 245768 | tf_op jit(solution)/shard_map/ppermute | solution.py:21
  23.4 1.4 %collective-permute-start.5 = (f32[32,1280]{1,0:T(8,128)S(1)}, f32[32,1280]{1,0:T(8,128)S(1)}, u32[]{:S(2)}, u32[]{:S(2)}) collective-permute-start(f32[32,1280]{1,0:T(8,128)S(1)} %pad_maximum_fusion.2), channel_id=1, source_target_pairs={{0,2},{1,9},{2,0},{3,11},{4,6},{5,13},{6,4},{7,15},{8,10},{9,1},{1... | collective-permute-start | bytes 491528 | tf_op jit(solution)/shard_map/ppermute | solution.py:36
  24.8 2.6 %collective-permute-start.6 = (f32[32,1280]{1,0:T(8,128)S(1)}, f32[32,1280]{1,0:T(8,128)S(1)}, u32[]{:S(2)}, u32[]{:S(2)}) collective-permute-start(f32[32,1280]{1,0:T(8,128)S(1)} %pad_maximum_fusion.2), channel_id=1, source_target_pairs={{0,4},{1,17},{2,6},{3,19},{4,0},{5,21},{6,2},{7,23},{8,12},{9,25},... | collective-permute-start | bytes 491528 | tf_op jit(solution)/shard_map/ppermute | solution.py:36
  27.9 4.2 %collective-permute-done.6 = f32[32,1280]{1,0:T(8,128)S(1)} collective-permute-done((f32[32,1280]{1,0:T(8,128)S(1)}, f32[32,1280]{1,0:T(8,128)S(1)}, u32[]{:S(2)}, u32[]{:S(2)}) %collective-permute-start.6) | collective-permute-done | bytes 163872 | tf_op jit(solution)/shard_map/ppermute | solution.py:36
  32.2 1.8 %collective-permute-done.7 = f32[32,1280]{1,0:T(8,128)S(1)} collective-permute-done((f32[32,1280]{1,0:T(8,128)S(1)}, f32[32,1280]{1,0:T(8,128)S(1)}, u32[]{:S(2)}, u32[]{:S(2)}) %collective-permute-start.7) | collective-permute-done | bytes 163872 | tf_op jit(solution)/shard_map/ppermute | solution.py:36
  33.9 2.3 %collective-permute-start.10 = (f32[128,256]{1,0:T(8,128)S(1)}, f32[128,256]{1,0:T(8,128)S(1)}, u32[]{:S(2)}, u32[]{:S(2)}) collective-permute-start(f32[128,256]{1,0:T(8,128)S(1)} %pad_maximum_fusion.3.refs_0_), channel_id=1, source_target_pairs={{0,24},{1,7},{2,26},{3,5},{4,28},{5,3},{6,30},{7,1},{8,16},{9,15},... | collective-permute-start | bytes 393224 | tf_op jit(solution)/shard_map/ppermute | solution.py:36
  36.2 1.7 %collective-permute-start.9 = (f32[128,256]{1,0:T(8,128)S(1)}, f32[128,256]{1,0:T(8,128)S(1)}, u32[]{:S(2)}, u32[]{:S(2)}) collective-permute-start(f32[128,256]{1,0:T(8,128)S(1)} %pad_maximum_fusion.3.refs_0_), channel_id=1, source_target_pairs={{0,16},{1,5},{2,18},{3,7},{4,20},{5,1},{6,22},{7,3},{8,24},{9,13},... | collective-permute-start | bytes 393224 | tf_op jit(solution)/shard_map/ppermute | solution.py:36
  39.0 1.3 %collective-permute-done.8.refs_1_ = f32[128,256]{1,0:T(8,128)S(1)} collective-permute-done((f32[128,256]{1,0:T(8,128)S(1)}, f32[128,256]{1,0:T(8,128)S(1)}, u32[]{:S(2)}, u32[]{:S(2)}) %collective-permute-start.8) | collective-permute-done | bytes 131104 | tf_op jit(solution)/shard_map/ppermute | solution.py:36
  40.3 1.3 %collective-permute-done.9.refs_2_ = f32[128,256]{1,0:T(8,128)S(1)} collective-permute-done((f32[128,256]{1,0:T(8,128)S(1)}, f32[128,256]{1,0:T(8,128)S(1)}, u32[]{:S(2)}, u32[]{:S(2)}) %collective-permute-start.9) | collective-permute-done | bytes 131104 | tf_op jit(solution)/shard_map/ppermute | solution.py:36
  41.6 3.0 %collective-permute-start.14 = (f32[128,256]{1,0:T(8,128)S(1)}, f32[128,256]{1,0:T(8,128)S(1)}, u32[]{:S(2)}, u32[]{:S(2)}) collective-permute-start(f32[128,256]{1,0:T(8,128)S(1)} %pad_maximum_fusion.3.refs_0_), channel_id=1, source_target_pairs={{0,1},{1,0},{2,3},{3,2},{4,5},{5,4},{6,7},{7,6},{8,9},{9,8},{10,11... | collective-permute-start | bytes 393224 | tf_op jit(solution)/shard_map/ppermute | solution.py:21
  45.6 1.6 %collective-permute-start.12 = (f32[128,1024]{1,0:T(8,128)S(1)}, f32[128,1024]{1,0:T(8,128)S(1)}, u32[]{:S(2)}, u32[]{:S(2)}) collective-permute-start(f32[128,1024]{1,0:T(8,128)S(1)} %pad_maximum_fusion.refs_0_), channel_id=1, source_target_pairs={{0,16},{1,5},{2,18},{3,7},{4,20},{5,1},{6,22},{7,3},{8,24},{9,13},... | collective-permute-start | bytes 1572872 | tf_op jit(solution)/shard_map/ppermute | solution.py:36
  47.2 1.8 %collective-permute-start.13 = (f32[128,1024]{1,0:T(8,128)S(1)}, f32[128,1024]{1,0:T(8,128)S(1)}, u32[]{:S(2)}, u32[]{:S(2)}) collective-permute-start(f32[128,1024]{1,0:T(8,128)S(1)} %pad_maximum_fusion.refs_0_), channel_id=1, source_target_pairs={{0,24},{1,7},{2,26},{3,5},{4,28},{5,3},{6,30},{7,1},{8,16},{9,15},... | collective-permute-start | bytes 1572872 | tf_op jit(solution)/shard_map/ppermute | solution.py:36
  50.8 1.5 %split_tall.1.refs_10_ = bf16[6144,512]{1,0:T(8,128)(2,1)S(1)} custom-call(f32[2048,384]{1,0:T(8,128)S(1)} %copy-done.1, f32[16,2048]{1,0:T(8,128)S(1)} %bitcast.14), custom_call_target="tpu_custom_call" | custom-call | flops 3000000000 | bytes 9437184 | tf_op jit(solution)/shard_map/split_tall/pallas_call | solution.py:248
  52.3 2.7 %copy-done.6 = bf16[6144,512]{1,0:T(8,128)(2,1)} copy-done((bf16[6144,512]{1,0:T(8,128)(2,1)}, bf16[6144,512]{1,0:T(8,128)(2,1)S(1)}, u32[]{:S(2)}) %copy-start.6) | copy-done | bytes 6291480
  55.1 1.5 %collective-permute-start.19 = (f32[64,384]{1,0:T(8,128)S(1)}, f32[64,384]{1,0:T(8,128)S(1)}, u32[]{:S(2)}, u32[]{:S(2)}) collective-permute-start(f32[64,384]{1,0:T(8,128)S(1)} %copy-done), channel_id=1, source_target_pairs={{0,128},{32,160},{64,192},{96,224},{128,0},{160,32},{192,64},{224,... | collective-permute-start | bytes 294920 | tf_op jit(solution)/shard_map/ppermute | solution.py:17
  56.6 3.0 %collective-permute-start.20 = (f32[64,384]{1,0:T(8,128)S(1)}, f32[64,384]{1,0:T(8,128)S(1)}, u32[]{:S(2)}, u32[]{:S(2)}) collective-permute-start(f32[64,384]{1,0:T(8,128)S(1)} %copy-done), channel_id=1, source_target_pairs={{0,192},{32,224},{64,128},{96,160},{128,64},{160,96},{192,0},{224,... | collective-permute-start | bytes 294920 | tf_op jit(solution)/shard_map/ppermute | solution.py:17
  60.5 4.8 %invert.1 = (bf16[256,1536]{1,0:T(8,128)(2,1)S(1)}, bf16[256,768]{1,0:T(8,128)(2,1)S(1)}) custom-call(s32[6]{0:T(128)S(1)} %stack.27.ids, f32[128,256]{1,0:T(8,128)S(1)} %pad_maximum_fusion.3.refs_0_, f32[128,256]{1,0:T(8,128)S(1)} %collective-permute-done.8.refs_1_, f32[128,256]{1,0:T(8,128)S(1)} %collective-permute-done.9.refs_2_, ...), custom_call_target="tpu_custom_call" | custom-call | flops 4000000000 | bytes 2097152 | tf_op jit(solution)/shard_map/invert/pallas_call | solution.py:234
  65.3 2.5 %collective-permute-start.21 = (f32[128,1024]{1,0:T(8,128)S(1)}, f32[128,1024]{1,0:T(8,128)S(1)}, u32[]{:S(2)}, u32[]{:S(2)}) collective-permute-start(f32[128,1024]{1,0:T(8,128)S(1)} %pad_maximum_fusion.refs_0_), channel_id=1, source_target_pairs={{0,1},{1,0},{2,3},{3,2},{4,5},{5,4},{6,7},{7,6},{8,9},{9,8},{10,11... | collective-permute-start | bytes 1572872 | tf_op jit(solution)/shard_map/ppermute | solution.py:21
  71.5 7.7 %solve.1 = (f32[512,2048]{1,0:T(8,128)S(1)}, f32[16,2048]{1,0:T(8,128)}, f32[288,384]{1,0:T(8,128)S(1)}, f32[72,384]{1,0:T(8,128)S(1)}, f32[72,384]{1,0:T(8,128)...) custom-call(s32[6]{0:T(128)S(1)} %stack.27.ids, f32[128,1024]{1,0:T(8,128)S(1)} %pad_maximum_fusion.refs_0_, ...), custom_call_target="tpu_custom_call" | custom-call | flops 6000000000 | bytes 12582912 | tf_op jit(solution)/shard_map/solve/pallas_call | solution.py:261
  79.2 2.0 %copy-done.8 = f32[512,2048]{1,0:T(8,128)} copy-done((f32[512,2048]{1,0:T(8,128)}, f32[512,2048]{1,0:T(8,128)S(1)}, u32[]{:S(2)}) %copy-start.8) | copy-done | bytes 4194328
  81.7 2.3 %collective-permute-start.25 = (f32[256,384]{1,0:T(8,128)S(1)}, f32[256,384]{1,0:T(8,128)S(1)}, u32[]{:S(2)}, u32[]{:S(2)}) collective-permute-start(f32[256,384]{1,0:T(8,128)S(1)} %pad_maximum_fusion.1), channel_id=1, source_target_pairs={{0,32},{1,225},{2,34},{3,227},{4,36},{5,229},{6,38},{7,231},{8,40}... | collective-permute-start | bytes 1179656 | tf_op jit(solution)/shard_map/ppermute | solution.py:30
  84.0 5.6 %collective-permute-done.26 = f32[288,384]{1,0:T(8,128)S(1)} collective-permute-done((f32[288,384]{1,0:T(8,128)S(1)}, f32[288,384]{1,0:T(8,128)S(1)}, u32[]{:S(2)}, u32[]{:S(2)}) %collective-permute-start.26) | collective-permute-done | bytes 442400 | tf_op jit(solution)/shard_map/ppermute | solution.py:30
  89.6 2.0 %collective-permute-start.27 = (f32[72,384]{1,0:T(8,128)S(1)}, f32[72,384]{1,0:T(8,128)S(1)}, u32[]{:S(2)}, u32[]{:S(2)}) collective-permute-start(f32[72,384]{1,0:T(8,128)S(1)} %get-tuple-element.72), channel_id=1, source_target_pairs={{0,64},{32,96},{64,0},{96,32},{128,192},{160,224},{192,128},{224,1... | collective-permute-start | bytes 331784 | tf_op jit(solution)/shard_map/ppermute | solution.py:17
  91.6 1.8 %collective-permute-start.28 = (f32[72,384]{1,0:T(8,128)S(1)}, f32[72,384]{1,0:T(8,128)S(1)}, u32[]{:S(2)}, u32[]{:S(2)}) collective-permute-start(f32[72,384]{1,0:T(8,128)S(1)} %get-tuple-element.70), channel_id=1, source_target_pairs={{0,128},{32,160},{64,192},{96,224},{128,0},{160,32},{192,64},{224,... | collective-permute-start | bytes 331784 | tf_op jit(solution)/shard_map/ppermute | solution.py:17
  93.4 2.0 %collective-permute-start.29 = (f32[72,384]{1,0:T(8,128)S(1)}, f32[72,384]{1,0:T(8,128)S(1)}, u32[]{:S(2)}, u32[]{:S(2)}) collective-permute-start(f32[72,384]{1,0:T(8,128)S(1)} %get-tuple-element.71), channel_id=1, source_target_pairs={{0,192},{32,224},{64,128},{96,160},{128,64},{160,96},{192,0},{224,... | collective-permute-start | bytes 331784 | tf_op jit(solution)/shard_map/ppermute | solution.py:17
  95.3 1.9 %copy-done.2 = f32[2048,384]{1,0:T(8,128)S(1)} copy-done((f32[2048,384]{1,0:T(8,128)S(1)}, f32[2048,384]{1,0:T(8,128)}, u32[]{:S(2)}) %copy-start.2) | copy-done | bytes 3145752
  97.2 2.2 %copy-done.9 = f32[512,2048]{1,0:T(8,128)S(1)} copy-done((f32[512,2048]{1,0:T(8,128)S(1)}, f32[512,2048]{1,0:T(8,128)}, u32[]{:S(2)}) %copy-start.9) | copy-done | bytes 4194328
  99.4 7.0 %trailing.3 = f32[2048,384]{1,0:T(8,128)} custom-call(s32[6]{0:T(128)S(1)} %stack.27.ids, f32[64,384]{1,0:T(8,128)S(1)} %copy-done, f32[64,384]{1,0:T(8,128)S(1)} %collective-permute-done.18.refs_1_, f32[64,384]{1,0:T(8,128)S(1)} %collective-permute-done.19.refs_2_, f32[64,384]{1,0:T(8,128)S(1)} %collective-permute-done.20.refs_3_, ...), custom_call_target="tpu_custom_call" | custom-call | flops 4000000000 | bytes 11534336 | tf_op jit(solution)/shard_map/trailing/pallas_call | solution.py:280
  (82 shorter events, 16.6 us)
Async XLA Ops:
  0.6 49.0 %copy-start = (f32[64,384]{1,0:T(8,128)S(1)}, f32[64,384]{1,0:T(8,128)}, u32[]{:S(2)}) copy-start(f32[64,384]{1,0:T(8,128)} %refs_0_) | copy-start | bytes 294916
  0.6 50.2 %copy-start.3 = (f32[2048,16]{0,1:T(8,128)S(1)}, f32[2048,16]{0,1:T(8,128)}, u32[]{:S(2)}) copy-start(f32[2048,16]{0,1:T(8,128)} %param.9) | copy-start | bytes 393220
  0.7 9.0 %collective-permute-start = (f32[16,64]{1,0:T(8,128)}, f32[16,64]{1,0:T(8,128)S(1)}, u32[]{:S(2)}, u32[]{:S(2)}) collective-permute-start(f32[16,64]{1,0:T(8,128)} %bitcast.16), channel_id=1, source_target_pairs={{0,64},{32,96},{64,0},{96,32},{128,192},{160,224},{192,128},{224,1... | collective-permute-start | bytes 12296 | tf_op jit(solution)/shard_map/ppermute | solution.py:17
  4.6 6.6 %collective-permute-start.1 = (f32[16,64]{1,0:T(8,128)}, f32[16,64]{1,0:T(8,128)S(1)}, u32[]{:S(2)}, u32[]{:S(2)}) collective-permute-start(f32[16,64]{1,0:T(8,128)} %bitcast.17), channel_id=1, source_target_pairs={{0,128},{32,160},{64,192},{96,224},{128,0},{160,32},{192,64},{224,... | collective-permute-start | bytes 12296 | tf_op jit(solution)/shard_map/ppermute | solution.py:17
  9.7 4.8 %collective-permute-start.2 = (f32[16,64]{1,0:T(8,128)}, f32[16,64]{1,0:T(8,128)S(1)}, u32[]{:S(2)}, u32[]{:S(2)}) collective-permute-start(f32[16,64]{1,0:T(8,128)} %bitcast.18), channel_id=1, source_target_pairs={{0,192},{32,224},{64,128},{96,160},{128,64},{160,96},{192,0},{224,... | collective-permute-start | bytes 12296 | tf_op jit(solution)/shard_map/ppermute | solution.py:17
  15.3 2.6 %collective-permute-start.3 = (f32[16,256]{1,0:T(8,128)S(1)}, f32[16,256]{1,0:T(8,128)S(1)}, u32[]{:S(2)}, u32[]{:S(2)}) collective-permute-start(f32[16,256]{1,0:T(8,128)S(1)} %pad_maximum_fusion.4), channel_id=1, source_target_pairs={{0,32},{32,0},{64,96},{96,64},{128,160},{160,128},{192,224},{224,1... | collective-permute-start | bytes 49160 | tf_op jit(solution)/shard_map/ppermute | solution.py:17
  18.8 4.5 %collective-permute-start.4 = (f32[16,1280]{1,0:T(8,128)S(1)}, f32[16,1280]{1,0:T(8,128)S(1)}, u32[]{:S(2)}, u32[]{:S(2)}) collective-permute-start(f32[16,1280]{1,0:T(8,128)S(1)} %get-tuple-element.74), channel_id=1, source_target_pairs={{0,1},{1,0},{2,3},{3,2},{4,5},{5,4},{6,7},{7,6},{8,9},{9,8},{10,11... | collective-permute-start | bytes 245768 | tf_op jit(solution)/shard_map/ppermute | solution.py:21
  23.4 4.6 %collective-permute-start.5 = (f32[32,1280]{1,0:T(8,128)S(1)}, f32[32,1280]{1,0:T(8,128)S(1)}, u32[]{:S(2)}, u32[]{:S(2)}) collective-permute-start(f32[32,1280]{1,0:T(8,128)S(1)} %pad_maximum_fusion.2), channel_id=1, source_target_pairs={{0,2},{1,9},{2,0},{3,11},{4,6},{5,13},{6,4},{7,15},{8,10},{9,1},{1... | collective-permute-start | bytes 491528 | tf_op jit(solution)/shard_map/ppermute | solution.py:36
  24.8 7.4 %collective-permute-start.6 = (f32[32,1280]{1,0:T(8,128)S(1)}, f32[32,1280]{1,0:T(8,128)S(1)}, u32[]{:S(2)}, u32[]{:S(2)}) collective-permute-start(f32[32,1280]{1,0:T(8,128)S(1)} %pad_maximum_fusion.2), channel_id=1, source_target_pairs={{0,4},{1,17},{2,6},{3,19},{4,0},{5,21},{6,2},{7,23},{8,12},{9,25},... | collective-permute-start | bytes 491528 | tf_op jit(solution)/shard_map/ppermute | solution.py:36
  27.4 6.5 %collective-permute-start.7 = (f32[32,1280]{1,0:T(8,128)S(1)}, f32[32,1280]{1,0:T(8,128)S(1)}, u32[]{:S(2)}, u32[]{:S(2)}) collective-permute-start(f32[32,1280]{1,0:T(8,128)S(1)} %pad_maximum_fusion.2), channel_id=1, source_target_pairs={{0,6},{1,25},{2,4},{3,27},{4,2},{5,29},{6,0},{7,31},{8,14},{9,17},... | collective-permute-start | bytes 491528 | tf_op jit(solution)/shard_map/ppermute | solution.py:36
  33.9 5.1 %collective-permute-start.10 = (f32[128,256]{1,0:T(8,128)S(1)}, f32[128,256]{1,0:T(8,128)S(1)}, u32[]{:S(2)}, u32[]{:S(2)}) collective-permute-start(f32[128,256]{1,0:T(8,128)S(1)} %pad_maximum_fusion.3.refs_0_), channel_id=1, source_target_pairs={{0,24},{1,7},{2,26},{3,5},{4,28},{5,3},{6,30},{7,1},{8,16},{9,15},... | collective-permute-start | bytes 393224 | tf_op jit(solution)/shard_map/ppermute | solution.py:36
  36.2 4.1 %collective-permute-start.8 = (f32[128,256]{1,0:T(8,128)S(1)}, f32[128,256]{1,0:T(8,128)S(1)}, u32[]{:S(2)}, u32[]{:S(2)}) collective-permute-start(f32[128,256]{1,0:T(8,128)S(1)} %pad_maximum_fusion.3.refs_0_), channel_id=1, source_target_pairs={{0,8},{1,3},{2,10},{3,1},{4,12},{5,7},{6,14},{7,5},{8,0},{9,11},{1... | collective-permute-start | bytes 393224 | tf_op jit(solution)/shard_map/ppermute | solution.py:36
  36.2 5.4 %collective-permute-start.9 = (f32[128,256]{1,0:T(8,128)S(1)}, f32[128,256]{1,0:T(8,128)S(1)}, u32[]{:S(2)}, u32[]{:S(2)}) collective-permute-start(f32[128,256]{1,0:T(8,128)S(1)} %pad_maximum_fusion.3.refs_0_), channel_id=1, source_target_pairs={{0,16},{1,5},{2,18},{3,7},{4,20},{5,1},{6,22},{7,3},{8,24},{9,13},... | collective-permute-start | bytes 393224 | tf_op jit(solution)/shard_map/ppermute | solution.py:36
  41.6 4.0 %collective-permute-start.14 = (f32[128,256]{1,0:T(8,128)S(1)}, f32[128,256]{1,0:T(8,128)S(1)}, u32[]{:S(2)}, u32[]{:S(2)}) collective-permute-start(f32[128,256]{1,0:T(8,128)S(1)} %pad_maximum_fusion.3.refs_0_), channel_id=1, source_target_pairs={{0,1},{1,0},{2,3},{3,2},{4,5},{5,4},{6,7},{7,6},{8,9},{9,8},{10,11... | collective-permute-start | bytes 393224 | tf_op jit(solution)/shard_map/ppermute | solution.py:21
  44.6 2.6 %collective-permute-start.15 = (f32[128,256]{1,0:T(8,128)S(1)}, f32[128,256]{1,0:T(8,128)S(1)}, u32[]{:S(2)}, u32[]{:S(2)}) collective-permute-start(f32[128,256]{1,0:T(8,128)S(1)} %collective-permute-done.8.refs_1_), channel_id=1, source_target_pairs={{0,1},{1,0},{2,3},{3,2},{4,5},{5,4},{6,7},{7,6},{8,9},{9,8},{10,11... | collective-permute-start | bytes 393224 | tf_op jit(solution)/shard_map/ppermute | solution.py:21
  44.6 4.4 %collective-permute-start.16 = (f32[128,256]{1,0:T(8,128)S(1)}, f32[128,256]{1,0:T(8,128)S(1)}, u32[]{:S(2)}, u32[]{:S(2)}) collective-permute-start(f32[128,256]{1,0:T(8,128)S(1)} %collective-permute-done.9.refs_2_), channel_id=1, source_target_pairs={{0,1},{1,0},{2,3},{3,2},{4,5},{5,4},{6,7},{7,6},{8,9},{9,8},{10,11... | collective-permute-start | bytes 393224 | tf_op jit(solution)/shard_map/ppermute | solution.py:21
  45.1 3.9 %collective-permute-start.17 = (f32[128,256]{1,0:T(8,128)S(1)}, f32[128,256]{1,0:T(8,128)S(1)}, u32[]{:S(2)}, u32[]{:S(2)}) collective-permute-start(f32[128,256]{1,0:T(8,128)S(1)} %collective-permute-done.10.refs_3_), channel_id=1, source_target_pairs={{0,1},{1,0},{2,3},{3,2},{4,5},{5,4},{6,7},{7,6},{8,9},{9,8},{10,11... | collective-permute-start | bytes 393224 | tf_op jit(solution)/shard_map/ppermute | solution.py:21
  45.1 22.6 %collective-permute-start.11 = (f32[128,1024]{1,0:T(8,128)S(1)}, f32[128,1024]{1,0:T(8,128)S(1)}, u32[]{:S(2)}, u32[]{:S(2)}) collective-permute-start(f32[128,1024]{1,0:T(8,128)S(1)} %pad_maximum_fusion.refs_0_), channel_id=1, source_target_pairs={{0,8},{1,3},{2,10},{3,1},{4,12},{5,7},{6,14},{7,5},{8,0},{9,11},{1... | collective-permute-start | bytes 1572872 | tf_op jit(solution)/shard_map/ppermute | solution.py:36
  45.6 22.2 %collective-permute-start.12 = (f32[128,1024]{1,0:T(8,128)S(1)}, f32[128,1024]{1,0:T(8,128)S(1)}, u32[]{:S(2)}, u32[]{:S(2)}) collective-permute-start(f32[128,1024]{1,0:T(8,128)S(1)} %pad_maximum_fusion.refs_0_), channel_id=1, source_target_pairs={{0,16},{1,5},{2,18},{3,7},{4,20},{5,1},{6,22},{7,3},{8,24},{9,13},... | collective-permute-start | bytes 1572872 | tf_op jit(solution)/shard_map/ppermute | solution.py:36
  47.2 20.6 %collective-permute-start.13 = (f32[128,1024]{1,0:T(8,128)S(1)}, f32[128,1024]{1,0:T(8,128)S(1)}, u32[]{:S(2)}, u32[]{:S(2)}) collective-permute-start(f32[128,1024]{1,0:T(8,128)S(1)} %pad_maximum_fusion.refs_0_), channel_id=1, source_target_pairs={{0,24},{1,7},{2,26},{3,5},{4,28},{5,3},{6,30},{7,1},{8,16},{9,15},... | collective-permute-start | bytes 1572872 | tf_op jit(solution)/shard_map/ppermute | solution.py:36
  49.6 7.0 %collective-permute-start.18 = (f32[64,384]{1,0:T(8,128)S(1)}, f32[64,384]{1,0:T(8,128)S(1)}, u32[]{:S(2)}, u32[]{:S(2)}) collective-permute-start(f32[64,384]{1,0:T(8,128)S(1)} %copy-done), channel_id=1, source_target_pairs={{0,64},{32,96},{64,0},{96,32},{128,192},{160,224},{192,128},{224,1... | collective-permute-start | bytes 294920 | tf_op jit(solution)/shard_map/ppermute | solution.py:17
  55.1 10.2 %collective-permute-start.19 = (f32[64,384]{1,0:T(8,128)S(1)}, f32[64,384]{1,0:T(8,128)S(1)}, u32[]{:S(2)}, u32[]{:S(2)}) collective-permute-start(f32[64,384]{1,0:T(8,128)S(1)} %copy-done), channel_id=1, source_target_pairs={{0,128},{32,160},{64,192},{96,224},{128,0},{160,32},{192,64},{224,... | collective-permute-start | bytes 294920 | tf_op jit(solution)/shard_map/ppermute | solution.py:17
  56.6 11.2 %collective-permute-start.20 = (f32[64,384]{1,0:T(8,128)S(1)}, f32[64,384]{1,0:T(8,128)S(1)}, u32[]{:S(2)}, u32[]{:S(2)}) collective-permute-start(f32[64,384]{1,0:T(8,128)S(1)} %copy-done), channel_id=1, source_target_pairs={{0,192},{32,224},{64,128},{96,160},{128,64},{160,96},{192,0},{224,... | collective-permute-start | bytes 294920 | tf_op jit(solution)/shard_map/ppermute | solution.py:17
  65.3 4.0 %collective-permute-start.21 = (f32[128,1024]{1,0:T(8,128)S(1)}, f32[128,1024]{1,0:T(8,128)S(1)}, u32[]{:S(2)}, u32[]{:S(2)}) collective-permute-start(f32[128,1024]{1,0:T(8,128)S(1)} %pad_maximum_fusion.refs_0_), channel_id=1, source_target_pairs={{0,1},{1,0},{2,3},{3,2},{4,5},{5,4},{6,7},{7,6},{8,9},{9,8},{10,11... | collective-permute-start | bytes 1572872 | tf_op jit(solution)/shard_map/ppermute | solution.py:21
  67.8 2.3 %collective-permute-start.22 = (f32[128,1024]{1,0:T(8,128)S(1)}, f32[128,1024]{1,0:T(8,128)S(1)}, u32[]{:S(2)}, u32[]{:S(2)}) collective-permute-start(f32[128,1024]{1,0:T(8,128)S(1)} %collective-permute-done.11.refs_1_), channel_id=1, source_target_pairs={{0,1},{1,0},{2,3},{3,2},{4,5},{5,4},{6,7},{7,6},{8,9},{9,8},{10,11... | collective-permute-start | bytes 1572872 | tf_op jit(solution)/shard_map/ppermute | solution.py:21
  67.9 2.9 %collective-permute-start.23 = (f32[128,1024]{1,0:T(8,128)S(1)}, f32[128,1024]{1,0:T(8,128)S(1)}, u32[]{:S(2)}, u32[]{:S(2)}) collective-permute-start(f32[128,1024]{1,0:T(8,128)S(1)} %collective-permute-done.12.refs_2_), channel_id=1, source_target_pairs={{0,1},{1,0},{2,3},{3,2},{4,5},{5,4},{6,7},{7,6},{8,9},{9,8},{10,11... | collective-permute-start | bytes 1572872 | tf_op jit(solution)/shard_map/ppermute | solution.py:21
  68.4 3.2 %collective-permute-start.24 = (f32[128,1024]{1,0:T(8,128)S(1)}, f32[128,1024]{1,0:T(8,128)S(1)}, u32[]{:S(2)}, u32[]{:S(2)}) collective-permute-start(f32[128,1024]{1,0:T(8,128)S(1)} %collective-permute-done.13.refs_3_), channel_id=1, source_target_pairs={{0,1},{1,0},{2,3},{3,2},{4,5},{5,4},{6,7},{7,6},{8,9},{9,8},{10,11... | collective-permute-start | bytes 1572872 | tf_op jit(solution)/shard_map/ppermute | solution.py:21
  81.2 8.4 %collective-permute-start.26 = (f32[288,384]{1,0:T(8,128)S(1)}, f32[288,384]{1,0:T(8,128)S(1)}, u32[]{:S(2)}, u32[]{:S(2)}) collective-permute-start(f32[288,384]{1,0:T(8,128)S(1)} %get-tuple-element.66), channel_id=1, source_target_pairs={{0,32},{1,225},{2,34},{3,227},{4,36},{5,229},{6,38},{7,231},{8,40}... | collective-permute-start | bytes 1327112 | tf_op jit(solution)/shard_map/ppermute | solution.py:30
  81.7 13.6 %collective-permute-start.25 = (f32[256,384]{1,0:T(8,128)S(1)}, f32[256,384]{1,0:T(8,128)S(1)}, u32[]{:S(2)}, u32[]{:S(2)}) collective-permute-start(f32[256,384]{1,0:T(8,128)S(1)} %pad_maximum_fusion.1), channel_id=1, source_target_pairs={{0,32},{1,225},{2,34},{3,227},{4,36},{5,229},{6,38},{7,231},{8,40}... | collective-permute-start | bytes 1179656 | tf_op jit(solution)/shard_map/ppermute | solution.py:30
  89.6 16.8 %collective-permute-start.27 = (f32[72,384]{1,0:T(8,128)S(1)}, f32[72,384]{1,0:T(8,128)S(1)}, u32[]{:S(2)}, u32[]{:S(2)}) collective-permute-start(f32[72,384]{1,0:T(8,128)S(1)} %get-tuple-element.72), channel_id=1, source_target_pairs={{0,64},{32,96},{64,0},{96,32},{128,192},{160,224},{192,128},{224,1... | collective-permute-start | bytes 331784 | tf_op jit(solution)/shard_map/ppermute | solution.py:17
  91.6 14.8 %collective-permute-start.28 = (f32[72,384]{1,0:T(8,128)S(1)}, f32[72,384]{1,0:T(8,128)S(1)}, u32[]{:S(2)}, u32[]{:S(2)}) collective-permute-start(f32[72,384]{1,0:T(8,128)S(1)} %get-tuple-element.70), channel_id=1, source_target_pairs={{0,128},{32,160},{64,192},{96,224},{128,0},{160,32},{192,64},{224,... | collective-permute-start | bytes 331784 | tf_op jit(solution)/shard_map/ppermute | solution.py:17
  93.4 13.1 %collective-permute-start.29 = (f32[72,384]{1,0:T(8,128)S(1)}, f32[72,384]{1,0:T(8,128)S(1)}, u32[]{:S(2)}, u32[]{:S(2)}) collective-permute-start(f32[72,384]{1,0:T(8,128)S(1)} %get-tuple-element.71), channel_id=1, source_target_pairs={{0,192},{32,224},{64,128},{96,160},{128,64},{160,96},{192,0},{224,... | collective-permute-start | bytes 331784 | tf_op jit(solution)/shard_map/ppermute | solution.py:17
  (10 other events, 68.3 us)

commit v3 on v2

v3 whole, which is shorter than its diff:
```python
import jax
import jax.numpy as jnp
from jax import lax
from jax.experimental import pallas as pl
from jax.experimental.pallas import tpu as pltpu
from jax.sharding import PartitionSpec as P

F32 = jnp.float32
BF16 = jnp.bfloat16
ROWS = 8
COLS = 32
B = 512
MIB = 1 << 20


def with_row_partner(v, k):
    return lax.ppermute(v, "row", [(i, i ^ k) for i in range(ROWS)])


def with_sibling(v):
    return lax.ppermute(v, "col", [(i, i ^ 1) for i in range(COLS)])


def with_neighbour(v):
    perm = []
    for r in range(ROWS):
        for c in range(COLS):
            to = r ^ 1 if c % 2 == 0 else (r - 1 + 2 * (r % 2)) % ROWS
            perm.append((r * COLS + c, to * COLS + c))
    return lax.ppermute(v, ("row", "col"), perm)


def with_col_partner(v, phase, k):
    shift = {0: 1, 1: 3}
    perm = [(i, i ^ (k << shift[phase ^ (i & 1)])) for i in range(COLS)]
    return lax.ppermute(v, "col", perm)


def place(ids, blocks, rows, store):
    y, x, core = ids[1], ids[2], ids[3]
    for other in range(2):
        half = core ^ other
        for k, block in enumerate(blocks[4 * other : 4 * other + 4]):
            for j in range(4):
                along_x = jnp.where(half == 0, x ^ j, x ^ k)
                along_y = jnp.where(half == 0, y ^ k, y ^ j)
                for r in range(2):
                    at = (j * 2 + r) * rows
                    store(half, along_y * 8 + along_x * 2 + (half ^ r), block[at : at + rows, :])


def split(v):
    high = v.astype(BF16)
    return high, (v - high.astype(F32)).astype(BF16)


def dot(a, b):
    return lax.dot_general(a, b, (((1,), (0,)), ((), ())), preferred_element_type=F32)


def dot_full(a, b):
    return lax.dot_general(
        a, b, (((1,), (0,)), ((), ())), precision=lax.Precision.HIGHEST, preferred_element_type=F32
    )


def invert(ids, blocks, top_out, low_out, held):
    odd = jnp.broadcast_to(ids[0] % 2, (8, 128)) == 1

    def store(half, chunk, piece):
        row = pl.multiple_of(chunk * 16 + half * 8, 8)
        for q in range(4):
            lanes = piece[:, 128 * q : 128 * q + 128]
            swapped = jnp.concatenate([lanes[:, 64:], lanes[:, :64]], axis=1)
            held[q ^ (ids[0] // 2), pl.ds(row, 8), :] = jnp.where(odd, swapped, lanes)

    place(ids, blocks, 8, store)

    def part(r, c, n):
        return jnp.concatenate([held[c // 128 + q, r : r + n, :] for q in range(n // 128)], axis=1)

    n = 128
    rows = lax.broadcasted_iota(jnp.int32, (n, n), 0)
    cols = lax.broadcasted_iota(jnp.int32, (n, n), 1)
    in_block = rows // 16 == cols // 16
    diag = [part(n * g, n * g, n) for g in range(4)]
    packed = []
    for d in diag:
        kept = jnp.where(in_block, d, 0.0)
        packed.append(sum(kept[16 * b : 16 * b + 16, :] for b in range(1, 8)) + kept[0:16, :])
    packed = jnp.concatenate(packed, axis=0)
    sub = lax.broadcasted_iota(jnp.int32, (64, n), 0) % 16
    lane = lax.broadcasted_iota(jnp.int32, (64, n), 1) % 16
    inverse = jnp.where(sub == lane, 1.0, 0.0).astype(F32)
    spread = []
    for k in range(16):
        pick = jnp.where(in_block & (rows % 16 == k), 1.0, 0.0).astype(F32)
        spread.append(dot_full(packed, pick))
    for k in range(15, -1, -1):
        factor = spread[k]
        pivot = []
        for g in range(4):
            at = 16 * g + k
            row = inverse[at : at + 1, :] / factor[at : at + 1, :]
            pivot.append(jnp.broadcast_to(row, (16, n)))
        pivot = jnp.concatenate(pivot, axis=0)
        inverse = jnp.where(sub == k, pivot, inverse - jnp.where(sub < k, factor, 0.0) * pivot)
    blocks = []
    for g in range(4):
        tall = jnp.concatenate([inverse[16 * g : 16 * g + 16, :]] * 8, axis=0)
        blocks.append(jnp.where(in_block, tall, 0.0))
    for b in (16, 32, 64):
        off = (rows // (2 * b) == cols // (2 * b)) & (rows // b < cols // b)
        lefts = [dot_full(blocks[g], jnp.where(off, diag[g], 0.0)) for g in range(4)]
        blocks = [blocks[g] - dot_full(lefts[g], blocks[g]) for g in range(4)]
    pairs = []
    for g in (0, 2):
        corner = -dot_full(dot_full(blocks[g], part(n * g, n * g + n, n)), blocks[g + 1])
        top = jnp.concatenate([blocks[g], corner], axis=1)
        low = jnp.concatenate([jnp.zeros_like(corner), blocks[g + 1]], axis=1)
        pairs.append(jnp.concatenate([top, low], axis=0))
    corner = -dot_full(dot_full(pairs[0], part(0, 256, 256)), pairs[1])
    for at, out, m in ((0, top_out, pairs[0]), (768, top_out, corner), (0, low_out, pairs[1])):
        high, low = split(m)
        out[:, at : at + 256] = high
        out[:, at + 256 : at + 512] = high
        out[:, at + 512 : at + 768] = low


def split_tall(trailing, panel, out):
    n = trailing.shape[0]
    side = jnp.concatenate([panel, jnp.zeros((112, n), F32)], axis=0).T
    for v, lanes in ((trailing, slice(0, 384)), (side, slice(384, 512))):
        high, low = split(v)
        out[0:n, lanes] = high
        out[n : 2 * n, lanes] = low
        out[2 * n : 3 * n, lanes] = high


def prepare_kernel(ids, *refs):
    blocks = [whole.at[64 * k : 64 * k + 64] for whole in refs[:2] for k in range(4)]
    trailing, panel, top_out, low_out, tall_out, done_out, held, rows, sems = refs[2:]
    n = TILE
    loads = [
        pltpu.make_async_copy(trailing.at[t * n : t * n + n, :], rows.at[t], sems.at[t]) for t in range(2048 // n)
    ]
    for load in loads:
        load.start()
    done_out[...] = jnp.zeros_like(done_out)
    invert(ids, blocks, top_out, low_out, held)
    for t, load in enumerate(loads):
        load.wait()
        split_tall(rows[t], panel[:, t * n : t * n + n], tall_out.at[3 * n * t : 3 * n * t + 3 * n])


def solve_kernel(ids, *refs):
    blocks = refs[:8]
    inv_top, inv_low, tall = refs[8:11]
    solved_out, own_out, given_out = refs[11:14]
    kept_outs = refs[14:18]
    g, x, xs, total, corner, sems = refs[18:]

    def store(half, chunk, piece):
        high, low = split(piece)
        row = chunk * 16
        row = pl.multiple_of(jnp.where(row < 256, row, row + 512), 16)
        g[half, pl.ds(row, 16), :] = high
        g[half, pl.ds(row + 256, 16), :] = low
        g[half, pl.ds(row + 512, 16), :] = high

    place(ids, blocks, 16, store)
    n = TILE
    own = pl.ds(pl.multiple_of(ids[4] * 16, 16), 16)
    copies = []
    for t in range(2048 // n):
        half, lane = divmod(t * n, 1024)
        slot = t % 2
        for rows, lhs, k in ((slice(0, 256), inv_top, 0), (slice(256, 512), inv_low, 768)):
            part = dot(lhs[...], g[half, k:, lane : lane + n])
            x[t, rows, :] = part
            high, low = split(part)
            xs[slot, rows, 0:n] = high
            xs[slot, rows, n : 2 * n] = high
            xs[slot, rows, 2 * n : 3 * n] = low
        copies.append(pltpu.make_async_copy(x.at[t], solved_out.at[:, t * n : t * n + n], sems.at[t]))
        copies[t].start()
        own_out[:, t * n : t * n + n] = x[t, own, :]
        term = dot(xs[slot], tall[3 * n * t : 3 * n * t + 3 * n, :])
        if t == 0:
            total[...] = term
        else:
            total[...] += term

    corner[...] = jnp.zeros_like(corner)
    summed = total[:, 384:512].T
    for t in range(ROWS):
        corner[t, :, 0:64] = summed[0:8, 64 * t : 64 * t + 64]
        corner[t, :, 64:128] = summed[8:16, 64 * t : 64 * t + 64]
    for j in range(4):
        for first, out, at in ((ids[5], given_out, 72 * j), (ids[0], kept_outs[j], 0)):
            target = first ^ (2 * j)
            out[at : at + 64, :] = total[pl.ds(pl.multiple_of(target * 64, 64), 64), 0:384]
            out[at + 64 : at + 72, :] = corner[target]
    for copy in copies:
        copy.wait()


def trailing_kernel(ids, *refs):
    own_parity, other_parity = refs[:4], refs[4]
    solved, grad, out, rs, x_in, grad_in, result, sems = refs[5:]
    n = TRAILING_TILE
    tiles = 2048 // n
    loads, stores = [], []
    for t in range(tiles):
        loads.append(
            (
                pltpu.make_async_copy(solved.at[:, t * n : t * n + n], x_in.at[t], sems.at[0, t]),
                pltpu.make_async_copy(grad.at[t * n : t * n + n, :], grad_in.at[t], sems.at[1, t]),
            )
        )
        stores.append(pltpu.make_async_copy(result.at[t], out.at[t * n : t * n + n, :], sems.at[2, t]))
        for load in loads[t]:
            load.start()
    for j in range(4):
        for first, piece in ((ids[0], own_parity[j][...]), (ids[5], other_parity[64 * j : 64 * j + 64, :])):
            high, low = split(piece)
            row = (first ^ (2 * j)) * 64
            rs[pl.ds(pl.multiple_of(row, 64), 64), :] = high
            rs[pl.ds(pl.multiple_of(row + 512, 64), 64), :] = low
            rs[pl.ds(pl.multiple_of(row + 1024, 64), 64), :] = high
    for t in range(tiles):
        for load in loads[t]:
            load.wait()
        high, low = split(x_in[t].T)
        result[t] = grad_in[t] - dot(jnp.concatenate([high, high, low], axis=1), rs[...])
        stores[t].start()
    for store in stores:
        store.wait()


TRAILING_TILE = 256
TILE = 512
SMEM = pl.BlockSpec(memory_space=pltpu.SMEM)
VMEM = pl.BlockSpec(memory_space=pltpu.VMEM)
HBM = pl.BlockSpec(memory_space=pltpu.HBM)


def shape(dims, dtype=F32):
    return jax.ShapeDtypeStruct(dims, dtype)


def prepare(ids, blocks, trailing, panel):
    tiles = 2048 // TILE
    return pl.pallas_call(
        prepare_kernel,
        out_shape=[shape((256, 1536), BF16), shape((256, 768), BF16), shape((3 * 2048, 512), BF16), shape((8, 128))],
        in_specs=[SMEM] + [VMEM] * 2 + [HBM, VMEM],
        out_specs=[VMEM] * 4,
        scratch_shapes=[
            pltpu.VMEM((4, B, 128), F32),
            pltpu.VMEM((tiles, TILE, 384), F32),
            pltpu.SemaphoreType.DMA((tiles,)),
        ],
        compiler_params=pltpu.CompilerParams(vmem_limit_bytes=16 * MIB),
        cost_estimate=pl.CostEstimate(flops=4_000_000_000, bytes_accessed=10 * MIB, transcendentals=0),
        name="prepare",
    )(ids, *blocks, trailing, panel)


def solve(ids, blocks, inverse, tall):
    return pl.pallas_call(
        solve_kernel,
        out_shape=[shape((B, 2048)), shape((16, 2048)), shape((288, 384))] + [shape((72, 384))] * 4,
        in_specs=[SMEM] + [VMEM] * 11,
        out_specs=[HBM] + [VMEM] * 6,
        scratch_shapes=[
            pltpu.VMEM((2, 3 * B, 1024), BF16),
            pltpu.VMEM((2048 // TILE, B, TILE), F32),
            pltpu.VMEM((2, B, 3 * TILE), BF16),
            pltpu.VMEM((B, 512), F32),
            pltpu.VMEM((ROWS, 8, 384), F32),
            pltpu.SemaphoreType.DMA((2048 // TILE,)),
        ],
        compiler_params=pltpu.CompilerParams(vmem_limit_bytes=17 * MIB),
        cost_estimate=pl.CostEstimate(flops=6_000_000_000, bytes_accessed=12 * MIB, transcendentals=0),
        name="solve",
    )(ids, *blocks, *inverse, tall)


def trailing_update(ids, pieces, solved, grad):
    n = TRAILING_TILE
    tiles = 2048 // n
    return pl.pallas_call(
        trailing_kernel,
        out_shape=shape((2048, 384)),
        in_specs=[SMEM] + [VMEM] * 5 + [HBM] * 2,
        out_specs=HBM,
        scratch_shapes=[
            pltpu.VMEM((3 * B, 384), BF16),
            pltpu.VMEM((tiles, B, n), F32),
            pltpu.VMEM((tiles, n, 384), F32),
            pltpu.VMEM((tiles, n, 384), F32),
            pltpu.SemaphoreType.DMA((3, tiles)),
        ],
        compiler_params=pltpu.CompilerParams(vmem_limit_bytes=13 * MIB),
        cost_estimate=pl.CostEstimate(flops=4_000_000_000, bytes_accessed=11 * MIB, transcendentals=0),
        name="trailing",
    )(ids, *pieces, solved, grad)


def on_device(
    diag_factor,
    panel_factor,
    row_factor,
    trailing_factor,
    panel_grad,
    diag_grad,
    row_grad,
    trailing_grad,
):
    z = lax.axis_index("row")
    col = lax.axis_index("col")
    core = col % 2
    neighbour = jnp.where(core == 0, z ^ 1, (z - 1 + 2 * (z % 2)) % ROWS)
    ids = jnp.stack([z, col // 8, (col // 2) % 4, core, col, neighbour]).astype(jnp.int32)

    grad = panel_grad.T
    kept = jnp.where(core == 0, grad[:, :1024], grad[:, 1024:])
    given = jnp.where(core == 0, grad[:, 1024:], grad[:, :1024])
    grad_pair = jnp.concatenate([kept, with_sibling(given)], axis=0)
    tile = diag_factor.T
    kept = jnp.where(core == 0, tile[:8], tile[8:])
    given = jnp.where(core == 0, tile[8:], tile[:8])
    tile = jnp.concatenate([kept, with_sibling(given)], axis=0)

    even = [tile] + [with_row_partner(tile, k) for k in (2, 4, 6)]
    grad_pairs = [grad_pair] + [with_col_partner(grad_pair, 0, k) for k in (1, 2, 3)]
    even, grad_pairs = lax.optimization_barrier((even, grad_pairs))
    odd = with_row_partner(jnp.concatenate(even, axis=1), 1)
    grad_quad = jnp.concatenate(grad_pairs, axis=0)
    grad_2 = with_col_partner(grad_quad, 1, 2)
    diag_pair = jnp.concatenate([t for j in range(4) for t in (even[j], odd[:, 64 * j : 64 * j + 64])], axis=1)
    diag_quad = jnp.concatenate([diag_pair] + [with_col_partner(diag_pair, 0, k) for k in (1, 2, 3)], axis=0)
    diag_quad, grad_2 = lax.optimization_barrier((diag_quad, grad_2))
    diag_blocks = [diag_quad] + [with_col_partner(diag_quad, 1, k) for k in (1, 2, 3)]
    later_quad, row_factor, diag_blocks = lax.optimization_barrier((grad_quad, row_factor, diag_blocks))
    grad_far = [with_col_partner(later_quad, 1, 1), grad_2, with_col_partner(later_quad, 1, 3)]
    diag_mine = jnp.concatenate(diag_blocks, axis=0)
    diag_blocks = [diag_mine, with_sibling(diag_mine)]
    quad_swapped = with_sibling(grad_quad)

    row_pieces = [row_factor] + [with_row_partner(row_factor, k) for k in (2, 4, 6)]
    *inverse, tall, ready = prepare(ids, diag_blocks, trailing_factor, panel_factor.T)
    grad_far, row_pieces, _ = lax.optimization_barrier((grad_far, row_pieces, ready))
    row_pieces = row_pieces + [with_neighbour(jnp.concatenate(row_pieces, axis=0))]
    grad_blocks = [grad_quad] + grad_far + [quad_swapped] + [with_sibling(b) for b in grad_far]
    solved, own, given, *kept = solve(ids, grad_blocks, inverse, tall)
    trailing_out = trailing_update(ids, row_pieces, solved, trailing_grad)
    taken = with_neighbour(given)
    taken, trailing_out = lax.optimization_barrier((taken, trailing_out))
    sums = [kept[j] + taken[72 * j : 72 * j + 72] for j in range(4)]
    came = [with_row_partner(sums[j], 2 * j) for j in range(1, 4)]

    total = sums[0] + (came[0] + came[1] + came[2])
    row_out = row_grad - total[0:64, :]
    diag_sum = jnp.concatenate([total[64:72, 0:64], total[64:72, 64:128]], axis=0)
    global_rows = z * 64 + jnp.arange(64)[None, :]
    global_cols = col * 16 + jnp.arange(16)[:, None]
    diag_out = jnp.where(global_rows >= global_cols, diag_grad.T - diag_sum, jnp.float32(0.0))
    return (own.T, trailing_out, row_out, diag_out.T)


def solution(mesh):
    both = P("row", "col")
    return jax.shard_map(
        on_device,
        mesh=mesh,
        in_specs=(both,) * 8,
        out_specs=(both,) * 4,
        check_vma=False,
    )
```

time: 109 us -> 118 us (1.083)
  local copies, waits for them, and re-layouts: 12.3 us -> 3.22 us
  waiting for transfers between devices: 26 us -> 33.2 us
  starting transfers between devices: 45.6 us -> 50.9 us
  Pallas kernels: 21 us -> 25.9 us
    ppermute x10, waiting for transfers between devices: 5.78 us -> 22.5 us  [with_row_partner(): return lax.ppermute(v, 'row', [(i, i ^ k) for i in range(ROWS)])]
    unnamed x24 -> x18, local copies, waits for them, and re-layouts: 10.3 us -> 2.88 us
    ppermute x2, waiting for transfers between devices: 5.57 us -> 0.01 us  [with_neighbour(): return lax.ppermute(v, ('row', 'col'), perm)]
    ppermute x9 -> x7, starting transfers between devices: 10.3 us -> 14.9 us  [with_sibling(): return lax.ppermute(v, 'col', [(i, i ^ 1) for i in range(COLS)])]
    ppermute x9 -> x12, starting transfers between devices: 11.3 us -> 14.2 us  [with_col_partner(): return lax.ppermute(v, 'col', perm)]
    ppermute x10, starting transfers between devices: 21.2 us -> 18.4 us  [with_row_partner(): return lax.ppermute(v, 'row', [(i, i ^ k) for i in range(ROWS)])]
    ppermute x9 -> x7, waiting for transfers between devices: 4.46 us -> 1.74 us  [with_sibling(): return lax.ppermute(v, 'col', [(i, i ^ 1) for i in range(COLS)])]
    pallas_call x1, Pallas kernels: 7.68 us -> 10.2 us  [solve(): pl.pallas_call(solve_kernel, out_shape=[shape((B, 2048)), shape((16, 2048...]
  transfers between devices with their start and end apart: 30 -> 31, of which waited for: 16 -> 12; matrix products, arithmetic and copies ran while one was open for 1% -> 1% of each run, Pallas kernels for 12% -> 22%
where the time goes in v3:
time: 118 us; the launch traced here: 117 us
  starting transfers between devices  50.9 us (43%)
  waiting for transfers between devices  33.2 us (28%)
  Pallas kernels  25.9 us (22%)
  local copies, waits for them, and re-layouts  3.22 us (3%)
  other arithmetic  3.16 us (3%)
    ppermute x10, waiting for transfers between devices, with_row_partner(): return lax.ppermute(v, 'row', [(i, i ^ k) for i in range(ROWS)])  22.5 us
    ppermute x10, starting transfers between devices, with_row_partner(): return lax.ppermute(v, 'row', [(i, i ^ k) for i in range(ROWS)])  18.4 us
    ppermute x7, starting transfers between devices, with_sibling(): return lax.ppermute(v, 'col', [(i, i ^ 1) for i in range(COLS)])  14.9 us
    ppermute x12, starting transfers between devices, with_col_partner(): return lax.ppermute(v, 'col', perm)  14.2 us
    pallas_call x1, Pallas kernels, solve(): pl.pallas_call(solve_kernel, out_shape=[shape((B, 2048)), shape((16, 2048...  10.2 us
    ppermute x12, waiting for transfers between devices, with_col_partner(): return lax.ppermute(v, 'col', perm)  8.98 us
    pallas_call x1, Pallas kernels, trailing_update(): pl.pallas_call(trailing_kernel, out_shape=shape((2048, 384)), in_specs=[S...  8.71 us
    pallas_call x1, Pallas kernels, prepare(): pl.pallas_call(prepare_kernel, out_shape=[shape((256, 1536), BF16), shape...  7.01 us
  transfers between devices with their start and end apart: 31, of which 12 were waited for; matrix products, arithmetic and copies ran while one was open for 1% of the time, Pallas kernels for 22%

profile of v3, /device:TPU:1, one launch (start us, length us, event | category | flops | bytes accessed | tf_op | source)
XLA Modules:
  0.0 117.3 jit_solution(9789456929770759427)
XLA Ops:
  1.6 3.3 %collective-permute-start.4 = (f32[16,1024]{1,0:T(8,128)S(1)}, f32[16,1024]{1,0:T(8,128)S(1)}, u32[]{:S(2)}, u32[]{:S(2)}) collective-permute-start(f32[16,1024]{1,0:T(8,128)S(1)} %get-tuple-element.78), channel_id=1, source_target_pairs={{0,1},{1,0},{2,3},{3,2},{4,5},{5,4},{6,7},{7,6},{8,9},{9,8},{10,11... | collective-permute-start | bytes 196616 | tf_op jit(solution)/shard_map/ppermute | solution.py:21
  5.9 2.2 %collective-permute-start.6 = (f32[32,1024]{1,0:T(8,128)S(1)}, f32[32,1024]{1,0:T(8,128)S(1)}, u32[]{:S(2)}, u32[]{:S(2)}) collective-permute-start(f32[32,1024]{1,0:T(8,128)S(1)} %pad_maximum_fusion.1), channel_id=1, source_target_pairs={{0,4},{1,17},{2,6},{3,19},{4,0},{5,21},{6,2},{7,23},{8,12},{9,25},... | collective-permute-start | bytes 393224 | tf_op jit(solution)/shard_map/ppermute | solution.py:36
  8.1 1.7 %collective-permute-start.7 = (f32[32,1024]{1,0:T(8,128)S(1)}, f32[32,1024]{1,0:T(8,128)S(1)}, u32[]{:S(2)}, u32[]{:S(2)}) collective-permute-start(f32[32,1024]{1,0:T(8,128)S(1)} %pad_maximum_fusion.1), channel_id=1, source_target_pairs={{0,6},{1,25},{2,4},{3,27},{4,2},{5,29},{6,0},{7,31},{8,14},{9,17},... | collective-permute-start | bytes 393224 | tf_op jit(solution)/shard_map/ppermute | solution.py:36
  10.5 1.2 %collective-permute-start = (f32[8,64]{1,0:T(8,128)S(1)}, f32[8,64]{1,0:T(8,128)S(1)}, u32[]{:S(2)}, u32[]{:S(2)}) collective-permute-start(f32[8,64]{1,0:T(8,128)S(1)} %get-tuple-element.86), channel_id=1, source_target_pairs={{0,1},{1,0},{2,3},{3,2},{4,5},{5,4},{6,7},{7,6},{8,9},{9,8},{10,11... | collective-permute-start | bytes 6152 | tf_op jit(solution)/shard_map/ppermute | solution.py:21
  12.5 1.3 %collective-permute-start.1 = (f32[16,64]{1,0:T(8,128)S(1)}, f32[16,64]{1,0:T(8,128)S(1)}, u32[]{:S(2)}, u32[]{:S(2)}) collective-permute-start(f32[16,64]{1,0:T(8,128)S(1)} %pad_maximum_fusion.4), channel_id=1, source_target_pairs={{0,64},{32,96},{64,0},{96,32},{128,192},{160,224},{192,128},{224,1... | collective-permute-start | bytes 12296 | tf_op jit(solution)/shard_map/ppermute | solution.py:17
  13.7 5.1 %collective-permute-start.2 = (f32[16,64]{1,0:T(8,128)S(1)}, f32[16,64]{1,0:T(8,128)S(1)}, u32[]{:S(2)}, u32[]{:S(2)}) collective-permute-start(f32[16,64]{1,0:T(8,128)S(1)} %pad_maximum_fusion.4), channel_id=1, source_target_pairs={{0,128},{32,160},{64,192},{96,224},{128,0},{160,32},{192,64},{224,... | collective-permute-start | bytes 12296 | tf_op jit(solution)/shard_map/ppermute | solution.py:17
  18.9 1.6 %collective-permute-start.3 = (f32[16,64]{1,0:T(8,128)S(1)}, f32[16,64]{1,0:T(8,128)S(1)}, u32[]{:S(2)}, u32[]{:S(2)}) collective-permute-start(f32[16,64]{1,0:T(8,128)S(1)} %pad_maximum_fusion.4), channel_id=1, source_target_pairs={{0,192},{32,224},{64,128},{96,160},{128,64},{160,96},{192,0},{224,... | collective-permute-start | bytes 12296 | tf_op jit(solution)/shard_map/ppermute | solution.py:17
  20.5 3.0 %collective-permute-done.3 = f32[16,64]{1,0:T(8,128)S(1)} collective-permute-done((f32[16,64]{1,0:T(8,128)S(1)}, f32[16,64]{1,0:T(8,128)S(1)}, u32[]{:S(2)}, u32[]{:S(2)}) %collective-permute-start.3) | collective-permute-done | bytes 4128 | tf_op jit(solution)/shard_map/ppermute | solution.py:17
  23.6 2.0 %collective-permute-start.12 = (f32[128,1024]{1,0:T(8,128)S(1)}, f32[128,1024]{1,0:T(8,128)S(1)}, u32[]{:S(2)}, u32[]{:S(2)}) collective-permute-start(f32[128,1024]{1,0:T(8,128)S(1)} %constant_dynamic-update-slice_fusion.refs_0_), channel_id=1, source_target_pairs={{0,16},{1,5},{2,18},{3,7},{4,20},{5,1},{6,22},{7,3},{8,24},{9,13},... | collective-permute-start | bytes 1572872 | tf_op jit(solution)/shard_map/ppermute | solution.py:36
  26.4 1.9 %collective-permute-done.8 = f32[16,256]{1,0:T(8,128)S(1)} collective-permute-done((f32[16,256]{1,0:T(8,128)S(1)}, f32[16,256]{1,0:T(8,128)S(1)}, u32[]{:S(2)}, u32[]{:S(2)}) %collective-permute-start.8) | collective-permute-done | bytes 16416 | tf_op jit(solution)/shard_map/ppermute | solution.py:17
  28.5 2.8 %collective-permute-start.11 = (f32[16,512]{1,0:T(8,128)S(1)}, f32[16,512]{1,0:T(8,128)S(1)}, u32[]{:S(2)}, u32[]{:S(2)}) collective-permute-start(f32[16,512]{1,0:T(8,128)S(1)} %concatenate.31), channel_id=1, source_target_pairs={{0,6},{1,25},{2,4},{3,27},{4,2},{5,29},{6,0},{7,31},{8,14},{9,17},... | collective-permute-start | bytes 98312 | tf_op jit(solution)/shard_map/ppermute | solution.py:36
  31.9 4.7 %collective-permute-done.11 = f32[16,512]{1,0:T(8,128)S(1)} collective-permute-done((f32[16,512]{1,0:T(8,128)S(1)}, f32[16,512]{1,0:T(8,128)S(1)}, u32[]{:S(2)}, u32[]{:S(2)}) %collective-permute-start.11) | collective-permute-done | bytes 32800 | tf_op jit(solution)/shard_map/ppermute | solution.py:36
  36.8 2.2 %collective-permute-start.14 = (f32[64,512]{1,0:T(8,128)S(1)}, f32[64,512]{1,0:T(8,128)S(1)}, u32[]{:S(2)}, u32[]{:S(2)}) collective-permute-start(f32[64,512]{1,0:T(8,128)S(1)} %pad_maximum_fusion.2), channel_id=1, source_target_pairs={{0,16},{1,5},{2,18},{3,7},{4,20},{5,1},{6,22},{7,3},{8,24},{9,13},... | collective-permute-start | bytes 393224 | tf_op jit(solution)/shard_map/ppermute | solution.py:36
  39.0 1.6 %collective-permute-start.15 = (f32[64,512]{1,0:T(8,128)S(1)}, f32[64,512]{1,0:T(8,128)S(1)}, u32[]{:S(2)}, u32[]{:S(2)}) collective-permute-start(f32[64,512]{1,0:T(8,128)S(1)} %pad_maximum_fusion.2), channel_id=1, source_target_pairs={{0,24},{1,7},{2,26},{3,5},{4,28},{5,3},{6,30},{7,1},{8,16},{9,15},... | collective-permute-start | bytes 393224 | tf_op jit(solution)/shard_map/ppermute | solution.py:36
  40.8 2.7 %collective-permute-done.14 = f32[64,512]{1,0:T(8,128)S(1)} collective-permute-done((f32[64,512]{1,0:T(8,128)S(1)}, f32[64,512]{1,0:T(8,128)S(1)}, u32[]{:S(2)}, u32[]{:S(2)}) %collective-permute-start.14) | collective-permute-done | bytes 131104 | tf_op jit(solution)/shard_map/ppermute | solution.py:36
  43.5 1.3 %collective-permute-done.15 = f32[64,512]{1,0:T(8,128)S(1)} collective-permute-done((f32[64,512]{1,0:T(8,128)S(1)}, f32[64,512]{1,0:T(8,128)S(1)}, u32[]{:S(2)}, u32[]{:S(2)}) %collective-permute-start.15) | collective-permute-done | bytes 131104 | tf_op jit(solution)/shard_map/ppermute | solution.py:36
  45.8 6.9 %collective-permute-start.25 = (f32[256,512]{1,0:T(8,128)S(1)}, f32[256,512]{1,0:T(8,128)}, u32[]{:S(2)}, u32[]{:S(2)}) collective-permute-start(f32[256,512]{1,0:T(8,128)S(1)} %constant_dynamic-update-slice_fusion.4.refs_0_), channel_id=1, source_target_pairs={{0,1},{1,0},{2,3},{3,2},{4,5},{5,4},{6,7},{7,6},{8,9},{9,8},{10,11... | collective-permute-start | bytes 1572872 | tf_op jit(solution)/shard_map/ppermute | solution.py:21
  52.7 1.2 %collective-permute-start.18 = (f32[64,384]{1,0:T(8,128)S(1)}, f32[64,384]{1,0:T(8,128)S(1)}, u32[]{:S(2)}, u32[]{:S(2)}) collective-permute-start(f32[64,384]{1,0:T(8,128)S(1)} %copy-done), channel_id=1, source_target_pairs={{0,64},{32,96},{64,0},{96,32},{128,192},{160,224},{192,128},{224,1... | collective-permute-start | bytes 294920 | tf_op jit(solution)/shard_map/ppermute | solution.py:17
  53.9 2.7 %collective-permute-start.19 = (f32[64,384]{1,0:T(8,128)S(1)}, f32[64,384]{1,0:T(8,128)S(1)}, u32[]{:S(2)}, u32[]{:S(2)}) collective-permute-start(f32[64,384]{1,0:T(8,128)S(1)} %copy-done), channel_id=1, source_target_pairs={{0,128},{32,160},{64,192},{96,224},{128,0},{160,32},{192,64},{224,... | collective-permute-start | bytes 294920 | tf_op jit(solution)/shard_map/ppermute | solution.py:17
  56.6 6.2 %collective-permute-done.18.refs_1_ = f32[64,384]{1,0:T(8,128)S(1)} collective-permute-done((f32[64,384]{1,0:T(8,128)S(1)}, f32[64,384]{1,0:T(8,128)S(1)}, u32[]{:S(2)}, u32[]{:S(2)}) %collective-permute-start.18) | collective-permute-done | bytes 98336 | tf_op jit(solution)/shard_map/ppermute | solution.py:17
  63.7 4.6 %collective-permute-done.20.refs_3_ = f32[64,384]{1,0:T(8,128)S(1)} collective-permute-done((f32[64,384]{1,0:T(8,128)S(1)}, f32[64,384]{1,0:T(8,128)S(1)}, u32[]{:S(2)}, u32[]{:S(2)}) %collective-permute-start.20) | collective-permute-done | bytes 98336 | tf_op jit(solution)/shard_map/ppermute | solution.py:17
  68.4 2.1 %collective-permute-start.22 = (f32[128,1024]{1,0:T(8,128)S(1)}, f32[128,1024]{1,0:T(8,128)}, u32[]{:S(2)}, u32[]{:S(2)}) collective-permute-start(f32[128,1024]{1,0:T(8,128)S(1)} %collective-permute-done.16.refs_1_), channel_id=1, source_target_pairs={{0,1},{1,0},{2,3},{3,2},{4,5},{5,4},{6,7},{7,6},{8,9},{9,8},{10,11... | collective-permute-start | bytes 1572872 | tf_op jit(solution)/shard_map/ppermute | solution.py:21
  71.1 1.5 %collective-permute-start.27 = (f32[256,384]{1,0:T(8,128)S(1)}, f32[256,384]{1,0:T(8,128)S(1)}, u32[]{:S(2)}, u32[]{:S(2)}) collective-permute-start(f32[256,384]{1,0:T(8,128)S(1)} %pad_maximum_fusion), channel_id=1, source_target_pairs={{0,32},{1,225},{2,34},{3,227},{4,36},{5,229},{6,38},{7,231},{8,40}... | collective-permute-start | bytes 1179656 | tf_op jit(solution)/shard_map/ppermute | solution.py:30
  72.6 1.9 %copy-done.1 = f32[2048,384]{1,0:T(8,128)S(1)} copy-done((f32[2048,384]{1,0:T(8,128)S(1)}, f32[2048,384]{1,0:T(8,128)}, u32[]{:S(2)}) %copy-start.1) | copy-done | bytes 3145752
  75.4 7.0 %prepare.1 = (bf16[256,1536]{1,0:T(8,128)(2,1)S(1)}, bf16[256,768]{1,0:T(8,128)(2,1)S(1)}, bf16[6144,512]{1,0:T(8,128)(2,1)S(1)}, f32[8,128]{1,0:T(8,128)}) custom-call(s32[6]{0:T(128)S(1)} %stack.27.ids, f32[256,512]{1,0:T(8,128)S(1)} %constant_dynamic-update-slice_fusion.4.refs_0_, f32[256,512]{1,0:T(8,128)} %collective-permute-done.25.refs_1_, ...), custom_call_target="tpu_custom_call" | custom-call | flops 4000000000 | bytes 10485760 | tf_op jit(solution)/shard_map/prepare/pallas_call | solution.py:254
  82.5 10.2 %solve.1 = (f32[512,2048]{1,0:T(8,128)S(1)}, f32[16,2048]{1,0:T(8,128)}, f32[288,384]{1,0:T(8,128)S(1)}, f32[72,384]{1,0:T(8,128)S(1)}, f32[72,384]{1,0:T(8,128)...) custom-call(s32[6]{0:T(128)S(1)} %stack.27.ids, f32[128,1024]{1,0:T(8,128)S(1)} %constant_dynamic-update-slice_fusion.refs_0_, ...), custom_call_target="tpu_custom_call" | custom-call | flops 6000000000 | bytes 12582912 | tf_op jit(solution)/shard_map/solve/pallas_call | solution.py:271
  92.7 1.8 %collective-permute-start.26 = (f32[288,384]{1,0:T(8,128)S(1)}, f32[288,384]{1,0:T(8,128)S(1)}, u32[]{:S(2)}, u32[]{:S(2)}) collective-permute-start(f32[288,384]{1,0:T(8,128)S(1)} %get-tuple-element.62), channel_id=1, source_target_pairs={{0,32},{1,225},{2,34},{3,227},{4,36},{5,229},{6,38},{7,231},{8,40}... | collective-permute-start | bytes 1327112 | tf_op jit(solution)/shard_map/ppermute | solution.py:30
  94.6 8.7 %trailing.1 = f32[2048,384]{1,0:T(8,128)} custom-call(s32[6]{0:T(128)S(1)} %stack.27.ids, f32[64,384]{1,0:T(8,128)S(1)} %copy-done, f32[64,384]{1,0:T(8,128)S(1)} %collective-permute-done.18.refs_1_, f32[64,384]{1,0:T(8,128)S(1)} %collective-permute-done.19.refs_2_, f32[64,384]{1,0:T(8,128)S(1)} %collective-permute-done.20.refs_3_, ...), custom_call_target="tpu_custom_call" | custom-call | flops 4000000000 | bytes 11534336 | tf_op jit(solution)/shard_map/trailing/pallas_call | solution.py:293
  103.4 2.8 %collective-permute-start.28 = (f32[72,384]{1,0:T(8,128)S(1)}, f32[72,384]{1,0:T(8,128)S(1)}, u32[]{:S(2)}, u32[]{:S(2)}) collective-permute-start(f32[72,384]{1,0:T(8,128)S(1)} %get-tuple-element.76), channel_id=1, source_target_pairs={{0,64},{32,96},{64,0},{96,32},{128,192},{160,224},{192,128},{224,1... | collective-permute-start | bytes 331784 | tf_op jit(solution)/shard_map/ppermute | solution.py:17
  106.2 2.8 %collective-permute-start.29 = (f32[72,384]{1,0:T(8,128)S(1)}, f32[72,384]{1,0:T(8,128)S(1)}, u32[]{:S(2)}, u32[]{:S(2)}) collective-permute-start(f32[72,384]{1,0:T(8,128)S(1)} %get-tuple-element.74), channel_id=1, source_target_pairs={{0,128},{32,160},{64,192},{96,224},{128,0},{160,32},{192,64},{224,... | collective-permute-start | bytes 331784 | tf_op jit(solution)/shard_map/ppermute | solution.py:17
  109.1 3.4 %collective-permute-done.30 = f32[72,384]{1,0:T(8,128)S(1)} collective-permute-done((f32[72,384]{1,0:T(8,128)S(1)}, f32[72,384]{1,0:T(8,128)S(1)}, u32[]{:S(2)}, u32[]{:S(2)}) %collective-permute-start.30) | collective-permute-done | bytes 110624 | tf_op jit(solution)/shard_map/ppermute | solution.py:17
  112.5 3.4 %collective-permute-done.29 = f32[72,384]{1,0:T(8,128)S(1)} collective-permute-done((f32[72,384]{1,0:T(8,128)S(1)}, f32[72,384]{1,0:T(8,128)S(1)}, u32[]{:S(2)}, u32[]{:S(2)}) %collective-permute-start.29) | collective-permute-done | bytes 110624 | tf_op jit(solution)/shard_map/ppermute | solution.py:17
  (70 shorter events, 10.6 us)
Async XLA Ops:
  0.6 52.0 %copy-start = (f32[64,384]{1,0:T(8,128)S(1)}, f32[64,384]{1,0:T(8,128)}, u32[]{:S(2)}) copy-start(f32[64,384]{1,0:T(8,128)} %refs_0_) | copy-start | bytes 294916
  1.6 4.2 %collective-permute-start.4 = (f32[16,1024]{1,0:T(8,128)S(1)}, f32[16,1024]{1,0:T(8,128)S(1)}, u32[]{:S(2)}, u32[]{:S(2)}) collective-permute-start(f32[16,1024]{1,0:T(8,128)S(1)} %get-tuple-element.78), channel_id=1, source_target_pairs={{0,1},{1,0},{2,3},{3,2},{4,5},{5,4},{6,7},{7,6},{8,9},{9,8},{10,11... | collective-permute-start | bytes 196616 | tf_op jit(solution)/shard_map/ppermute | solution.py:21
  5.8 17.7 %collective-permute-start.5 = (f32[32,1024]{1,0:T(8,128)S(1)}, f32[32,1024]{1,0:T(8,128)S(1)}, u32[]{:S(2)}, u32[]{:S(2)}) collective-permute-start(f32[32,1024]{1,0:T(8,128)S(1)} %pad_maximum_fusion.1), channel_id=1, source_target_pairs={{0,2},{1,9},{2,0},{3,11},{4,6},{5,13},{6,4},{7,15},{8,10},{9,1},{1... | collective-permute-start | bytes 393224 | tf_op jit(solution)/shard_map/ppermute | solution.py:36
  5.9 17.6 %collective-permute-start.6 = (f32[32,1024]{1,0:T(8,128)S(1)}, f32[32,1024]{1,0:T(8,128)S(1)}, u32[]{:S(2)}, u32[]{:S(2)}) collective-permute-start(f32[32,1024]{1,0:T(8,128)S(1)} %pad_maximum_fusion.1), channel_id=1, source_target_pairs={{0,4},{1,17},{2,6},{3,19},{4,0},{5,21},{6,2},{7,23},{8,12},{9,25},... | collective-permute-start | bytes 393224 | tf_op jit(solution)/shard_map/ppermute | solution.py:36
  8.1 15.4 %collective-permute-start.7 = (f32[32,1024]{1,0:T(8,128)S(1)}, f32[32,1024]{1,0:T(8,128)S(1)}, u32[]{:S(2)}, u32[]{:S(2)}) collective-permute-start(f32[32,1024]{1,0:T(8,128)S(1)} %pad_maximum_fusion.1), channel_id=1, source_target_pairs={{0,6},{1,25},{2,4},{3,27},{4,2},{5,29},{6,0},{7,31},{8,14},{9,17},... | collective-permute-start | bytes 393224 | tf_op jit(solution)/shard_map/ppermute | solution.py:36
  10.5 2.0 %collective-permute-start = (f32[8,64]{1,0:T(8,128)S(1)}, f32[8,64]{1,0:T(8,128)S(1)}, u32[]{:S(2)}, u32[]{:S(2)}) collective-permute-start(f32[8,64]{1,0:T(8,128)S(1)} %get-tuple-element.86), channel_id=1, source_target_pairs={{0,1},{1,0},{2,3},{3,2},{4,5},{5,4},{6,7},{7,6},{8,9},{9,8},{10,11... | collective-permute-start | bytes 6152 | tf_op jit(solution)/shard_map/ppermute | solution.py:21
  12.5 6.4 %collective-permute-start.1 = (f32[16,64]{1,0:T(8,128)S(1)}, f32[16,64]{1,0:T(8,128)S(1)}, u32[]{:S(2)}, u32[]{:S(2)}) collective-permute-start(f32[16,64]{1,0:T(8,128)S(1)} %pad_maximum_fusion.4), channel_id=1, source_target_pairs={{0,64},{32,96},{64,0},{96,32},{128,192},{160,224},{192,128},{224,1... | collective-permute-start | bytes 12296 | tf_op jit(solution)/shard_map/ppermute | solution.py:17
  13.7 6.7 %collective-permute-start.2 = (f32[16,64]{1,0:T(8,128)S(1)}, f32[16,64]{1,0:T(8,128)S(1)}, u32[]{:S(2)}, u32[]{:S(2)}) collective-permute-start(f32[16,64]{1,0:T(8,128)S(1)} %pad_maximum_fusion.4), channel_id=1, source_target_pairs={{0,128},{32,160},{64,192},{96,224},{128,0},{160,32},{192,64},{224,... | collective-permute-start | bytes 12296 | tf_op jit(solution)/shard_map/ppermute | solution.py:17
  18.9 4.6 %collective-permute-start.3 = (f32[16,64]{1,0:T(8,128)S(1)}, f32[16,64]{1,0:T(8,128)S(1)}, u32[]{:S(2)}, u32[]{:S(2)}) collective-permute-start(f32[16,64]{1,0:T(8,128)S(1)} %pad_maximum_fusion.4), channel_id=1, source_target_pairs={{0,192},{32,224},{64,128},{96,160},{128,64},{160,96},{192,0},{224,... | collective-permute-start | bytes 12296 | tf_op jit(solution)/shard_map/ppermute | solution.py:17
  23.6 13.0 %collective-permute-start.12 = (f32[128,1024]{1,0:T(8,128)S(1)}, f32[128,1024]{1,0:T(8,128)S(1)}, u32[]{:S(2)}, u32[]{:S(2)}) collective-permute-start(f32[128,1024]{1,0:T(8,128)S(1)} %constant_dynamic-update-slice_fusion.refs_0_), channel_id=1, source_target_pairs={{0,16},{1,5},{2,18},{3,7},{4,20},{5,1},{6,22},{7,3},{8,24},{9,13},... | collective-permute-start | bytes 1572872 | tf_op jit(solution)/shard_map/ppermute | solution.py:36
  25.7 2.6 %collective-permute-start.8 = (f32[16,256]{1,0:T(8,128)S(1)}, f32[16,256]{1,0:T(8,128)S(1)}, u32[]{:S(2)}, u32[]{:S(2)}) collective-permute-start(f32[16,256]{1,0:T(8,128)S(1)} %pad_maximum_fusion.3), channel_id=1, source_target_pairs={{0,32},{32,0},{64,96},{96,64},{128,160},{160,128},{192,224},{224,1... | collective-permute-start | bytes 49160 | tf_op jit(solution)/shard_map/ppermute | solution.py:17
  28.5 8.1 %collective-permute-start.11 = (f32[16,512]{1,0:T(8,128)S(1)}, f32[16,512]{1,0:T(8,128)S(1)}, u32[]{:S(2)}, u32[]{:S(2)}) collective-permute-start(f32[16,512]{1,0:T(8,128)S(1)} %concatenate.31), channel_id=1, source_target_pairs={{0,6},{1,25},{2,4},{3,27},{4,2},{5,29},{6,0},{7,31},{8,14},{9,17},... | collective-permute-start | bytes 98312 | tf_op jit(solution)/shard_map/ppermute | solution.py:36
  31.2 5.4 %collective-permute-start.10 = (f32[16,512]{1,0:T(8,128)S(1)}, f32[16,512]{1,0:T(8,128)S(1)}, u32[]{:S(2)}, u32[]{:S(2)}) collective-permute-start(f32[16,512]{1,0:T(8,128)S(1)} %concatenate.31), channel_id=1, source_target_pairs={{0,4},{1,17},{2,6},{3,19},{4,0},{5,21},{6,2},{7,23},{8,12},{9,25},... | collective-permute-start | bytes 98312 | tf_op jit(solution)/shard_map/ppermute | solution.py:36
  31.2 5.4 %collective-permute-start.9 = (f32[16,512]{1,0:T(8,128)S(1)}, f32[16,512]{1,0:T(8,128)S(1)}, u32[]{:S(2)}, u32[]{:S(2)}) collective-permute-start(f32[16,512]{1,0:T(8,128)S(1)} %concatenate.31), channel_id=1, source_target_pairs={{0,2},{1,9},{2,0},{3,11},{4,6},{5,13},{6,4},{7,15},{8,10},{9,1},{1... | collective-permute-start | bytes 98312 | tf_op jit(solution)/shard_map/ppermute | solution.py:36
  36.6 4.2 %collective-permute-start.13 = (f32[64,512]{1,0:T(8,128)S(1)}, f32[64,512]{1,0:T(8,128)S(1)}, u32[]{:S(2)}, u32[]{:S(2)}) collective-permute-start(f32[64,512]{1,0:T(8,128)S(1)} %pad_maximum_fusion.2), channel_id=1, source_target_pairs={{0,8},{1,3},{2,10},{3,1},{4,12},{5,7},{6,14},{7,5},{8,0},{9,11},{1... | collective-permute-start | bytes 393224 | tf_op jit(solution)/shard_map/ppermute | solution.py:36
  36.8 6.8 %collective-permute-start.14 = (f32[64,512]{1,0:T(8,128)S(1)}, f32[64,512]{1,0:T(8,128)S(1)}, u32[]{:S(2)}, u32[]{:S(2)}) collective-permute-start(f32[64,512]{1,0:T(8,128)S(1)} %pad_maximum_fusion.2), channel_id=1, source_target_pairs={{0,16},{1,5},{2,18},{3,7},{4,20},{5,1},{6,22},{7,3},{8,24},{9,13},... | collective-permute-start | bytes 393224 | tf_op jit(solution)/shard_map/ppermute | solution.py:36
  39.0 5.9 %collective-permute-start.15 = (f32[64,512]{1,0:T(8,128)S(1)}, f32[64,512]{1,0:T(8,128)S(1)}, u32[]{:S(2)}, u32[]{:S(2)}) collective-permute-start(f32[64,512]{1,0:T(8,128)S(1)} %pad_maximum_fusion.2), channel_id=1, source_target_pairs={{0,24},{1,7},{2,26},{3,5},{4,28},{5,3},{6,30},{7,1},{8,16},{9,15},... | collective-permute-start | bytes 393224 | tf_op jit(solution)/shard_map/ppermute | solution.py:36
  44.8 23.6 %collective-permute-start.16 = (f32[128,1024]{1,0:T(8,128)S(1)}, f32[128,1024]{1,0:T(8,128)S(1)}, u32[]{:S(2)}, u32[]{:S(2)}) collective-permute-start(f32[128,1024]{1,0:T(8,128)S(1)} %constant_dynamic-update-slice_fusion.refs_0_), channel_id=1, source_target_pairs={{0,8},{1,3},{2,10},{3,1},{4,12},{5,7},{6,14},{7,5},{8,0},{9,11},{1... | collective-permute-start | bytes 1572872 | tf_op jit(solution)/shard_map/ppermute | solution.py:36
  44.8 23.6 %collective-permute-start.17 = (f32[128,1024]{1,0:T(8,128)S(1)}, f32[128,1024]{1,0:T(8,128)S(1)}, u32[]{:S(2)}, u32[]{:S(2)}) collective-permute-start(f32[128,1024]{1,0:T(8,128)S(1)} %constant_dynamic-update-slice_fusion.refs_0_), channel_id=1, source_target_pairs={{0,24},{1,7},{2,26},{3,5},{4,28},{5,3},{6,30},{7,1},{8,16},{9,15},... | collective-permute-start | bytes 1572872 | tf_op jit(solution)/shard_map/ppermute | solution.py:36
  45.8 25.3 %collective-permute-start.25 = (f32[256,512]{1,0:T(8,128)S(1)}, f32[256,512]{1,0:T(8,128)}, u32[]{:S(2)}, u32[]{:S(2)}) collective-permute-start(f32[256,512]{1,0:T(8,128)S(1)} %constant_dynamic-update-slice_fusion.4.refs_0_), channel_id=1, source_target_pairs={{0,1},{1,0},{2,3},{3,2},{4,5},{5,4},{6,7},{7,6},{8,9},{9,8},{10,11... | collective-permute-start | bytes 1572872 | tf_op jit(solution)/shard_map/ppermute | solution.py:21
  52.7 10.1 %collective-permute-start.18 = (f32[64,384]{1,0:T(8,128)S(1)}, f32[64,384]{1,0:T(8,128)S(1)}, u32[]{:S(2)}, u32[]{:S(2)}) collective-permute-start(f32[64,384]{1,0:T(8,128)S(1)} %copy-done), channel_id=1, source_target_pairs={{0,64},{32,96},{64,0},{96,32},{128,192},{160,224},{192,128},{224,1... | collective-permute-start | bytes 294920 | tf_op jit(solution)/shard_map/ppermute | solution.py:17
  53.9 8.9 %collective-permute-start.19 = (f32[64,384]{1,0:T(8,128)S(1)}, f32[64,384]{1,0:T(8,128)S(1)}, u32[]{:S(2)}, u32[]{:S(2)}) collective-permute-start(f32[64,384]{1,0:T(8,128)S(1)} %copy-done), channel_id=1, source_target_pairs={{0,128},{32,160},{64,192},{96,224},{128,0},{160,32},{192,64},{224,... | collective-permute-start | bytes 294920 | tf_op jit(solution)/shard_map/ppermute | solution.py:17
  62.8 5.6 %collective-permute-start.20 = (f32[64,384]{1,0:T(8,128)S(1)}, f32[64,384]{1,0:T(8,128)S(1)}, u32[]{:S(2)}, u32[]{:S(2)}) collective-permute-start(f32[64,384]{1,0:T(8,128)S(1)} %copy-done), channel_id=1, source_target_pairs={{0,192},{32,224},{64,128},{96,160},{128,64},{160,96},{192,0},{224,... | collective-permute-start | bytes 294920 | tf_op jit(solution)/shard_map/ppermute | solution.py:17
  62.8 19.6 %collective-permute-start.21 = (f32[128,1024]{1,0:T(8,128)S(1)}, f32[128,1024]{1,0:T(8,128)S(1)}, u32[]{:S(2)}, u32[]{:S(2)}) collective-permute-start(f32[128,1024]{1,0:T(8,128)S(1)} %constant_dynamic-update-slice_fusion.refs_0_), channel_id=1, source_target_pairs={{0,1},{1,0},{2,3},{3,2},{4,5},{5,4},{6,7},{7,6},{8,9},{9,8},{10,11... | collective-permute-start | bytes 1572872 | tf_op jit(solution)/shard_map/ppermute | solution.py:21
  68.4 14.0 %collective-permute-start.22 = (f32[128,1024]{1,0:T(8,128)S(1)}, f32[128,1024]{1,0:T(8,128)}, u32[]{:S(2)}, u32[]{:S(2)}) collective-permute-start(f32[128,1024]{1,0:T(8,128)S(1)} %collective-permute-done.16.refs_1_), channel_id=1, source_target_pairs={{0,1},{1,0},{2,3},{3,2},{4,5},{5,4},{6,7},{7,6},{8,9},{9,8},{10,11... | collective-permute-start | bytes 1572872 | tf_op jit(solution)/shard_map/ppermute | solution.py:21
  70.5 12.0 %collective-permute-start.23 = (f32[128,1024]{1,0:T(8,128)S(1)}, f32[128,1024]{1,0:T(8,128)}, u32[]{:S(2)}, u32[]{:S(2)}) collective-permute-start(f32[128,1024]{1,0:T(8,128)S(1)} %collective-permute-done.12.refs_2_), channel_id=1, source_target_pairs={{0,1},{1,0},{2,3},{3,2},{4,5},{5,4},{6,7},{7,6},{8,9},{9,8},{10,11... | collective-permute-start | bytes 1572872 | tf_op jit(solution)/shard_map/ppermute | solution.py:21
  70.6 11.9 %collective-permute-start.24 = (f32[128,1024]{1,0:T(8,128)S(1)}, f32[128,1024]{1,0:T(8,128)}, u32[]{:S(2)}, u32[]{:S(2)}) collective-permute-start(f32[128,1024]{1,0:T(8,128)S(1)} %collective-permute-done.17.refs_3_), channel_id=1, source_target_pairs={{0,1},{1,0},{2,3},{3,2},{4,5},{5,4},{6,7},{7,6},{8,9},{9,8},{10,11... | collective-permute-start | bytes 1572872 | tf_op jit(solution)/shard_map/ppermute | solution.py:21
  71.1 23.4 %collective-permute-start.27 = (f32[256,384]{1,0:T(8,128)S(1)}, f32[256,384]{1,0:T(8,128)S(1)}, u32[]{:S(2)}, u32[]{:S(2)}) collective-permute-start(f32[256,384]{1,0:T(8,128)S(1)} %pad_maximum_fusion), channel_id=1, source_target_pairs={{0,32},{1,225},{2,34},{3,227},{4,36},{5,229},{6,38},{7,231},{8,40}... | collective-permute-start | bytes 1179656 | tf_op jit(solution)/shard_map/ppermute | solution.py:30
  92.7 10.6 %collective-permute-start.26 = (f32[288,384]{1,0:T(8,128)S(1)}, f32[288,384]{1,0:T(8,128)S(1)}, u32[]{:S(2)}, u32[]{:S(2)}) collective-permute-start(f32[288,384]{1,0:T(8,128)S(1)} %get-tuple-element.62), channel_id=1, source_target_pairs={{0,32},{1,225},{2,34},{3,227},{4,36},{5,229},{6,38},{7,231},{8,40}... | collective-permute-start | bytes 1327112 | tf_op jit(solution)/shard_map/ppermute | solution.py:30
  103.3 9.2 %collective-permute-start.30 = (f32[72,384]{1,0:T(8,128)S(1)}, f32[72,384]{1,0:T(8,128)S(1)}, u32[]{:S(2)}, u32[]{:S(2)}) collective-permute-start(f32[72,384]{1,0:T(8,128)S(1)} %get-tuple-element.75), channel_id=1, source_target_pairs={{0,192},{32,224},{64,128},{96,160},{128,64},{160,96},{192,0},{224,... | collective-permute-start | bytes 331784 | tf_op jit(solution)/shard_map/ppermute | solution.py:17
  103.4 9.1 %collective-permute-start.28 = (f32[72,384]{1,0:T(8,128)S(1)}, f32[72,384]{1,0:T(8,128)S(1)}, u32[]{:S(2)}, u32[]{:S(2)}) collective-permute-start(f32[72,384]{1,0:T(8,128)S(1)} %get-tuple-element.76), channel_id=1, source_target_pairs={{0,64},{32,96},{64,0},{96,32},{128,192},{160,224},{192,128},{224,1... | collective-permute-start | bytes 331784 | tf_op jit(solution)/shard_map/ppermute | solution.py:17
  106.2 9.6 %collective-permute-start.29 = (f32[72,384]{1,0:T(8,128)S(1)}, f32[72,384]{1,0:T(8,128)S(1)}, u32[]{:S(2)}, u32[]{:S(2)}) collective-permute-start(f32[72,384]{1,0:T(8,128)S(1)} %get-tuple-element.74), channel_id=1, source_target_pairs={{0,128},{32,160},{64,192},{96,224},{128,0},{160,32},{192,64},{224,... | collective-permute-start | bytes 331784 | tf_op jit(solution)/shard_map/ppermute | solution.py:17
  (5 other events, 58.4 us)

commit v4 on v2

--- a/solution.py
+++ b/solution.py
@@ -36,23 +36,7 @@
     return lax.ppermute(v, "col", perm)
 
 
-def gather_cols(diag, grad, core):
-    wide, narrow = grad.shape[1] // 2, diag.shape[1] // 2
-    low = jnp.concatenate([grad[:, :wide], diag[:, :narrow]], axis=1)
-    high = jnp.concatenate([grad[:, wide:], diag[:, narrow:]], axis=1)
-    kept = jnp.where(core == 0, low, high)
-    given = jnp.where(core == 0, high, low)
-    pair = jnp.concatenate([kept, with_sibling(given)], axis=0)
-    pairs = [pair] + [with_col_partner(pair, 0, k) for k in (1, 2, 3)]
-    diag_quad = jnp.concatenate([p[:, wide:] for p in pairs], axis=0)
-    grad_quad = jnp.concatenate([p[:, :wide] for p in pairs], axis=0)
-    diag_blocks = [diag_quad] + [with_col_partner(diag_quad, 1, k) for k in (1, 2, 3)]
-    grad_quad, diag_blocks = lax.optimization_barrier((grad_quad, diag_blocks))
-    diag_blocks = diag_blocks + [with_sibling(b) for b in diag_blocks]
-    return diag_blocks, grad_quad, [with_col_partner(grad_quad, 1, k) for k in (1, 2, 3)]
-
-
-def place(ids, blocks, store):
+def place(ids, blocks, rows, store):
     y, x, core = ids[1], ids[2], ids[3]
     for other in range(2):
         half = core ^ other
@@ -61,9 +45,8 @@
                 along_x = jnp.where(half == 0, x ^ j, x ^ k)
                 along_y = jnp.where(half == 0, y ^ k, y ^ j)
                 for r in range(2):
-                    row = (along_y * 8 + along_x * 2 + (half ^ r)) * 16
-                    at = (j * 2 + r) * 16
-                    store(half, pl.multiple_of(row, 16), block[at : at + 16, :])
+                    at = (j * 2 + r) * rows
+                    store(half, along_y * 8 + along_x * 2 + (half ^ r), block[at : at + rows, :])
 
 
 def split(v):
@@ -81,19 +64,29 @@
     )
 
 
-def invert_kernel(ids, *refs):
-    blocks = refs[:8]
-    top_out, low_out, held = refs[8:]
-
-    odd = jnp.broadcast_to(ids[0] % 2, (16, 128)) == 1
-
-    def store(half, row, piece):
-        for q in range(2):
-            lanes = piece[:, 128 * q : 128 * q + 128]
-            swapped = jnp.concatenate([lanes[:, 64:], lanes[:, :64]], axis=1)
-            held[(half * 2 + q) ^ (ids[0] // 2), pl.ds(row, 16), :] = jnp.where(odd, swapped, lanes)
-
-    place(ids, blocks, store)
+def invert(ids, blocks, top_out, low_out, held):
+    y, x, core = ids[1], ids[2], ids[3]
+    odd = jnp.broadcast_to(ids[0] % 2, (8, 128)) == 1
+    left = lax.broadcasted_iota(jnp.int32, (8, 128), 1) < 64
+    for other in range(2):
+        even, rest = blocks[2 * other : 2 * other + 2]
+        half = core ^ other
+        for m in range(4):
+            near = (m ^ (ids[0] // 2)) * 32
+            far = (m ^ (ids[5 + other] // 2)) * 32
+            for k in range(4):
+                for j in range(4):
+                    lanes = slice(128 * j, 128 * j + 128)
+                    own_parity = even[pl.ds(pl.multiple_of(near + 8 * k, 8), 8), lanes]
+                    other_parity = rest[pl.ds(pl.multiple_of(far + 8 * k, 8), 8), lanes]
+                    low = jnp.where(odd, other_parity, own_parity)
+                    high = jnp.where(odd, own_parity, other_parity)
+                    along_x = jnp.where(half == 0, x ^ j, x ^ k)
+                    along_y = jnp.where(half == 0, y ^ k, y ^ j)
+                    row = (along_y * 8 + along_x * 2 + half) * 16 + half * 8
+                    held[m, pl.ds(pl.multiple_of(row, 8), 8), :] = jnp.where(left, low, pltpu.roll(high, 64, 1))
+                    row = (along_y * 8 + along_x * 2 + (half ^ 1)) * 16 + half * 8
+                    held[m, pl.ds(pl.multiple_of(row, 8), 8), :] = jnp.where(left, pltpu.roll(low, 64, 1), high)
 
     def part(r, c, n):
         return jnp.concatenate([held[c // 128 + q, r : r + n, :] for q in range(n // 128)], axis=1)
@@ -146,50 +139,58 @@
         out[:, at + 512 : at + 768] = low
 
 
-def split_kernel(trailing, panel, out):
+def split_tall(trailing, panel, out):
     n = trailing.shape[0]
-    side = jnp.concatenate([panel[...], jnp.zeros((112, n), F32)], axis=0).T
-    for v, lanes in ((trailing[...], slice(0, 384)), (side, slice(384, 512))):
+    side = jnp.concatenate([panel, jnp.zeros((112, n), F32)], axis=0).T
+    for v, lanes in ((trailing, slice(0, 384)), (side, slice(384, 512))):
         high, low = split(v)
         out[0:n, lanes] = high
         out[n : 2 * n, lanes] = low
         out[2 * n : 3 * n, lanes] = high
 
 
+def prepare_kernel(ids, *refs):
+    blocks = refs[:4]
+    top_out, low_out, done_out, held = refs[4:]
+    done_out[...] = jnp.zeros_like(done_out)
+    invert(ids, blocks, top_out, low_out, held)
+
+
 def solve_kernel(ids, *refs):
     blocks = refs[:8]
-    inv_top, inv_low, tall = refs[8:11]
-    solved_out, own_out, given_out = refs[11:14]
-    kept_outs = refs[14:18]
-    g, xs, total, corner = refs[18:]
-
-    def store(half, row, piece):
+    inv_top, inv_low, trailing, panel = refs[8:12]
+    solved_out, own_out, given_out = refs[13:16]
+    kept_outs = refs[16:20]
+    g, xs, tall, total, corner = refs[20:]
+
+    def store(half, chunk, piece):
         high, low = split(piece)
+        row = chunk * 16
         row = pl.multiple_of(jnp.where(row < 256, row, row + 512), 16)
         g[half, pl.ds(row, 16), :] = high
         g[half, pl.ds(row + 256, 16), :] = low
         g[half, pl.ds(row + 512, 16), :] = high
 
-    place(ids, blocks, store)
+    place(ids, blocks, 16, store)
     n = TILE
+    own = pl.ds(pl.multiple_of(ids[4] * 16, 16), 16)
     for t in range(2048 // n):
         half, lane = divmod(t * n, 1024)
         slot = t % 2
-        rhs = g[half, :, lane : lane + n]
+        split_tall(trailing[t * n : t * n + n, :], panel[:, t * n : t * n + n], tall.at[slot])
         for rows, lhs, k in ((slice(0, 256), inv_top, 0), (slice(256, 512), inv_low, 768)):
-            x = dot(lhs[...], g[half, k:, lane : lane + n])
-            solved_out[rows, t * n : t * n + n] = x
-            high, low = split(x)
+            part = dot(lhs[...], g[half, k:, lane : lane + n])
+            solved_out[rows, t * n : t * n + n] = part
+            high, low = split(part)
             xs[slot, rows, 0:n] = high
             xs[slot, rows, n : 2 * n] = high
             xs[slot, rows, 2 * n : 3 * n] = low
-        term = dot(xs[slot], tall[3 * n * t : 3 * n * t + 3 * n, :])
+        term = dot(xs[slot], tall[slot])
         if t == 0:
             total[...] = term
         else:
             total[...] += term
 
-    own = pl.ds(pl.multiple_of(ids[4] * 16, 16), 16)
     own_out[...] = solved_out[own, :]
     corner[...] = jnp.zeros_like(corner)
     summed = total[:, 384:512].T
@@ -224,55 +225,43 @@
 TILE = 512
 SMEM = pl.BlockSpec(memory_space=pltpu.SMEM)
 VMEM = pl.BlockSpec(memory_space=pltpu.VMEM)
+HBM = pl.BlockSpec(memory_space=pltpu.HBM)
 
 
 def shape(dims, dtype=F32):
     return jax.ShapeDtypeStruct(dims, dtype)
 
 
-def invert(ids, blocks):
+def prepare(ids, blocks):
     return pl.pallas_call(
-        invert_kernel,
-        out_shape=[shape((256, 1536), BF16), shape((256, 768), BF16)],
-        in_specs=[SMEM] + [VMEM] * 8,
-        out_specs=[VMEM] * 2,
+        prepare_kernel,
+        out_shape=[shape((256, 1536), BF16), shape((256, 768), BF16), shape((8, 128))],
+        in_specs=[SMEM] + [VMEM] * 4,
+        out_specs=[VMEM] * 3,
         scratch_shapes=[pltpu.VMEM((4, B, 128), F32)],
-        compiler_params=pltpu.CompilerParams(vmem_limit_bytes=10 * MIB),
-        cost_estimate=pl.CostEstimate(flops=4_000_000_000, bytes_accessed=2 * MIB, transcendentals=0),
-        name="invert",
+        compiler_params=pltpu.CompilerParams(vmem_limit_bytes=8 * MIB),
+        cost_estimate=pl.CostEstimate(flops=1_000_000, bytes_accessed=1 << 16, transcendentals=0),
+        name="prepare",
     )(ids, *blocks)
 
 
-def split_tall(trailing, panel):
-    n = TILE
-    return pl.pallas_call(
-        split_kernel,
-        grid=(2048 // n,),
-        out_shape=shape((3 * 2048, 512), BF16),
-        in_specs=[pl.BlockSpec((n, 384), lambda i: (i, 0)), pl.BlockSpec((16, n), lambda i: (0, i))],
-        out_specs=pl.BlockSpec((3 * n, 512), lambda i: (i, 0)),
-        compiler_params=pltpu.CompilerParams(vmem_limit_bytes=10 * MIB),
-        cost_estimate=pl.CostEstimate(flops=3_000_000_000, bytes_accessed=9 * MIB, transcendentals=0),
-        name="split_tall",
-    )(trailing, panel)
-
-
-def solve(ids, blocks, inverse, tall):
+def solve(ids, blocks, inverse, trailing, panel, ready):
     return pl.pallas_call(
         solve_kernel,
         out_shape=[shape((B, 2048)), shape((16, 2048)), shape((288, 384))] + [shape((72, 384))] * 4,
-        in_specs=[SMEM] + [VMEM] * 11,
+        in_specs=[SMEM] + [VMEM] * 13,
         out_specs=[VMEM] * 7,
         scratch_shapes=[
             pltpu.VMEM((2, 3 * B, 1024), BF16),
             pltpu.VMEM((2, B, 3 * TILE), BF16),
+            pltpu.VMEM((2, 3 * TILE, 512), BF16),
             pltpu.VMEM((B, 512), F32),
             pltpu.VMEM((ROWS, 8, 384), F32),
         ],
-        compiler_params=pltpu.CompilerParams(vmem_limit_bytes=24 * MIB),
+        compiler_params=pltpu.CompilerParams(vmem_limit_bytes=20 * MIB),
         cost_estimate=pl.CostEstimate(flops=6_000_000_000, bytes_accessed=12 * MIB, transcendentals=0),
         name="solve",
-    )(ids, *blocks, *inverse, tall)
+    )(ids, *blocks, *inverse, trailing, panel, ready)
 
 
 def trailing_update(ids, pieces, solved, grad):
@@ -307,28 +296,43 @@
     col = lax.axis_index("col")
     core = col % 2
     neighbour = jnp.where(core == 0, z ^ 1, (z - 1 + 2 * (z % 2)) % ROWS)
-    ids = jnp.stack([z, col // 8, (col // 2) % 4, core, col, neighbour]).astype(jnp.int32)
-
+    other_neighbour = jnp.where(core == 1, z ^ 1, (z - 1 + 2 * (z % 2)) % ROWS)
+    ids = jnp.stack([z, col // 8, (col // 2) % 4, core, col, neighbour, other_neighbour]).astype(jnp.int32)
+
+    grad = panel_grad.T
+    kept = jnp.where(core == 0, grad[:, :1024], grad[:, 1024:])
+    given = jnp.where(core == 0, grad[:, 1024:], grad[:, :1024])
+    grad_pair = jnp.concatenate([kept, with_sibling(given)], axis=0)
     tile = diag_factor.T
-    even = [tile] + [with_row_partner(tile, k) for k in (2, 4, 6)]
-    odd = with_row_partner(jnp.concatenate(even, axis=1), 1)
-    tiles = [t for j in range(4) for t in (even[j], odd[:, 64 * j : 64 * j + 64])]
-    diag_chunk = jnp.concatenate(tiles, axis=1)
-    diag_blocks, grad_quad, grad_far = gather_cols(diag_chunk, panel_grad.T, core)
+    kept = jnp.where(core == 0, tile[:8], tile[8:])
+    given = jnp.where(core == 0, tile[8:], tile[:8])
+    diag_pair = jnp.concatenate([kept, with_sibling(given)], axis=1)
+
+    both = jnp.concatenate([grad_pair, jnp.pad(diag_pair, ((0, 0), (0, 1024 - 128)))], axis=0)
+    both = [both] + [with_col_partner(both, 0, k) for k in (1, 2, 3)]
+    diag_quad = jnp.concatenate([b[32:, :128] for b in both], axis=1)
+    diag_far = [with_col_partner(diag_quad, 1, k) for k in (1, 2, 3)]
+    diag_far, both = lax.optimization_barrier((diag_far, both))
+    grad_quad = jnp.concatenate([b[:32] for b in both], axis=0)
+    grad_far = [with_col_partner(grad_quad, 1, k) for k in (1, 2, 3)]
+    diag_even = jnp.concatenate([diag_quad] + diag_far, axis=0)
+    diag_even = jnp.concatenate([diag_even] + [with_row_partner(diag_even, k) for k in (2, 4, 6)], axis=0)
+    diag_odd = with_neighbour(diag_even)
+    row_factor, diag_odd = lax.optimization_barrier((row_factor, diag_odd))
+    diag_blocks = [diag_even, diag_odd, with_sibling(diag_even), with_sibling(diag_odd)]
     quad_swapped = with_sibling(grad_quad)
 
-    row_factor, diag_blocks = lax.optimization_barrier((row_factor, diag_blocks))
     row_pieces = [row_factor] + [with_row_partner(row_factor, k) for k in (2, 4, 6)]
-    inverse = invert(ids, diag_blocks)
-    tall = split_tall(trailing_factor, panel_factor.T)
-    grad_far, row_pieces, inverse, tall = lax.optimization_barrier((grad_far, row_pieces, inverse, tall))
+    *inverse, ready = prepare(ids, diag_blocks)
+    grad_far, row_pieces, ready = lax.optimization_barrier((grad_far, row_pieces, ready))
     row_pieces = row_pieces + [with_neighbour(jnp.concatenate(row_pieces, axis=0))]
     grad_blocks = [grad_quad] + grad_far + [quad_swapped] + [with_sibling(b) for b in grad_far]
-    solved, own, given, *kept = solve(ids, grad_blocks, inverse, tall)
+    solved, own, given, *kept = solve(ids, grad_blocks, inverse, trailing_factor, panel_factor.T, ready)
+    trailing_out = trailing_update(ids, row_pieces, solved, trailing_grad)
     taken = with_neighbour(given)
+    taken, trailing_out = lax.optimization_barrier((taken, trailing_out))
     sums = [kept[j] + taken[72 * j : 72 * j + 72] for j in range(4)]
     came = [with_row_partner(sums[j], 2 * j) for j in range(1, 4)]
-    trailing_out = trailing_update(ids, row_pieces, solved, trailing_grad)
 
     total = sums[0] + (came[0] + came[1] + came[2])
     row_out = row_grad - total[0:64, :]

time: 109 us -> 109 us (level)
  waiting for transfers between devices: 26 us -> 39 us
  local copies, waits for them, and re-layouts: 12.3 us -> 3.96 us
  starting transfers between devices: 45.6 us -> 40.3 us
    ppermute x10 -> x9, waiting for transfers between devices: 5.78 us -> 24.1 us  [with_row_partner(): return lax.ppermute(v, 'row', [(i, i ^ k) for i in range(ROWS)])]
    unnamed x24 -> x22, local copies, waits for them, and re-layouts: 10.3 us -> 3.68 us
    ppermute x10 -> x9, starting transfers between devices: 21.2 us -> 16.7 us  [with_row_partner(): return lax.ppermute(v, 'row', [(i, i ^ k) for i in range(ROWS)])]
    ppermute x2 -> x3, waiting for transfers between devices: 5.57 us -> 1.29 us  [with_neighbour(): return lax.ppermute(v, ('row', 'col'), perm)]
    ppermute x9, waiting for transfers between devices: 10.1 us -> 8.25 us  [with_col_partner(): return lax.ppermute(v, 'col', perm)]
    pallas_call x1, Pallas kernels: 7.68 us -> 9.51 us  [solve(): pl.pallas_call(solve_kernel, out_shape=[shape((B, 2048)), shape((16, 2048...]
    ppermute x2 -> x3, starting transfers between devices: 2.76 us -> 1.1 us  [with_neighbour(): return lax.ppermute(v, ('row', 'col'), perm)]
    select_n x1 -> x2, other arithmetic: 0.01 us -> 1.64 us  [the longest x1 0.88 us: on_device(): kept = jnp.where(core == 0, grad[:, :1024], grad[:, 1024:])]
  transfers between devices with their start and end apart: 30 -> 29, of which waited for: 16 -> 18; matrix products, arithmetic and copies ran while one was open for 1% -> 1% of each run, Pallas kernels for 12% -> 20%
where the time goes in v4:
time: 109 us
  starting transfers between devices  40.3 us (37%)
  waiting for transfers between devices  39 us (36%)
  Pallas kernels  21.4 us (20%)
  local copies, waits for them, and re-layouts  3.96 us (4%)
  other arithmetic  3.22 us (3%)
    ppermute x9, waiting for transfers between devices, with_row_partner(): return lax.ppermute(v, 'row', [(i, i ^ k) for i in range(ROWS)])  24.1 us
    ppermute x9, starting transfers between devices, with_row_partner(): return lax.ppermute(v, 'row', [(i, i ^ k) for i in range(ROWS)])  16.7 us
    ppermute x9, starting transfers between devices, with_col_partner(): return lax.ppermute(v, 'col', perm)  11.8 us
    ppermute x8, starting transfers between devices, with_sibling(): return lax.ppermute(v, 'col', [(i, i ^ 1) for i in range(COLS)])  10.7 us
    pallas_call x1, Pallas kernels, solve(): pl.pallas_call(solve_kernel, out_shape=[shape((B, 2048)), shape((16, 2048...  9.51 us
    ppermute x9, waiting for transfers between devices, with_col_partner(): return lax.ppermute(v, 'col', perm)  8.25 us
    pallas_call x1, Pallas kernels, trailing_update(): pl.pallas_call(trailing_kernel, grid=(2048 // tile,), out_shape=shape((20...  7.03 us
    ppermute x8, waiting for transfers between devices, with_sibling(): return lax.ppermute(v, 'col', [(i, i ^ 1) for i in range(COLS)])  5.37 us
  transfers between devices with their start and end apart: 29, of which 18 were waited for; matrix products, arithmetic and copies ran while one was open for 1% of the time, Pallas kernels for 20%

profile of v4, /device:TPU:1, one launch (start us, length us, event | category | flops | bytes accessed | tf_op | source)
XLA Modules:
  0.0 108.8 jit_solution(14787675091535239799)
XLA Ops:
  1.4 3.2 %collective-permute-start = (f32[8,64]{1,0:T(8,128)S(1)}, f32[8,64]{1,0:T(8,128)S(1)}, u32[]{:S(2)}, u32[]{:S(2)}) collective-permute-start(f32[8,64]{1,0:T(8,128)S(1)} %get-tuple-element.69), channel_id=1, source_target_pairs={{0,1},{1,0},{2,3},{3,2},{4,5},{5,4},{6,7},{7,6},{8,9},{9,8},{10,11... | collective-permute-start | bytes 6152 | tf_op jit(solution)/shard_map/ppermute | solution.py:21
  5.7 1.2 %collective-permute-done.1 = f32[16,1024]{1,0:T(8,128)S(1)} collective-permute-done((f32[16,1024]{1,0:T(8,128)S(1)}, f32[16,1024]{1,0:T(8,128)S(1)}, u32[]{:S(2)}, u32[]{:S(2)}) %collective-permute-start.1) | collective-permute-done | bytes 65568 | tf_op jit(solution)/shard_map/ppermute | solution.py:21
  7.0 2.2 %collective-permute-start.3 = (f32[40,1024]{1,0:T(8,128)S(1)}, f32[40,1024]{1,0:T(8,128)S(1)}, u32[]{:S(2)}, u32[]{:S(2)}) collective-permute-start(f32[40,1024]{1,0:T(8,128)S(1)} %pad_maximum_fusion.2), channel_id=1, source_target_pairs={{0,4},{1,17},{2,6},{3,19},{4,0},{5,21},{6,2},{7,23},{8,12},{9,25},... | collective-permute-start | bytes 491528 | tf_op jit(solution)/shard_map/ppermute | solution.py:36
  9.2 1.7 %collective-permute-start.4 = (f32[40,1024]{1,0:T(8,128)S(1)}, f32[40,1024]{1,0:T(8,128)S(1)}, u32[]{:S(2)}, u32[]{:S(2)}) collective-permute-start(f32[40,1024]{1,0:T(8,128)S(1)} %pad_maximum_fusion.2), channel_id=1, source_target_pairs={{0,6},{1,25},{2,4},{3,27},{4,2},{5,29},{6,0},{7,31},{8,14},{9,17},... | collective-permute-start | bytes 491528 | tf_op jit(solution)/shard_map/ppermute | solution.py:36
  11.5 2.5 %collective-permute-done.3 = f32[40,1024]{1,0:T(8,128)S(1)} collective-permute-done((f32[40,1024]{1,0:T(8,128)S(1)}, f32[40,1024]{1,0:T(8,128)S(1)}, u32[]{:S(2)}, u32[]{:S(2)}) %collective-permute-start.3) | collective-permute-done | bytes 163872 | tf_op jit(solution)/shard_map/ppermute | solution.py:36
  13.9 1.8 %collective-permute-done.4 = f32[40,1024]{1,0:T(8,128)S(1)} collective-permute-done((f32[40,1024]{1,0:T(8,128)S(1)}, f32[40,1024]{1,0:T(8,128)S(1)}, u32[]{:S(2)}, u32[]{:S(2)}) %collective-permute-start.4) | collective-permute-done | bytes 163872 | tf_op jit(solution)/shard_map/ppermute | solution.py:36
  16.7 2.6 %collective-permute-start.6 = (f32[8,512]{1,0:T(8,128)S(1)}, f32[8,512]{1,0:T(8,128)S(1)}, u32[]{:S(2)}, u32[]{:S(2)}) collective-permute-start(f32[8,512]{1,0:T(8,128)S(1)} %concatenate.28), channel_id=1, source_target_pairs={{0,16},{1,5},{2,18},{3,7},{4,20},{5,1},{6,22},{7,3},{8,24},{9,13},... | collective-permute-start | bytes 49160 | tf_op jit(solution)/shard_map/ppermute | solution.py:36
  19.7 1.1 %collective-permute-done.6 = f32[8,512]{1,0:T(8,128)S(1)} collective-permute-done((f32[8,512]{1,0:T(8,128)S(1)}, f32[8,512]{1,0:T(8,128)S(1)}, u32[]{:S(2)}, u32[]{:S(2)}) %collective-permute-start.6) | collective-permute-done | bytes 16416 | tf_op jit(solution)/shard_map/ppermute | solution.py:36
  20.8 2.3 %collective-permute-done.7 = f32[8,512]{1,0:T(8,128)S(1)} collective-permute-done((f32[8,512]{1,0:T(8,128)S(1)}, f32[8,512]{1,0:T(8,128)S(1)}, u32[]{:S(2)}, u32[]{:S(2)}) %collective-permute-start.7) | collective-permute-done | bytes 16416 | tf_op jit(solution)/shard_map/ppermute | solution.py:36
  23.1 2.9 %collective-permute-start.11 = (f32[32,512]{1,0:T(8,128)S(1)}, f32[32,512]{1,0:T(8,128)S(1)}, u32[]{:S(2)}, u32[]{:S(2)}) collective-permute-start(f32[32,512]{1,0:T(8,128)S(1)} %pad_maximum_fusion.3), channel_id=1, source_target_pairs={{0,64},{32,96},{64,0},{96,32},{128,192},{160,224},{192,128},{224,1... | collective-permute-start | bytes 196616 | tf_op jit(solution)/shard_map/ppermute | solution.py:17
  26.0 5.1 %collective-permute-start.12 = (f32[32,512]{1,0:T(8,128)S(1)}, f32[32,512]{1,0:T(8,128)S(1)}, u32[]{:S(2)}, u32[]{:S(2)}) collective-permute-start(f32[32,512]{1,0:T(8,128)S(1)} %pad_maximum_fusion.3), channel_id=1, source_target_pairs={{0,128},{32,160},{64,192},{96,224},{128,0},{160,32},{192,64},{224,... | collective-permute-start | bytes 196616 | tf_op jit(solution)/shard_map/ppermute | solution.py:17
  31.2 2.3 %collective-permute-done.12 = f32[32,512]{1,0:T(8,128)S(1)} collective-permute-done((f32[32,512]{1,0:T(8,128)S(1)}, f32[32,512]{1,0:T(8,128)S(1)}, u32[]{:S(2)}, u32[]{:S(2)}) %collective-permute-start.12) | collective-permute-done | bytes 65568 | tf_op jit(solution)/shard_map/ppermute | solution.py:17
  33.5 3.2 %collective-permute-done.13 = f32[32,512]{1,0:T(8,128)S(1)} collective-permute-done((f32[32,512]{1,0:T(8,128)S(1)}, f32[32,512]{1,0:T(8,128)S(1)}, u32[]{:S(2)}, u32[]{:S(2)}) %collective-permute-start.13) | collective-permute-done | bytes 65568 | tf_op jit(solution)/shard_map/ppermute | solution.py:17
  37.6 1.9 %collective-permute-start.9 = (f32[128,1024]{1,0:T(8,128)S(1)}, f32[128,1024]{1,0:T(8,128)}, u32[]{:S(2)}, u32[]{:S(2)}) collective-permute-start(f32[128,1024]{1,0:T(8,128)S(1)} %pad_maximum_fusion.refs_0_), channel_id=1, source_target_pairs={{0,16},{1,5},{2,18},{3,7},{4,20},{5,1},{6,22},{7,3},{8,24},{9,13},... | collective-permute-start | bytes 1572872 | tf_op jit(solution)/shard_map/ppermute | solution.py:36
  39.6 1.9 %collective-permute-start.10 = (f32[128,1024]{1,0:T(8,128)S(1)}, f32[128,1024]{1,0:T(8,128)}, u32[]{:S(2)}, u32[]{:S(2)}) collective-permute-start(f32[128,1024]{1,0:T(8,128)S(1)} %pad_maximum_fusion.refs_0_), channel_id=1, source_target_pairs={{0,24},{1,7},{2,26},{3,5},{4,28},{5,3},{6,30},{7,1},{8,16},{9,15},... | collective-permute-start | bytes 1572872 | tf_op jit(solution)/shard_map/ppermute | solution.py:36
  41.5 6.2 %collective-permute-start.18 = (f32[128,512]{1,0:T(8,128)S(1)}, f32[128,512]{1,0:T(8,128)S(1)}, u32[]{:S(2)}, u32[]{:S(2)}) collective-permute-start(f32[128,512]{1,0:T(8,128)S(1)} %constant_dynamic-update-slice_fusion.refs_0_), channel_id=1, source_target_pairs={{0,1},{1,0},{2,3},{3,2},{4,5},{5,4},{6,7},{7,6},{8,9},{9,8},{10,11... | collective-permute-start | bytes 786440 | tf_op jit(solution)/shard_map/ppermute | solution.py:21
  47.7 1.2 %collective-permute-done.18.refs_2_ = f32[128,512]{1,0:T(8,128)S(1)} collective-permute-done((f32[128,512]{1,0:T(8,128)S(1)}, f32[128,512]{1,0:T(8,128)S(1)}, u32[]{:S(2)}, u32[]{:S(2)}) %collective-permute-start.18) | collective-permute-done | bytes 262176 | tf_op jit(solution)/shard_map/ppermute | solution.py:21
  49.4 7.2 %collective-permute-done.15.refs_1_ = f32[64,384]{1,0:T(8,128)S(1)} collective-permute-done((f32[64,384]{1,0:T(8,128)S(1)}, f32[64,384]{1,0:T(8,128)S(1)}, u32[]{:S(2)}, u32[]{:S(2)}) %collective-permute-start.15) | collective-permute-done | bytes 98336 | tf_op jit(solution)/shard_map/ppermute | solution.py:17
  56.5 2.4 %collective-permute-start.16 = (f32[64,384]{1,0:T(8,128)S(1)}, f32[64,384]{1,0:T(8,128)S(1)}, u32[]{:S(2)}, u32[]{:S(2)}) collective-permute-start(f32[64,384]{1,0:T(8,128)S(1)} %copy-done), channel_id=1, source_target_pairs={{0,128},{32,160},{64,192},{96,224},{128,0},{160,32},{192,64},{224,... | collective-permute-start | bytes 294920 | tf_op jit(solution)/shard_map/ppermute | solution.py:17
  59.1 4.9 %prepare.1 = (bf16[256,1536]{1,0:T(8,128)(2,1)S(1)}, bf16[256,768]{1,0:T(8,128)(2,1)S(1)}, f32[8,128]{1,0:T(8,128)S(1)}) custom-call(s32[7]{0:T(128)S(1)} %stack.31.ids, f32[128,512]{1,0:T(8,128)S(1)} %constant_dynamic-update-slice_fusion.refs_0_, f32[128,512]{1,0:T(8,128)S(1)} %collective-permute-done.14.refs_1_, ...), custom_call_target="tpu_custom_call" | custom-call | flops 1000000 | bytes 65536 | tf_op jit(solution)/shard_map/prepare/pallas_call | solution.py:236
  64.7 3.7 %collective-permute-done.16.refs_2_ = f32[64,384]{1,0:T(8,128)S(1)} collective-permute-done((f32[64,384]{1,0:T(8,128)S(1)}, f32[64,384]{1,0:T(8,128)S(1)}, u32[]{:S(2)}, u32[]{:S(2)}) %collective-permute-start.16) | collective-permute-done | bytes 98336 | tf_op jit(solution)/shard_map/ppermute | solution.py:17
  70.5 1.5 %collective-permute-done.21.refs_5_ = f32[128,1024]{1,0:T(8,128)S(1)} collective-permute-done((f32[128,1024]{1,0:T(8,128)S(1)}, f32[128,1024]{1,0:T(8,128)S(1)}, u32[]{:S(2)}, u32[]{:S(2)}) %collective-permute-start.21) | collective-permute-done | bytes 524320 | tf_op jit(solution)/shard_map/ppermute | solution.py:21
  73.1 1.9 %copy-done.1 = f32[2048,384]{1,0:T(8,128)S(1)} copy-done((f32[2048,384]{1,0:T(8,128)S(1)}, f32[2048,384]{1,0:T(8,128)}, u32[]{:S(2)}) %copy-start.1) | copy-done | bytes 3145752
  74.9 1.0 copy-done.4
  75.9 9.5 %solve.1 = (f32[512,2048]{1,0:T(8,128)S(1)}, f32[16,2048]{1,0:T(8,128)}, f32[288,384]{1,0:T(8,128)S(1)}, f32[72,384]{1,0:T(8,128)S(1)}, f32[72,384]{1,0:T(8,128)...) custom-call(s32[7]{0:T(128)S(1)} %stack.31.ids, f32[128,1024]{1,0:T(8,128)S(1)} %pad_maximum_fusion.refs_0_, ...), custom_call_target="tpu_custom_call" | custom-call | flops 6000000000 | bytes 12582912 | tf_op jit(solution)/shard_map/solve/pallas_call | solution.py:249
  85.5 7.0 %trailing.1 = f32[2048,384]{1,0:T(8,128)} custom-call(s32[7]{0:T(128)S(1)} %stack.31.ids, f32[64,384]{1,0:T(8,128)S(1)} %copy-done, f32[64,384]{1,0:T(8,128)S(1)} %collective-permute-done.15.refs_1_, f32[64,384]{1,0:T(8,128)S(1)} %collective-permute-done.16.refs_2_, f32[64,384]{1,0:T(8,128)S(1)} %collective-permute-done.17.refs_3_, ...), custom_call_target="tpu_custom_call" | custom-call | flops 4000000000 | bytes 11534336 | tf_op jit(solution)/shard_map/trailing/pallas_call | solution.py:269
  92.5 1.3 %collective-permute-done.24 = f32[288,384]{1,0:T(8,128)S(1)} collective-permute-done((f32[288,384]{1,0:T(8,128)S(1)}, f32[288,384]{1,0:T(8,128)S(1)}, u32[]{:S(2)}, u32[]{:S(2)}) %collective-permute-start.24) | collective-permute-done | bytes 442400 | tf_op jit(solution)/shard_map/ppermute | solution.py:30
  93.9 1.0 collective-permute-start.28
  94.8 1.8 %collective-permute-start.26 = (f32[72,384]{1,0:T(8,128)S(1)}, f32[72,384]{1,0:T(8,128)S(1)}, u32[]{:S(2)}, u32[]{:S(2)}) collective-permute-start(f32[72,384]{1,0:T(8,128)S(1)} %get-tuple-element.64), channel_id=1, source_target_pairs={{0,64},{32,96},{64,0},{96,32},{128,192},{160,224},{192,128},{224,1... | collective-permute-start | bytes 331784 | tf_op jit(solution)/shard_map/ppermute | solution.py:17
  96.6 3.0 %collective-permute-start.27 = (f32[72,384]{1,0:T(8,128)S(1)}, f32[72,384]{1,0:T(8,128)S(1)}, u32[]{:S(2)}, u32[]{:S(2)}) collective-permute-start(f32[72,384]{1,0:T(8,128)S(1)} %get-tuple-element.62), channel_id=1, source_target_pairs={{0,128},{32,160},{64,192},{96,224},{128,0},{160,32},{192,64},{224,... | collective-permute-start | bytes 331784 | tf_op jit(solution)/shard_map/ppermute | solution.py:17
  99.6 2.0 %collective-permute-done.28 = f32[72,384]{1,0:T(8,128)S(1)} collective-permute-done((f32[72,384]{1,0:T(8,128)S(1)}, f32[72,384]{1,0:T(8,128)S(1)}, u32[]{:S(2)}, u32[]{:S(2)}) %collective-permute-start.28) | collective-permute-done | bytes 110624 | tf_op jit(solution)/shard_map/ppermute | solution.py:17
  101.6 5.7 %collective-permute-done.27 = f32[72,384]{1,0:T(8,128)S(1)} collective-permute-done((f32[72,384]{1,0:T(8,128)S(1)}, f32[72,384]{1,0:T(8,128)S(1)}, u32[]{:S(2)}, u32[]{:S(2)}) %collective-permute-start.27) | collective-permute-done | bytes 110624 | tf_op jit(solution)/shard_map/ppermute | solution.py:17
  (75 shorter events, 10.9 us)
Async XLA Ops:
  0.6 48.2 %copy-start = (f32[64,384]{1,0:T(8,128)S(1)}, f32[64,384]{1,0:T(8,128)}, u32[]{:S(2)}) copy-start(f32[64,384]{1,0:T(8,128)} %refs_0_) | copy-start | bytes 294916
  0.6 72.4 %copy-start.5 = (f32[2048,16]{0,1:T(8,128)S(1)}, f32[2048,16]{0,1:T(8,128)}, u32[]{:S(2)}) copy-start(f32[2048,16]{0,1:T(8,128)} %param.9) | copy-start | bytes 393220
  1.4 4.2 %collective-permute-start = (f32[8,64]{1,0:T(8,128)S(1)}, f32[8,64]{1,0:T(8,128)S(1)}, u32[]{:S(2)}, u32[]{:S(2)}) collective-permute-start(f32[8,64]{1,0:T(8,128)S(1)} %get-tuple-element.69), channel_id=1, source_target_pairs={{0,1},{1,0},{2,3},{3,2},{4,5},{5,4},{6,7},{7,6},{8,9},{9,8},{10,11... | collective-permute-start | bytes 6152 | tf_op jit(solution)/shard_map/ppermute | solution.py:21
  5.6 1.3 %collective-permute-start.1 = (f32[16,1024]{1,0:T(8,128)S(1)}, f32[16,1024]{1,0:T(8,128)S(1)}, u32[]{:S(2)}, u32[]{:S(2)}) collective-permute-start(f32[16,1024]{1,0:T(8,128)S(1)} %get-tuple-element.66), channel_id=1, source_target_pairs={{0,1},{1,0},{2,3},{3,2},{4,5},{5,4},{6,7},{7,6},{8,9},{9,8},{10,11... | collective-permute-start | bytes 196616 | tf_op jit(solution)/shard_map/ppermute | solution.py:21
  6.9 4.6 %collective-permute-start.2 = (f32[40,1024]{1,0:T(8,128)S(1)}, f32[40,1024]{1,0:T(8,128)S(1)}, u32[]{:S(2)}, u32[]{:S(2)}) collective-permute-start(f32[40,1024]{1,0:T(8,128)S(1)} %pad_maximum_fusion.2), channel_id=1, source_target_pairs={{0,2},{1,9},{2,0},{3,11},{4,6},{5,13},{6,4},{7,15},{8,10},{9,1},{1... | collective-permute-start | bytes 491528 | tf_op jit(solution)/shard_map/ppermute | solution.py:36
  7.0 6.9 %collective-permute-start.3 = (f32[40,1024]{1,0:T(8,128)S(1)}, f32[40,1024]{1,0:T(8,128)S(1)}, u32[]{:S(2)}, u32[]{:S(2)}) collective-permute-start(f32[40,1024]{1,0:T(8,128)S(1)} %pad_maximum_fusion.2), channel_id=1, source_target_pairs={{0,4},{1,17},{2,6},{3,19},{4,0},{5,21},{6,2},{7,23},{8,12},{9,25},... | collective-permute-start | bytes 491528 | tf_op jit(solution)/shard_map/ppermute | solution.py:36
  9.2 6.5 %collective-permute-start.4 = (f32[40,1024]{1,0:T(8,128)S(1)}, f32[40,1024]{1,0:T(8,128)S(1)}, u32[]{:S(2)}, u32[]{:S(2)}) collective-permute-start(f32[40,1024]{1,0:T(8,128)S(1)} %pad_maximum_fusion.2), channel_id=1, source_target_pairs={{0,6},{1,25},{2,4},{3,27},{4,2},{5,29},{6,0},{7,31},{8,14},{9,17},... | collective-permute-start | bytes 491528 | tf_op jit(solution)/shard_map/ppermute | solution.py:36
  15.8 3.9 %collective-permute-start.5 = (f32[8,512]{1,0:T(8,128)S(1)}, f32[8,512]{1,0:T(8,128)S(1)}, u32[]{:S(2)}, u32[]{:S(2)}) collective-permute-start(f32[8,512]{1,0:T(8,128)S(1)} %concatenate.28), channel_id=1, source_target_pairs={{0,8},{1,3},{2,10},{3,1},{4,12},{5,7},{6,14},{7,5},{8,0},{9,11},{1... | collective-permute-start | bytes 49160 | tf_op jit(solution)/shard_map/ppermute | solution.py:36
  16.7 4.1 %collective-permute-start.6 = (f32[8,512]{1,0:T(8,128)S(1)}, f32[8,512]{1,0:T(8,128)S(1)}, u32[]{:S(2)}, u32[]{:S(2)}) collective-permute-start(f32[8,512]{1,0:T(8,128)S(1)} %concatenate.28), channel_id=1, source_target_pairs={{0,16},{1,5},{2,18},{3,7},{4,20},{5,1},{6,22},{7,3},{8,24},{9,13},... | collective-permute-start | bytes 49160 | tf_op jit(solution)/shard_map/ppermute | solution.py:36
  19.3 3.8 %collective-permute-start.7 = (f32[8,512]{1,0:T(8,128)S(1)}, f32[8,512]{1,0:T(8,128)S(1)}, u32[]{:S(2)}, u32[]{:S(2)}) collective-permute-start(f32[8,512]{1,0:T(8,128)S(1)} %concatenate.28), channel_id=1, source_target_pairs={{0,24},{1,7},{2,26},{3,5},{4,28},{5,3},{6,30},{7,1},{8,16},{9,15},... | collective-permute-start | bytes 49160 | tf_op jit(solution)/shard_map/ppermute | solution.py:36
  23.1 8.1 %collective-permute-start.11 = (f32[32,512]{1,0:T(8,128)S(1)}, f32[32,512]{1,0:T(8,128)S(1)}, u32[]{:S(2)}, u32[]{:S(2)}) collective-permute-start(f32[32,512]{1,0:T(8,128)S(1)} %pad_maximum_fusion.3), channel_id=1, source_target_pairs={{0,64},{32,96},{64,0},{96,32},{128,192},{160,224},{192,128},{224,1... | collective-permute-start | bytes 196616 | tf_op jit(solution)/shard_map/ppermute | solution.py:17
  26.0 7.6 %collective-permute-start.12 = (f32[32,512]{1,0:T(8,128)S(1)}, f32[32,512]{1,0:T(8,128)S(1)}, u32[]{:S(2)}, u32[]{:S(2)}) collective-permute-start(f32[32,512]{1,0:T(8,128)S(1)} %pad_maximum_fusion.3), channel_id=1, source_target_pairs={{0,128},{32,160},{64,192},{96,224},{128,0},{160,32},{192,64},{224,... | collective-permute-start | bytes 196616 | tf_op jit(solution)/shard_map/ppermute | solution.py:17
  31.1 5.6 %collective-permute-start.13 = (f32[32,512]{1,0:T(8,128)S(1)}, f32[32,512]{1,0:T(8,128)S(1)}, u32[]{:S(2)}, u32[]{:S(2)}) collective-permute-start(f32[32,512]{1,0:T(8,128)S(1)} %pad_maximum_fusion.3), channel_id=1, source_target_pairs={{0,192},{32,224},{64,128},{96,160},{128,64},{160,96},{192,0},{224,... | collective-permute-start | bytes 196616 | tf_op jit(solution)/shard_map/ppermute | solution.py:17
  36.7 11.0 %collective-permute-start.14 = (f32[128,512]{1,0:T(8,128)S(1)}, f32[128,512]{1,0:T(8,128)S(1)}, u32[]{:S(2)}, u32[]{:S(2)}) collective-permute-start(f32[128,512]{1,0:T(8,128)S(1)} %constant_dynamic-update-slice_fusion.refs_0_), channel_id=1, source_target_pairs={{0,32},{1,225},{2,34},{3,227},{4,36},{5,229},{6,38},{7,231},{8,40}... | collective-permute-start | bytes 786440 | tf_op jit(solution)/shard_map/ppermute | solution.py:30
  37.5 31.4 %collective-permute-start.8 = (f32[128,1024]{1,0:T(8,128)S(1)}, f32[128,1024]{1,0:T(8,128)S(1)}, u32[]{:S(2)}, u32[]{:S(2)}) collective-permute-start(f32[128,1024]{1,0:T(8,128)S(1)} %pad_maximum_fusion.refs_0_), channel_id=1, source_target_pairs={{0,8},{1,3},{2,10},{3,1},{4,12},{5,7},{6,14},{7,5},{8,0},{9,11},{1... | collective-permute-start | bytes 1572872 | tf_op jit(solution)/shard_map/ppermute | solution.py:36
  37.6 31.3 %collective-permute-start.9 = (f32[128,1024]{1,0:T(8,128)S(1)}, f32[128,1024]{1,0:T(8,128)}, u32[]{:S(2)}, u32[]{:S(2)}) collective-permute-start(f32[128,1024]{1,0:T(8,128)S(1)} %pad_maximum_fusion.refs_0_), channel_id=1, source_target_pairs={{0,16},{1,5},{2,18},{3,7},{4,20},{5,1},{6,22},{7,3},{8,24},{9,13},... | collective-permute-start | bytes 1572872 | tf_op jit(solution)/shard_map/ppermute | solution.py:36
  39.6 29.4 %collective-permute-start.10 = (f32[128,1024]{1,0:T(8,128)S(1)}, f32[128,1024]{1,0:T(8,128)}, u32[]{:S(2)}, u32[]{:S(2)}) collective-permute-start(f32[128,1024]{1,0:T(8,128)S(1)} %pad_maximum_fusion.refs_0_), channel_id=1, source_target_pairs={{0,24},{1,7},{2,26},{3,5},{4,28},{5,3},{6,30},{7,1},{8,16},{9,15},... | collective-permute-start | bytes 1572872 | tf_op jit(solution)/shard_map/ppermute | solution.py:36
  41.5 7.4 %collective-permute-start.18 = (f32[128,512]{1,0:T(8,128)S(1)}, f32[128,512]{1,0:T(8,128)S(1)}, u32[]{:S(2)}, u32[]{:S(2)}) collective-permute-start(f32[128,512]{1,0:T(8,128)S(1)} %constant_dynamic-update-slice_fusion.refs_0_), channel_id=1, source_target_pairs={{0,1},{1,0},{2,3},{3,2},{4,5},{5,4},{6,7},{7,6},{8,9},{9,8},{10,11... | collective-permute-start | bytes 786440 | tf_op jit(solution)/shard_map/ppermute | solution.py:21
  47.7 11.2 %collective-permute-start.19 = (f32[128,512]{1,0:T(8,128)S(1)}, f32[128,512]{1,0:T(8,128)S(1)}, u32[]{:S(2)}, u32[]{:S(2)}) collective-permute-start(f32[128,512]{1,0:T(8,128)S(1)} %collective-permute-done.14.refs_1_), channel_id=1, source_target_pairs={{0,1},{1,0},{2,3},{3,2},{4,5},{5,4},{6,7},{7,6},{8,9},{9,8},{10,11... | collective-permute-start | bytes 786440 | tf_op jit(solution)/shard_map/ppermute | solution.py:21
  48.9 7.7 %collective-permute-start.15 = (f32[64,384]{1,0:T(8,128)S(1)}, f32[64,384]{1,0:T(8,128)S(1)}, u32[]{:S(2)}, u32[]{:S(2)}) collective-permute-start(f32[64,384]{1,0:T(8,128)S(1)} %copy-done), channel_id=1, source_target_pairs={{0,64},{32,96},{64,0},{96,32},{128,192},{160,224},{192,128},{224,1... | collective-permute-start | bytes 294920 | tf_op jit(solution)/shard_map/ppermute | solution.py:17
  56.5 11.9 %collective-permute-start.16 = (f32[64,384]{1,0:T(8,128)S(1)}, f32[64,384]{1,0:T(8,128)S(1)}, u32[]{:S(2)}, u32[]{:S(2)}) collective-permute-start(f32[64,384]{1,0:T(8,128)S(1)} %copy-done), channel_id=1, source_target_pairs={{0,128},{32,160},{64,192},{96,224},{128,0},{160,32},{192,64},{224,... | collective-permute-start | bytes 294920 | tf_op jit(solution)/shard_map/ppermute | solution.py:17
  59.0 10.0 %collective-permute-start.17 = (f32[64,384]{1,0:T(8,128)S(1)}, f32[64,384]{1,0:T(8,128)S(1)}, u32[]{:S(2)}, u32[]{:S(2)}) collective-permute-start(f32[64,384]{1,0:T(8,128)S(1)} %copy-done), channel_id=1, source_target_pairs={{0,192},{32,224},{64,128},{96,160},{128,64},{160,96},{192,0},{224,... | collective-permute-start | bytes 294920 | tf_op jit(solution)/shard_map/ppermute | solution.py:17
  68.4 2.0 %collective-permute-start.20 = (f32[128,1024]{1,0:T(8,128)S(1)}, f32[128,1024]{1,0:T(8,128)S(1)}, u32[]{:S(2)}, u32[]{:S(2)}) collective-permute-start(f32[128,1024]{1,0:T(8,128)S(1)} %pad_maximum_fusion.refs_0_), channel_id=1, source_target_pairs={{0,1},{1,0},{2,3},{3,2},{4,5},{5,4},{6,7},{7,6},{8,9},{9,8},{10,11... | collective-permute-start | bytes 1572872 | tf_op jit(solution)/shard_map/ppermute | solution.py:21
  68.9 3.0 %collective-permute-start.21 = (f32[128,1024]{1,0:T(8,128)S(1)}, f32[128,1024]{1,0:T(8,128)S(1)}, u32[]{:S(2)}, u32[]{:S(2)}) collective-permute-start(f32[128,1024]{1,0:T(8,128)S(1)} %collective-permute-done.8.refs_1_), channel_id=1, source_target_pairs={{0,1},{1,0},{2,3},{3,2},{4,5},{5,4},{6,7},{7,6},{8,9},{9,8},{10,11... | collective-permute-start | bytes 1572872 | tf_op jit(solution)/shard_map/ppermute | solution.py:21
  69.1 3.2 %collective-permute-start.22 = (f32[128,1024]{1,0:T(8,128)}, f32[128,1024]{1,0:T(8,128)}, u32[]{:S(2)}, u32[]{:S(2)}) collective-permute-start(f32[128,1024]{1,0:T(8,128)} %collective-permute-done.9.refs_2_), channel_id=1, source_target_pairs={{0,1},{1,0},{2,3},{3,2},{4,5},{5,4},{6,7},{7,6},{8,9},{9,8},{10,11... | collective-permute-start | bytes 1572872 | tf_op jit(solution)/shard_map/ppermute | solution.py:21
  69.5 3.5 %collective-permute-start.23 = (f32[128,1024]{1,0:T(8,128)}, f32[128,1024]{1,0:T(8,128)}, u32[]{:S(2)}, u32[]{:S(2)}) collective-permute-start(f32[128,1024]{1,0:T(8,128)} %collective-permute-done.10.refs_3_), channel_id=1, source_target_pairs={{0,1},{1,0},{2,3},{3,2},{4,5},{5,4},{6,7},{7,6},{8,9},{9,8},{10,11... | collective-permute-start | bytes 1572872 | tf_op jit(solution)/shard_map/ppermute | solution.py:21
  69.7 15.8 %collective-permute-start.25 = (f32[256,384]{1,0:T(8,128)S(1)}, f32[256,384]{1,0:T(8,128)S(1)}, u32[]{:S(2)}, u32[]{:S(2)}) collective-permute-start(f32[256,384]{1,0:T(8,128)S(1)} %pad_maximum_fusion.1), channel_id=1, source_target_pairs={{0,32},{1,225},{2,34},{3,227},{4,36},{5,229},{6,38},{7,231},{8,40}... | collective-permute-start | bytes 1179656 | tf_op jit(solution)/shard_map/ppermute | solution.py:30
  85.4 8.4 %collective-permute-start.24 = (f32[288,384]{1,0:T(8,128)S(1)}, f32[288,384]{1,0:T(8,128)S(1)}, u32[]{:S(2)}, u32[]{:S(2)}) collective-permute-start(f32[288,384]{1,0:T(8,128)S(1)} %get-tuple-element.50), channel_id=1, source_target_pairs={{0,32},{1,225},{2,34},{3,227},{4,36},{5,229},{6,38},{7,231},{8,40}... | collective-permute-start | bytes 1327112 | tf_op jit(solution)/shard_map/ppermute | solution.py:30
  85.5 22.6 %copy-start.7 = (f32[64,16]{0,1:T(8,128)S(1)}, f32[64,16]{0,1:T(8,128)}, u32[]{:S(2)}) copy-start(f32[64,16]{0,1:T(8,128)} %param.13) | copy-start | bytes 12292
  93.9 7.7 %collective-permute-start.28 = (f32[72,384]{1,0:T(8,128)S(1)}, f32[72,384]{1,0:T(8,128)S(1)}, u32[]{:S(2)}, u32[]{:S(2)}) collective-permute-start(f32[72,384]{1,0:T(8,128)S(1)} %get-tuple-element.63), channel_id=1, source_target_pairs={{0,192},{32,224},{64,128},{96,160},{128,64},{160,96},{192,0},{224,... | collective-permute-start | bytes 331784 | tf_op jit(solution)/shard_map/ppermute | solution.py:17
  94.8 6.7 %collective-permute-start.26 = (f32[72,384]{1,0:T(8,128)S(1)}, f32[72,384]{1,0:T(8,128)S(1)}, u32[]{:S(2)}, u32[]{:S(2)}) collective-permute-start(f32[72,384]{1,0:T(8,128)S(1)} %get-tuple-element.64), channel_id=1, source_target_pairs={{0,64},{32,96},{64,0},{96,32},{128,192},{160,224},{192,128},{224,1... | collective-permute-start | bytes 331784 | tf_op jit(solution)/shard_map/ppermute | solution.py:17
  96.6 10.7 %collective-permute-start.27 = (f32[72,384]{1,0:T(8,128)S(1)}, f32[72,384]{1,0:T(8,128)S(1)}, u32[]{:S(2)}, u32[]{:S(2)}) collective-permute-start(f32[72,384]{1,0:T(8,128)S(1)} %get-tuple-element.62), channel_id=1, source_target_pairs={{0,128},{32,160},{64,192},{96,224},{128,0},{160,32},{192,64},{224,... | collective-permute-start | bytes 331784 | tf_op jit(solution)/shard_map/ppermute | solution.py:17
  (5 other events, 35.1 us)

commit v5 on v4

--- a/solution.py
+++ b/solution.py
@@ -36,17 +36,15 @@
     return lax.ppermute(v, "col", perm)
 
 
-def place(ids, blocks, rows, store):
-    y, x, core = ids[1], ids[2], ids[3]
-    for other in range(2):
-        half = core ^ other
-        for k, block in enumerate(blocks[4 * other : 4 * other + 4]):
-            for j in range(4):
-                along_x = jnp.where(half == 0, x ^ j, x ^ k)
-                along_y = jnp.where(half == 0, y ^ k, y ^ j)
-                for r in range(2):
-                    at = (j * 2 + r) * rows
-                    store(half, along_y * 8 + along_x * 2 + (half ^ r), block[at : at + rows, :])
+def place(ids, blocks, other, store):
+    y, x, half = ids[1], ids[2], ids[3] ^ other
+    for k, block in enumerate(blocks):
+        for j in range(4):
+            along_x = jnp.where(half == 0, x ^ j, x ^ k)
+            along_y = jnp.where(half == 0, y ^ k, y ^ j)
+            for r in range(2):
+                at = (j * 2 + r) * 16
+                store((along_y * 8 + along_x * 2 + (half ^ r)) * 16, block[at : at + 16, :])
 
 
 def split(v):
@@ -151,36 +149,36 @@
 
 def prepare_kernel(ids, *refs):
     blocks = refs[:4]
-    top_out, low_out, done_out, held = refs[4:]
-    done_out[...] = jnp.zeros_like(done_out)
+    top_out, low_out, held = refs[4:]
     invert(ids, blocks, top_out, low_out, held)
 
 
 def solve_kernel(ids, *refs):
     blocks = refs[:8]
     inv_top, inv_low, trailing, panel = refs[8:12]
-    solved_out, own_out, given_out = refs[13:16]
-    kept_outs = refs[16:20]
-    g, xs, tall, total, corner = refs[20:]
-
-    def store(half, chunk, piece):
-        high, low = split(piece)
-        row = chunk * 16
-        row = pl.multiple_of(jnp.where(row < 256, row, row + 512), 16)
-        g[half, pl.ds(row, 16), :] = high
-        g[half, pl.ds(row + 256, 16), :] = low
-        g[half, pl.ds(row + 512, 16), :] = high
-
-    place(ids, blocks, 16, store)
+    solved_out, own_out, given_out = refs[12:15]
+    kept_outs = refs[15:19]
+    g, xs, tall, total, corner = refs[19:]
+
     n = TILE
-    own = pl.ds(pl.multiple_of(ids[4] * 16, 16), 16)
     for t in range(2048 // n):
-        half, lane = divmod(t * n, 1024)
+        other, lane = divmod(t * n, 1024)
+        if lane == 0:
+
+            def store(row, piece):
+                high, low = split(piece)
+                row = pl.multiple_of(jnp.where(row < 256, row, row + 512), 16)
+                g[other, pl.ds(row, 16), :] = high
+                g[other, pl.ds(row + 256, 16), :] = low
+                g[other, pl.ds(row + 512, 16), :] = high
+
+            place(ids, blocks[4 * other : 4 * other + 4], other, store)
         slot = t % 2
-        split_tall(trailing[t * n : t * n + n, :], panel[:, t * n : t * n + n], tall.at[slot])
+        here = pl.ds(pl.multiple_of((ids[3] ^ other) * 1024 + lane, n), n)
+        split_tall(trailing[here, :], panel[:, here], tall.at[slot])
         for rows, lhs, k in ((slice(0, 256), inv_top, 0), (slice(256, 512), inv_low, 768)):
-            part = dot(lhs[...], g[half, k:, lane : lane + n])
-            solved_out[rows, t * n : t * n + n] = part
+            part = dot(lhs[...], g[other, k:, lane : lane + n])
+            solved_out[rows, here] = part
             high, low = split(part)
             xs[slot, rows, 0:n] = high
             xs[slot, rows, n : 2 * n] = high
@@ -191,6 +189,7 @@
         else:
             total[...] += term
 
+    own = pl.ds(pl.multiple_of(ids[4] * 16, 16), 16)
     own_out[...] = solved_out[own, :]
     corner[...] = jnp.zeros_like(corner)
     summed = total[:, 384:512].T
@@ -235,9 +234,9 @@
 def prepare(ids, blocks):
     return pl.pallas_call(
         prepare_kernel,
-        out_shape=[shape((256, 1536), BF16), shape((256, 768), BF16), shape((8, 128))],
+        out_shape=[shape((256, 1536), BF16), shape((256, 768), BF16)],
         in_specs=[SMEM] + [VMEM] * 4,
-        out_specs=[VMEM] * 3,
+        out_specs=[VMEM] * 2,
         scratch_shapes=[pltpu.VMEM((4, B, 128), F32)],
         compiler_params=pltpu.CompilerParams(vmem_limit_bytes=8 * MIB),
         cost_estimate=pl.CostEstimate(flops=1_000_000, bytes_accessed=1 << 16, transcendentals=0),
@@ -245,11 +244,11 @@
     )(ids, *blocks)
 
 
-def solve(ids, blocks, inverse, trailing, panel, ready):
+def solve(ids, blocks, inverse, trailing, panel):
     return pl.pallas_call(
         solve_kernel,
         out_shape=[shape((B, 2048)), shape((16, 2048)), shape((288, 384))] + [shape((72, 384))] * 4,
-        in_specs=[SMEM] + [VMEM] * 13,
+        in_specs=[SMEM] + [VMEM] * 12,
         out_specs=[VMEM] * 7,
         scratch_shapes=[
             pltpu.VMEM((2, 3 * B, 1024), BF16),
@@ -261,7 +260,7 @@
         compiler_params=pltpu.CompilerParams(vmem_limit_bytes=20 * MIB),
         cost_estimate=pl.CostEstimate(flops=6_000_000_000, bytes_accessed=12 * MIB, transcendentals=0),
         name="solve",
-    )(ids, *blocks, *inverse, trailing, panel, ready)
+    )(ids, *blocks, *inverse, trailing, panel)
 
 
 def trailing_update(ids, pieces, solved, grad):
@@ -316,18 +315,21 @@
     grad_quad = jnp.concatenate([b[:32] for b in both], axis=0)
     grad_far = [with_col_partner(grad_quad, 1, k) for k in (1, 2, 3)]
     diag_even = jnp.concatenate([diag_quad] + diag_far, axis=0)
-    diag_even = jnp.concatenate([diag_even] + [with_row_partner(diag_even, k) for k in (2, 4, 6)], axis=0)
+    diag_even = [diag_even] + [with_row_partner(diag_even, k) for k in (2, 4, 6)]
+    diag_even, grad_far[0], grad_far[2] = lax.optimization_barrier((diag_even, grad_far[0], grad_far[2]))
+    diag_even = jnp.concatenate(diag_even, axis=0)
+    row_factor, diag_even = lax.optimization_barrier((row_factor, diag_even))
     diag_odd = with_neighbour(diag_even)
-    row_factor, diag_odd = lax.optimization_barrier((row_factor, diag_odd))
     diag_blocks = [diag_even, diag_odd, with_sibling(diag_even), with_sibling(diag_odd)]
     quad_swapped = with_sibling(grad_quad)
 
     row_pieces = [row_factor] + [with_row_partner(row_factor, k) for k in (2, 4, 6)]
-    *inverse, ready = prepare(ids, diag_blocks)
-    grad_far, row_pieces, ready = lax.optimization_barrier((grad_far, row_pieces, ready))
-    row_pieces = row_pieces + [with_neighbour(jnp.concatenate(row_pieces, axis=0))]
+    inverse = prepare(ids, diag_blocks)
+    row_joined = jnp.concatenate(row_pieces, axis=0)
+    panel, row_joined = lax.optimization_barrier((panel_factor.T, row_joined))
+    row_pieces = row_pieces + [with_neighbour(row_joined)]
     grad_blocks = [grad_quad] + grad_far + [quad_swapped] + [with_sibling(b) for b in grad_far]
-    solved, own, given, *kept = solve(ids, grad_blocks, inverse, trailing_factor, panel_factor.T, ready)
+    solved, own, given, *kept = solve(ids, grad_blocks, inverse, trailing_factor, panel)
     trailing_out = trailing_update(ids, row_pieces, solved, trailing_grad)
     taken = with_neighbour(given)
     taken, trailing_out = lax.optimization_barrier((taken, trailing_out))

time: 109 us -> 107 us (0.982)
  waiting for transfers between devices: 39 us -> 31.5 us
  starting transfers between devices: 40.3 us -> 46.8 us
    ppermute x3, starting transfers between devices: 1.1 us -> 5.05 us  [with_neighbour(): return lax.ppermute(v, ('row', 'col'), perm)]
    ppermute x9, waiting for transfers between devices: 24.1 us -> 20.4 us  [with_row_partner(): return lax.ppermute(v, 'row', [(i, i ^ k) for i in range(ROWS)])]
    ppermute x8, waiting for transfers between devices: 5.37 us -> 2.82 us  [with_sibling(): return lax.ppermute(v, 'col', [(i, i ^ 1) for i in range(COLS)])]
    ppermute x9, starting transfers between devices: 16.7 us -> 19.2 us  [with_row_partner(): return lax.ppermute(v, 'row', [(i, i ^ k) for i in range(ROWS)])]
    ppermute x8, starting transfers between devices: 10.7 us -> 12 us  [with_sibling(): return lax.ppermute(v, 'col', [(i, i ^ 1) for i in range(COLS)])]
    ppermute x9, waiting for transfers between devices: 8.25 us -> 7.04 us  [with_col_partner(): return lax.ppermute(v, 'col', perm)]
    ppermute x9, starting transfers between devices: 11.8 us -> 10.6 us  [with_col_partner(): return lax.ppermute(v, 'col', perm)]
    unnamed x22 -> x12, local copies, waits for them, and re-layouts: 3.68 us -> 2.81 us
  transfers between devices with their start and end apart: 29 -> 29, of which waited for: 18 -> 14; matrix products, arithmetic and copies ran while one was open for 1% -> 1% of each run, Pallas kernels for 20% -> 20%
where the time goes in v5:
time: 107 us
  starting transfers between devices  46.8 us (44%)
  waiting for transfers between devices  31.5 us (29%)
  Pallas kernels  21.2 us (20%)
  other arithmetic  3.21 us (3%)
  local copies, waits for them, and re-layouts  3.09 us (3%)
    ppermute x9, waiting for transfers between devices, with_row_partner(): return lax.ppermute(v, 'row', [(i, i ^ k) for i in range(ROWS)])  20.4 us
    ppermute x9, starting transfers between devices, with_row_partner(): return lax.ppermute(v, 'row', [(i, i ^ k) for i in range(ROWS)])  19.2 us
    ppermute x8, starting transfers between devices, with_sibling(): return lax.ppermute(v, 'col', [(i, i ^ 1) for i in range(COLS)])  12 us
    ppermute x9, starting transfers between devices, with_col_partner(): return lax.ppermute(v, 'col', perm)  10.6 us
    pallas_call x1, Pallas kernels, solve(): pl.pallas_call(solve_kernel, out_shape=[shape((B, 2048)), shape((16, 2048...  9.29 us
    ppermute x9, waiting for transfers between devices, with_col_partner(): return lax.ppermute(v, 'col', perm)  7.04 us
    pallas_call x1, Pallas kernels, trailing_update(): pl.pallas_call(trailing_kernel, grid=(2048 // tile,), out_shape=shape((20...  7.03 us
    ppermute x3, starting transfers between devices, with_neighbour(): return lax.ppermute(v, ('row', 'col'), perm)  5.05 us
  transfers between devices with their start and end apart: 29, of which 14 were waited for; matrix products, arithmetic and copies ran while one was open for 1% of the time, Pallas kernels for 20%

profile of v5, /device:TPU:1, one launch (start us, length us, event | category | flops | bytes accessed | tf_op | source)
XLA Modules:
  0.0 106.6 jit_solution(11149447096431809586)
XLA Ops:
  1.4 3.2 %collective-permute-start = (f32[8,64]{1,0:T(8,128)S(1)}, f32[8,64]{1,0:T(8,128)S(1)}, u32[]{:S(2)}, u32[]{:S(2)}) collective-permute-start(f32[8,64]{1,0:T(8,128)S(1)} %get-tuple-element.67), channel_id=1, source_target_pairs={{0,1},{1,0},{2,3},{3,2},{4,5},{5,4},{6,7},{7,6},{8,9},{9,8},{10,11... | collective-permute-start | bytes 6152 | tf_op jit(solution)/shard_map/ppermute | solution.py:21
  5.7 1.2 %collective-permute-done.1 = f32[16,1024]{1,0:T(8,128)S(1)} collective-permute-done((f32[16,1024]{1,0:T(8,128)S(1)}, f32[16,1024]{1,0:T(8,128)S(1)}, u32[]{:S(2)}, u32[]{:S(2)}) %collective-permute-start.1) | collective-permute-done | bytes 65568 | tf_op jit(solution)/shard_map/ppermute | solution.py:21
  6.9 1.1 %collective-permute-start.4 = (f32[40,1024]{1,0:T(8,128)S(1)}, f32[40,1024]{1,0:T(8,128)S(1)}, u32[]{:S(2)}, u32[]{:S(2)}) collective-permute-start(f32[40,1024]{1,0:T(8,128)S(1)} %pad_maximum_fusion.3), channel_id=1, source_target_pairs={{0,6},{1,25},{2,4},{3,27},{4,2},{5,29},{6,0},{7,31},{8,14},{9,17},... | collective-permute-start | bytes 491528 | tf_op jit(solution)/shard_map/ppermute | solution.py:36
  8.3 1.9 %collective-permute-start.2 = (f32[40,1024]{1,0:T(8,128)S(1)}, f32[40,1024]{1,0:T(8,128)S(1)}, u32[]{:S(2)}, u32[]{:S(2)}) collective-permute-start(f32[40,1024]{1,0:T(8,128)S(1)} %pad_maximum_fusion.3), channel_id=1, source_target_pairs={{0,2},{1,9},{2,0},{3,11},{4,6},{5,13},{6,4},{7,15},{8,10},{9,1},{1... | collective-permute-start | bytes 491528 | tf_op jit(solution)/shard_map/ppermute | solution.py:36
  10.2 4.2 %collective-permute-done.4 = f32[40,1024]{1,0:T(8,128)S(1)} collective-permute-done((f32[40,1024]{1,0:T(8,128)S(1)}, f32[40,1024]{1,0:T(8,128)S(1)}, u32[]{:S(2)}, u32[]{:S(2)}) %collective-permute-start.4) | collective-permute-done | bytes 163872 | tf_op jit(solution)/shard_map/ppermute | solution.py:36
  15.1 1.5 %collective-permute-start.7 = (f32[8,512]{1,0:T(8,128)S(1)}, f32[8,512]{1,0:T(8,128)S(1)}, u32[]{:S(2)}, u32[]{:S(2)}) collective-permute-start(f32[8,512]{1,0:T(8,128)S(1)} %concatenate.27), channel_id=1, source_target_pairs={{0,24},{1,7},{2,26},{3,5},{4,28},{5,3},{6,30},{7,1},{8,16},{9,15},... | collective-permute-start | bytes 49160 | tf_op jit(solution)/shard_map/ppermute | solution.py:36
  16.7 1.6 %collective-permute-start.5 = (f32[8,512]{1,0:T(8,128)S(1)}, f32[8,512]{1,0:T(8,128)S(1)}, u32[]{:S(2)}, u32[]{:S(2)}) collective-permute-start(f32[8,512]{1,0:T(8,128)S(1)} %concatenate.27), channel_id=1, source_target_pairs={{0,8},{1,3},{2,10},{3,1},{4,12},{5,7},{6,14},{7,5},{8,0},{9,11},{1... | collective-permute-start | bytes 49160 | tf_op jit(solution)/shard_map/ppermute | solution.py:36
  18.9 1.7 %collective-permute-done.6 = f32[8,512]{1,0:T(8,128)S(1)} collective-permute-done((f32[8,512]{1,0:T(8,128)S(1)}, f32[8,512]{1,0:T(8,128)S(1)}, u32[]{:S(2)}, u32[]{:S(2)}) %collective-permute-start.6) | collective-permute-done | bytes 16416 | tf_op jit(solution)/shard_map/ppermute | solution.py:36
  20.7 1.3 %collective-permute-start.12 = (f32[128,1024]{1,0:T(8,128)S(1)}, f32[128,1024]{1,0:T(8,128)S(1)}, u32[]{:S(2)}, u32[]{:S(2)}) collective-permute-start(f32[128,1024]{1,0:T(8,128)S(1)} %pad_maximum_fusion.refs_0_), channel_id=1, source_target_pairs={{0,24},{1,7},{2,26},{3,5},{4,28},{5,3},{6,30},{7,1},{8,16},{9,15},... | collective-permute-start | bytes 1572872 | tf_op jit(solution)/shard_map/ppermute | solution.py:36
  22.1 2.6 %collective-permute-start.13 = (f32[128,1024]{1,0:T(8,128)S(1)}, f32[128,1024]{1,0:T(8,128)S(1)}, u32[]{:S(2)}, u32[]{:S(2)}) collective-permute-start(f32[128,1024]{1,0:T(8,128)S(1)} %pad_maximum_fusion.refs_0_), channel_id=1, source_target_pairs={{0,16},{1,5},{2,18},{3,7},{4,20},{5,1},{6,22},{7,3},{8,24},{9,13},... | collective-permute-start | bytes 1572872 | tf_op jit(solution)/shard_map/ppermute | solution.py:36
  24.7 5.7 %collective-permute-start.10 = (f32[32,512]{1,0:T(8,128)S(1)}, f32[32,512]{1,0:T(8,128)S(1)}, u32[]{:S(2)}, u32[]{:S(2)}) collective-permute-start(f32[32,512]{1,0:T(8,128)S(1)} %pad_maximum_fusion.4), channel_id=1, source_target_pairs={{0,192},{32,224},{64,128},{96,160},{128,64},{160,96},{192,0},{224,... | collective-permute-start | bytes 196616 | tf_op jit(solution)/shard_map/ppermute | solution.py:17
  32.2 1.1 %collective-permute-start.8 = (f32[32,512]{1,0:T(8,128)S(1)}, f32[32,512]{1,0:T(8,128)S(1)}, u32[]{:S(2)}, u32[]{:S(2)}) collective-permute-start(f32[32,512]{1,0:T(8,128)S(1)} %pad_maximum_fusion.4), channel_id=1, source_target_pairs={{0,64},{32,96},{64,0},{96,32},{128,192},{160,224},{192,128},{224,1... | collective-permute-start | bytes 196616 | tf_op jit(solution)/shard_map/ppermute | solution.py:17
  33.2 4.7 %collective-permute-done.9 = f32[32,512]{1,0:T(8,128)S(1)} collective-permute-done((f32[32,512]{1,0:T(8,128)S(1)}, f32[32,512]{1,0:T(8,128)S(1)}, u32[]{:S(2)}, u32[]{:S(2)}) %collective-permute-start.9) | collective-permute-done | bytes 65568 | tf_op jit(solution)/shard_map/ppermute | solution.py:17
  38.0 5.2 %collective-permute-start.19 = (f32[128,512]{1,0:T(8,128)S(1)}, f32[128,512]{1,0:T(8,128)S(1)}, u32[]{:S(2)}, u32[]{:S(2)}) collective-permute-start(f32[128,512]{1,0:T(8,128)S(1)} %pad_maximum_fusion.2.refs_0_), channel_id=1, source_target_pairs={{0,1},{1,0},{2,3},{3,2},{4,5},{5,4},{6,7},{7,6},{8,9},{9,8},{10,11... | collective-permute-start | bytes 786440 | tf_op jit(solution)/shard_map/ppermute | solution.py:21
  43.2 3.4 %collective-permute-start.23 = (f32[64,384]{1,0:T(8,128)S(1)}, f32[64,384]{1,0:T(8,128)S(1)}, u32[]{:S(2)}, u32[]{:S(2)}) collective-permute-start(f32[64,384]{1,0:T(8,128)S(1)} %copy-done), channel_id=1, source_target_pairs={{0,192},{32,224},{64,128},{96,160},{128,64},{160,96},{192,0},{224,... | collective-permute-start | bytes 294920 | tf_op jit(solution)/shard_map/ppermute | solution.py:17
  46.7 1.3 %collective-permute-start.22 = (f32[64,384]{1,0:T(8,128)S(1)}, f32[64,384]{1,0:T(8,128)S(1)}, u32[]{:S(2)}, u32[]{:S(2)}) collective-permute-start(f32[64,384]{1,0:T(8,128)S(1)} %copy-done), channel_id=1, source_target_pairs={{0,128},{32,160},{64,192},{96,224},{128,0},{160,32},{192,64},{224,... | collective-permute-start | bytes 294920 | tf_op jit(solution)/shard_map/ppermute | solution.py:17
  48.9 2.4 %collective-permute-start.18 = (f32[128,512]{1,0:T(8,128)S(1)}, f32[128,512]{1,0:T(8,128)S(1)}, u32[]{:S(2)}, u32[]{:S(2)}) collective-permute-start(f32[128,512]{1,0:T(8,128)S(1)} %pad_maximum_fusion.2.refs_0_), channel_id=1, source_target_pairs={{0,32},{1,225},{2,34},{3,227},{4,36},{5,229},{6,38},{7,231},{8,40}... | collective-permute-start | bytes 786440 | tf_op jit(solution)/shard_map/ppermute | solution.py:30
  51.3 3.9 %collective-permute-done.23.refs_3_ = f32[64,384]{1,0:T(8,128)S(1)} collective-permute-done((f32[64,384]{1,0:T(8,128)S(1)}, f32[64,384]{1,0:T(8,128)S(1)}, u32[]{:S(2)}, u32[]{:S(2)}) %collective-permute-start.23) | collective-permute-done | bytes 98336 | tf_op jit(solution)/shard_map/ppermute | solution.py:17
  55.8 1.8 %collective-permute-start.15 = (f32[128,1024]{1,0:T(8,128)S(1)}, f32[128,1024]{1,0:T(8,128)}, u32[]{:S(2)}, u32[]{:S(2)}) collective-permute-start(f32[128,1024]{1,0:T(8,128)S(1)} %collective-permute-done.11.refs_1_), channel_id=1, source_target_pairs={{0,1},{1,0},{2,3},{3,2},{4,5},{5,4},{6,7},{7,6},{8,9},{9,8},{10,11... | collective-permute-start | bytes 1572872 | tf_op jit(solution)/shard_map/ppermute | solution.py:21
  57.6 1.8 %collective-permute-done.21.refs_1_ = f32[64,384]{1,0:T(8,128)S(1)} collective-permute-done((f32[64,384]{1,0:T(8,128)S(1)}, f32[64,384]{1,0:T(8,128)S(1)}, u32[]{:S(2)}, u32[]{:S(2)}) %collective-permute-start.21) | collective-permute-done | bytes 98336 | tf_op jit(solution)/shard_map/ppermute | solution.py:17
  60.6 1.7 %collective-permute-done.20.refs_3_ = f32[128,512]{1,0:T(8,128)S(1)} collective-permute-done((f32[128,512]{1,0:T(8,128)S(1)}, f32[128,512]{1,0:T(8,128)S(1)}, u32[]{:S(2)}, u32[]{:S(2)}) %collective-permute-start.20) | collective-permute-done | bytes 262176 | tf_op jit(solution)/shard_map/ppermute | solution.py:21
  62.2 2.6 %collective-permute-start.25 = (f32[256,384]{1,0:T(8,128)S(1)}, f32[256,384]{1,0:T(8,128)S(1)}, u32[]{:S(2)}, u32[]{:S(2)}) collective-permute-start(f32[256,384]{1,0:T(8,128)S(1)} %pad_maximum_fusion.1), channel_id=1, source_target_pairs={{0,32},{1,225},{2,34},{3,227},{4,36},{5,229},{6,38},{7,231},{8,40}... | collective-permute-start | bytes 1179656 | tf_op jit(solution)/shard_map/ppermute | solution.py:30
  64.8 4.9 %prepare.1 = (bf16[256,1536]{1,0:T(8,128)(2,1)S(1)}, bf16[256,768]{1,0:T(8,128)(2,1)S(1)}) custom-call(s32[7]{0:T(128)S(1)} %stack.31.ids, f32[128,512]{1,0:T(8,128)S(1)} %pad_maximum_fusion.2.refs_0_, f32[128,512]{1,0:T(8,128)S(1)} %collective-permute-done.18.refs_1_, f32[128,512]{1,0:T(8,128)S(1)} %collective-permute-done.19.refs_2_, ...), custom_call_target="tpu_custom_call" | custom-call | flops 1000000 | bytes 65536 | tf_op jit(solution)/shard_map/prepare/pallas_call | solution.py:235
  69.8 1.9 %copy-done.1 = f32[2048,384]{1,0:T(8,128)S(1)} copy-done((f32[2048,384]{1,0:T(8,128)S(1)}, f32[2048,384]{1,0:T(8,128)}, u32[]{:S(2)}) %copy-start.1) | copy-done | bytes 3145752
  72.5 9.3 %solve.1 = (f32[512,2048]{1,0:T(8,128)S(1)}, f32[16,2048]{1,0:T(8,128)}, f32[288,384]{1,0:T(8,128)S(1)}, f32[72,384]{1,0:T(8,128)S(1)}, f32[72,384]{1,0:T(8,128)...) custom-call(s32[7]{0:T(128)S(1)} %stack.31.ids, f32[128,1024]{1,0:T(8,128)S(1)} %pad_maximum_fusion.refs_0_, ...), custom_call_target="tpu_custom_call" | custom-call | flops 6000000000 | bytes 12582912 | tf_op jit(solution)/shard_map/solve/pallas_call | solution.py:248
  81.9 7.0 %trailing.1 = f32[2048,384]{1,0:T(8,128)} custom-call(s32[7]{0:T(128)S(1)} %stack.31.ids, f32[64,384]{1,0:T(8,128)S(1)} %copy-done, f32[64,384]{1,0:T(8,128)S(1)} %collective-permute-done.21.refs_1_, f32[64,384]{1,0:T(8,128)S(1)} %collective-permute-done.22.refs_2_, f32[64,384]{1,0:T(8,128)S(1)} %collective-permute-done.23.refs_3_, ...), custom_call_target="tpu_custom_call" | custom-call | flops 4000000000 | bytes 11534336 | tf_op jit(solution)/shard_map/trailing/pallas_call | solution.py:268
  89.0 1.3 %collective-permute-done.24 = f32[288,384]{1,0:T(8,128)S(1)} collective-permute-done((f32[288,384]{1,0:T(8,128)S(1)}, f32[288,384]{1,0:T(8,128)S(1)}, u32[]{:S(2)}, u32[]{:S(2)}) %collective-permute-start.24) | collective-permute-done | bytes 442400 | tf_op jit(solution)/shard_map/ppermute | solution.py:30
  90.3 2.7 %collective-permute-start.27 = (f32[72,384]{1,0:T(8,128)S(1)}, f32[72,384]{1,0:T(8,128)S(1)}, u32[]{:S(2)}, u32[]{:S(2)}) collective-permute-start(f32[72,384]{1,0:T(8,128)S(1)} %get-tuple-element.60), channel_id=1, source_target_pairs={{0,128},{32,160},{64,192},{96,224},{128,0},{160,32},{192,64},{224,... | collective-permute-start | bytes 331784 | tf_op jit(solution)/shard_map/ppermute | solution.py:17
  93.0 3.0 %collective-permute-start.26 = (f32[72,384]{1,0:T(8,128)S(1)}, f32[72,384]{1,0:T(8,128)S(1)}, u32[]{:S(2)}, u32[]{:S(2)}) collective-permute-start(f32[72,384]{1,0:T(8,128)S(1)} %get-tuple-element.62), channel_id=1, source_target_pairs={{0,64},{32,96},{64,0},{96,32},{128,192},{160,224},{192,128},{224,1... | collective-permute-start | bytes 331784 | tf_op jit(solution)/shard_map/ppermute | solution.py:17
  96.0 5.1 %collective-permute-done.27 = f32[72,384]{1,0:T(8,128)S(1)} collective-permute-done((f32[72,384]{1,0:T(8,128)S(1)}, f32[72,384]{1,0:T(8,128)S(1)}, u32[]{:S(2)}, u32[]{:S(2)}) %collective-permute-start.27) | collective-permute-done | bytes 110624 | tf_op jit(solution)/shard_map/ppermute | solution.py:17
  101.1 1.7 %collective-permute-done.28 = f32[72,384]{1,0:T(8,128)S(1)} collective-permute-done((f32[72,384]{1,0:T(8,128)S(1)}, f32[72,384]{1,0:T(8,128)S(1)}, u32[]{:S(2)}, u32[]{:S(2)}) %collective-permute-start.28) | collective-permute-done | bytes 110624 | tf_op jit(solution)/shard_map/ppermute | solution.py:17
  102.8 2.5 %collective-permute-done.26 = f32[72,384]{1,0:T(8,128)S(1)} collective-permute-done((f32[72,384]{1,0:T(8,128)S(1)}, f32[72,384]{1,0:T(8,128)S(1)}, u32[]{:S(2)}, u32[]{:S(2)}) %collective-permute-start.26) | collective-permute-done | bytes 110624 | tf_op jit(solution)/shard_map/ppermute | solution.py:17
  (65 shorter events, 10.7 us)
Async XLA Ops:
  0.6 42.6 %copy-start = (f32[64,384]{1,0:T(8,128)S(1)}, f32[64,384]{1,0:T(8,128)}, u32[]{:S(2)}) copy-start(f32[64,384]{1,0:T(8,128)} %refs_0_) | copy-start | bytes 294916
  1.4 4.2 %collective-permute-start = (f32[8,64]{1,0:T(8,128)S(1)}, f32[8,64]{1,0:T(8,128)S(1)}, u32[]{:S(2)}, u32[]{:S(2)}) collective-permute-start(f32[8,64]{1,0:T(8,128)S(1)} %get-tuple-element.67), channel_id=1, source_target_pairs={{0,1},{1,0},{2,3},{3,2},{4,5},{5,4},{6,7},{7,6},{8,9},{9,8},{10,11... | collective-permute-start | bytes 6152 | tf_op jit(solution)/shard_map/ppermute | solution.py:21
  5.5 1.3 %collective-permute-start.1 = (f32[16,1024]{1,0:T(8,128)S(1)}, f32[16,1024]{1,0:T(8,128)S(1)}, u32[]{:S(2)}, u32[]{:S(2)}) collective-permute-start(f32[16,1024]{1,0:T(8,128)S(1)} %get-tuple-element.64), channel_id=1, source_target_pairs={{0,1},{1,0},{2,3},{3,2},{4,5},{5,4},{6,7},{7,6},{8,9},{9,8},{10,11... | collective-permute-start | bytes 196616 | tf_op jit(solution)/shard_map/ppermute | solution.py:21
  6.9 7.5 %collective-permute-start.4 = (f32[40,1024]{1,0:T(8,128)S(1)}, f32[40,1024]{1,0:T(8,128)S(1)}, u32[]{:S(2)}, u32[]{:S(2)}) collective-permute-start(f32[40,1024]{1,0:T(8,128)S(1)} %pad_maximum_fusion.3), channel_id=1, source_target_pairs={{0,6},{1,25},{2,4},{3,27},{4,2},{5,29},{6,0},{7,31},{8,14},{9,17},... | collective-permute-start | bytes 491528 | tf_op jit(solution)/shard_map/ppermute | solution.py:36
  8.0 6.4 %collective-permute-start.3 = (f32[40,1024]{1,0:T(8,128)S(1)}, f32[40,1024]{1,0:T(8,128)S(1)}, u32[]{:S(2)}, u32[]{:S(2)}) collective-permute-start(f32[40,1024]{1,0:T(8,128)S(1)} %pad_maximum_fusion.3), channel_id=1, source_target_pairs={{0,4},{1,17},{2,6},{3,19},{4,0},{5,21},{6,2},{7,23},{8,12},{9,25},... | collective-permute-start | bytes 491528 | tf_op jit(solution)/shard_map/ppermute | solution.py:36
  8.3 6.7 %collective-permute-start.2 = (f32[40,1024]{1,0:T(8,128)S(1)}, f32[40,1024]{1,0:T(8,128)S(1)}, u32[]{:S(2)}, u32[]{:S(2)}) collective-permute-start(f32[40,1024]{1,0:T(8,128)S(1)} %pad_maximum_fusion.3), channel_id=1, source_target_pairs={{0,2},{1,9},{2,0},{3,11},{4,6},{5,13},{6,4},{7,15},{8,10},{9,1},{1... | collective-permute-start | bytes 491528 | tf_op jit(solution)/shard_map/ppermute | solution.py:36
  15.1 3.8 %collective-permute-start.7 = (f32[8,512]{1,0:T(8,128)S(1)}, f32[8,512]{1,0:T(8,128)S(1)}, u32[]{:S(2)}, u32[]{:S(2)}) collective-permute-start(f32[8,512]{1,0:T(8,128)S(1)} %concatenate.27), channel_id=1, source_target_pairs={{0,24},{1,7},{2,26},{3,5},{4,28},{5,3},{6,30},{7,1},{8,16},{9,15},... | collective-permute-start | bytes 49160 | tf_op jit(solution)/shard_map/ppermute | solution.py:36
  16.5 4.1 %collective-permute-start.6 = (f32[8,512]{1,0:T(8,128)S(1)}, f32[8,512]{1,0:T(8,128)S(1)}, u32[]{:S(2)}, u32[]{:S(2)}) collective-permute-start(f32[8,512]{1,0:T(8,128)S(1)} %concatenate.27), channel_id=1, source_target_pairs={{0,16},{1,5},{2,18},{3,7},{4,20},{5,1},{6,22},{7,3},{8,24},{9,13},... | collective-permute-start | bytes 49160 | tf_op jit(solution)/shard_map/ppermute | solution.py:36
  16.7 3.9 %collective-permute-start.5 = (f32[8,512]{1,0:T(8,128)S(1)}, f32[8,512]{1,0:T(8,128)S(1)}, u32[]{:S(2)}, u32[]{:S(2)}) collective-permute-start(f32[8,512]{1,0:T(8,128)S(1)} %concatenate.27), channel_id=1, source_target_pairs={{0,8},{1,3},{2,10},{3,1},{4,12},{5,7},{6,14},{7,5},{8,0},{9,11},{1... | collective-permute-start | bytes 49160 | tf_op jit(solution)/shard_map/ppermute | solution.py:36
  20.7 17.2 %collective-permute-start.12 = (f32[128,1024]{1,0:T(8,128)S(1)}, f32[128,1024]{1,0:T(8,128)S(1)}, u32[]{:S(2)}, u32[]{:S(2)}) collective-permute-start(f32[128,1024]{1,0:T(8,128)S(1)} %pad_maximum_fusion.refs_0_), channel_id=1, source_target_pairs={{0,24},{1,7},{2,26},{3,5},{4,28},{5,3},{6,30},{7,1},{8,16},{9,15},... | collective-permute-start | bytes 1572872 | tf_op jit(solution)/shard_map/ppermute | solution.py:36
  22.1 15.9 %collective-permute-start.11 = (f32[128,1024]{1,0:T(8,128)S(1)}, f32[128,1024]{1,0:T(8,128)S(1)}, u32[]{:S(2)}, u32[]{:S(2)}) collective-permute-start(f32[128,1024]{1,0:T(8,128)S(1)} %pad_maximum_fusion.refs_0_), channel_id=1, source_target_pairs={{0,8},{1,3},{2,10},{3,1},{4,12},{5,7},{6,14},{7,5},{8,0},{9,11},{1... | collective-permute-start | bytes 1572872 | tf_op jit(solution)/shard_map/ppermute | solution.py:36
  22.1 26.8 %collective-permute-start.13 = (f32[128,1024]{1,0:T(8,128)S(1)}, f32[128,1024]{1,0:T(8,128)S(1)}, u32[]{:S(2)}, u32[]{:S(2)}) collective-permute-start(f32[128,1024]{1,0:T(8,128)S(1)} %pad_maximum_fusion.refs_0_), channel_id=1, source_target_pairs={{0,16},{1,5},{2,18},{3,7},{4,20},{5,1},{6,22},{7,3},{8,24},{9,13},... | collective-permute-start | bytes 1572872 | tf_op jit(solution)/shard_map/ppermute | solution.py:36
  24.7 7.5 %collective-permute-start.10 = (f32[32,512]{1,0:T(8,128)S(1)}, f32[32,512]{1,0:T(8,128)S(1)}, u32[]{:S(2)}, u32[]{:S(2)}) collective-permute-start(f32[32,512]{1,0:T(8,128)S(1)} %pad_maximum_fusion.4), channel_id=1, source_target_pairs={{0,192},{32,224},{64,128},{96,160},{128,64},{160,96},{192,0},{224,... | collective-permute-start | bytes 196616 | tf_op jit(solution)/shard_map/ppermute | solution.py:17
  30.4 7.5 %collective-permute-start.9 = (f32[32,512]{1,0:T(8,128)S(1)}, f32[32,512]{1,0:T(8,128)S(1)}, u32[]{:S(2)}, u32[]{:S(2)}) collective-permute-start(f32[32,512]{1,0:T(8,128)S(1)} %pad_maximum_fusion.4), channel_id=1, source_target_pairs={{0,128},{32,160},{64,192},{96,224},{128,0},{160,32},{192,64},{224,... | collective-permute-start | bytes 196616 | tf_op jit(solution)/shard_map/ppermute | solution.py:17
  32.2 5.8 %collective-permute-start.8 = (f32[32,512]{1,0:T(8,128)S(1)}, f32[32,512]{1,0:T(8,128)S(1)}, u32[]{:S(2)}, u32[]{:S(2)}) collective-permute-start(f32[32,512]{1,0:T(8,128)S(1)} %pad_maximum_fusion.4), channel_id=1, source_target_pairs={{0,64},{32,96},{64,0},{96,32},{128,192},{160,224},{192,128},{224,1... | collective-permute-start | bytes 196616 | tf_op jit(solution)/shard_map/ppermute | solution.py:17
  38.0 21.9 %collective-permute-start.19 = (f32[128,512]{1,0:T(8,128)S(1)}, f32[128,512]{1,0:T(8,128)S(1)}, u32[]{:S(2)}, u32[]{:S(2)}) collective-permute-start(f32[128,512]{1,0:T(8,128)S(1)} %pad_maximum_fusion.2.refs_0_), channel_id=1, source_target_pairs={{0,1},{1,0},{2,3},{3,2},{4,5},{5,4},{6,7},{7,6},{8,9},{9,8},{10,11... | collective-permute-start | bytes 786440 | tf_op jit(solution)/shard_map/ppermute | solution.py:21
  43.2 11.9 %collective-permute-start.23 = (f32[64,384]{1,0:T(8,128)S(1)}, f32[64,384]{1,0:T(8,128)S(1)}, u32[]{:S(2)}, u32[]{:S(2)}) collective-permute-start(f32[64,384]{1,0:T(8,128)S(1)} %copy-done), channel_id=1, source_target_pairs={{0,192},{32,224},{64,128},{96,160},{128,64},{160,96},{192,0},{224,... | collective-permute-start | bytes 294920 | tf_op jit(solution)/shard_map/ppermute | solution.py:17
  46.7 9.1 %collective-permute-start.22 = (f32[64,384]{1,0:T(8,128)S(1)}, f32[64,384]{1,0:T(8,128)S(1)}, u32[]{:S(2)}, u32[]{:S(2)}) collective-permute-start(f32[64,384]{1,0:T(8,128)S(1)} %copy-done), channel_id=1, source_target_pairs={{0,128},{32,160},{64,192},{96,224},{128,0},{160,32},{192,64},{224,... | collective-permute-start | bytes 294920 | tf_op jit(solution)/shard_map/ppermute | solution.py:17
  48.0 11.4 %collective-permute-start.21 = (f32[64,384]{1,0:T(8,128)S(1)}, f32[64,384]{1,0:T(8,128)S(1)}, u32[]{:S(2)}, u32[]{:S(2)}) collective-permute-start(f32[64,384]{1,0:T(8,128)S(1)} %copy-done), channel_id=1, source_target_pairs={{0,64},{32,96},{64,0},{96,32},{128,192},{160,224},{192,128},{224,1... | collective-permute-start | bytes 294920 | tf_op jit(solution)/shard_map/ppermute | solution.py:17
  48.9 11.0 %collective-permute-start.18 = (f32[128,512]{1,0:T(8,128)S(1)}, f32[128,512]{1,0:T(8,128)S(1)}, u32[]{:S(2)}, u32[]{:S(2)}) collective-permute-start(f32[128,512]{1,0:T(8,128)S(1)} %pad_maximum_fusion.2.refs_0_), channel_id=1, source_target_pairs={{0,32},{1,225},{2,34},{3,227},{4,36},{5,229},{6,38},{7,231},{8,40}... | collective-permute-start | bytes 786440 | tf_op jit(solution)/shard_map/ppermute | solution.py:30
  55.1 14.6 %collective-permute-start.14 = (f32[128,1024]{1,0:T(8,128)S(1)}, f32[128,1024]{1,0:T(8,128)}, u32[]{:S(2)}, u32[]{:S(2)}) collective-permute-start(f32[128,1024]{1,0:T(8,128)S(1)} %pad_maximum_fusion.refs_0_), channel_id=1, source_target_pairs={{0,1},{1,0},{2,3},{3,2},{4,5},{5,4},{6,7},{7,6},{8,9},{9,8},{10,11... | collective-permute-start | bytes 1572872 | tf_op jit(solution)/shard_map/ppermute | solution.py:21
  55.8 14.0 %collective-permute-start.15 = (f32[128,1024]{1,0:T(8,128)S(1)}, f32[128,1024]{1,0:T(8,128)}, u32[]{:S(2)}, u32[]{:S(2)}) collective-permute-start(f32[128,1024]{1,0:T(8,128)S(1)} %collective-permute-done.11.refs_1_), channel_id=1, source_target_pairs={{0,1},{1,0},{2,3},{3,2},{4,5},{5,4},{6,7},{7,6},{8,9},{9,8},{10,11... | collective-permute-start | bytes 1572872 | tf_op jit(solution)/shard_map/ppermute | solution.py:21
  59.4 10.4 %collective-permute-start.16 = (f32[128,1024]{1,0:T(8,128)S(1)}, f32[128,1024]{1,0:T(8,128)}, u32[]{:S(2)}, u32[]{:S(2)}) collective-permute-start(f32[128,1024]{1,0:T(8,128)S(1)} %collective-permute-done.13.refs_2_), channel_id=1, source_target_pairs={{0,1},{1,0},{2,3},{3,2},{4,5},{5,4},{6,7},{7,6},{8,9},{9,8},{10,11... | collective-permute-start | bytes 1572872 | tf_op jit(solution)/shard_map/ppermute | solution.py:21
  59.9 9.8 %collective-permute-start.17 = (f32[128,1024]{1,0:T(8,128)S(1)}, f32[128,1024]{1,0:T(8,128)}, u32[]{:S(2)}, u32[]{:S(2)}) collective-permute-start(f32[128,1024]{1,0:T(8,128)S(1)} %collective-permute-done.12.refs_3_), channel_id=1, source_target_pairs={{0,1},{1,0},{2,3},{3,2},{4,5},{5,4},{6,7},{7,6},{8,9},{9,8},{10,11... | collective-permute-start | bytes 1572872 | tf_op jit(solution)/shard_map/ppermute | solution.py:21
  59.9 2.3 %collective-permute-start.20 = (f32[128,512]{1,0:T(8,128)S(1)}, f32[128,512]{1,0:T(8,128)S(1)}, u32[]{:S(2)}, u32[]{:S(2)}) collective-permute-start(f32[128,512]{1,0:T(8,128)S(1)} %collective-permute-done.18.refs_1_), channel_id=1, source_target_pairs={{0,1},{1,0},{2,3},{3,2},{4,5},{5,4},{6,7},{7,6},{8,9},{9,8},{10,11... | collective-permute-start | bytes 786440 | tf_op jit(solution)/shard_map/ppermute | solution.py:21
  62.2 19.7 %collective-permute-start.25 = (f32[256,384]{1,0:T(8,128)S(1)}, f32[256,384]{1,0:T(8,128)S(1)}, u32[]{:S(2)}, u32[]{:S(2)}) collective-permute-start(f32[256,384]{1,0:T(8,128)S(1)} %pad_maximum_fusion.1), channel_id=1, source_target_pairs={{0,32},{1,225},{2,34},{3,227},{4,36},{5,229},{6,38},{7,231},{8,40}... | collective-permute-start | bytes 1179656 | tf_op jit(solution)/shard_map/ppermute | solution.py:30
  81.8 8.4 %collective-permute-start.24 = (f32[288,384]{1,0:T(8,128)S(1)}, f32[288,384]{1,0:T(8,128)S(1)}, u32[]{:S(2)}, u32[]{:S(2)}) collective-permute-start(f32[288,384]{1,0:T(8,128)S(1)} %get-tuple-element.51), channel_id=1, source_target_pairs={{0,32},{1,225},{2,34},{3,227},{4,36},{5,229},{6,38},{7,231},{8,40}... | collective-permute-start | bytes 1327112 | tf_op jit(solution)/shard_map/ppermute | solution.py:30
  81.9 23.4 %copy-start.4 = (f32[64,384]{1,0:T(8,128)S(1)}, f32[64,384]{1,0:T(8,128)}, u32[]{:S(2)}) copy-start(f32[64,384]{1,0:T(8,128)} %param.14) | copy-start | bytes 294916
  81.9 24.1 %copy-start.5 = (f32[64,16]{0,1:T(8,128)S(1)}, f32[64,16]{0,1:T(8,128)}, u32[]{:S(2)}) copy-start(f32[64,16]{0,1:T(8,128)} %param.13) | copy-start | bytes 12292
  90.3 10.8 %collective-permute-start.27 = (f32[72,384]{1,0:T(8,128)S(1)}, f32[72,384]{1,0:T(8,128)S(1)}, u32[]{:S(2)}, u32[]{:S(2)}) collective-permute-start(f32[72,384]{1,0:T(8,128)S(1)} %get-tuple-element.60), channel_id=1, source_target_pairs={{0,128},{32,160},{64,192},{96,224},{128,0},{160,32},{192,64},{224,... | collective-permute-start | bytes 331784 | tf_op jit(solution)/shard_map/ppermute | solution.py:17
  93.0 9.7 %collective-permute-start.28 = (f32[72,384]{1,0:T(8,128)S(1)}, f32[72,384]{1,0:T(8,128)S(1)}, u32[]{:S(2)}, u32[]{:S(2)}) collective-permute-start(f32[72,384]{1,0:T(8,128)S(1)} %get-tuple-element.61), channel_id=1, source_target_pairs={{0,192},{32,224},{64,128},{96,160},{128,64},{160,96},{192,0},{224,... | collective-permute-start | bytes 331784 | tf_op jit(solution)/shard_map/ppermute | solution.py:17
  93.0 12.2 %collective-permute-start.26 = (f32[72,384]{1,0:T(8,128)S(1)}, f32[72,384]{1,0:T(8,128)S(1)}, u32[]{:S(2)}, u32[]{:S(2)}) collective-permute-start(f32[72,384]{1,0:T(8,128)S(1)} %get-tuple-element.62), channel_id=1, source_target_pairs={{0,64},{32,96},{64,0},{96,32},{128,192},{160,224},{192,128},{224,1... | collective-permute-start | bytes 331784 | tf_op jit(solution)/shard_map/ppermute | solution.py:17
  (3 other events, 12.2 us)

commit v6 on v5

--- a/solution.py
+++ b/solution.py
@@ -204,15 +204,15 @@
 
 
 def trailing_kernel(ids, *refs):
-    own_parity, other_parity = refs[:4], refs[4]
-    solved, grad, out, rs = refs[5:]
+    own_parity, other_parity, solved, grad, out, rs = refs
 
     @pl.when(pl.program_id(0) == 0)
     def _():
-        for j in range(4):
-            for first, piece in ((ids[0], own_parity[j][...]), (ids[5], other_parity[64 * j : 64 * j + 64, :])):
+        for j, distance in enumerate((0, 4, 2, 6)):
+            for first, pieces in ((ids[0], own_parity), (ids[5], other_parity)):
+                piece = pieces[64 * j : 64 * j + 64, :]
                 high, low = split(piece)
-                row = (first ^ (2 * j)) * 64
+                row = (first ^ distance) * 64
                 rs[pl.ds(pl.multiple_of(row, 64), 64), :] = high
                 rs[pl.ds(pl.multiple_of(row + 512, 64), 64), :] = low
                 rs[pl.ds(pl.multiple_of(row + 1024, 64), 64), :] = high
@@ -270,8 +270,7 @@
         grid=(2048 // tile,),
         out_shape=shape((2048, 384)),
         in_specs=[SMEM]
-        + [pl.BlockSpec((64, 384), lambda i: (0, 0))] * 4
-        + [pl.BlockSpec((256, 384), lambda i: (0, 0))]
+        + [pl.BlockSpec((256, 384), lambda i: (0, 0))] * 2
         + [pl.BlockSpec((B, tile), lambda i: (0, i)), pl.BlockSpec((tile, 384), lambda i: (i, 0))],
         out_specs=pl.BlockSpec((tile, 384), lambda i: (i, 0)),
         scratch_shapes=[pltpu.VMEM((3 * B, 384), BF16)],
@@ -310,27 +309,28 @@
     both = jnp.concatenate([grad_pair, jnp.pad(diag_pair, ((0, 0), (0, 1024 - 128)))], axis=0)
     both = [both] + [with_col_partner(both, 0, k) for k in (1, 2, 3)]
     diag_quad = jnp.concatenate([b[32:, :128] for b in both], axis=1)
-    diag_far = [with_col_partner(diag_quad, 1, k) for k in (1, 2, 3)]
-    diag_far, both = lax.optimization_barrier((diag_far, both))
+    row_pair = jnp.concatenate([row_factor, with_row_partner(row_factor, 4)], axis=0)
+    row_pair, both = lax.optimization_barrier((row_pair, both))
+    row_even = jnp.concatenate([row_pair, with_row_partner(row_pair, 2)], axis=0)
+    diag_quad = jnp.concatenate([diag_quad, with_col_partner(diag_quad, 1, 1)], axis=0)
+    diag_quad = jnp.concatenate([diag_quad, with_col_partner(diag_quad, 1, 2)], axis=0)
+    diag_quad, both, row_even = lax.optimization_barrier((diag_quad, both, row_even))
+    row_odd = with_neighbour(row_even)
     grad_quad = jnp.concatenate([b[:32] for b in both], axis=0)
     grad_far = [with_col_partner(grad_quad, 1, k) for k in (1, 2, 3)]
-    diag_even = jnp.concatenate([diag_quad] + diag_far, axis=0)
-    diag_even = [diag_even] + [with_row_partner(diag_even, k) for k in (2, 4, 6)]
-    diag_even, grad_far[0], grad_far[2] = lax.optimization_barrier((diag_even, grad_far[0], grad_far[2]))
-    diag_even = jnp.concatenate(diag_even, axis=0)
-    row_factor, diag_even = lax.optimization_barrier((row_factor, diag_even))
+    diag_even = jnp.concatenate([diag_quad, with_row_partner(diag_quad, 2)], axis=0)
+    diag_even = jnp.concatenate([diag_even, with_row_partner(diag_even, 4)], axis=0)
+    diag_even, row_odd, grad_far[0], grad_far[2] = lax.optimization_barrier(
+        (diag_even, row_odd, grad_far[0], grad_far[2])
+    )
     diag_odd = with_neighbour(diag_even)
     diag_blocks = [diag_even, diag_odd, with_sibling(diag_even), with_sibling(diag_odd)]
     quad_swapped = with_sibling(grad_quad)
 
-    row_pieces = [row_factor] + [with_row_partner(row_factor, k) for k in (2, 4, 6)]
     inverse = prepare(ids, diag_blocks)
-    row_joined = jnp.concatenate(row_pieces, axis=0)
-    panel, row_joined = lax.optimization_barrier((panel_factor.T, row_joined))
-    row_pieces = row_pieces + [with_neighbour(row_joined)]
     grad_blocks = [grad_quad] + grad_far + [quad_swapped] + [with_sibling(b) for b in grad_far]
-    solved, own, given, *kept = solve(ids, grad_blocks, inverse, trailing_factor, panel)
-    trailing_out = trailing_update(ids, row_pieces, solved, trailing_grad)
+    solved, own, given, *kept = solve(ids, grad_blocks, inverse, trailing_factor, panel_factor.T)
+    trailing_out = trailing_update(ids, [row_even, row_odd], solved, trailing_grad)
     taken = with_neighbour(given)
     taken, trailing_out = lax.optimization_barrier((taken, trailing_out))
     sums = [kept[j] + taken[72 * j : 72 * j + 72] for j in range(4)]

time: 107 us -> 106 us (level)
  starting transfers between devices: 46.8 us -> 39.8 us
  waiting for transfers between devices: 31.5 us -> 35.6 us
    ppermute x9 -> x8, waiting for transfers between devices: 7.04 us -> 1.51 us  [with_col_partner(): return lax.ppermute(v, 'col', perm)]
    ppermute x9 -> x7, waiting for transfers between devices: 20.4 us -> 25.5 us  [with_row_partner(): return lax.ppermute(v, 'row', [(i, i ^ k) for i in range(ROWS)])]
    ppermute x3, waiting for transfers between devices: 1.26 us -> 6.26 us  [with_neighbour(): return lax.ppermute(v, ('row', 'col'), perm)]
    ppermute x8, starting transfers between devices: 12 us -> 7.86 us  [with_sibling(): return lax.ppermute(v, 'col', [(i, i ^ 1) for i in range(COLS)])]
    ppermute x9 -> x7, starting transfers between devices: 19.2 us -> 15.2 us  [with_row_partner(): return lax.ppermute(v, 'row', [(i, i ^ k) for i in range(ROWS)])]
    ppermute x9 -> x8, starting transfers between devices: 10.6 us -> 12.1 us  [with_col_partner(): return lax.ppermute(v, 'col', perm)]
    unnamed x12 -> x14, local copies, waits for them, and re-layouts: 2.81 us -> 3.55 us
  transfers between devices with their start and end apart: 29 -> 26, of which waited for: 14 -> 12; matrix products, arithmetic and copies ran while one was open for 1% -> 2% of each run, Pallas kernels for 20% -> 11%
where the time goes in v6:
time: 106 us; the launch traced here: 105 us
  starting transfers between devices  39.8 us (38%)
  waiting for transfers between devices  35.6 us (34%)
  Pallas kernels  21.2 us (20%)
  other arithmetic  4.1 us (4%)
  local copies, waits for them, and re-layouts  3.83 us (4%)
    ppermute x7, waiting for transfers between devices, with_row_partner(): return lax.ppermute(v, 'row', [(i, i ^ k) for i in range(ROWS)])  25.5 us
    ppermute x7, starting transfers between devices, with_row_partner(): return lax.ppermute(v, 'row', [(i, i ^ k) for i in range(ROWS)])  15.2 us
    ppermute x8, starting transfers between devices, with_col_partner(): return lax.ppermute(v, 'col', perm)  12.1 us
    pallas_call x1, Pallas kernels, solve(): pl.pallas_call(solve_kernel, out_shape=[shape((B, 2048)), shape((16, 2048...  9.29 us
    ppermute x8, starting transfers between devices, with_sibling(): return lax.ppermute(v, 'col', [(i, i ^ 1) for i in range(COLS)])  7.86 us
    pallas_call x1, Pallas kernels, trailing_update(): pl.pallas_call(trailing_kernel, grid=(2048 // tile,), out_shape=shape((20...  7.02 us
    ppermute x3, waiting for transfers between devices, with_neighbour(): return lax.ppermute(v, ('row', 'col'), perm)  6.26 us
    pallas_call x1, Pallas kernels, prepare(): pl.pallas_call(prepare_kernel, out_shape=[shape((256, 1536), BF16), shape...  4.86 us
  transfers between devices with their start and end apart: 26, of which 12 were waited for; matrix products, arithmetic and copies ran while one was open for 2% of the time, Pallas kernels for 11%

profile of v6, /device:TPU:1, one launch (start us, length us, event | category | flops | bytes accessed | tf_op | source)
XLA Modules:
  0.0 105.4 jit_solution(15151577131849653083)
XLA Ops:
  1.4 3.2 %collective-permute-start = (f32[8,64]{1,0:T(8,128)S(1)}, f32[8,64]{1,0:T(8,128)S(1)}, u32[]{:S(2)}, u32[]{:S(2)}) collective-permute-start(f32[8,64]{1,0:T(8,128)S(1)} %get-tuple-element.63), channel_id=1, source_target_pairs={{0,1},{1,0},{2,3},{3,2},{4,5},{5,4},{6,7},{7,6},{8,9},{9,8},{10,11... | collective-permute-start | bytes 6152 | tf_op jit(solution)/shard_map/ppermute | solution.py:21
  4.6 0.9 slice_select_fusion.1
  5.7 1.2 %collective-permute-done.1 = f32[16,1024]{1,0:T(8,128)S(1)} collective-permute-done((f32[16,1024]{1,0:T(8,128)S(1)}, f32[16,1024]{1,0:T(8,128)S(1)}, u32[]{:S(2)}, u32[]{:S(2)}) %collective-permute-start.1) | collective-permute-done | bytes 65568 | tf_op jit(solution)/shard_map/ppermute | solution.py:21
  6.8 1.1 %collective-permute-start.4 = (f32[40,1024]{1,0:T(8,128)S(1)}, f32[40,1024]{1,0:T(8,128)S(1)}, u32[]{:S(2)}, u32[]{:S(2)}) collective-permute-start(f32[40,1024]{1,0:T(8,128)S(1)} %pad_maximum_fusion.4), channel_id=1, source_target_pairs={{0,6},{1,25},{2,4},{3,27},{4,2},{5,29},{6,0},{7,31},{8,14},{9,17},... | collective-permute-start | bytes 491528 | tf_op jit(solution)/shard_map/ppermute | solution.py:36
  8.3 1.9 %collective-permute-start.2 = (f32[40,1024]{1,0:T(8,128)S(1)}, f32[40,1024]{1,0:T(8,128)S(1)}, u32[]{:S(2)}, u32[]{:S(2)}) collective-permute-start(f32[40,1024]{1,0:T(8,128)S(1)} %pad_maximum_fusion.4), channel_id=1, source_target_pairs={{0,2},{1,9},{2,0},{3,11},{4,6},{5,13},{6,4},{7,15},{8,10},{9,1},{1... | collective-permute-start | bytes 491528 | tf_op jit(solution)/shard_map/ppermute | solution.py:36
  10.2 5.3 %collective-permute-start.7 = (f32[64,384]{1,0:T(8,128)}, f32[64,384]{1,0:T(8,128)S(1)}, u32[]{:S(2)}, u32[]{:S(2)}) collective-permute-start(f32[64,384]{1,0:T(8,128)} %param.10), channel_id=1, source_target_pairs={{0,128},{32,160},{64,192},{96,224},{128,0},{160,32},{192,64},{224,... | collective-permute-start | bytes 294920 | tf_op jit(solution)/shard_map/ppermute | solution.py:17
  15.6 1.2 %collective-permute-start.5 = (f32[8,512]{1,0:T(8,128)S(1)}, f32[8,512]{1,0:T(8,128)S(1)}, u32[]{:S(2)}, u32[]{:S(2)}) collective-permute-start(f32[8,512]{1,0:T(8,128)S(1)} %concatenate.38), channel_id=1, source_target_pairs={{0,8},{1,3},{2,10},{3,1},{4,12},{5,7},{6,14},{7,5},{8,0},{9,11},{1... | collective-permute-start | bytes 49160 | tf_op jit(solution)/shard_map/ppermute | solution.py:36
  16.9 1.0 collective-permute-done.7
  17.9 0.9 pad_maximum_fusion.3
  18.8 4.0 %collective-permute-start.8 = (f32[128,384]{1,0:T(8,128)S(1)}, f32[128,384]{1,0:T(8,128)S(1)}, u32[]{:S(2)}, u32[]{:S(2)}) collective-permute-start(f32[128,384]{1,0:T(8,128)S(1)} %pad_maximum_fusion.3), channel_id=1, source_target_pairs={{0,64},{32,96},{64,0},{96,32},{128,192},{160,224},{192,128},{224,1... | collective-permute-start | bytes 589832 | tf_op jit(solution)/shard_map/ppermute | solution.py:17
  22.8 2.8 %collective-permute-start.6 = (f32[16,512]{1,0:T(8,128)S(1)}, f32[16,512]{1,0:T(8,128)S(1)}, u32[]{:S(2)}, u32[]{:S(2)}) collective-permute-start(f32[16,512]{1,0:T(8,128)S(1)} %pad_maximum_fusion.7), channel_id=1, source_target_pairs={{0,16},{1,5},{2,18},{3,7},{4,20},{5,1},{6,22},{7,3},{8,24},{9,13},... | collective-permute-start | bytes 98312 | tf_op jit(solution)/shard_map/ppermute | solution.py:36
  25.6 1.5 %collective-permute-done.6 = f32[16,512]{1,0:T(8,128)S(1)} collective-permute-done((f32[16,512]{1,0:T(8,128)S(1)}, f32[16,512]{1,0:T(8,128)S(1)}, u32[]{:S(2)}, u32[]{:S(2)}) %collective-permute-start.6) | collective-permute-done | bytes 32800 | tf_op jit(solution)/shard_map/ppermute | solution.py:36
  27.1 4.0 %collective-permute-done.8 = f32[128,384]{1,0:T(8,128)S(1)} collective-permute-done((f32[128,384]{1,0:T(8,128)S(1)}, f32[128,384]{1,0:T(8,128)S(1)}, u32[]{:S(2)}, u32[]{:S(2)}) %collective-permute-start.8) | collective-permute-done | bytes 196640 | tf_op jit(solution)/shard_map/ppermute | solution.py:17
  31.2 3.4 %collective-permute-start.13 = (f32[128,1024]{1,0:T(8,128)S(1)}, f32[128,1024]{1,0:T(8,128)S(1)}, u32[]{:S(2)}, u32[]{:S(2)}) collective-permute-start(f32[128,1024]{1,0:T(8,128)S(1)} %pad_maximum_fusion.refs_0_), channel_id=1, source_target_pairs={{0,24},{1,7},{2,26},{3,5},{4,28},{5,3},{6,30},{7,1},{8,16},{9,15},... | collective-permute-start | bytes 1572872 | tf_op jit(solution)/shard_map/ppermute | solution.py:36
  34.6 4.6 %collective-permute-start.11 = (f32[256,384]{1,0:T(8,128)S(1)}, f32[256,384]{1,0:T(8,128)S(1)}, u32[]{:S(2)}, u32[]{:S(2)}) collective-permute-start(f32[256,384]{1,0:T(8,128)S(1)} %pad_maximum_fusion.1.refs_0_), channel_id=1, source_target_pairs={{0,32},{1,225},{2,34},{3,227},{4,36},{5,229},{6,38},{7,231},{8,40}... | collective-permute-start | bytes 1179656 | tf_op jit(solution)/shard_map/ppermute | solution.py:30
  39.2 1.3 %collective-permute-start.14 = (f32[128,1024]{1,0:T(8,128)S(1)}, f32[128,1024]{1,0:T(8,128)S(1)}, u32[]{:S(2)}, u32[]{:S(2)}) collective-permute-start(f32[128,1024]{1,0:T(8,128)S(1)} %pad_maximum_fusion.refs_0_), channel_id=1, source_target_pairs={{0,16},{1,5},{2,18},{3,7},{4,20},{5,1},{6,22},{7,3},{8,24},{9,13},... | collective-permute-start | bytes 1572872 | tf_op jit(solution)/shard_map/ppermute | solution.py:36
  40.7 12.0 %collective-permute-done.10 = f32[64,512]{1,0:T(8,128)S(1)} collective-permute-done((f32[64,512]{1,0:T(8,128)S(1)}, f32[64,512]{1,0:T(8,128)S(1)}, u32[]{:S(2)}, u32[]{:S(2)}) %collective-permute-start.10) | collective-permute-done | bytes 131104 | tf_op jit(solution)/shard_map/ppermute | solution.py:17
  53.5 2.7 %collective-permute-start.20 = (f32[128,512]{1,0:T(8,128)S(1)}, f32[128,512]{1,0:T(8,128)S(1)}, u32[]{:S(2)}, u32[]{:S(2)}) collective-permute-start(f32[128,512]{1,0:T(8,128)S(1)} %pad_maximum_fusion.2.refs_0_), channel_id=1, source_target_pairs={{0,1},{1,0},{2,3},{3,2},{4,5},{5,4},{6,7},{7,6},{8,9},{9,8},{10,11... | collective-permute-start | bytes 786440 | tf_op jit(solution)/shard_map/ppermute | solution.py:21
  56.3 0.9 collective-permute-start.16
  57.7 5.0 %collective-permute-done.19.refs_1_ = f32[128,512]{1,0:T(8,128)S(1)} collective-permute-done((f32[128,512]{1,0:T(8,128)S(1)}, f32[128,512]{1,0:T(8,128)S(1)}, u32[]{:S(2)}, u32[]{:S(2)}) %collective-permute-start.19) | collective-permute-done | bytes 262176 | tf_op jit(solution)/shard_map/ppermute | solution.py:30
  63.1 1.1 %collective-permute-done.21.refs_3_ = f32[128,512]{1,0:T(8,128)S(1)} collective-permute-done((f32[128,512]{1,0:T(8,128)S(1)}, f32[128,512]{1,0:T(8,128)S(1)}, u32[]{:S(2)}, u32[]{:S(2)}) %collective-permute-start.21) | collective-permute-done | bytes 262176 | tf_op jit(solution)/shard_map/ppermute | solution.py:21
  64.2 4.9 %prepare.1 = (bf16[256,1536]{1,0:T(8,128)(2,1)S(1)}, bf16[256,768]{1,0:T(8,128)(2,1)S(1)}) custom-call(s32[7]{0:T(128)S(1)} %stack.31.ids, f32[128,512]{1,0:T(8,128)S(1)} %pad_maximum_fusion.2.refs_0_, f32[128,512]{1,0:T(8,128)S(1)} %collective-permute-done.19.refs_1_, f32[128,512]{1,0:T(8,128)S(1)} %collective-permute-done.20.refs_2_, ...), custom_call_target="tpu_custom_call" | custom-call | flops 1000000 | bytes 65536 | tf_op jit(solution)/shard_map/prepare/pallas_call | solution.py:235
  69.2 1.9 %copy-done = f32[2048,384]{1,0:T(8,128)S(1)} copy-done((f32[2048,384]{1,0:T(8,128)S(1)}, f32[2048,384]{1,0:T(8,128)}, u32[]{:S(2)}) %copy-start) | copy-done | bytes 3145752
  71.0 0.9 copy-done.4
  72.0 9.3 %solve.1 = (f32[512,2048]{1,0:T(8,128)S(1)}, f32[16,2048]{1,0:T(8,128)}, f32[288,384]{1,0:T(8,128)S(1)}, f32[72,384]{1,0:T(8,128)S(1)}, f32[72,384]{1,0:T(8,128)...) custom-call(s32[7]{0:T(128)S(1)} %stack.31.ids, f32[128,1024]{1,0:T(8,128)S(1)} %pad_maximum_fusion.refs_0_, ...), custom_call_target="tpu_custom_call" | custom-call | flops 6000000000 | bytes 12582912 | tf_op jit(solution)/shard_map/solve/pallas_call | solution.py:248
  81.3 7.0 %trailing.1 = f32[2048,384]{1,0:T(8,128)} custom-call(s32[7]{0:T(128)S(1)} %stack.31.ids, f32[256,384]{1,0:T(8,128)S(1)} %pad_maximum_fusion.1.refs_0_, f32[256,384]{1,0:T(8,128)S(1)} %copy-done.3, f32[512,2048]{1,0:T(8,128)S(1)} %get-tuple-element.49.refs_2_, f32[2048,384]{1,0:T(8,128)S(1)} %copy-done.1), custom_call_target="tpu_custom_call" | custom-call | flops 4000000000 | bytes 11534336 | tf_op jit(solution)/shard_map/trailing/pallas_call | solution.py:268
  88.3 1.3 %collective-permute-done.22 = f32[288,384]{1,0:T(8,128)S(1)} collective-permute-done((f32[288,384]{1,0:T(8,128)S(1)}, f32[288,384]{1,0:T(8,128)S(1)}, u32[]{:S(2)}, u32[]{:S(2)}) %collective-permute-start.22) | collective-permute-done | bytes 442400 | tf_op jit(solution)/shard_map/ppermute | solution.py:30
  90.1 3.0 %collective-permute-start.25 = (f32[72,384]{1,0:T(8,128)S(1)}, f32[72,384]{1,0:T(8,128)S(1)}, u32[]{:S(2)}, u32[]{:S(2)}) collective-permute-start(f32[72,384]{1,0:T(8,128)S(1)} %get-tuple-element.57), channel_id=1, source_target_pairs={{0,192},{32,224},{64,128},{96,160},{128,64},{160,96},{192,0},{224,... | collective-permute-start | bytes 331784 | tf_op jit(solution)/shard_map/ppermute | solution.py:17
  93.2 2.3 %collective-permute-start.23 = (f32[72,384]{1,0:T(8,128)S(1)}, f32[72,384]{1,0:T(8,128)S(1)}, u32[]{:S(2)}, u32[]{:S(2)}) collective-permute-start(f32[72,384]{1,0:T(8,128)S(1)} %get-tuple-element.58), channel_id=1, source_target_pairs={{0,64},{32,96},{64,0},{96,32},{128,192},{160,224},{192,128},{224,1... | collective-permute-start | bytes 331784 | tf_op jit(solution)/shard_map/ppermute | solution.py:17
  95.4 2.8 %collective-permute-done.24 = f32[72,384]{1,0:T(8,128)S(1)} collective-permute-done((f32[72,384]{1,0:T(8,128)S(1)}, f32[72,384]{1,0:T(8,128)S(1)}, u32[]{:S(2)}, u32[]{:S(2)}) %collective-permute-start.24) | collective-permute-done | bytes 110624 | tf_op jit(solution)/shard_map/ppermute | solution.py:17
  98.2 3.4 %collective-permute-done.25 = f32[72,384]{1,0:T(8,128)S(1)} collective-permute-done((f32[72,384]{1,0:T(8,128)S(1)}, f32[72,384]{1,0:T(8,128)S(1)}, u32[]{:S(2)}, u32[]{:S(2)}) %collective-permute-start.25) | collective-permute-done | bytes 110624 | tf_op jit(solution)/shard_map/ppermute | solution.py:17
  101.5 2.4 %collective-permute-done.23 = f32[72,384]{1,0:T(8,128)S(1)} collective-permute-done((f32[72,384]{1,0:T(8,128)S(1)}, f32[72,384]{1,0:T(8,128)S(1)}, u32[]{:S(2)}, u32[]{:S(2)}) %collective-permute-start.23) | collective-permute-done | bytes 110624 | tf_op jit(solution)/shard_map/ppermute | solution.py:17
  (64 shorter events, 5.4 us)
Async XLA Ops:
  1.4 4.2 %collective-permute-start = (f32[8,64]{1,0:T(8,128)S(1)}, f32[8,64]{1,0:T(8,128)S(1)}, u32[]{:S(2)}, u32[]{:S(2)}) collective-permute-start(f32[8,64]{1,0:T(8,128)S(1)} %get-tuple-element.63), channel_id=1, source_target_pairs={{0,1},{1,0},{2,3},{3,2},{4,5},{5,4},{6,7},{7,6},{8,9},{9,8},{10,11... | collective-permute-start | bytes 6152 | tf_op jit(solution)/shard_map/ppermute | solution.py:21
  5.5 1.3 %collective-permute-start.1 = (f32[16,1024]{1,0:T(8,128)S(1)}, f32[16,1024]{1,0:T(8,128)S(1)}, u32[]{:S(2)}, u32[]{:S(2)}) collective-permute-start(f32[16,1024]{1,0:T(8,128)S(1)} %get-tuple-element.60), channel_id=1, source_target_pairs={{0,1},{1,0},{2,3},{3,2},{4,5},{5,4},{6,7},{7,6},{8,9},{9,8},{10,11... | collective-permute-start | bytes 196616 | tf_op jit(solution)/shard_map/ppermute | solution.py:21
  6.8 8.7 %collective-permute-start.4 = (f32[40,1024]{1,0:T(8,128)S(1)}, f32[40,1024]{1,0:T(8,128)S(1)}, u32[]{:S(2)}, u32[]{:S(2)}) collective-permute-start(f32[40,1024]{1,0:T(8,128)S(1)} %pad_maximum_fusion.4), channel_id=1, source_target_pairs={{0,6},{1,25},{2,4},{3,27},{4,2},{5,29},{6,0},{7,31},{8,14},{9,17},... | collective-permute-start | bytes 491528 | tf_op jit(solution)/shard_map/ppermute | solution.py:36
  7.9 7.6 %collective-permute-start.3 = (f32[40,1024]{1,0:T(8,128)S(1)}, f32[40,1024]{1,0:T(8,128)S(1)}, u32[]{:S(2)}, u32[]{:S(2)}) collective-permute-start(f32[40,1024]{1,0:T(8,128)S(1)} %pad_maximum_fusion.4), channel_id=1, source_target_pairs={{0,4},{1,17},{2,6},{3,19},{4,0},{5,21},{6,2},{7,23},{8,12},{9,25},... | collective-permute-start | bytes 491528 | tf_op jit(solution)/shard_map/ppermute | solution.py:36
  8.3 7.3 %collective-permute-start.2 = (f32[40,1024]{1,0:T(8,128)S(1)}, f32[40,1024]{1,0:T(8,128)S(1)}, u32[]{:S(2)}, u32[]{:S(2)}) collective-permute-start(f32[40,1024]{1,0:T(8,128)S(1)} %pad_maximum_fusion.4), channel_id=1, source_target_pairs={{0,2},{1,9},{2,0},{3,11},{4,6},{5,13},{6,4},{7,15},{8,10},{9,1},{1... | collective-permute-start | bytes 491528 | tf_op jit(solution)/shard_map/ppermute | solution.py:36
  10.2 7.7 %collective-permute-start.7 = (f32[64,384]{1,0:T(8,128)}, f32[64,384]{1,0:T(8,128)S(1)}, u32[]{:S(2)}, u32[]{:S(2)}) collective-permute-start(f32[64,384]{1,0:T(8,128)} %param.10), channel_id=1, source_target_pairs={{0,128},{32,160},{64,192},{96,224},{128,0},{160,32},{192,64},{224,... | collective-permute-start | bytes 294920 | tf_op jit(solution)/shard_map/ppermute | solution.py:17
  15.6 7.2 %collective-permute-start.5 = (f32[8,512]{1,0:T(8,128)S(1)}, f32[8,512]{1,0:T(8,128)S(1)}, u32[]{:S(2)}, u32[]{:S(2)}) collective-permute-start(f32[8,512]{1,0:T(8,128)S(1)} %concatenate.38), channel_id=1, source_target_pairs={{0,8},{1,3},{2,10},{3,1},{4,12},{5,7},{6,14},{7,5},{8,0},{9,11},{1... | collective-permute-start | bytes 49160 | tf_op jit(solution)/shard_map/ppermute | solution.py:36
  18.8 12.3 %collective-permute-start.8 = (f32[128,384]{1,0:T(8,128)S(1)}, f32[128,384]{1,0:T(8,128)S(1)}, u32[]{:S(2)}, u32[]{:S(2)}) collective-permute-start(f32[128,384]{1,0:T(8,128)S(1)} %pad_maximum_fusion.3), channel_id=1, source_target_pairs={{0,64},{32,96},{64,0},{96,32},{128,192},{160,224},{192,128},{224,1... | collective-permute-start | bytes 589832 | tf_op jit(solution)/shard_map/ppermute | solution.py:17
  22.8 4.3 %collective-permute-start.6 = (f32[16,512]{1,0:T(8,128)S(1)}, f32[16,512]{1,0:T(8,128)S(1)}, u32[]{:S(2)}, u32[]{:S(2)}) collective-permute-start(f32[16,512]{1,0:T(8,128)S(1)} %pad_maximum_fusion.7), channel_id=1, source_target_pairs={{0,16},{1,5},{2,18},{3,7},{4,20},{5,1},{6,22},{7,3},{8,24},{9,13},... | collective-permute-start | bytes 98312 | tf_op jit(solution)/shard_map/ppermute | solution.py:36
  31.2 22.2 %collective-permute-start.13 = (f32[128,1024]{1,0:T(8,128)S(1)}, f32[128,1024]{1,0:T(8,128)S(1)}, u32[]{:S(2)}, u32[]{:S(2)}) collective-permute-start(f32[128,1024]{1,0:T(8,128)S(1)} %pad_maximum_fusion.refs_0_), channel_id=1, source_target_pairs={{0,24},{1,7},{2,26},{3,5},{4,28},{5,3},{6,30},{7,1},{8,16},{9,15},... | collective-permute-start | bytes 1572872 | tf_op jit(solution)/shard_map/ppermute | solution.py:36
  34.6 18.8 %collective-permute-start.12 = (f32[128,1024]{1,0:T(8,128)S(1)}, f32[128,1024]{1,0:T(8,128)S(1)}, u32[]{:S(2)}, u32[]{:S(2)}) collective-permute-start(f32[128,1024]{1,0:T(8,128)S(1)} %pad_maximum_fusion.refs_0_), channel_id=1, source_target_pairs={{0,8},{1,3},{2,10},{3,1},{4,12},{5,7},{6,14},{7,5},{8,0},{9,11},{1... | collective-permute-start | bytes 1572872 | tf_op jit(solution)/shard_map/ppermute | solution.py:36
  34.6 5.9 %collective-permute-start.9 = (f32[32,512]{1,0:T(8,128)S(1)}, f32[32,512]{1,0:T(8,128)S(1)}, u32[]{:S(2)}, u32[]{:S(2)}) collective-permute-start(f32[32,512]{1,0:T(8,128)S(1)} %pad_maximum_fusion.6), channel_id=1, source_target_pairs={{0,64},{32,96},{64,0},{96,32},{128,192},{160,224},{192,128},{224,1... | collective-permute-start | bytes 196616 | tf_op jit(solution)/shard_map/ppermute | solution.py:17
  34.6 18.1 %collective-permute-start.11 = (f32[256,384]{1,0:T(8,128)S(1)}, f32[256,384]{1,0:T(8,128)S(1)}, u32[]{:S(2)}, u32[]{:S(2)}) collective-permute-start(f32[256,384]{1,0:T(8,128)S(1)} %pad_maximum_fusion.1.refs_0_), channel_id=1, source_target_pairs={{0,32},{1,225},{2,34},{3,227},{4,36},{5,229},{6,38},{7,231},{8,40}... | collective-permute-start | bytes 1179656 | tf_op jit(solution)/shard_map/ppermute | solution.py:30
  39.2 18.0 %collective-permute-start.14 = (f32[128,1024]{1,0:T(8,128)S(1)}, f32[128,1024]{1,0:T(8,128)S(1)}, u32[]{:S(2)}, u32[]{:S(2)}) collective-permute-start(f32[128,1024]{1,0:T(8,128)S(1)} %pad_maximum_fusion.refs_0_), channel_id=1, source_target_pairs={{0,16},{1,5},{2,18},{3,7},{4,20},{5,1},{6,22},{7,3},{8,24},{9,13},... | collective-permute-start | bytes 1572872 | tf_op jit(solution)/shard_map/ppermute | solution.py:36
  40.6 12.1 %collective-permute-start.10 = (f32[64,512]{1,0:T(8,128)S(1)}, f32[64,512]{1,0:T(8,128)S(1)}, u32[]{:S(2)}, u32[]{:S(2)}) collective-permute-start(f32[64,512]{1,0:T(8,128)S(1)} %pad_maximum_fusion.5), channel_id=1, source_target_pairs={{0,128},{32,160},{64,192},{96,224},{128,0},{160,32},{192,64},{224,... | collective-permute-start | bytes 393224 | tf_op jit(solution)/shard_map/ppermute | solution.py:17
  53.5 3.9 %collective-permute-start.20 = (f32[128,512]{1,0:T(8,128)S(1)}, f32[128,512]{1,0:T(8,128)S(1)}, u32[]{:S(2)}, u32[]{:S(2)}) collective-permute-start(f32[128,512]{1,0:T(8,128)S(1)} %pad_maximum_fusion.2.refs_0_), channel_id=1, source_target_pairs={{0,1},{1,0},{2,3},{3,2},{4,5},{5,4},{6,7},{7,6},{8,9},{9,8},{10,11... | collective-permute-start | bytes 786440 | tf_op jit(solution)/shard_map/ppermute | solution.py:21
  56.2 12.9 %collective-permute-start.15 = (f32[128,1024]{1,0:T(8,128)S(1)}, f32[128,1024]{1,0:T(8,128)}, u32[]{:S(2)}, u32[]{:S(2)}) collective-permute-start(f32[128,1024]{1,0:T(8,128)S(1)} %pad_maximum_fusion.refs_0_), channel_id=1, source_target_pairs={{0,1},{1,0},{2,3},{3,2},{4,5},{5,4},{6,7},{7,6},{8,9},{9,8},{10,11... | collective-permute-start | bytes 1572872 | tf_op jit(solution)/shard_map/ppermute | solution.py:21
  56.3 6.4 %collective-permute-start.19 = (f32[128,512]{1,0:T(8,128)S(1)}, f32[128,512]{1,0:T(8,128)S(1)}, u32[]{:S(2)}, u32[]{:S(2)}) collective-permute-start(f32[128,512]{1,0:T(8,128)S(1)} %pad_maximum_fusion.2.refs_0_), channel_id=1, source_target_pairs={{0,32},{1,225},{2,34},{3,227},{4,36},{5,229},{6,38},{7,231},{8,40}... | collective-permute-start | bytes 786440 | tf_op jit(solution)/shard_map/ppermute | solution.py:30
  56.3 12.9 %collective-permute-start.16 = (f32[128,1024]{1,0:T(8,128)S(1)}, f32[128,1024]{1,0:T(8,128)}, u32[]{:S(2)}, u32[]{:S(2)}) collective-permute-start(f32[128,1024]{1,0:T(8,128)S(1)} %collective-permute-done.12.refs_1_), channel_id=1, source_target_pairs={{0,1},{1,0},{2,3},{3,2},{4,5},{5,4},{6,7},{7,6},{8,9},{9,8},{10,11... | collective-permute-start | bytes 1572872 | tf_op jit(solution)/shard_map/ppermute | solution.py:21
  57.2 11.9 %collective-permute-start.17 = (f32[128,1024]{1,0:T(8,128)S(1)}, f32[128,1024]{1,0:T(8,128)}, u32[]{:S(2)}, u32[]{:S(2)}) collective-permute-start(f32[128,1024]{1,0:T(8,128)S(1)} %collective-permute-done.14.refs_2_), channel_id=1, source_target_pairs={{0,1},{1,0},{2,3},{3,2},{4,5},{5,4},{6,7},{7,6},{8,9},{9,8},{10,11... | collective-permute-start | bytes 1572872 | tf_op jit(solution)/shard_map/ppermute | solution.py:21
  57.3 11.8 %collective-permute-start.18 = (f32[128,1024]{1,0:T(8,128)S(1)}, f32[128,1024]{1,0:T(8,128)}, u32[]{:S(2)}, u32[]{:S(2)}) collective-permute-start(f32[128,1024]{1,0:T(8,128)S(1)} %collective-permute-done.13.refs_3_), channel_id=1, source_target_pairs={{0,1},{1,0},{2,3},{3,2},{4,5},{5,4},{6,7},{7,6},{8,9},{9,8},{10,11... | collective-permute-start | bytes 1572872 | tf_op jit(solution)/shard_map/ppermute | solution.py:21
  62.7 1.5 %collective-permute-start.21 = (f32[128,512]{1,0:T(8,128)S(1)}, f32[128,512]{1,0:T(8,128)S(1)}, u32[]{:S(2)}, u32[]{:S(2)}) collective-permute-start(f32[128,512]{1,0:T(8,128)S(1)} %collective-permute-done.19.refs_1_), channel_id=1, source_target_pairs={{0,1},{1,0},{2,3},{3,2},{4,5},{5,4},{6,7},{7,6},{8,9},{9,8},{10,11... | collective-permute-start | bytes 786440 | tf_op jit(solution)/shard_map/ppermute | solution.py:21
  69.2 1.9 %copy-start = (f32[2048,384]{1,0:T(8,128)S(1)}, f32[2048,384]{1,0:T(8,128)}, u32[]{:S(2)}) copy-start(f32[2048,384]{1,0:T(8,128)} %refs_10_.1) | copy-start | bytes 9437188
  71.0 0.9 copy-start.4
  72.0 9.3 %copy-start.1 = (f32[2048,384]{1,0:T(8,128)S(1)}, f32[2048,384]{1,0:T(8,128)}, u32[]{:S(2)}) copy-start(f32[2048,384]{1,0:T(8,128)} %refs_3_.1) | copy-start | bytes 9437188
  72.0 9.3 %copy-start.3 = (f32[256,384]{1,0:T(8,128)S(1)}, f32[256,384]{1,0:T(8,128)}, u32[]{:S(2)}) copy-start(f32[256,384]{1,0:T(8,128)} %copy-done.2) | copy-start | bytes 1179652
  81.2 8.4 %collective-permute-start.22 = (f32[288,384]{1,0:T(8,128)S(1)}, f32[288,384]{1,0:T(8,128)S(1)}, u32[]{:S(2)}, u32[]{:S(2)}) collective-permute-start(f32[288,384]{1,0:T(8,128)S(1)} %get-tuple-element.47), channel_id=1, source_target_pairs={{0,32},{1,225},{2,34},{3,227},{4,36},{5,229},{6,38},{7,231},{8,40}... | collective-permute-start | bytes 1327112 | tf_op jit(solution)/shard_map/ppermute | solution.py:30
  81.3 22.8 %copy-start.5 = (f32[64,384]{1,0:T(8,128)S(1)}, f32[64,384]{1,0:T(8,128)}, u32[]{:S(2)}) copy-start(f32[64,384]{1,0:T(8,128)} %param.14) | copy-start | bytes 294916
  81.3 23.4 %copy-start.6 = (f32[64,16]{0,1:T(8,128)S(1)}, f32[64,16]{0,1:T(8,128)}, u32[]{:S(2)}) copy-start(f32[64,16]{0,1:T(8,128)} %param.13) | copy-start | bytes 12292
  89.7 8.5 %collective-permute-start.24 = (f32[72,384]{1,0:T(8,128)S(1)}, f32[72,384]{1,0:T(8,128)S(1)}, u32[]{:S(2)}, u32[]{:S(2)}) collective-permute-start(f32[72,384]{1,0:T(8,128)S(1)} %get-tuple-element.56), channel_id=1, source_target_pairs={{0,128},{32,160},{64,192},{96,224},{128,0},{160,32},{192,64},{224,... | collective-permute-start | bytes 331784 | tf_op jit(solution)/shard_map/ppermute | solution.py:17
  90.1 11.4 %collective-permute-start.25 = (f32[72,384]{1,0:T(8,128)S(1)}, f32[72,384]{1,0:T(8,128)S(1)}, u32[]{:S(2)}, u32[]{:S(2)}) collective-permute-start(f32[72,384]{1,0:T(8,128)S(1)} %get-tuple-element.57), channel_id=1, source_target_pairs={{0,192},{32,224},{64,128},{96,160},{128,64},{160,96},{192,0},{224,... | collective-permute-start | bytes 331784 | tf_op jit(solution)/shard_map/ppermute | solution.py:17
  93.2 10.8 %collective-permute-start.23 = (f32[72,384]{1,0:T(8,128)S(1)}, f32[72,384]{1,0:T(8,128)S(1)}, u32[]{:S(2)}, u32[]{:S(2)}) collective-permute-start(f32[72,384]{1,0:T(8,128)S(1)} %get-tuple-element.58), channel_id=1, source_target_pairs={{0,64},{32,96},{64,0},{96,32},{128,192},{160,224},{192,128},{224,1... | collective-permute-start | bytes 331784 | tf_op jit(solution)/shard_map/ppermute | solution.py:17
  (1 other events, 0.7 us)

commit v7 on v6

--- a/solution.py
+++ b/solution.py
@@ -239,7 +239,7 @@
         out_specs=[VMEM] * 2,
         scratch_shapes=[pltpu.VMEM((4, B, 128), F32)],
         compiler_params=pltpu.CompilerParams(vmem_limit_bytes=8 * MIB),
-        cost_estimate=pl.CostEstimate(flops=1_000_000, bytes_accessed=1 << 16, transcendentals=0),
+        cost_estimate=pl.CostEstimate(flops=4_000_000_000, bytes_accessed=2 * MIB, transcendentals=0),
         name="prepare",
     )(ids, *blocks)
 
@@ -314,16 +314,16 @@
     row_even = jnp.concatenate([row_pair, with_row_partner(row_pair, 2)], axis=0)
     diag_quad = jnp.concatenate([diag_quad, with_col_partner(diag_quad, 1, 1)], axis=0)
     diag_quad = jnp.concatenate([diag_quad, with_col_partner(diag_quad, 1, 2)], axis=0)
-    diag_quad, both, row_even = lax.optimization_barrier((diag_quad, both, row_even))
-    row_odd = with_neighbour(row_even)
+    diag_quad, both = lax.optimization_barrier((diag_quad, both))
     grad_quad = jnp.concatenate([b[:32] for b in both], axis=0)
     grad_far = [with_col_partner(grad_quad, 1, k) for k in (1, 2, 3)]
     diag_even = jnp.concatenate([diag_quad, with_row_partner(diag_quad, 2)], axis=0)
+    row_even, diag_even = lax.optimization_barrier((row_even, diag_even))
     diag_even = jnp.concatenate([diag_even, with_row_partner(diag_even, 4)], axis=0)
-    diag_even, row_odd, grad_far[0], grad_far[2] = lax.optimization_barrier(
-        (diag_even, row_odd, grad_far[0], grad_far[2])
-    )
+    diag_even, grad_far[0], grad_far[2] = lax.optimization_barrier((diag_even, grad_far[0], grad_far[2]))
     diag_odd = with_neighbour(diag_even)
+    row_even, diag_odd = lax.optimization_barrier((row_even, diag_odd))
+    row_odd = with_neighbour(row_even)
     diag_blocks = [diag_even, diag_odd, with_sibling(diag_even), with_sibling(diag_odd)]
     quad_swapped = with_sibling(grad_quad)
 

time: 106 us -> 106 us (level)
  starting transfers between devices: 39.8 us -> 45.3 us
  waiting for transfers between devices: 35.6 us -> 32.2 us
  local copies, waits for them, and re-layouts: 3.83 us -> 1.95 us
    ppermute x7, starting transfers between devices: 15.2 us -> 21.3 us  [with_row_partner(): return lax.ppermute(v, 'row', [(i, i ^ k) for i in range(ROWS)])]
    ppermute x7, waiting for transfers between devices: 25.5 us -> 21.2 us  [with_row_partner(): return lax.ppermute(v, 'row', [(i, i ^ k) for i in range(ROWS)])]
    ppermute x8, waiting for transfers between devices: 1.51 us -> 4.84 us  [with_col_partner(): return lax.ppermute(v, 'col', perm)]
    unnamed x14, local copies, waits for them, and re-layouts: 3.55 us -> 1.67 us
    ppermute x8, starting transfers between devices: 12.1 us -> 13.6 us  [with_col_partner(): return lax.ppermute(v, 'col', perm)]
    ppermute x8, starting transfers between devices: 7.86 us -> 6.32 us  [with_sibling(): return lax.ppermute(v, 'col', [(i, i ^ 1) for i in range(COLS)])]
    ppermute x3, waiting for transfers between devices: 6.26 us -> 4.98 us  [with_neighbour(): return lax.ppermute(v, ('row', 'col'), perm)]
    ppermute x8, waiting for transfers between devices: 2.37 us -> 1.17 us  [with_sibling(): return lax.ppermute(v, 'col', [(i, i ^ 1) for i in range(COLS)])]
  transfers between devices with their start and end apart: 26 -> 26, of which waited for: 12 -> 10; matrix products, arithmetic and copies ran while one was open for 2% -> 2% of each run, Pallas kernels for 11% -> 20%
where the time goes in v7:
time: 106 us
  starting transfers between devices  45.3 us (43%)
  waiting for transfers between devices  32.2 us (30%)
  Pallas kernels  21.5 us (20%)
  other arithmetic  4.1 us (4%)
  local copies, waits for them, and re-layouts  1.95 us (2%)
    ppermute x7, starting transfers between devices, with_row_partner(): return lax.ppermute(v, 'row', [(i, i ^ k) for i in range(ROWS)])  21.3 us
    ppermute x7, waiting for transfers between devices, with_row_partner(): return lax.ppermute(v, 'row', [(i, i ^ k) for i in range(ROWS)])  21.2 us
    ppermute x8, starting transfers between devices, with_col_partner(): return lax.ppermute(v, 'col', perm)  13.6 us
    pallas_call x1, Pallas kernels, solve(): pl.pallas_call(solve_kernel, out_shape=[shape((B, 2048)), shape((16, 2048...  9.14 us
    pallas_call x1, Pallas kernels, trailing_update(): pl.pallas_call(trailing_kernel, grid=(2048 // tile,), out_shape=shape((20...  7.02 us
    ppermute x8, starting transfers between devices, with_sibling(): return lax.ppermute(v, 'col', [(i, i ^ 1) for i in range(COLS)])  6.32 us
    pallas_call x1, Pallas kernels, prepare(): pl.pallas_call(prepare_kernel, out_shape=[shape((256, 1536), BF16), shape...  5.31 us
    ppermute x3, waiting for transfers between devices, with_neighbour(): return lax.ppermute(v, ('row', 'col'), perm)  4.98 us
  transfers between devices with their start and end apart: 26, of which 10 were waited for; matrix products, arithmetic and copies ran while one was open for 2% of the time, Pallas kernels for 20%

profile of v7, /device:TPU:1, one launch (start us, length us, event | category | flops | bytes accessed | tf_op | source)
XLA Modules:
  0.0 105.9 jit_solution(16216712603585630253)
XLA Ops:
  0.6 0.7 slice_select_fusion.2
  1.4 3.2 %collective-permute-start = (f32[8,64]{1,0:T(8,128)S(1)}, f32[8,64]{1,0:T(8,128)S(1)}, u32[]{:S(2)}, u32[]{:S(2)}) collective-permute-start(f32[8,64]{1,0:T(8,128)S(1)} %get-tuple-element.67), channel_id=1, source_target_pairs={{0,1},{1,0},{2,3},{3,2},{4,5},{5,4},{6,7},{7,6},{8,9},{9,8},{10,11... | collective-permute-start | bytes 6152 | tf_op jit(solution)/shard_map/ppermute | solution.py:21
  4.6 0.9 slice_select_fusion.1
  5.7 1.2 %collective-permute-done.1 = f32[16,1024]{1,0:T(8,128)S(1)} collective-permute-done((f32[16,1024]{1,0:T(8,128)S(1)}, f32[16,1024]{1,0:T(8,128)S(1)}, u32[]{:S(2)}, u32[]{:S(2)}) %collective-permute-start.1) | collective-permute-done | bytes 65568 | tf_op jit(solution)/shard_map/ppermute | solution.py:21
  6.9 2.2 %collective-permute-start.3 = (f32[40,1024]{1,0:T(8,128)S(1)}, f32[40,1024]{1,0:T(8,128)S(1)}, u32[]{:S(2)}, u32[]{:S(2)}) collective-permute-start(f32[40,1024]{1,0:T(8,128)S(1)} %pad_maximum_fusion.4), channel_id=1, source_target_pairs={{0,4},{1,17},{2,6},{3,19},{4,0},{5,21},{6,2},{7,23},{8,12},{9,25},... | collective-permute-start | bytes 491528 | tf_op jit(solution)/shard_map/ppermute | solution.py:36
  9.1 1.7 %collective-permute-start.4 = (f32[40,1024]{1,0:T(8,128)S(1)}, f32[40,1024]{1,0:T(8,128)S(1)}, u32[]{:S(2)}, u32[]{:S(2)}) collective-permute-start(f32[40,1024]{1,0:T(8,128)S(1)} %pad_maximum_fusion.4), channel_id=1, source_target_pairs={{0,6},{1,25},{2,4},{3,27},{4,2},{5,29},{6,0},{7,31},{8,14},{9,17},... | collective-permute-start | bytes 491528 | tf_op jit(solution)/shard_map/ppermute | solution.py:36
  11.4 2.5 %collective-permute-done.3 = f32[40,1024]{1,0:T(8,128)S(1)} collective-permute-done((f32[40,1024]{1,0:T(8,128)S(1)}, f32[40,1024]{1,0:T(8,128)S(1)}, u32[]{:S(2)}, u32[]{:S(2)}) %collective-permute-start.3) | collective-permute-done | bytes 163872 | tf_op jit(solution)/shard_map/ppermute | solution.py:36
  13.9 1.8 %collective-permute-done.4 = f32[40,1024]{1,0:T(8,128)S(1)} collective-permute-done((f32[40,1024]{1,0:T(8,128)S(1)}, f32[40,1024]{1,0:T(8,128)S(1)}, u32[]{:S(2)}, u32[]{:S(2)}) %collective-permute-start.4) | collective-permute-done | bytes 163872 | tf_op jit(solution)/shard_map/ppermute | solution.py:36
  15.7 0.9 collective-permute-start.5
  16.6 6.9 %collective-permute-start.7 = (f32[64,384]{1,0:T(8,128)}, f32[64,384]{1,0:T(8,128)S(1)}, u32[]{:S(2)}, u32[]{:S(2)}) collective-permute-start(f32[64,384]{1,0:T(8,128)} %param.10), channel_id=1, source_target_pairs={{0,128},{32,160},{64,192},{96,224},{128,0},{160,32},{192,64},{224,... | collective-permute-start | bytes 294920 | tf_op jit(solution)/shard_map/ppermute | solution.py:17
  23.5 2.5 %collective-permute-start.6 = (f32[16,512]{1,0:T(8,128)S(1)}, f32[16,512]{1,0:T(8,128)S(1)}, u32[]{:S(2)}, u32[]{:S(2)}) collective-permute-start(f32[16,512]{1,0:T(8,128)S(1)} %pad_maximum_fusion.7), channel_id=1, source_target_pairs={{0,16},{1,5},{2,18},{3,7},{4,20},{5,1},{6,22},{7,3},{8,24},{9,13},... | collective-permute-start | bytes 98312 | tf_op jit(solution)/shard_map/ppermute | solution.py:36
  26.0 0.9 pad_maximum_fusion.3
  26.9 3.9 %collective-permute-start.8 = (f32[128,384]{1,0:T(8,128)S(1)}, f32[128,384]{1,0:T(8,128)S(1)}, u32[]{:S(2)}, u32[]{:S(2)}) collective-permute-start(f32[128,384]{1,0:T(8,128)S(1)} %pad_maximum_fusion.3), channel_id=1, source_target_pairs={{0,64},{32,96},{64,0},{96,32},{128,192},{160,224},{192,128},{224,1... | collective-permute-start | bytes 589832 | tf_op jit(solution)/shard_map/ppermute | solution.py:17
  31.0 0.8 collective-permute-start.11
  31.8 2.7 %collective-permute-start.12 = (f32[128,1024]{1,0:T(8,128)S(1)}, f32[128,1024]{1,0:T(8,128)S(1)}, u32[]{:S(2)}, u32[]{:S(2)}) collective-permute-start(f32[128,1024]{1,0:T(8,128)S(1)} %pad_maximum_fusion.refs_0_), channel_id=1, source_target_pairs={{0,24},{1,7},{2,26},{3,5},{4,28},{5,3},{6,30},{7,1},{8,16},{9,15},... | collective-permute-start | bytes 1572872 | tf_op jit(solution)/shard_map/ppermute | solution.py:36
  34.5 7.6 %collective-permute-done.9 = f32[32,512]{1,0:T(8,128)S(1)} collective-permute-done((f32[32,512]{1,0:T(8,128)S(1)}, f32[32,512]{1,0:T(8,128)S(1)}, u32[]{:S(2)}, u32[]{:S(2)}) %collective-permute-start.9) | collective-permute-done | bytes 65568 | tf_op jit(solution)/shard_map/ppermute | solution.py:17
  42.2 4.7 %collective-permute-start.10 = (f32[64,512]{1,0:T(8,128)S(1)}, f32[64,512]{1,0:T(8,128)S(1)}, u32[]{:S(2)}, u32[]{:S(2)}) collective-permute-start(f32[64,512]{1,0:T(8,128)S(1)} %pad_maximum_fusion.5), channel_id=1, source_target_pairs={{0,128},{32,160},{64,192},{96,224},{128,0},{160,32},{192,64},{224,... | collective-permute-start | bytes 393224 | tf_op jit(solution)/shard_map/ppermute | solution.py:17
  46.9 2.8 %collective-permute-start.13 = (f32[128,1024]{1,0:T(8,128)S(1)}, f32[128,1024]{1,0:T(8,128)S(1)}, u32[]{:S(2)}, u32[]{:S(2)}) collective-permute-start(f32[128,1024]{1,0:T(8,128)S(1)} %pad_maximum_fusion.refs_0_), channel_id=1, source_target_pairs={{0,16},{1,5},{2,18},{3,7},{4,20},{5,1},{6,22},{7,3},{8,24},{9,13},... | collective-permute-start | bytes 1572872 | tf_op jit(solution)/shard_map/ppermute | solution.py:36
  49.7 3.8 %collective-permute-done.10 = f32[64,512]{1,0:T(8,128)S(1)} collective-permute-done((f32[64,512]{1,0:T(8,128)S(1)}, f32[64,512]{1,0:T(8,128)S(1)}, u32[]{:S(2)}, u32[]{:S(2)}) %collective-permute-start.10) | collective-permute-done | bytes 131104 | tf_op jit(solution)/shard_map/ppermute | solution.py:17
  53.5 1.1 %collective-permute-start.18 = (f32[128,512]{1,0:T(8,128)S(1)}, f32[128,512]{1,0:T(8,128)S(1)}, u32[]{:S(2)}, u32[]{:S(2)}) collective-permute-start(f32[128,512]{1,0:T(8,128)S(1)} %pad_maximum_fusion.2.refs_0_), channel_id=1, source_target_pairs={{0,32},{1,225},{2,34},{3,227},{4,36},{5,229},{6,38},{7,231},{8,40}... | collective-permute-start | bytes 786440 | tf_op jit(solution)/shard_map/ppermute | solution.py:30
  55.1 4.9 %collective-permute-done.18.refs_1_ = f32[128,512]{1,0:T(8,128)S(1)} collective-permute-done((f32[128,512]{1,0:T(8,128)S(1)}, f32[128,512]{1,0:T(8,128)S(1)}, u32[]{:S(2)}, u32[]{:S(2)}) %collective-permute-start.18) | collective-permute-done | bytes 262176 | tf_op jit(solution)/shard_map/ppermute | solution.py:30
  60.0 1.4 %collective-permute-start.20 = (f32[128,512]{1,0:T(8,128)S(1)}, f32[128,512]{1,0:T(8,128)}, u32[]{:S(2)}, u32[]{:S(2)}) collective-permute-start(f32[128,512]{1,0:T(8,128)S(1)} %collective-permute-done.18.refs_1_), channel_id=1, source_target_pairs={{0,1},{1,0},{2,3},{3,2},{4,5},{5,4},{6,7},{7,6},{8,9},{9,8},{10,11... | collective-permute-start | bytes 786440 | tf_op jit(solution)/shard_map/ppermute | solution.py:21
  63.2 1.7 %collective-permute-start.22 = (f32[256,384]{1,0:T(8,128)S(1)}, f32[256,384]{1,0:T(8,128)S(1)}, u32[]{:S(2)}, u32[]{:S(2)}) collective-permute-start(f32[256,384]{1,0:T(8,128)S(1)} %pad_maximum_fusion.1.refs_0_), channel_id=1, source_target_pairs={{0,32},{1,225},{2,34},{3,227},{4,36},{5,229},{6,38},{7,231},{8,40}... | collective-permute-start | bytes 1179656 | tf_op jit(solution)/shard_map/ppermute | solution.py:30
  64.9 0.9 copy-done.3
  65.9 5.3 %prepare.1 = (bf16[256,1536]{1,0:T(8,128)(2,1)S(1)}, bf16[256,768]{1,0:T(8,128)(2,1)S(1)}) custom-call(s32[7]{0:T(128)S(1)} %stack.31.ids, f32[128,512]{1,0:T(8,128)S(1)} %pad_maximum_fusion.2.refs_0_, f32[128,512]{1,0:T(8,128)S(1)} %collective-permute-done.18.refs_1_, f32[128,512]{1,0:T(8,128)S(1)} %copy-done.3, f32[128,512]{1,0:T(8,128)} %collective-permute-done.20.refs_3_), custom_call_target="tpu_custom_call" | custom-call | flops 4000000000 | bytes 2097152 | tf_op jit(solution)/shard_map/prepare/pallas_call | solution.py:235
  71.3 9.1 %solve.1 = (f32[512,2048]{1,0:T(8,128)S(1)}, f32[16,2048]{1,0:T(8,128)}, f32[288,384]{1,0:T(8,128)S(1)}, f32[72,384]{1,0:T(8,128)S(1)}, f32[72,384]{1,0:T(8,128)...) custom-call(s32[7]{0:T(128)S(1)} %stack.31.ids, f32[128,1024]{1,0:T(8,128)S(1)} %pad_maximum_fusion.refs_0_, ...), custom_call_target="tpu_custom_call" | custom-call | flops 6000000000 | bytes 12582912 | tf_op jit(solution)/shard_map/solve/pallas_call | solution.py:248
  80.4 1.2 %collective-permute-start.21 = (f32[288,384]{1,0:T(8,128)S(1)}, f32[288,384]{1,0:T(8,128)S(1)}, u32[]{:S(2)}, u32[]{:S(2)}) collective-permute-start(f32[288,384]{1,0:T(8,128)S(1)} %get-tuple-element.51), channel_id=1, source_target_pairs={{0,32},{1,225},{2,34},{3,227},{4,36},{5,229},{6,38},{7,231},{8,40}... | collective-permute-start | bytes 1327112 | tf_op jit(solution)/shard_map/ppermute | solution.py:30
  81.7 7.0 %trailing.1 = f32[2048,384]{1,0:T(8,128)} custom-call(s32[7]{0:T(128)S(1)} %stack.31.ids, f32[256,384]{1,0:T(8,128)S(1)} %pad_maximum_fusion.1.refs_0_, f32[256,384]{1,0:T(8,128)S(1)} %collective-permute-done.22.refs_1_, f32[512,2048]{1,0:T(8,128)S(1)} %get-tuple-element.53.refs_2_, f32[2048,384]{1,0:T(8,128)S(1)} %copy-done.1), custom_call_target="tpu_custom_call" | custom-call | flops 4000000000 | bytes 11534336 | tf_op jit(solution)/shard_map/trailing/pallas_call | solution.py:268
  88.9 2.5 %collective-permute-start.24 = (f32[72,384]{1,0:T(8,128)S(1)}, f32[72,384]{1,0:T(8,128)S(1)}, u32[]{:S(2)}, u32[]{:S(2)}) collective-permute-start(f32[72,384]{1,0:T(8,128)S(1)} %get-tuple-element.60), channel_id=1, source_target_pairs={{0,128},{32,160},{64,192},{96,224},{128,0},{160,32},{192,64},{224,... | collective-permute-start | bytes 331784 | tf_op jit(solution)/shard_map/ppermute | solution.py:17
  91.5 3.1 %collective-permute-start.25 = (f32[72,384]{1,0:T(8,128)S(1)}, f32[72,384]{1,0:T(8,128)S(1)}, u32[]{:S(2)}, u32[]{:S(2)}) collective-permute-start(f32[72,384]{1,0:T(8,128)S(1)} %get-tuple-element.61), channel_id=1, source_target_pairs={{0,192},{32,224},{64,128},{96,160},{128,64},{160,96},{192,0},{224,... | collective-permute-start | bytes 331784 | tf_op jit(solution)/shard_map/ppermute | solution.py:17
  94.6 4.2 %collective-permute-done.23 = f32[72,384]{1,0:T(8,128)S(1)} collective-permute-done((f32[72,384]{1,0:T(8,128)S(1)}, f32[72,384]{1,0:T(8,128)S(1)}, u32[]{:S(2)}, u32[]{:S(2)}) %collective-permute-start.23) | collective-permute-done | bytes 110624 | tf_op jit(solution)/shard_map/ppermute | solution.py:17
  98.8 5.6 %collective-permute-done.25 = f32[72,384]{1,0:T(8,128)S(1)} collective-permute-done((f32[72,384]{1,0:T(8,128)S(1)}, f32[72,384]{1,0:T(8,128)S(1)}, u32[]{:S(2)}, u32[]{:S(2)}) %collective-permute-start.25) | collective-permute-done | bytes 110624 | tf_op jit(solution)/shard_map/ppermute | solution.py:17
  (64 shorter events, 5.3 us)
Async XLA Ops:
  1.4 4.2 %collective-permute-start = (f32[8,64]{1,0:T(8,128)S(1)}, f32[8,64]{1,0:T(8,128)S(1)}, u32[]{:S(2)}, u32[]{:S(2)}) collective-permute-start(f32[8,64]{1,0:T(8,128)S(1)} %get-tuple-element.67), channel_id=1, source_target_pairs={{0,1},{1,0},{2,3},{3,2},{4,5},{5,4},{6,7},{7,6},{8,9},{9,8},{10,11... | collective-permute-start | bytes 6152 | tf_op jit(solution)/shard_map/ppermute | solution.py:21
  5.5 1.3 %collective-permute-start.1 = (f32[16,1024]{1,0:T(8,128)S(1)}, f32[16,1024]{1,0:T(8,128)S(1)}, u32[]{:S(2)}, u32[]{:S(2)}) collective-permute-start(f32[16,1024]{1,0:T(8,128)S(1)} %get-tuple-element.64), channel_id=1, source_target_pairs={{0,1},{1,0},{2,3},{3,2},{4,5},{5,4},{6,7},{7,6},{8,9},{9,8},{10,11... | collective-permute-start | bytes 196616 | tf_op jit(solution)/shard_map/ppermute | solution.py:21
  6.8 4.6 %collective-permute-start.2 = (f32[40,1024]{1,0:T(8,128)S(1)}, f32[40,1024]{1,0:T(8,128)S(1)}, u32[]{:S(2)}, u32[]{:S(2)}) collective-permute-start(f32[40,1024]{1,0:T(8,128)S(1)} %pad_maximum_fusion.4), channel_id=1, source_target_pairs={{0,2},{1,9},{2,0},{3,11},{4,6},{5,13},{6,4},{7,15},{8,10},{9,1},{1... | collective-permute-start | bytes 491528 | tf_op jit(solution)/shard_map/ppermute | solution.py:36
  6.9 6.9 %collective-permute-start.3 = (f32[40,1024]{1,0:T(8,128)S(1)}, f32[40,1024]{1,0:T(8,128)S(1)}, u32[]{:S(2)}, u32[]{:S(2)}) collective-permute-start(f32[40,1024]{1,0:T(8,128)S(1)} %pad_maximum_fusion.4), channel_id=1, source_target_pairs={{0,4},{1,17},{2,6},{3,19},{4,0},{5,21},{6,2},{7,23},{8,12},{9,25},... | collective-permute-start | bytes 491528 | tf_op jit(solution)/shard_map/ppermute | solution.py:36
  9.1 6.5 %collective-permute-start.4 = (f32[40,1024]{1,0:T(8,128)S(1)}, f32[40,1024]{1,0:T(8,128)S(1)}, u32[]{:S(2)}, u32[]{:S(2)}) collective-permute-start(f32[40,1024]{1,0:T(8,128)S(1)} %pad_maximum_fusion.4), channel_id=1, source_target_pairs={{0,6},{1,25},{2,4},{3,27},{4,2},{5,29},{6,0},{7,31},{8,14},{9,17},... | collective-permute-start | bytes 491528 | tf_op jit(solution)/shard_map/ppermute | solution.py:36
  15.7 7.8 %collective-permute-start.5 = (f32[8,512]{1,0:T(8,128)S(1)}, f32[8,512]{1,0:T(8,128)S(1)}, u32[]{:S(2)}, u32[]{:S(2)}) collective-permute-start(f32[8,512]{1,0:T(8,128)S(1)} %concatenate.37), channel_id=1, source_target_pairs={{0,8},{1,3},{2,10},{3,1},{4,12},{5,7},{6,14},{7,5},{8,0},{9,11},{1... | collective-permute-start | bytes 49160 | tf_op jit(solution)/shard_map/ppermute | solution.py:36
  16.6 9.4 %collective-permute-start.7 = (f32[64,384]{1,0:T(8,128)}, f32[64,384]{1,0:T(8,128)S(1)}, u32[]{:S(2)}, u32[]{:S(2)}) collective-permute-start(f32[64,384]{1,0:T(8,128)} %param.10), channel_id=1, source_target_pairs={{0,128},{32,160},{64,192},{96,224},{128,0},{160,32},{192,64},{224,... | collective-permute-start | bytes 294920 | tf_op jit(solution)/shard_map/ppermute | solution.py:17
  23.5 7.2 %collective-permute-start.6 = (f32[16,512]{1,0:T(8,128)S(1)}, f32[16,512]{1,0:T(8,128)S(1)}, u32[]{:S(2)}, u32[]{:S(2)}) collective-permute-start(f32[16,512]{1,0:T(8,128)S(1)} %pad_maximum_fusion.7), channel_id=1, source_target_pairs={{0,16},{1,5},{2,18},{3,7},{4,20},{5,1},{6,22},{7,3},{8,24},{9,13},... | collective-permute-start | bytes 98312 | tf_op jit(solution)/shard_map/ppermute | solution.py:36
  26.9 15.2 %collective-permute-start.8 = (f32[128,384]{1,0:T(8,128)S(1)}, f32[128,384]{1,0:T(8,128)S(1)}, u32[]{:S(2)}, u32[]{:S(2)}) collective-permute-start(f32[128,384]{1,0:T(8,128)S(1)} %pad_maximum_fusion.3), channel_id=1, source_target_pairs={{0,64},{32,96},{64,0},{96,32},{128,192},{160,224},{192,128},{224,1... | collective-permute-start | bytes 589832 | tf_op jit(solution)/shard_map/ppermute | solution.py:17
  30.8 11.3 %collective-permute-start.9 = (f32[32,512]{1,0:T(8,128)S(1)}, f32[32,512]{1,0:T(8,128)S(1)}, u32[]{:S(2)}, u32[]{:S(2)}) collective-permute-start(f32[32,512]{1,0:T(8,128)S(1)} %pad_maximum_fusion.6), channel_id=1, source_target_pairs={{0,64},{32,96},{64,0},{96,32},{128,192},{160,224},{192,128},{224,1... | collective-permute-start | bytes 196616 | tf_op jit(solution)/shard_map/ppermute | solution.py:17
  31.0 22.4 %collective-permute-start.11 = (f32[128,1024]{1,0:T(8,128)S(1)}, f32[128,1024]{1,0:T(8,128)S(1)}, u32[]{:S(2)}, u32[]{:S(2)}) collective-permute-start(f32[128,1024]{1,0:T(8,128)S(1)} %pad_maximum_fusion.refs_0_), channel_id=1, source_target_pairs={{0,8},{1,3},{2,10},{3,1},{4,12},{5,7},{6,14},{7,5},{8,0},{9,11},{1... | collective-permute-start | bytes 1572872 | tf_op jit(solution)/shard_map/ppermute | solution.py:36
  31.8 21.7 %collective-permute-start.12 = (f32[128,1024]{1,0:T(8,128)S(1)}, f32[128,1024]{1,0:T(8,128)S(1)}, u32[]{:S(2)}, u32[]{:S(2)}) collective-permute-start(f32[128,1024]{1,0:T(8,128)S(1)} %pad_maximum_fusion.refs_0_), channel_id=1, source_target_pairs={{0,24},{1,7},{2,26},{3,5},{4,28},{5,3},{6,30},{7,1},{8,16},{9,15},... | collective-permute-start | bytes 1572872 | tf_op jit(solution)/shard_map/ppermute | solution.py:36
  42.2 11.3 %collective-permute-start.10 = (f32[64,512]{1,0:T(8,128)S(1)}, f32[64,512]{1,0:T(8,128)S(1)}, u32[]{:S(2)}, u32[]{:S(2)}) collective-permute-start(f32[64,512]{1,0:T(8,128)S(1)} %pad_maximum_fusion.5), channel_id=1, source_target_pairs={{0,128},{32,160},{64,192},{96,224},{128,0},{160,32},{192,64},{224,... | collective-permute-start | bytes 393224 | tf_op jit(solution)/shard_map/ppermute | solution.py:17
  46.9 15.0 %collective-permute-start.13 = (f32[128,1024]{1,0:T(8,128)S(1)}, f32[128,1024]{1,0:T(8,128)S(1)}, u32[]{:S(2)}, u32[]{:S(2)}) collective-permute-start(f32[128,1024]{1,0:T(8,128)S(1)} %pad_maximum_fusion.refs_0_), channel_id=1, source_target_pairs={{0,16},{1,5},{2,18},{3,7},{4,20},{5,1},{6,22},{7,3},{8,24},{9,13},... | collective-permute-start | bytes 1572872 | tf_op jit(solution)/shard_map/ppermute | solution.py:36
  53.5 6.5 %collective-permute-start.18 = (f32[128,512]{1,0:T(8,128)S(1)}, f32[128,512]{1,0:T(8,128)S(1)}, u32[]{:S(2)}, u32[]{:S(2)}) collective-permute-start(f32[128,512]{1,0:T(8,128)S(1)} %pad_maximum_fusion.2.refs_0_), channel_id=1, source_target_pairs={{0,32},{1,225},{2,34},{3,227},{4,36},{5,229},{6,38},{7,231},{8,40}... | collective-permute-start | bytes 786440 | tf_op jit(solution)/shard_map/ppermute | solution.py:30
  54.5 7.4 %collective-permute-start.19 = (f32[128,512]{1,0:T(8,128)S(1)}, f32[128,512]{1,0:T(8,128)S(1)}, u32[]{:S(2)}, u32[]{:S(2)}) collective-permute-start(f32[128,512]{1,0:T(8,128)S(1)} %pad_maximum_fusion.2.refs_0_), channel_id=1, source_target_pairs={{0,1},{1,0},{2,3},{3,2},{4,5},{5,4},{6,7},{7,6},{8,9},{9,8},{10,11... | collective-permute-start | bytes 786440 | tf_op jit(solution)/shard_map/ppermute | solution.py:21
  60.0 3.2 %collective-permute-start.20 = (f32[128,512]{1,0:T(8,128)S(1)}, f32[128,512]{1,0:T(8,128)}, u32[]{:S(2)}, u32[]{:S(2)}) collective-permute-start(f32[128,512]{1,0:T(8,128)S(1)} %collective-permute-done.18.refs_1_), channel_id=1, source_target_pairs={{0,1},{1,0},{2,3},{3,2},{4,5},{5,4},{6,7},{7,6},{8,9},{9,8},{10,11... | collective-permute-start | bytes 786440 | tf_op jit(solution)/shard_map/ppermute | solution.py:21
  61.4 9.8 %collective-permute-start.14 = (f32[128,1024]{1,0:T(8,128)S(1)}, f32[128,1024]{1,0:T(8,128)S(1)}, u32[]{:S(2)}, u32[]{:S(2)}) collective-permute-start(f32[128,1024]{1,0:T(8,128)S(1)} %pad_maximum_fusion.refs_0_), channel_id=1, source_target_pairs={{0,1},{1,0},{2,3},{3,2},{4,5},{5,4},{6,7},{7,6},{8,9},{9,8},{10,11... | collective-permute-start | bytes 1572872 | tf_op jit(solution)/shard_map/ppermute | solution.py:21
  61.4 9.8 %collective-permute-start.15 = (f32[128,1024]{1,0:T(8,128)S(1)}, f32[128,1024]{1,0:T(8,128)}, u32[]{:S(2)}, u32[]{:S(2)}) collective-permute-start(f32[128,1024]{1,0:T(8,128)S(1)} %collective-permute-done.11.refs_1_), channel_id=1, source_target_pairs={{0,1},{1,0},{2,3},{3,2},{4,5},{5,4},{6,7},{7,6},{8,9},{9,8},{10,11... | collective-permute-start | bytes 1572872 | tf_op jit(solution)/shard_map/ppermute | solution.py:21
  61.9 9.3 %collective-permute-start.17 = (f32[128,1024]{1,0:T(8,128)S(1)}, f32[128,1024]{1,0:T(8,128)}, u32[]{:S(2)}, u32[]{:S(2)}) collective-permute-start(f32[128,1024]{1,0:T(8,128)S(1)} %collective-permute-done.12.refs_3_), channel_id=1, source_target_pairs={{0,1},{1,0},{2,3},{3,2},{4,5},{5,4},{6,7},{7,6},{8,9},{9,8},{10,11... | collective-permute-start | bytes 1572872 | tf_op jit(solution)/shard_map/ppermute | solution.py:21
  62.6 8.6 %collective-permute-start.16 = (f32[128,1024]{1,0:T(8,128)S(1)}, f32[128,1024]{1,0:T(8,128)}, u32[]{:S(2)}, u32[]{:S(2)}) collective-permute-start(f32[128,1024]{1,0:T(8,128)S(1)} %collective-permute-done.13.refs_2_), channel_id=1, source_target_pairs={{0,1},{1,0},{2,3},{3,2},{4,5},{5,4},{6,7},{7,6},{8,9},{9,8},{10,11... | collective-permute-start | bytes 1572872 | tf_op jit(solution)/shard_map/ppermute | solution.py:21
  63.2 8.1 %copy-start = (f32[2048,384]{1,0:T(8,128)S(1)}, f32[2048,384]{1,0:T(8,128)}, u32[]{:S(2)}) copy-start(f32[2048,384]{1,0:T(8,128)} %refs_10_.1) | copy-start | bytes 9437188
  63.2 18.4 %collective-permute-start.22 = (f32[256,384]{1,0:T(8,128)S(1)}, f32[256,384]{1,0:T(8,128)S(1)}, u32[]{:S(2)}, u32[]{:S(2)}) collective-permute-start(f32[256,384]{1,0:T(8,128)S(1)} %pad_maximum_fusion.1.refs_0_), channel_id=1, source_target_pairs={{0,32},{1,225},{2,34},{3,227},{4,36},{5,229},{6,38},{7,231},{8,40}... | collective-permute-start | bytes 1179656 | tf_op jit(solution)/shard_map/ppermute | solution.py:30
  64.9 0.9 copy-start.3
  65.9 5.4 %copy-start.4 = (f32[2048,16]{0,1:T(8,128)S(1)}, f32[2048,16]{0,1:T(8,128)}, u32[]{:S(2)}) copy-start(f32[2048,16]{0,1:T(8,128)} %param.9) | copy-start | bytes 393220
  71.3 10.4 %copy-start.1 = (f32[2048,384]{1,0:T(8,128)S(1)}, f32[2048,384]{1,0:T(8,128)}, u32[]{:S(2)}) copy-start(f32[2048,384]{1,0:T(8,128)} %refs_3_.1) | copy-start | bytes 9437188
  80.4 8.4 %collective-permute-start.21 = (f32[288,384]{1,0:T(8,128)S(1)}, f32[288,384]{1,0:T(8,128)S(1)}, u32[]{:S(2)}, u32[]{:S(2)}) collective-permute-start(f32[288,384]{1,0:T(8,128)S(1)} %get-tuple-element.51), channel_id=1, source_target_pairs={{0,32},{1,225},{2,34},{3,227},{4,36},{5,229},{6,38},{7,231},{8,40}... | collective-permute-start | bytes 1327112 | tf_op jit(solution)/shard_map/ppermute | solution.py:30
  81.6 22.9 %copy-start.5 = (f32[64,384]{1,0:T(8,128)S(1)}, f32[64,384]{1,0:T(8,128)}, u32[]{:S(2)}) copy-start(f32[64,384]{1,0:T(8,128)} %param.14) | copy-start | bytes 294916
  81.7 23.6 %copy-start.6 = (f32[64,16]{0,1:T(8,128)S(1)}, f32[64,16]{0,1:T(8,128)}, u32[]{:S(2)}) copy-start(f32[64,16]{0,1:T(8,128)} %param.13) | copy-start | bytes 12292
  88.8 10.0 %collective-permute-start.23 = (f32[72,384]{1,0:T(8,128)S(1)}, f32[72,384]{1,0:T(8,128)S(1)}, u32[]{:S(2)}, u32[]{:S(2)}) collective-permute-start(f32[72,384]{1,0:T(8,128)S(1)} %get-tuple-element.62), channel_id=1, source_target_pairs={{0,64},{32,96},{64,0},{96,32},{128,192},{160,224},{192,128},{224,1... | collective-permute-start | bytes 331784 | tf_op jit(solution)/shard_map/ppermute | solution.py:17
  88.9 9.9 %collective-permute-start.24 = (f32[72,384]{1,0:T(8,128)S(1)}, f32[72,384]{1,0:T(8,128)S(1)}, u32[]{:S(2)}, u32[]{:S(2)}) collective-permute-start(f32[72,384]{1,0:T(8,128)S(1)} %get-tuple-element.60), channel_id=1, source_target_pairs={{0,128},{32,160},{64,192},{96,224},{128,0},{160,32},{192,64},{224,... | collective-permute-start | bytes 331784 | tf_op jit(solution)/shard_map/ppermute | solution.py:17
  91.5 13.0 %collective-permute-start.25 = (f32[72,384]{1,0:T(8,128)S(1)}, f32[72,384]{1,0:T(8,128)S(1)}, u32[]{:S(2)}, u32[]{:S(2)}) collective-permute-start(f32[72,384]{1,0:T(8,128)S(1)} %get-tuple-element.61), channel_id=1, source_target_pairs={{0,192},{32,224},{64,128},{96,160},{128,64},{160,96},{192,0},{224,... | collective-permute-start | bytes 331784 | tf_op jit(solution)/shard_map/ppermute | solution.py:17
  (1 other events, 0.7 us)

commit v8 on v7

--- a/solution.py
+++ b/solution.py
@@ -15,6 +15,14 @@
 
 def with_row_partner(v, k):
     return lax.ppermute(v, "row", [(i, i ^ k) for i in range(ROWS)])
+
+
+def with_second(v):
+    perm = []
+    for r in range(ROWS):
+        for c in range(COLS):
+            perm.append((r * COLS + c, (r ^ (2 if c % 2 == 0 else 6)) * COLS + c))
+    return lax.ppermute(v, ("row", "col"), perm)
 
 
 def with_sibling(v):
@@ -70,8 +78,10 @@
         even, rest = blocks[2 * other : 2 * other + 2]
         half = core ^ other
         for m in range(4):
-            near = (m ^ (ids[0] // 2)) * 32
-            far = (m ^ (ids[5 + other] // 2)) * 32
+            near = m ^ (ids[0] // 2)
+            near = jnp.where(half == 0, near, (4 - near) % 4) * 32
+            far = m ^ (ids[5 + other] // 2)
+            far = jnp.where(half == 0, far, (4 - far) % 4) * 32
             for k in range(4):
                 for j in range(4):
                     lanes = slice(128 * j, 128 * j + 128)
@@ -209,6 +219,7 @@
     @pl.when(pl.program_id(0) == 0)
     def _():
         for j, distance in enumerate((0, 4, 2, 6)):
+            distance = distance if j < 2 else jnp.where(ids[3] == 0, distance, 8 - distance)
             for first, pieces in ((ids[0], own_parity), (ids[5], other_parity)):
                 piece = pieces[64 * j : 64 * j + 64, :]
                 high, low = split(piece)
@@ -309,22 +320,21 @@
     both = jnp.concatenate([grad_pair, jnp.pad(diag_pair, ((0, 0), (0, 1024 - 128)))], axis=0)
     both = [both] + [with_col_partner(both, 0, k) for k in (1, 2, 3)]
     diag_quad = jnp.concatenate([b[32:, :128] for b in both], axis=1)
-    row_pair = jnp.concatenate([row_factor, with_row_partner(row_factor, 4)], axis=0)
-    row_pair, both = lax.optimization_barrier((row_pair, both))
-    row_even = jnp.concatenate([row_pair, with_row_partner(row_pair, 2)], axis=0)
     diag_quad = jnp.concatenate([diag_quad, with_col_partner(diag_quad, 1, 1)], axis=0)
     diag_quad = jnp.concatenate([diag_quad, with_col_partner(diag_quad, 1, 2)], axis=0)
-    diag_quad, both = lax.optimization_barrier((diag_quad, both))
+    row_pair = jnp.concatenate([row_factor, with_row_partner(row_factor, 4)], axis=0)
+    diag_quad, both, row_pair = lax.optimization_barrier((diag_quad, both, row_pair))
     grad_quad = jnp.concatenate([b[:32] for b in both], axis=0)
     grad_far = [with_col_partner(grad_quad, 1, k) for k in (1, 2, 3)]
-    diag_even = jnp.concatenate([diag_quad, with_row_partner(diag_quad, 2)], axis=0)
-    row_even, diag_even = lax.optimization_barrier((row_even, diag_even))
+    diag_even = jnp.concatenate([diag_quad, with_second(diag_quad)], axis=0)
     diag_even = jnp.concatenate([diag_even, with_row_partner(diag_even, 4)], axis=0)
-    diag_even, grad_far[0], grad_far[2] = lax.optimization_barrier((diag_even, grad_far[0], grad_far[2]))
+    diag_even, row_pair, grad_far[0], grad_far[2] = lax.optimization_barrier(
+        (diag_even, row_pair, grad_far[0], grad_far[2])
+    )
     diag_odd = with_neighbour(diag_even)
-    row_even, diag_odd = lax.optimization_barrier((row_even, diag_odd))
+    diag_blocks = [diag_even, diag_odd, with_sibling(diag_even), with_sibling(diag_odd)]
+    row_even = jnp.concatenate([row_pair, with_second(row_pair)], axis=0)
     row_odd = with_neighbour(row_even)
-    diag_blocks = [diag_even, diag_odd, with_sibling(diag_even), with_sibling(diag_odd)]
     quad_swapped = with_sibling(grad_quad)
 
     inverse = prepare(ids, diag_blocks)

time: 106 us -> 103 us (0.972)
  starting transfers between devices: 45.3 us -> 49.4 us
  waiting for transfers between devices: 32.2 us -> 28.4 us
  local copies, waits for them, and re-layouts: 1.95 us -> 0.34 us
  Pallas kernels: 21.5 us -> 20.1 us
    ppermute x0 -> x2, starting transfers between devices: none -> 8.26 us  [with_second(): return lax.ppermute(v, ('row', 'col'), perm)]
    ppermute x7 -> x5, starting transfers between devices: 21.3 us -> 15.2 us  [with_row_partner(): return lax.ppermute(v, 'row', [(i, i ^ k) for i in range(ROWS)])]
    ppermute x7 -> x5, waiting for transfers between devices: 21.2 us -> 15.3 us  [with_row_partner(): return lax.ppermute(v, 'row', [(i, i ^ k) for i in range(ROWS)])]
    ppermute x0 -> x2, waiting for transfers between devices: none -> 5.71 us  [with_second(): return lax.ppermute(v, ('row', 'col'), perm)]
    ppermute x3, waiting for transfers between devices: 4.98 us -> 0.47 us  [with_neighbour(): return lax.ppermute(v, ('row', 'col'), perm)]
    ppermute x8, starting transfers between devices: 13.6 us -> 10.4 us  [with_col_partner(): return lax.ppermute(v, 'col', perm)]
    ppermute x3, starting transfers between devices: 4.01 us -> 6.96 us  [with_neighbour(): return lax.ppermute(v, ('row', 'col'), perm)]
    ppermute x8, starting transfers between devices: 6.32 us -> 8.46 us  [with_sibling(): return lax.ppermute(v, 'col', [(i, i ^ 1) for i in range(COLS)])]
  transfers between devices with their start and end apart: 26 -> 26, of which waited for: 10 -> 11; matrix products, arithmetic and copies ran while one was open for 2% -> 2% of each run, Pallas kernels for 20% -> 19%
where the time goes in v8:
time: 103 us
  starting transfers between devices  49.4 us (48%)
  waiting for transfers between devices  28.4 us (28%)
  Pallas kernels  20.1 us (20%)
  other arithmetic  4.07 us (4%)
    ppermute x5, waiting for transfers between devices, with_row_partner(): return lax.ppermute(v, 'row', [(i, i ^ k) for i in range(ROWS)])  15.3 us
    ppermute x5, starting transfers between devices, with_row_partner(): return lax.ppermute(v, 'row', [(i, i ^ k) for i in range(ROWS)])  15.2 us
    ppermute x8, starting transfers between devices, with_col_partner(): return lax.ppermute(v, 'col', perm)  10.4 us
    ppermute x8, starting transfers between devices, with_sibling(): return lax.ppermute(v, 'col', [(i, i ^ 1) for i in range(COLS)])  8.46 us
    ppermute x2, starting transfers between devices, with_second(): return lax.ppermute(v, ('row', 'col'), perm)  8.26 us
    pallas_call x1, Pallas kernels, solve(): pl.pallas_call(solve_kernel, out_shape=[shape((B, 2048)), shape((16, 2048...  8.18 us
    pallas_call x1, Pallas kernels, trailing_update(): pl.pallas_call(trailing_kernel, grid=(2048 // tile,), out_shape=shape((20...  7.02 us
    ppermute x3, starting transfers between devices, with_neighbour(): return lax.ppermute(v, ('row', 'col'), perm)  6.96 us
  transfers between devices with their start and end apart: 26, of which 11 were waited for; matrix products, arithmetic and copies ran while one was open for 2% of the time, Pallas kernels for 19%

profile of v8, /device:TPU:1, one launch (start us, length us, event | category | flops | bytes accessed | tf_op | source)
XLA Modules:
  0.0 103.2 jit_solution(1383525872707631773)
XLA Ops:
  0.6 0.7 slice_select_fusion.2
  1.4 3.2 %collective-permute-start = (f32[8,64]{1,0:T(8,128)S(1)}, f32[8,64]{1,0:T(8,128)S(1)}, u32[]{:S(2)}, u32[]{:S(2)}) collective-permute-start(f32[8,64]{1,0:T(8,128)S(1)} %get-tuple-element.53), channel_id=1, source_target_pairs={{0,1},{1,0},{2,3},{3,2},{4,5},{5,4},{6,7},{7,6},{8,9},{9,8},{10,11... | collective-permute-start | bytes 6152 | tf_op jit(solution)/shard_map/ppermute | solution.py:29
  4.6 0.9 slice_select_fusion.1
  5.7 1.2 %collective-permute-done.1 = f32[16,1024]{1,0:T(8,128)S(1)} collective-permute-done((f32[16,1024]{1,0:T(8,128)S(1)}, f32[16,1024]{1,0:T(8,128)S(1)}, u32[]{:S(2)}, u32[]{:S(2)}) %collective-permute-start.1) | collective-permute-done | bytes 65568 | tf_op jit(solution)/shard_map/ppermute | solution.py:29
  6.9 2.2 %collective-permute-start.3 = (f32[40,1024]{1,0:T(8,128)S(1)}, f32[40,1024]{1,0:T(8,128)S(1)}, u32[]{:S(2)}, u32[]{:S(2)}) collective-permute-start(f32[40,1024]{1,0:T(8,128)S(1)} %pad_maximum_fusion.3), channel_id=1, source_target_pairs={{0,4},{1,17},{2,6},{3,19},{4,0},{5,21},{6,2},{7,23},{8,12},{9,25},... | collective-permute-start | bytes 491528 | tf_op jit(solution)/shard_map/ppermute | solution.py:44
  9.1 1.7 %collective-permute-start.4 = (f32[40,1024]{1,0:T(8,128)S(1)}, f32[40,1024]{1,0:T(8,128)S(1)}, u32[]{:S(2)}, u32[]{:S(2)}) collective-permute-start(f32[40,1024]{1,0:T(8,128)S(1)} %pad_maximum_fusion.3), channel_id=1, source_target_pairs={{0,6},{1,25},{2,4},{3,27},{4,2},{5,29},{6,0},{7,31},{8,14},{9,17},... | collective-permute-start | bytes 491528 | tf_op jit(solution)/shard_map/ppermute | solution.py:44
  11.4 2.5 %collective-permute-done.3 = f32[40,1024]{1,0:T(8,128)S(1)} collective-permute-done((f32[40,1024]{1,0:T(8,128)S(1)}, f32[40,1024]{1,0:T(8,128)S(1)}, u32[]{:S(2)}, u32[]{:S(2)}) %collective-permute-start.3) | collective-permute-done | bytes 163872 | tf_op jit(solution)/shard_map/ppermute | solution.py:44
  13.9 1.8 %collective-permute-done.4 = f32[40,1024]{1,0:T(8,128)S(1)} collective-permute-done((f32[40,1024]{1,0:T(8,128)S(1)}, f32[40,1024]{1,0:T(8,128)S(1)}, u32[]{:S(2)}, u32[]{:S(2)}) %collective-permute-start.4) | collective-permute-done | bytes 163872 | tf_op jit(solution)/shard_map/ppermute | solution.py:44
  15.7 0.9 collective-permute-start.5
  16.6 6.9 %collective-permute-start.7 = (f32[64,384]{1,0:T(8,128)}, f32[64,384]{1,0:T(8,128)S(1)}, u32[]{:S(2)}, u32[]{:S(2)}) collective-permute-start(f32[64,384]{1,0:T(8,128)} %param.10), channel_id=1, source_target_pairs={{0,128},{32,160},{64,192},{96,224},{128,0},{160,32},{192,64},{224,... | collective-permute-start | bytes 294920 | tf_op jit(solution)/shard_map/ppermute | solution.py:17
  23.5 2.5 %collective-permute-start.6 = (f32[16,512]{1,0:T(8,128)S(1)}, f32[16,512]{1,0:T(8,128)S(1)}, u32[]{:S(2)}, u32[]{:S(2)}) collective-permute-start(f32[16,512]{1,0:T(8,128)S(1)} %pad_maximum_fusion.6), channel_id=1, source_target_pairs={{0,16},{1,5},{2,18},{3,7},{4,20},{5,1},{6,22},{7,3},{8,24},{9,13},... | collective-permute-start | bytes 98312 | tf_op jit(solution)/shard_map/ppermute | solution.py:44
  26.0 0.9 pad_maximum_fusion.2
  26.9 0.9 collective-permute-done.6
  28.6 2.5 %collective-permute-start.11 = (f32[128,1024]{1,0:T(8,128)S(1)}, f32[128,1024]{1,0:T(8,128)S(1)}, u32[]{:S(2)}, u32[]{:S(2)}) collective-permute-start(f32[128,1024]{1,0:T(8,128)S(1)} %pad_maximum_fusion.refs_0_), channel_id=1, source_target_pairs={{0,24},{1,7},{2,26},{3,5},{4,28},{5,3},{6,30},{7,1},{8,16},{9,15},... | collective-permute-start | bytes 1572872 | tf_op jit(solution)/shard_map/ppermute | solution.py:44
  31.1 6.1 %collective-permute-start.8 = (f32[32,512]{1,0:T(8,128)S(1)}, f32[32,512]{1,0:T(8,128)S(1)}, u32[]{:S(2)}, u32[]{:S(2)}) collective-permute-start(f32[32,512]{1,0:T(8,128)S(1)} %pad_maximum_fusion.5), channel_id=1, source_target_pairs={{0,64},{1,193},{2,66},{3,195},{4,68},{5,197},{6,70},{7,199},{8,72}... | collective-permute-start | bytes 196616 | tf_op jit(solution)/shard_map/ppermute | solution.py:25
  37.2 1.7 %collective-permute-done.8 = f32[32,512]{1,0:T(8,128)S(1)} collective-permute-done((f32[32,512]{1,0:T(8,128)S(1)}, f32[32,512]{1,0:T(8,128)S(1)}, u32[]{:S(2)}, u32[]{:S(2)}) %collective-permute-start.8) | collective-permute-done | bytes 65568 | tf_op jit(solution)/shard_map/ppermute | solution.py:25
  38.9 2.6 %collective-permute-start.9 = (f32[64,512]{1,0:T(8,128)S(1)}, f32[64,512]{1,0:T(8,128)S(1)}, u32[]{:S(2)}, u32[]{:S(2)}) collective-permute-start(f32[64,512]{1,0:T(8,128)S(1)} %pad_maximum_fusion.4), channel_id=1, source_target_pairs={{0,128},{32,160},{64,192},{96,224},{128,0},{160,32},{192,64},{224,... | collective-permute-start | bytes 393224 | tf_op jit(solution)/shard_map/ppermute | solution.py:17
  41.5 5.7 %collective-permute-done.9 = f32[64,512]{1,0:T(8,128)S(1)} collective-permute-done((f32[64,512]{1,0:T(8,128)S(1)}, f32[64,512]{1,0:T(8,128)S(1)}, u32[]{:S(2)}, u32[]{:S(2)}) %collective-permute-start.9) | collective-permute-done | bytes 131104 | tf_op jit(solution)/shard_map/ppermute | solution.py:17
  47.2 4.0 %collective-permute-start.17 = (f32[128,512]{1,0:T(8,128)S(1)}, f32[128,512]{1,0:T(8,128)S(1)}, u32[]{:S(2)}, u32[]{:S(2)}) collective-permute-start(f32[128,512]{1,0:T(8,128)S(1)} %pad_maximum_fusion.1.refs_0_), channel_id=1, source_target_pairs={{0,32},{1,225},{2,34},{3,227},{4,36},{5,229},{6,38},{7,231},{8,40}... | collective-permute-start | bytes 786440 | tf_op jit(solution)/shard_map/ppermute | solution.py:38
  51.2 1.2 %collective-permute-start.18 = (f32[128,512]{1,0:T(8,128)S(1)}, f32[128,512]{1,0:T(8,128)S(1)}, u32[]{:S(2)}, u32[]{:S(2)}) collective-permute-start(f32[128,512]{1,0:T(8,128)S(1)} %pad_maximum_fusion.1.refs_0_), channel_id=1, source_target_pairs={{0,1},{1,0},{2,3},{3,2},{4,5},{5,4},{6,7},{7,6},{8,9},{9,8},{10,11... | collective-permute-start | bytes 786440 | tf_op jit(solution)/shard_map/ppermute | solution.py:29
  52.4 2.1 %collective-permute-start.21 = (f32[128,384]{1,0:T(8,128)S(1)}, f32[128,384]{1,0:T(8,128)S(1)}, u32[]{:S(2)}, u32[]{:S(2)}) collective-permute-start(f32[128,384]{1,0:T(8,128)S(1)} %pad_maximum_fusion.2), channel_id=1, source_target_pairs={{0,64},{1,193},{2,66},{3,195},{4,68},{5,197},{6,70},{7,199},{8,72}... | collective-permute-start | bytes 589832 | tf_op jit(solution)/shard_map/ppermute | solution.py:25
  55.0 2.9 %collective-permute-start.19 = (f32[128,512]{1,0:T(8,128)S(1)}, f32[128,512]{1,0:T(8,128)S(1)}, u32[]{:S(2)}, u32[]{:S(2)}) collective-permute-start(f32[128,512]{1,0:T(8,128)S(1)} %collective-permute-done.17.refs_1_), channel_id=1, source_target_pairs={{0,1},{1,0},{2,3},{3,2},{4,5},{5,4},{6,7},{7,6},{8,9},{9,8},{10,11... | collective-permute-start | bytes 786440 | tf_op jit(solution)/shard_map/ppermute | solution.py:29
  58.5 4.1 %collective-permute-done.21 = f32[128,384]{1,0:T(8,128)S(1)} collective-permute-done((f32[128,384]{1,0:T(8,128)S(1)}, f32[128,384]{1,0:T(8,128)S(1)}, u32[]{:S(2)}, u32[]{:S(2)}) %collective-permute-start.21) | collective-permute-done | bytes 196640 | tf_op jit(solution)/shard_map/ppermute | solution.py:25
  63.1 1.1 %collective-permute-start.22 = (f32[256,384]{1,0:T(8,128)S(1)}, f32[256,384]{1,0:T(8,128)S(1)}, u32[]{:S(2)}, u32[]{:S(2)}) collective-permute-start(f32[256,384]{1,0:T(8,128)S(1)} %constant_dynamic-update-slice_fusion.refs_0_), channel_id=1, source_target_pairs={{0,32},{1,225},{2,34},{3,227},{4,36},{5,229},{6,38},{7,231},{8,40}... | collective-permute-start | bytes 1179656 | tf_op jit(solution)/shard_map/ppermute | solution.py:38
  64.3 4.9 %prepare.1 = (bf16[256,1536]{1,0:T(8,128)(2,1)S(1)}, bf16[256,768]{1,0:T(8,128)(2,1)S(1)}) custom-call(s32[7]{0:T(128)S(1)} %stack.31.ids, f32[128,512]{1,0:T(8,128)S(1)} %pad_maximum_fusion.1.refs_0_, f32[128,512]{1,0:T(8,128)S(1)} %collective-permute-done.17.refs_1_, f32[128,512]{1,0:T(8,128)S(1)} %collective-permute-done.18.refs_2_, ...), custom_call_target="tpu_custom_call" | custom-call | flops 4000000000 | bytes 2097152 | tf_op jit(solution)/shard_map/prepare/pallas_call | solution.py:246
  69.2 8.2 %solve.1 = (f32[512,2048]{1,0:T(8,128)S(1)}, f32[16,2048]{1,0:T(8,128)}, f32[288,384]{1,0:T(8,128)S(1)}, f32[72,384]{1,0:T(8,128)S(1)}, f32[72,384]{1,0:T(8,128)...) custom-call(s32[7]{0:T(128)S(1)} %stack.31.ids, f32[128,1024]{1,0:T(8,128)S(1)} %pad_maximum_fusion.refs_0_, ...), custom_call_target="tpu_custom_call" | custom-call | flops 6000000000 | bytes 12582912 | tf_op jit(solution)/shard_map/solve/pallas_call | solution.py:259
  77.4 1.8 %collective-permute-start.20 = (f32[288,384]{1,0:T(8,128)S(1)}, f32[288,384]{1,0:T(8,128)S(1)}, u32[]{:S(2)}, u32[]{:S(2)}) collective-permute-start(f32[288,384]{1,0:T(8,128)S(1)} %get-tuple-element.37), channel_id=1, source_target_pairs={{0,32},{1,225},{2,34},{3,227},{4,36},{5,229},{6,38},{7,231},{8,40}... | collective-permute-start | bytes 1327112 | tf_op jit(solution)/shard_map/ppermute | solution.py:38
  79.3 7.0 %trailing.1 = f32[2048,384]{1,0:T(8,128)} custom-call(s32[7]{0:T(128)S(1)} %stack.31.ids, f32[256,384]{1,0:T(8,128)S(1)} %constant_dynamic-update-slice_fusion.refs_0_, f32[256,384]{1,0:T(8,128)S(1)} %collective-permute-done.22.refs_1_, f32[512,2048]{1,0:T(8,128)S(1)} %get-tuple-element.39.refs_2_, f32[2048,384]{1,0:T(8,128)S(1)} %copy-done.1), custom_call_target="tpu_custom_call" | custom-call | flops 4000000000 | bytes 11534336 | tf_op jit(solution)/shard_map/trailing/pallas_call | solution.py:279
  86.4 4.3 %collective-permute-start.24 = (f32[72,384]{1,0:T(8,128)S(1)}, f32[72,384]{1,0:T(8,128)S(1)}, u32[]{:S(2)}, u32[]{:S(2)}) collective-permute-start(f32[72,384]{1,0:T(8,128)S(1)} %get-tuple-element.46), channel_id=1, source_target_pairs={{0,128},{32,160},{64,192},{96,224},{128,0},{160,32},{192,64},{224,... | collective-permute-start | bytes 331784 | tf_op jit(solution)/shard_map/ppermute | solution.py:17
  90.7 1.4 %collective-permute-start.25 = (f32[72,384]{1,0:T(8,128)S(1)}, f32[72,384]{1,0:T(8,128)S(1)}, u32[]{:S(2)}, u32[]{:S(2)}) collective-permute-start(f32[72,384]{1,0:T(8,128)S(1)} %get-tuple-element.47), channel_id=1, source_target_pairs={{0,192},{32,224},{64,128},{96,160},{128,64},{160,96},{192,0},{224,... | collective-permute-start | bytes 331784 | tf_op jit(solution)/shard_map/ppermute | solution.py:17
  92.1 5.0 %collective-permute-done.23 = f32[72,384]{1,0:T(8,128)S(1)} collective-permute-done((f32[72,384]{1,0:T(8,128)S(1)}, f32[72,384]{1,0:T(8,128)S(1)}, u32[]{:S(2)}, u32[]{:S(2)}) %collective-permute-start.23) | collective-permute-done | bytes 110624 | tf_op jit(solution)/shard_map/ppermute | solution.py:17
  97.0 4.7 %collective-permute-done.25 = f32[72,384]{1,0:T(8,128)S(1)} collective-permute-done((f32[72,384]{1,0:T(8,128)S(1)}, f32[72,384]{1,0:T(8,128)S(1)}, u32[]{:S(2)}, u32[]{:S(2)}) %collective-permute-start.25) | collective-permute-done | bytes 110624 | tf_op jit(solution)/shard_map/ppermute | solution.py:17
  (61 shorter events, 5.0 us)
Async XLA Ops:
  1.4 4.2 %collective-permute-start = (f32[8,64]{1,0:T(8,128)S(1)}, f32[8,64]{1,0:T(8,128)S(1)}, u32[]{:S(2)}, u32[]{:S(2)}) collective-permute-start(f32[8,64]{1,0:T(8,128)S(1)} %get-tuple-element.53), channel_id=1, source_target_pairs={{0,1},{1,0},{2,3},{3,2},{4,5},{5,4},{6,7},{7,6},{8,9},{9,8},{10,11... | collective-permute-start | bytes 6152 | tf_op jit(solution)/shard_map/ppermute | solution.py:29
  5.5 1.3 %collective-permute-start.1 = (f32[16,1024]{1,0:T(8,128)S(1)}, f32[16,1024]{1,0:T(8,128)S(1)}, u32[]{:S(2)}, u32[]{:S(2)}) collective-permute-start(f32[16,1024]{1,0:T(8,128)S(1)} %get-tuple-element.50), channel_id=1, source_target_pairs={{0,1},{1,0},{2,3},{3,2},{4,5},{5,4},{6,7},{7,6},{8,9},{9,8},{10,11... | collective-permute-start | bytes 196616 | tf_op jit(solution)/shard_map/ppermute | solution.py:29
  6.8 4.6 %collective-permute-start.2 = (f32[40,1024]{1,0:T(8,128)S(1)}, f32[40,1024]{1,0:T(8,128)S(1)}, u32[]{:S(2)}, u32[]{:S(2)}) collective-permute-start(f32[40,1024]{1,0:T(8,128)S(1)} %pad_maximum_fusion.3), channel_id=1, source_target_pairs={{0,2},{1,9},{2,0},{3,11},{4,6},{5,13},{6,4},{7,15},{8,10},{9,1},{1... | collective-permute-start | bytes 491528 | tf_op jit(solution)/shard_map/ppermute | solution.py:44
  6.9 6.9 %collective-permute-start.3 = (f32[40,1024]{1,0:T(8,128)S(1)}, f32[40,1024]{1,0:T(8,128)S(1)}, u32[]{:S(2)}, u32[]{:S(2)}) collective-permute-start(f32[40,1024]{1,0:T(8,128)S(1)} %pad_maximum_fusion.3), channel_id=1, source_target_pairs={{0,4},{1,17},{2,6},{3,19},{4,0},{5,21},{6,2},{7,23},{8,12},{9,25},... | collective-permute-start | bytes 491528 | tf_op jit(solution)/shard_map/ppermute | solution.py:44
  9.1 6.5 %collective-permute-start.4 = (f32[40,1024]{1,0:T(8,128)S(1)}, f32[40,1024]{1,0:T(8,128)S(1)}, u32[]{:S(2)}, u32[]{:S(2)}) collective-permute-start(f32[40,1024]{1,0:T(8,128)S(1)} %pad_maximum_fusion.3), channel_id=1, source_target_pairs={{0,6},{1,25},{2,4},{3,27},{4,2},{5,29},{6,0},{7,31},{8,14},{9,17},... | collective-permute-start | bytes 491528 | tf_op jit(solution)/shard_map/ppermute | solution.py:44
  15.7 7.8 %collective-permute-start.5 = (f32[8,512]{1,0:T(8,128)S(1)}, f32[8,512]{1,0:T(8,128)S(1)}, u32[]{:S(2)}, u32[]{:S(2)}) collective-permute-start(f32[8,512]{1,0:T(8,128)S(1)} %concatenate.38), channel_id=1, source_target_pairs={{0,8},{1,3},{2,10},{3,1},{4,12},{5,7},{6,14},{7,5},{8,0},{9,11},{1... | collective-permute-start | bytes 49160 | tf_op jit(solution)/shard_map/ppermute | solution.py:44
  16.6 9.4 %collective-permute-start.7 = (f32[64,384]{1,0:T(8,128)}, f32[64,384]{1,0:T(8,128)S(1)}, u32[]{:S(2)}, u32[]{:S(2)}) collective-permute-start(f32[64,384]{1,0:T(8,128)} %param.10), channel_id=1, source_target_pairs={{0,128},{32,160},{64,192},{96,224},{128,0},{160,32},{192,64},{224,... | collective-permute-start | bytes 294920 | tf_op jit(solution)/shard_map/ppermute | solution.py:17
  23.5 4.3 %collective-permute-start.6 = (f32[16,512]{1,0:T(8,128)S(1)}, f32[16,512]{1,0:T(8,128)S(1)}, u32[]{:S(2)}, u32[]{:S(2)}) collective-permute-start(f32[16,512]{1,0:T(8,128)S(1)} %pad_maximum_fusion.6), channel_id=1, source_target_pairs={{0,16},{1,5},{2,18},{3,7},{4,20},{5,1},{6,22},{7,3},{8,24},{9,13},... | collective-permute-start | bytes 98312 | tf_op jit(solution)/shard_map/ppermute | solution.py:44
  27.9 19.2 %collective-permute-start.10 = (f32[128,1024]{1,0:T(8,128)S(1)}, f32[128,1024]{1,0:T(8,128)S(1)}, u32[]{:S(2)}, u32[]{:S(2)}) collective-permute-start(f32[128,1024]{1,0:T(8,128)S(1)} %pad_maximum_fusion.refs_0_), channel_id=1, source_target_pairs={{0,8},{1,3},{2,10},{3,1},{4,12},{5,7},{6,14},{7,5},{8,0},{9,11},{1... | collective-permute-start | bytes 1572872 | tf_op jit(solution)/shard_map/ppermute | solution.py:44
  28.6 18.6 %collective-permute-start.11 = (f32[128,1024]{1,0:T(8,128)S(1)}, f32[128,1024]{1,0:T(8,128)S(1)}, u32[]{:S(2)}, u32[]{:S(2)}) collective-permute-start(f32[128,1024]{1,0:T(8,128)S(1)} %pad_maximum_fusion.refs_0_), channel_id=1, source_target_pairs={{0,24},{1,7},{2,26},{3,5},{4,28},{5,3},{6,30},{7,1},{8,16},{9,15},... | collective-permute-start | bytes 1572872 | tf_op jit(solution)/shard_map/ppermute | solution.py:44
  31.1 7.8 %collective-permute-start.8 = (f32[32,512]{1,0:T(8,128)S(1)}, f32[32,512]{1,0:T(8,128)S(1)}, u32[]{:S(2)}, u32[]{:S(2)}) collective-permute-start(f32[32,512]{1,0:T(8,128)S(1)} %pad_maximum_fusion.5), channel_id=1, source_target_pairs={{0,64},{1,193},{2,66},{3,195},{4,68},{5,197},{6,70},{7,199},{8,72}... | collective-permute-start | bytes 196616 | tf_op jit(solution)/shard_map/ppermute | solution.py:25
  38.9 8.3 %collective-permute-start.9 = (f32[64,512]{1,0:T(8,128)S(1)}, f32[64,512]{1,0:T(8,128)S(1)}, u32[]{:S(2)}, u32[]{:S(2)}) collective-permute-start(f32[64,512]{1,0:T(8,128)S(1)} %pad_maximum_fusion.4), channel_id=1, source_target_pairs={{0,128},{32,160},{64,192},{96,224},{128,0},{160,32},{192,64},{224,... | collective-permute-start | bytes 393224 | tf_op jit(solution)/shard_map/ppermute | solution.py:17
  41.5 16.5 %collective-permute-start.12 = (f32[128,1024]{1,0:T(8,128)S(1)}, f32[128,1024]{1,0:T(8,128)S(1)}, u32[]{:S(2)}, u32[]{:S(2)}) collective-permute-start(f32[128,1024]{1,0:T(8,128)S(1)} %pad_maximum_fusion.refs_0_), channel_id=1, source_target_pairs={{0,16},{1,5},{2,18},{3,7},{4,20},{5,1},{6,22},{7,3},{8,24},{9,13},... | collective-permute-start | bytes 1572872 | tf_op jit(solution)/shard_map/ppermute | solution.py:44
  47.2 7.8 %collective-permute-start.17 = (f32[128,512]{1,0:T(8,128)S(1)}, f32[128,512]{1,0:T(8,128)S(1)}, u32[]{:S(2)}, u32[]{:S(2)}) collective-permute-start(f32[128,512]{1,0:T(8,128)S(1)} %pad_maximum_fusion.1.refs_0_), channel_id=1, source_target_pairs={{0,32},{1,225},{2,34},{3,227},{4,36},{5,229},{6,38},{7,231},{8,40}... | collective-permute-start | bytes 786440 | tf_op jit(solution)/shard_map/ppermute | solution.py:38
  51.2 11.4 %collective-permute-start.18 = (f32[128,512]{1,0:T(8,128)S(1)}, f32[128,512]{1,0:T(8,128)S(1)}, u32[]{:S(2)}, u32[]{:S(2)}) collective-permute-start(f32[128,512]{1,0:T(8,128)S(1)} %pad_maximum_fusion.1.refs_0_), channel_id=1, source_target_pairs={{0,1},{1,0},{2,3},{3,2},{4,5},{5,4},{6,7},{7,6},{8,9},{9,8},{10,11... | collective-permute-start | bytes 786440 | tf_op jit(solution)/shard_map/ppermute | solution.py:29
  52.4 10.2 %collective-permute-start.21 = (f32[128,384]{1,0:T(8,128)S(1)}, f32[128,384]{1,0:T(8,128)S(1)}, u32[]{:S(2)}, u32[]{:S(2)}) collective-permute-start(f32[128,384]{1,0:T(8,128)S(1)} %pad_maximum_fusion.2), channel_id=1, source_target_pairs={{0,64},{1,193},{2,66},{3,195},{4,68},{5,197},{6,70},{7,199},{8,72}... | collective-permute-start | bytes 589832 | tf_op jit(solution)/shard_map/ppermute | solution.py:25
  55.0 8.2 %collective-permute-start.19 = (f32[128,512]{1,0:T(8,128)S(1)}, f32[128,512]{1,0:T(8,128)S(1)}, u32[]{:S(2)}, u32[]{:S(2)}) collective-permute-start(f32[128,512]{1,0:T(8,128)S(1)} %collective-permute-done.17.refs_1_), channel_id=1, source_target_pairs={{0,1},{1,0},{2,3},{3,2},{4,5},{5,4},{6,7},{7,6},{8,9},{9,8},{10,11... | collective-permute-start | bytes 786440 | tf_op jit(solution)/shard_map/ppermute | solution.py:29
  58.0 11.2 %collective-permute-start.13 = (f32[128,1024]{1,0:T(8,128)S(1)}, f32[128,1024]{1,0:T(8,128)S(1)}, u32[]{:S(2)}, u32[]{:S(2)}) collective-permute-start(f32[128,1024]{1,0:T(8,128)S(1)} %pad_maximum_fusion.refs_0_), channel_id=1, source_target_pairs={{0,1},{1,0},{2,3},{3,2},{4,5},{5,4},{6,7},{7,6},{8,9},{9,8},{10,11... | collective-permute-start | bytes 1572872 | tf_op jit(solution)/shard_map/ppermute | solution.py:29
  58.0 11.2 %collective-permute-start.14 = (f32[128,1024]{1,0:T(8,128)S(1)}, f32[128,1024]{1,0:T(8,128)S(1)}, u32[]{:S(2)}, u32[]{:S(2)}) collective-permute-start(f32[128,1024]{1,0:T(8,128)S(1)} %collective-permute-done.10.refs_1_), channel_id=1, source_target_pairs={{0,1},{1,0},{2,3},{3,2},{4,5},{5,4},{6,7},{7,6},{8,9},{9,8},{10,11... | collective-permute-start | bytes 1572872 | tf_op jit(solution)/shard_map/ppermute | solution.py:29
  62.6 6.6 %collective-permute-start.16 = (f32[128,1024]{1,0:T(8,128)S(1)}, f32[128,1024]{1,0:T(8,128)S(1)}, u32[]{:S(2)}, u32[]{:S(2)}) collective-permute-start(f32[128,1024]{1,0:T(8,128)S(1)} %collective-permute-done.11.refs_3_), channel_id=1, source_target_pairs={{0,1},{1,0},{2,3},{3,2},{4,5},{5,4},{6,7},{7,6},{8,9},{9,8},{10,11... | collective-permute-start | bytes 1572872 | tf_op jit(solution)/shard_map/ppermute | solution.py:29
  62.6 6.6 %collective-permute-start.15 = (f32[128,1024]{1,0:T(8,128)S(1)}, f32[128,1024]{1,0:T(8,128)S(1)}, u32[]{:S(2)}, u32[]{:S(2)}) collective-permute-start(f32[128,1024]{1,0:T(8,128)S(1)} %collective-permute-done.12.refs_2_), channel_id=1, source_target_pairs={{0,1},{1,0},{2,3},{3,2},{4,5},{5,4},{6,7},{7,6},{8,9},{9,8},{10,11... | collective-permute-start | bytes 1572872 | tf_op jit(solution)/shard_map/ppermute | solution.py:29
  63.1 6.1 %copy-start = (f32[2048,384]{1,0:T(8,128)S(1)}, f32[2048,384]{1,0:T(8,128)}, u32[]{:S(2)}) copy-start(f32[2048,384]{1,0:T(8,128)} %refs_10_.1) | copy-start | bytes 9437188
  63.1 6.1 %copy-start.2 = (f32[2048,16]{0,1:T(8,128)S(1)}, f32[2048,16]{0,1:T(8,128)}, u32[]{:S(2)}) copy-start(f32[2048,16]{0,1:T(8,128)} %param.9) | copy-start | bytes 393220
  63.1 16.1 %collective-permute-start.22 = (f32[256,384]{1,0:T(8,128)S(1)}, f32[256,384]{1,0:T(8,128)S(1)}, u32[]{:S(2)}, u32[]{:S(2)}) collective-permute-start(f32[256,384]{1,0:T(8,128)S(1)} %constant_dynamic-update-slice_fusion.refs_0_), channel_id=1, source_target_pairs={{0,32},{1,225},{2,34},{3,227},{4,36},{5,229},{6,38},{7,231},{8,40}... | collective-permute-start | bytes 1179656 | tf_op jit(solution)/shard_map/ppermute | solution.py:38
  69.2 10.0 %copy-start.1 = (f32[2048,384]{1,0:T(8,128)S(1)}, f32[2048,384]{1,0:T(8,128)}, u32[]{:S(2)}) copy-start(f32[2048,384]{1,0:T(8,128)} %refs_3_.1) | copy-start | bytes 9437188
  77.4 8.9 %collective-permute-start.20 = (f32[288,384]{1,0:T(8,128)S(1)}, f32[288,384]{1,0:T(8,128)S(1)}, u32[]{:S(2)}, u32[]{:S(2)}) collective-permute-start(f32[288,384]{1,0:T(8,128)S(1)} %get-tuple-element.37), channel_id=1, source_target_pairs={{0,32},{1,225},{2,34},{3,227},{4,36},{5,229},{6,38},{7,231},{8,40}... | collective-permute-start | bytes 1327112 | tf_op jit(solution)/shard_map/ppermute | solution.py:38
  79.2 22.6 %copy-start.3 = (f32[64,384]{1,0:T(8,128)S(1)}, f32[64,384]{1,0:T(8,128)}, u32[]{:S(2)}) copy-start(f32[64,384]{1,0:T(8,128)} %param.14) | copy-start | bytes 294916
  79.2 23.3 %copy-start.4 = (f32[64,16]{0,1:T(8,128)S(1)}, f32[64,16]{0,1:T(8,128)}, u32[]{:S(2)}) copy-start(f32[64,16]{0,1:T(8,128)} %param.13) | copy-start | bytes 12292
  86.3 10.7 %collective-permute-start.23 = (f32[72,384]{1,0:T(8,128)S(1)}, f32[72,384]{1,0:T(8,128)S(1)}, u32[]{:S(2)}, u32[]{:S(2)}) collective-permute-start(f32[72,384]{1,0:T(8,128)S(1)} %get-tuple-element.48), channel_id=1, source_target_pairs={{0,64},{32,96},{64,0},{96,32},{128,192},{160,224},{192,128},{224,1... | collective-permute-start | bytes 331784 | tf_op jit(solution)/shard_map/ppermute | solution.py:17
  86.4 10.6 %collective-permute-start.24 = (f32[72,384]{1,0:T(8,128)S(1)}, f32[72,384]{1,0:T(8,128)S(1)}, u32[]{:S(2)}, u32[]{:S(2)}) collective-permute-start(f32[72,384]{1,0:T(8,128)S(1)} %get-tuple-element.46), channel_id=1, source_target_pairs={{0,128},{32,160},{64,192},{96,224},{128,0},{160,32},{192,64},{224,... | collective-permute-start | bytes 331784 | tf_op jit(solution)/shard_map/ppermute | solution.py:17
  90.7 11.1 %collective-permute-start.25 = (f32[72,384]{1,0:T(8,128)S(1)}, f32[72,384]{1,0:T(8,128)S(1)}, u32[]{:S(2)}, u32[]{:S(2)}) collective-permute-start(f32[72,384]{1,0:T(8,128)S(1)} %get-tuple-element.47), channel_id=1, source_target_pairs={{0,192},{32,224},{64,128},{96,160},{128,64},{160,96},{192,0},{224,... | collective-permute-start | bytes 331784 | tf_op jit(solution)/shard_map/ppermute | solution.py:17

commit v9 on v8

--- a/solution.py
+++ b/solution.py
@@ -79,9 +79,11 @@
         half = core ^ other
         for m in range(4):
             near = m ^ (ids[0] // 2)
-            near = jnp.where(half == 0, near, (4 - near) % 4) * 32
+            near = jnp.where(half == 0, near, (4 - near) % 4)
+            near = (near // 2 + near % 2 * 2) * 32
             far = m ^ (ids[5 + other] // 2)
-            far = jnp.where(half == 0, far, (4 - far) % 4) * 32
+            far = jnp.where(half == 0, far, (4 - far) % 4)
+            far = (far // 2 + far % 2 * 2) * 32
             for k in range(4):
                 for j in range(4):
                     lanes = slice(128 * j, 128 * j + 128)
@@ -166,9 +168,8 @@
 def solve_kernel(ids, *refs):
     blocks = refs[:8]
     inv_top, inv_low, trailing, panel = refs[8:12]
-    solved_out, own_out, given_out = refs[12:15]
-    kept_outs = refs[15:19]
-    g, xs, tall, total, corner = refs[19:]
+    solved_out, own_out, given_out, kept_out = refs[12:16]
+    g, xs, tall, total, corner = refs[16:]
 
     n = TILE
     for t in range(2048 // n):
@@ -206,9 +207,11 @@
     for t in range(ROWS):
         corner[t, :, 0:64] = summed[0:8, 64 * t : 64 * t + 64]
         corner[t, :, 64:128] = summed[8:16, 64 * t : 64 * t + 64]
-    for j in range(4):
-        for first, out, at in ((ids[5], given_out, 72 * j), (ids[0], kept_outs[j], 0)):
-            target = first ^ (2 * j)
+    for j, distance in enumerate((0, 4, 2, 6)):
+        distance = distance if j < 2 else jnp.where(ids[3] == 0, distance, 8 - distance)
+        at = 72 * j
+        for first, out in ((ids[5], given_out), (ids[0], kept_out)):
+            target = first ^ distance
             out[at : at + 64, :] = total[pl.ds(pl.multiple_of(target * 64, 64), 64), 0:384]
             out[at + 64 : at + 72, :] = corner[target]
 
@@ -258,9 +261,9 @@
 def solve(ids, blocks, inverse, trailing, panel):
     return pl.pallas_call(
         solve_kernel,
-        out_shape=[shape((B, 2048)), shape((16, 2048)), shape((288, 384))] + [shape((72, 384))] * 4,
+        out_shape=[shape((B, 2048)), shape((16, 2048)), shape((288, 384)), shape((288, 384))],
         in_specs=[SMEM] + [VMEM] * 12,
-        out_specs=[VMEM] * 7,
+        out_specs=[VMEM] * 4,
         scratch_shapes=[
             pltpu.VMEM((2, 3 * B, 1024), BF16),
             pltpu.VMEM((2, B, 3 * TILE), BF16),
@@ -319,15 +322,16 @@
 
     both = jnp.concatenate([grad_pair, jnp.pad(diag_pair, ((0, 0), (0, 1024 - 128)))], axis=0)
     both = [both] + [with_col_partner(both, 0, k) for k in (1, 2, 3)]
+    row_pair = jnp.concatenate([row_factor, with_row_partner(row_factor, 4)], axis=0)
+    both, row_pair = lax.optimization_barrier((both, row_pair))
     diag_quad = jnp.concatenate([b[32:, :128] for b in both], axis=1)
     diag_quad = jnp.concatenate([diag_quad, with_col_partner(diag_quad, 1, 1)], axis=0)
     diag_quad = jnp.concatenate([diag_quad, with_col_partner(diag_quad, 1, 2)], axis=0)
-    row_pair = jnp.concatenate([row_factor, with_row_partner(row_factor, 4)], axis=0)
-    diag_quad, both, row_pair = lax.optimization_barrier((diag_quad, both, row_pair))
+    diag_quad, both = lax.optimization_barrier((diag_quad, both))
     grad_quad = jnp.concatenate([b[:32] for b in both], axis=0)
     grad_far = [with_col_partner(grad_quad, 1, k) for k in (1, 2, 3)]
-    diag_even = jnp.concatenate([diag_quad, with_second(diag_quad)], axis=0)
-    diag_even = jnp.concatenate([diag_even, with_row_partner(diag_even, 4)], axis=0)
+    diag_even = jnp.concatenate([diag_quad, with_row_partner(diag_quad, 4)], axis=0)
+    diag_even = jnp.concatenate([diag_even, with_second(diag_even)], axis=0)
     diag_even, row_pair, grad_far[0], grad_far[2] = lax.optimization_barrier(
         (diag_even, row_pair, grad_far[0], grad_far[2])
     )
@@ -339,14 +343,13 @@
 
     inverse = prepare(ids, diag_blocks)
     grad_blocks = [grad_quad] + grad_far + [quad_swapped] + [with_sibling(b) for b in grad_far]
-    solved, own, given, *kept = solve(ids, grad_blocks, inverse, trailing_factor, panel_factor.T)
+    solved, own, given, kept = solve(ids, grad_blocks, inverse, trailing_factor, panel_factor.T)
     trailing_out = trailing_update(ids, [row_even, row_odd], solved, trailing_grad)
     taken = with_neighbour(given)
     taken, trailing_out = lax.optimization_barrier((taken, trailing_out))
-    sums = [kept[j] + taken[72 * j : 72 * j + 72] for j in range(4)]
-    came = [with_row_partner(sums[j], 2 * j) for j in range(1, 4)]
-
-    total = sums[0] + (came[0] + came[1] + came[2])
+    stays = kept[:144] + taken[:144]
+    stays = stays + with_second(kept[144:] + taken[144:])
+    total = stays[:72] + with_row_partner(stays[72:], 4)
     row_out = row_grad - total[0:64, :]
     diag_sum = jnp.concatenate([total[64:72, 0:64], total[64:72, 64:128]], axis=0)
     global_rows = z * 64 + jnp.arange(64)[None, :]

time: 103 us -> 109 us (1.058)
  waiting for transfers between devices: 28.4 us -> 35.5 us
  starting transfers between devices: 49.4 us -> 46.5 us
    ppermute x8, starting transfers between devices: 8.46 us -> 20.6 us  [with_sibling(): return lax.ppermute(v, 'col', [(i, i ^ 1) for i in range(COLS)])]
    ppermute x2 -> x3, waiting for transfers between devices: 5.71 us -> 13.6 us  [with_second(): return lax.ppermute(v, ('row', 'col'), perm)]
    ppermute x2 -> x3, starting transfers between devices: 8.26 us -> 1.02 us  [with_second(): return lax.ppermute(v, ('row', 'col'), perm)]
    ppermute x5 -> x3, starting transfers between devices: 15.2 us -> 9.35 us  [with_row_partner(): return lax.ppermute(v, 'row', [(i, i ^ k) for i in range(ROWS)])]
    ppermute x3, starting transfers between devices: 6.96 us -> 3.89 us  [with_neighbour(): return lax.ppermute(v, ('row', 'col'), perm)]
    ppermute x8, waiting for transfers between devices: 5.74 us -> 8.79 us  [with_col_partner(): return lax.ppermute(v, 'col', perm)]
    ppermute x5 -> x3, waiting for transfers between devices: 15.3 us -> 13.1 us  [with_row_partner(): return lax.ppermute(v, 'row', [(i, i ^ k) for i in range(ROWS)])]
    ppermute x8, waiting for transfers between devices: 1.17 us -> 0.02 us  [with_sibling(): return lax.ppermute(v, 'col', [(i, i ^ 1) for i in range(COLS)])]
  transfers between devices with their start and end apart: 26 -> 25, of which waited for: 11 -> 8; matrix products, arithmetic and copies ran while one was open for 2% -> 3% of each run, Pallas kernels for 19% -> 19%
where the time goes in v9:
time: 109 us; the launch traced here: 108 us
  starting transfers between devices  46.5 us (43%)
  waiting for transfers between devices  35.5 us (33%)
  Pallas kernels  20.1 us (18%)
  other arithmetic  4.07 us (4%)
  local copies, waits for them, and re-layouts  1.2 us (1%)
    ppermute x8, starting transfers between devices, with_sibling(): return lax.ppermute(v, 'col', [(i, i ^ 1) for i in range(COLS)])  20.6 us
    ppermute x3, waiting for transfers between devices, with_second(): return lax.ppermute(v, ('row', 'col'), perm)  13.6 us
    ppermute x3, waiting for transfers between devices, with_row_partner(): return lax.ppermute(v, 'row', [(i, i ^ k) for i in range(ROWS)])  13.1 us
    ppermute x8, starting transfers between devices, with_col_partner(): return lax.ppermute(v, 'col', perm)  11.6 us
    ppermute x3, starting transfers between devices, with_row_partner(): return lax.ppermute(v, 'row', [(i, i ^ k) for i in range(ROWS)])  9.35 us
    ppermute x8, waiting for transfers between devices, with_col_partner(): return lax.ppermute(v, 'col', perm)  8.79 us
    pallas_call x1, Pallas kernels, solve(): pl.pallas_call(solve_kernel, out_shape=[shape((B, 2048)), shape((16, 2048...  8.18 us
    pallas_call x1, Pallas kernels, trailing_update(): pl.pallas_call(trailing_kernel, grid=(2048 // tile,), out_shape=shape((20...  7.02 us
  transfers between devices with their start and end apart: 25, of which 8 were waited for; matrix products, arithmetic and copies ran while one was open for 3% of the time, Pallas kernels for 19%

profile of v9, /device:TPU:1, one launch (start us, length us, event | category | flops | bytes accessed | tf_op | source)
XLA Modules:
  0.0 108.4 jit_solution(819630088762989647)
XLA Ops:
  0.6 0.7 slice_select_fusion.3
  1.4 3.2 %collective-permute-start.1 = (f32[8,64]{1,0:T(8,128)S(1)}, f32[8,64]{1,0:T(8,128)S(1)}, u32[]{:S(2)}, u32[]{:S(2)}) collective-permute-start(f32[8,64]{1,0:T(8,128)S(1)} %get-tuple-element.53), channel_id=1, source_target_pairs={{0,1},{1,0},{2,3},{3,2},{4,5},{5,4},{6,7},{7,6},{8,9},{9,8},{10,11... | collective-permute-start | bytes 6152 | tf_op jit(solution)/shard_map/ppermute | solution.py:29
  4.6 0.9 slice_select_fusion.1
  5.6 5.3 %collective-permute-start.5 = (f32[64,384]{1,0:T(8,128)}, f32[64,384]{1,0:T(8,128)S(1)}, u32[]{:S(2)}, u32[]{:S(2)}) collective-permute-start(f32[64,384]{1,0:T(8,128)} %param.10), channel_id=1, source_target_pairs={{0,128},{32,160},{64,192},{96,224},{128,0},{160,32},{192,64},{224,... | collective-permute-start | bytes 294920 | tf_op jit(solution)/shard_map/ppermute | solution.py:17
  10.9 1.4 %collective-permute-start.2 = (f32[40,1024]{1,0:T(8,128)S(1)}, f32[40,1024]{1,0:T(8,128)S(1)}, u32[]{:S(2)}, u32[]{:S(2)}) collective-permute-start(f32[40,1024]{1,0:T(8,128)S(1)} %pad_maximum_fusion.3), channel_id=1, source_target_pairs={{0,2},{1,9},{2,0},{3,11},{4,6},{5,13},{6,4},{7,15},{8,10},{9,1},{1... | collective-permute-start | bytes 491528 | tf_op jit(solution)/shard_map/ppermute | solution.py:44
  12.3 2.6 %collective-permute-start.3 = (f32[40,1024]{1,0:T(8,128)S(1)}, f32[40,1024]{1,0:T(8,128)S(1)}, u32[]{:S(2)}, u32[]{:S(2)}) collective-permute-start(f32[40,1024]{1,0:T(8,128)S(1)} %pad_maximum_fusion.3), channel_id=1, source_target_pairs={{0,4},{1,17},{2,6},{3,19},{4,0},{5,21},{6,2},{7,23},{8,12},{9,25},... | collective-permute-start | bytes 491528 | tf_op jit(solution)/shard_map/ppermute | solution.py:44
  15.0 0.9 pad_maximum_fusion.2
  15.9 3.8 %collective-permute-done.3 = f32[40,1024]{1,0:T(8,128)S(1)} collective-permute-done((f32[40,1024]{1,0:T(8,128)S(1)}, f32[40,1024]{1,0:T(8,128)S(1)}, u32[]{:S(2)}, u32[]{:S(2)}) %collective-permute-start.3) | collective-permute-done | bytes 163872 | tf_op jit(solution)/shard_map/ppermute | solution.py:44
  19.7 1.8 %collective-permute-done.4 = f32[40,1024]{1,0:T(8,128)S(1)} collective-permute-done((f32[40,1024]{1,0:T(8,128)S(1)}, f32[40,1024]{1,0:T(8,128)S(1)}, u32[]{:S(2)}, u32[]{:S(2)}) %collective-permute-start.4) | collective-permute-done | bytes 163872 | tf_op jit(solution)/shard_map/ppermute | solution.py:44
  21.5 1.0 collective-permute-start.6
  22.5 1.7 %collective-permute-done.6 = f32[8,512]{1,0:T(8,128)S(1)} collective-permute-done((f32[8,512]{1,0:T(8,128)S(1)}, f32[8,512]{1,0:T(8,128)S(1)}, u32[]{:S(2)}, u32[]{:S(2)}) %collective-permute-start.6) | collective-permute-done | bytes 16416 | tf_op jit(solution)/shard_map/ppermute | solution.py:44
  24.2 2.7 %collective-permute-start.7 = (f32[16,512]{1,0:T(8,128)S(1)}, f32[16,512]{1,0:T(8,128)S(1)}, u32[]{:S(2)}, u32[]{:S(2)}) collective-permute-start(f32[16,512]{1,0:T(8,128)S(1)} %pad_maximum_fusion.6), channel_id=1, source_target_pairs={{0,16},{1,5},{2,18},{3,7},{4,20},{5,1},{6,22},{7,3},{8,24},{9,13},... | collective-permute-start | bytes 98312 | tf_op jit(solution)/shard_map/ppermute | solution.py:44
  26.9 1.5 %collective-permute-done.7 = f32[16,512]{1,0:T(8,128)S(1)} collective-permute-done((f32[16,512]{1,0:T(8,128)S(1)}, f32[16,512]{1,0:T(8,128)S(1)}, u32[]{:S(2)}, u32[]{:S(2)}) %collective-permute-start.7) | collective-permute-done | bytes 32800 | tf_op jit(solution)/shard_map/ppermute | solution.py:44
  28.6 1.0 collective-permute-start.10
  29.6 2.1 %collective-permute-start.11 = (f32[128,1024]{1,0:T(8,128)S(1)}, f32[128,1024]{1,0:T(8,128)S(1)}, u32[]{:S(2)}, u32[]{:S(2)}) collective-permute-start(f32[128,1024]{1,0:T(8,128)S(1)} %pad_maximum_fusion.refs_0_), channel_id=1, source_target_pairs={{0,24},{1,7},{2,26},{3,5},{4,28},{5,3},{6,30},{7,1},{8,16},{9,15},... | collective-permute-start | bytes 1572872 | tf_op jit(solution)/shard_map/ppermute | solution.py:44
  31.7 0.8 collective-permute-start.8
  32.4 6.6 %collective-permute-done.8 = f32[32,512]{1,0:T(8,128)S(1)} collective-permute-done((f32[32,512]{1,0:T(8,128)S(1)}, f32[32,512]{1,0:T(8,128)S(1)}, u32[]{:S(2)}, u32[]{:S(2)}) %collective-permute-start.8) | collective-permute-done | bytes 65568 | tf_op jit(solution)/shard_map/ppermute | solution.py:17
  39.1 0.7 collective-permute-start.12
  39.8 5.2 %collective-permute-done.9 = f32[64,512]{1,0:T(8,128)S(1)} collective-permute-done((f32[64,512]{1,0:T(8,128)S(1)}, f32[64,512]{1,0:T(8,128)S(1)}, u32[]{:S(2)}, u32[]{:S(2)}) %collective-permute-start.9) | collective-permute-done | bytes 131104 | tf_op jit(solution)/shard_map/ppermute | solution.py:25
  45.1 1.0 collective-permute-start.17
  46.0 6.8 %collective-permute-start.18 = (f32[128,512]{1,0:T(8,128)S(1)}, f32[128,512]{1,0:T(8,128)S(1)}, u32[]{:S(2)}, u32[]{:S(2)}) collective-permute-start(f32[128,512]{1,0:T(8,128)S(1)} %pad_maximum_fusion.1.refs_0_), channel_id=1, source_target_pairs={{0,1},{1,0},{2,3},{3,2},{4,5},{5,4},{6,7},{7,6},{8,9},{9,8},{10,11... | collective-permute-start | bytes 786440 | tf_op jit(solution)/shard_map/ppermute | solution.py:29
  52.8 0.8 collective-permute-start.21
  53.7 9.5 %collective-permute-start.19 = (f32[128,512]{1,0:T(8,128)S(1)}, f32[128,512]{1,0:T(8,128)S(1)}, u32[]{:S(2)}, u32[]{:S(2)}) collective-permute-start(f32[128,512]{1,0:T(8,128)S(1)} %collective-permute-done.17.refs_1_), channel_id=1, source_target_pairs={{0,1},{1,0},{2,3},{3,2},{4,5},{5,4},{6,7},{7,6},{8,9},{9,8},{10,11... | collective-permute-start | bytes 786440 | tf_op jit(solution)/shard_map/ppermute | solution.py:29
  64.3 0.9 constant_dynamic-update-slice_fusion.refs_0_
  65.8 4.9 %prepare.1 = (bf16[256,1536]{1,0:T(8,128)(2,1)S(1)}, bf16[256,768]{1,0:T(8,128)(2,1)S(1)}) custom-call(s32[7]{0:T(128)S(1)} %stack.31.ids, f32[128,512]{1,0:T(8,128)S(1)} %pad_maximum_fusion.1.refs_0_, f32[128,512]{1,0:T(8,128)S(1)} %collective-permute-done.17.refs_1_, f32[128,512]{1,0:T(8,128)S(1)} %collective-permute-done.18.refs_2_, ...), custom_call_target="tpu_custom_call" | custom-call | flops 4000000000 | bytes 2097152 | tf_op jit(solution)/shard_map/prepare/pallas_call | solution.py:249
  70.9 8.2 %solve.1 = (f32[512,2048]{1,0:T(8,128)S(1)}, f32[16,2048]{1,0:T(8,128)}, f32[288,384]{1,0:T(8,128)S(1)}, f32[288,384]{1,0:T(8,128)S(1)}) custom-call(s32[7]{0:T(128)S(1)} %stack.31.ids, f32[128,1024]{1,0:T(8,128)S(1)} %pad_maximum_fusion.refs_0_, f32[128,1024]{1,0:T(8,128)S(1)} %collective-permute-done.10.refs_1_, ...), custom_call_target="tpu_custom_call" | custom-call | flops 6000000000 | bytes 12582912 | tf_op jit(solution)/shard_map/solve/pallas_call | solution.py:262
  79.0 2.4 %collective-permute-start.20 = (f32[288,384]{1,0:T(8,128)S(1)}, f32[288,384]{1,0:T(8,128)S(1)}, u32[]{:S(2)}, u32[]{:S(2)}) collective-permute-start(f32[288,384]{1,0:T(8,128)S(1)} %get-tuple-element.42), channel_id=1, source_target_pairs={{0,32},{1,225},{2,34},{3,227},{4,36},{5,229},{6,38},{7,231},{8,40}... | collective-permute-start | bytes 1327112 | tf_op jit(solution)/shard_map/ppermute | solution.py:38
  81.4 7.0 %trailing.1 = f32[2048,384]{1,0:T(8,128)} custom-call(s32[7]{0:T(128)S(1)} %stack.31.ids, f32[256,384]{1,0:T(8,128)S(1)} %constant_dynamic-update-slice_fusion.refs_0_, f32[256,384]{1,0:T(8,128)S(1)} %collective-permute-done.22.refs_1_, f32[512,2048]{1,0:T(8,128)S(1)} %get-tuple-element.44.refs_2_, f32[2048,384]{1,0:T(8,128)S(1)} %copy-done.1), custom_call_target="tpu_custom_call" | custom-call | flops 4000000000 | bytes 11534336 | tf_op jit(solution)/shard_map/trailing/pallas_call | solution.py:282
  88.6 8.4 %collective-permute-done.23 = f32[144,384]{1,0:T(8,128)S(1)} collective-permute-done((f32[144,384]{1,0:T(8,128)S(1)}, f32[144,384]{1,0:T(8,128)S(1)}, u32[]{:S(2)}, u32[]{:S(2)}) %collective-permute-start.23) | collective-permute-done | bytes 221216 | tf_op jit(solution)/shard_map/ppermute | solution.py:25
  97.1 3.3 %collective-permute-start.24 = (f32[72,384]{1,0:T(8,128)S(1)}, f32[72,384]{1,0:T(8,128)S(1)}, u32[]{:S(2)}, u32[]{:S(2)}) collective-permute-start(f32[72,384]{1,0:T(8,128)S(1)} %slice.93), channel_id=1, source_target_pairs={{0,128},{32,160},{64,192},{96,224},{128,0},{160,32},{192,64},{224,... | collective-permute-start | bytes 331784 | tf_op jit(solution)/shard_map/ppermute | solution.py:17
  100.4 6.5 %collective-permute-done.24 = f32[72,384]{1,0:T(8,128)S(1)} collective-permute-done((f32[72,384]{1,0:T(8,128)S(1)}, f32[72,384]{1,0:T(8,128)S(1)}, u32[]{:S(2)}, u32[]{:S(2)}) %collective-permute-start.24) | collective-permute-done | bytes 110624 | tf_op jit(solution)/shard_map/ppermute | solution.py:17
  107.7 0.7 fusion.1
  (62 shorter events, 3.1 us)
Async XLA Ops:
  1.4 9.5 %collective-permute-start.1 = (f32[8,64]{1,0:T(8,128)S(1)}, f32[8,64]{1,0:T(8,128)S(1)}, u32[]{:S(2)}, u32[]{:S(2)}) collective-permute-start(f32[8,64]{1,0:T(8,128)S(1)} %get-tuple-element.53), channel_id=1, source_target_pairs={{0,1},{1,0},{2,3},{3,2},{4,5},{5,4},{6,7},{7,6},{8,9},{9,8},{10,11... | collective-permute-start | bytes 6152 | tf_op jit(solution)/shard_map/ppermute | solution.py:29
  5.5 5.4 %collective-permute-start = (f32[16,1024]{1,0:T(8,128)S(1)}, f32[16,1024]{1,0:T(8,128)S(1)}, u32[]{:S(2)}, u32[]{:S(2)}) collective-permute-start(f32[16,1024]{1,0:T(8,128)S(1)} %get-tuple-element.49), channel_id=1, source_target_pairs={{0,1},{1,0},{2,3},{3,2},{4,5},{5,4},{6,7},{7,6},{8,9},{9,8},{10,11... | collective-permute-start | bytes 196616 | tf_op jit(solution)/shard_map/ppermute | solution.py:29
  5.6 9.4 %collective-permute-start.5 = (f32[64,384]{1,0:T(8,128)}, f32[64,384]{1,0:T(8,128)S(1)}, u32[]{:S(2)}, u32[]{:S(2)}) collective-permute-start(f32[64,384]{1,0:T(8,128)} %param.10), channel_id=1, source_target_pairs={{0,128},{32,160},{64,192},{96,224},{128,0},{160,32},{192,64},{224,... | collective-permute-start | bytes 294920 | tf_op jit(solution)/shard_map/ppermute | solution.py:17
  10.9 4.9 %collective-permute-start.2 = (f32[40,1024]{1,0:T(8,128)S(1)}, f32[40,1024]{1,0:T(8,128)S(1)}, u32[]{:S(2)}, u32[]{:S(2)}) collective-permute-start(f32[40,1024]{1,0:T(8,128)S(1)} %pad_maximum_fusion.3), channel_id=1, source_target_pairs={{0,2},{1,9},{2,0},{3,11},{4,6},{5,13},{6,4},{7,15},{8,10},{9,1},{1... | collective-permute-start | bytes 491528 | tf_op jit(solution)/shard_map/ppermute | solution.py:44
  12.3 7.4 %collective-permute-start.3 = (f32[40,1024]{1,0:T(8,128)S(1)}, f32[40,1024]{1,0:T(8,128)S(1)}, u32[]{:S(2)}, u32[]{:S(2)}) collective-permute-start(f32[40,1024]{1,0:T(8,128)S(1)} %pad_maximum_fusion.3), channel_id=1, source_target_pairs={{0,4},{1,17},{2,6},{3,19},{4,0},{5,21},{6,2},{7,23},{8,12},{9,25},... | collective-permute-start | bytes 491528 | tf_op jit(solution)/shard_map/ppermute | solution.py:44
  14.9 6.5 %collective-permute-start.4 = (f32[40,1024]{1,0:T(8,128)S(1)}, f32[40,1024]{1,0:T(8,128)S(1)}, u32[]{:S(2)}, u32[]{:S(2)}) collective-permute-start(f32[40,1024]{1,0:T(8,128)S(1)} %pad_maximum_fusion.3), channel_id=1, source_target_pairs={{0,6},{1,25},{2,4},{3,27},{4,2},{5,29},{6,0},{7,31},{8,14},{9,17},... | collective-permute-start | bytes 491528 | tf_op jit(solution)/shard_map/ppermute | solution.py:44
  21.5 2.7 %collective-permute-start.6 = (f32[8,512]{1,0:T(8,128)S(1)}, f32[8,512]{1,0:T(8,128)S(1)}, u32[]{:S(2)}, u32[]{:S(2)}) collective-permute-start(f32[8,512]{1,0:T(8,128)S(1)} %pad_maximum_fusion.7), channel_id=1, source_target_pairs={{0,8},{1,3},{2,10},{3,1},{4,12},{5,7},{6,14},{7,5},{8,0},{9,11},{1... | collective-permute-start | bytes 49160 | tf_op jit(solution)/shard_map/ppermute | solution.py:44
  24.2 4.3 %collective-permute-start.7 = (f32[16,512]{1,0:T(8,128)S(1)}, f32[16,512]{1,0:T(8,128)S(1)}, u32[]{:S(2)}, u32[]{:S(2)}) collective-permute-start(f32[16,512]{1,0:T(8,128)S(1)} %pad_maximum_fusion.6), channel_id=1, source_target_pairs={{0,16},{1,5},{2,18},{3,7},{4,20},{5,1},{6,22},{7,3},{8,24},{9,13},... | collective-permute-start | bytes 98312 | tf_op jit(solution)/shard_map/ppermute | solution.py:44
  28.6 16.5 %collective-permute-start.10 = (f32[128,1024]{1,0:T(8,128)S(1)}, f32[128,1024]{1,0:T(8,128)S(1)}, u32[]{:S(2)}, u32[]{:S(2)}) collective-permute-start(f32[128,1024]{1,0:T(8,128)S(1)} %pad_maximum_fusion.refs_0_), channel_id=1, source_target_pairs={{0,8},{1,3},{2,10},{3,1},{4,12},{5,7},{6,14},{7,5},{8,0},{9,11},{1... | collective-permute-start | bytes 1572872 | tf_op jit(solution)/shard_map/ppermute | solution.py:44
  29.6 15.5 %collective-permute-start.11 = (f32[128,1024]{1,0:T(8,128)S(1)}, f32[128,1024]{1,0:T(8,128)S(1)}, u32[]{:S(2)}, u32[]{:S(2)}) collective-permute-start(f32[128,1024]{1,0:T(8,128)S(1)} %pad_maximum_fusion.refs_0_), channel_id=1, source_target_pairs={{0,24},{1,7},{2,26},{3,5},{4,28},{5,3},{6,30},{7,1},{8,16},{9,15},... | collective-permute-start | bytes 1572872 | tf_op jit(solution)/shard_map/ppermute | solution.py:44
  31.7 7.3 %collective-permute-start.8 = (f32[32,512]{1,0:T(8,128)S(1)}, f32[32,512]{1,0:T(8,128)S(1)}, u32[]{:S(2)}, u32[]{:S(2)}) collective-permute-start(f32[32,512]{1,0:T(8,128)S(1)} %pad_maximum_fusion.5), channel_id=1, source_target_pairs={{0,128},{32,160},{64,192},{96,224},{128,0},{160,32},{192,64},{224,... | collective-permute-start | bytes 196616 | tf_op jit(solution)/shard_map/ppermute | solution.py:17
  39.0 6.0 %collective-permute-start.9 = (f32[64,512]{1,0:T(8,128)S(1)}, f32[64,512]{1,0:T(8,128)S(1)}, u32[]{:S(2)}, u32[]{:S(2)}) collective-permute-start(f32[64,512]{1,0:T(8,128)S(1)} %pad_maximum_fusion.4), channel_id=1, source_target_pairs={{0,64},{1,193},{2,66},{3,195},{4,68},{5,197},{6,70},{7,199},{8,72}... | collective-permute-start | bytes 393224 | tf_op jit(solution)/shard_map/ppermute | solution.py:25
  39.1 24.1 %collective-permute-start.12 = (f32[128,1024]{1,0:T(8,128)S(1)}, f32[128,1024]{1,0:T(8,128)S(1)}, u32[]{:S(2)}, u32[]{:S(2)}) collective-permute-start(f32[128,1024]{1,0:T(8,128)S(1)} %pad_maximum_fusion.refs_0_), channel_id=1, source_target_pairs={{0,16},{1,5},{2,18},{3,7},{4,20},{5,1},{6,22},{7,3},{8,24},{9,13},... | collective-permute-start | bytes 1572872 | tf_op jit(solution)/shard_map/ppermute | solution.py:44
  45.1 8.6 %collective-permute-start.17 = (f32[128,512]{1,0:T(8,128)S(1)}, f32[128,512]{1,0:T(8,128)S(1)}, u32[]{:S(2)}, u32[]{:S(2)}) collective-permute-start(f32[128,512]{1,0:T(8,128)S(1)} %pad_maximum_fusion.1.refs_0_), channel_id=1, source_target_pairs={{0,32},{1,225},{2,34},{3,227},{4,36},{5,229},{6,38},{7,231},{8,40}... | collective-permute-start | bytes 786440 | tf_op jit(solution)/shard_map/ppermute | solution.py:38
  46.0 17.8 %collective-permute-start.18 = (f32[128,512]{1,0:T(8,128)S(1)}, f32[128,512]{1,0:T(8,128)S(1)}, u32[]{:S(2)}, u32[]{:S(2)}) collective-permute-start(f32[128,512]{1,0:T(8,128)S(1)} %pad_maximum_fusion.1.refs_0_), channel_id=1, source_target_pairs={{0,1},{1,0},{2,3},{3,2},{4,5},{5,4},{6,7},{7,6},{8,9},{9,8},{10,11... | collective-permute-start | bytes 786440 | tf_op jit(solution)/shard_map/ppermute | solution.py:29
  52.8 10.9 %collective-permute-start.21 = (f32[128,384]{1,0:T(8,128)S(1)}, f32[128,384]{1,0:T(8,128)}, u32[]{:S(2)}, u32[]{:S(2)}) collective-permute-start(f32[128,384]{1,0:T(8,128)S(1)} %pad_maximum_fusion.2), channel_id=1, source_target_pairs={{0,64},{1,193},{2,66},{3,195},{4,68},{5,197},{6,70},{7,199},{8,72}... | collective-permute-start | bytes 589832 | tf_op jit(solution)/shard_map/ppermute | solution.py:25
  53.7 11.6 %collective-permute-start.19 = (f32[128,512]{1,0:T(8,128)S(1)}, f32[128,512]{1,0:T(8,128)S(1)}, u32[]{:S(2)}, u32[]{:S(2)}) collective-permute-start(f32[128,512]{1,0:T(8,128)S(1)} %collective-permute-done.17.refs_1_), channel_id=1, source_target_pairs={{0,1},{1,0},{2,3},{3,2},{4,5},{5,4},{6,7},{7,6},{8,9},{9,8},{10,11... | collective-permute-start | bytes 786440 | tf_op jit(solution)/shard_map/ppermute | solution.py:29
  63.2 7.6 %collective-permute-start.13 = (f32[128,1024]{1,0:T(8,128)S(1)}, f32[128,1024]{1,0:T(8,128)S(1)}, u32[]{:S(2)}, u32[]{:S(2)}) collective-permute-start(f32[128,1024]{1,0:T(8,128)S(1)} %pad_maximum_fusion.refs_0_), channel_id=1, source_target_pairs={{0,1},{1,0},{2,3},{3,2},{4,5},{5,4},{6,7},{7,6},{8,9},{9,8},{10,11... | collective-permute-start | bytes 1572872 | tf_op jit(solution)/shard_map/ppermute | solution.py:29
  63.3 7.5 %collective-permute-start.14 = (f32[128,1024]{1,0:T(8,128)S(1)}, f32[128,1024]{1,0:T(8,128)S(1)}, u32[]{:S(2)}, u32[]{:S(2)}) collective-permute-start(f32[128,1024]{1,0:T(8,128)S(1)} %collective-permute-done.10.refs_1_), channel_id=1, source_target_pairs={{0,1},{1,0},{2,3},{3,2},{4,5},{5,4},{6,7},{7,6},{8,9},{9,8},{10,11... | collective-permute-start | bytes 1572872 | tf_op jit(solution)/shard_map/ppermute | solution.py:29
  63.8 7.1 %collective-permute-start.16 = (f32[128,1024]{1,0:T(8,128)S(1)}, f32[128,1024]{1,0:T(8,128)S(1)}, u32[]{:S(2)}, u32[]{:S(2)}) collective-permute-start(f32[128,1024]{1,0:T(8,128)S(1)} %collective-permute-done.11.refs_3_), channel_id=1, source_target_pairs={{0,1},{1,0},{2,3},{3,2},{4,5},{5,4},{6,7},{7,6},{8,9},{9,8},{10,11... | collective-permute-start | bytes 1572872 | tf_op jit(solution)/shard_map/ppermute | solution.py:29
  63.9 7.0 %collective-permute-start.15 = (f32[128,1024]{1,0:T(8,128)S(1)}, f32[128,1024]{1,0:T(8,128)S(1)}, u32[]{:S(2)}, u32[]{:S(2)}) collective-permute-start(f32[128,1024]{1,0:T(8,128)S(1)} %collective-permute-done.12.refs_2_), channel_id=1, source_target_pairs={{0,1},{1,0},{2,3},{3,2},{4,5},{5,4},{6,7},{7,6},{8,9},{9,8},{10,11... | collective-permute-start | bytes 1572872 | tf_op jit(solution)/shard_map/ppermute | solution.py:29
  65.2 5.6 %copy-start = (f32[2048,384]{1,0:T(8,128)S(1)}, f32[2048,384]{1,0:T(8,128)}, u32[]{:S(2)}) copy-start(f32[2048,384]{1,0:T(8,128)} %refs_10_.1) | copy-start | bytes 9437188
  65.2 5.6 %copy-start.2 = (f32[2048,16]{0,1:T(8,128)S(1)}, f32[2048,16]{0,1:T(8,128)}, u32[]{:S(2)}) copy-start(f32[2048,16]{0,1:T(8,128)} %param.9) | copy-start | bytes 393220
  65.3 16.2 %collective-permute-start.22 = (f32[256,384]{1,0:T(8,128)S(1)}, f32[256,384]{1,0:T(8,128)S(1)}, u32[]{:S(2)}, u32[]{:S(2)}) collective-permute-start(f32[256,384]{1,0:T(8,128)S(1)} %constant_dynamic-update-slice_fusion.refs_0_), channel_id=1, source_target_pairs={{0,32},{1,225},{2,34},{3,227},{4,36},{5,229},{6,38},{7,231},{8,40}... | collective-permute-start | bytes 1179656 | tf_op jit(solution)/shard_map/ppermute | solution.py:38
  70.9 10.6 %copy-start.1 = (f32[2048,384]{1,0:T(8,128)S(1)}, f32[2048,384]{1,0:T(8,128)}, u32[]{:S(2)}) copy-start(f32[2048,384]{1,0:T(8,128)} %refs_3_.1) | copy-start | bytes 9437188
  79.0 9.4 %collective-permute-start.20 = (f32[288,384]{1,0:T(8,128)S(1)}, f32[288,384]{1,0:T(8,128)S(1)}, u32[]{:S(2)}, u32[]{:S(2)}) collective-permute-start(f32[288,384]{1,0:T(8,128)S(1)} %get-tuple-element.42), channel_id=1, source_target_pairs={{0,32},{1,225},{2,34},{3,227},{4,36},{5,229},{6,38},{7,231},{8,40}... | collective-permute-start | bytes 1327112 | tf_op jit(solution)/shard_map/ppermute | solution.py:38
  81.4 25.6 %copy-start.3 = (f32[64,384]{1,0:T(8,128)S(1)}, f32[64,384]{1,0:T(8,128)}, u32[]{:S(2)}) copy-start(f32[64,384]{1,0:T(8,128)} %param.14) | copy-start | bytes 294916
  81.4 26.3 %copy-start.4 = (f32[64,16]{0,1:T(8,128)S(1)}, f32[64,16]{0,1:T(8,128)}, u32[]{:S(2)}) copy-start(f32[64,16]{0,1:T(8,128)} %param.13) | copy-start | bytes 12292
  88.5 8.6 %collective-permute-start.23 = (f32[144,384]{1,0:T(8,128)S(1)}, f32[144,384]{1,0:T(8,128)S(1)}, u32[]{:S(2)}, u32[]{:S(2)}) collective-permute-start(f32[144,384]{1,0:T(8,128)S(1)} %slice_add_fusion), channel_id=1, source_target_pairs={{0,64},{1,193},{2,66},{3,195},{4,68},{5,197},{6,70},{7,199},{8,72}... | collective-permute-start | bytes 663560 | tf_op jit(solution)/shard_map/ppermute | solution.py:25
  97.1 9.9 %collective-permute-start.24 = (f32[72,384]{1,0:T(8,128)S(1)}, f32[72,384]{1,0:T(8,128)S(1)}, u32[]{:S(2)}, u32[]{:S(2)}) collective-permute-start(f32[72,384]{1,0:T(8,128)S(1)} %slice.93), channel_id=1, source_target_pairs={{0,128},{32,160},{64,192},{96,224},{128,0},{160,32},{192,64},{224,... | collective-permute-start | bytes 331784 | tf_op jit(solution)/shard_map/ppermute | solution.py:17

commit v10 on v8

--- a/solution.py
+++ b/solution.py
@@ -323,15 +323,14 @@
     diag_quad = jnp.concatenate([diag_quad, with_col_partner(diag_quad, 1, 1)], axis=0)
     diag_quad = jnp.concatenate([diag_quad, with_col_partner(diag_quad, 1, 2)], axis=0)
     row_pair = jnp.concatenate([row_factor, with_row_partner(row_factor, 4)], axis=0)
-    diag_quad, both, row_pair = lax.optimization_barrier((diag_quad, both, row_pair))
+    diag_even = jnp.concatenate([diag_quad, with_second(diag_quad)], axis=0)
+    diag_even, both, row_pair = lax.optimization_barrier((diag_even, both, row_pair))
     grad_quad = jnp.concatenate([b[:32] for b in both], axis=0)
     grad_far = [with_col_partner(grad_quad, 1, k) for k in (1, 2, 3)]
-    diag_even = jnp.concatenate([diag_quad, with_second(diag_quad)], axis=0)
     diag_even = jnp.concatenate([diag_even, with_row_partner(diag_even, 4)], axis=0)
-    diag_even, row_pair, grad_far[0], grad_far[2] = lax.optimization_barrier(
-        (diag_even, row_pair, grad_far[0], grad_far[2])
-    )
+    diag_even, row_pair = lax.optimization_barrier((diag_even, row_pair))
     diag_odd = with_neighbour(diag_even)
+    diag_odd, grad_far[0], grad_far[2] = lax.optimization_barrier((diag_odd, grad_far[0], grad_far[2]))
     diag_blocks = [diag_even, diag_odd, with_sibling(diag_even), with_sibling(diag_odd)]
     row_even = jnp.concatenate([row_pair, with_second(row_pair)], axis=0)
     row_odd = with_neighbour(row_even)

time: 103 us -> 106 us (1.029)
  starting transfers between devices: 49.4 us -> 54.6 us
  waiting for transfers between devices: 28.4 us -> 25.4 us
    ppermute x8, starting transfers between devices: 8.46 us -> 20.1 us  [with_sibling(): return lax.ppermute(v, 'col', [(i, i ^ 1) for i in range(COLS)])]
    ppermute x2, starting transfers between devices: 8.26 us -> 4.03 us  [with_second(): return lax.ppermute(v, ('row', 'col'), perm)]
    ppermute x5, waiting for transfers between devices: 15.3 us -> 12 us  [with_row_partner(): return lax.ppermute(v, 'row', [(i, i ^ k) for i in range(ROWS)])]
    ppermute x3, starting transfers between devices: 6.96 us -> 4.71 us  [with_neighbour(): return lax.ppermute(v, ('row', 'col'), perm)]
    ppermute x2, waiting for transfers between devices: 5.71 us -> 3.53 us  [with_second(): return lax.ppermute(v, ('row', 'col'), perm)]
    ppermute x3, waiting for transfers between devices: 0.47 us -> 2.08 us  [with_neighbour(): return lax.ppermute(v, ('row', 'col'), perm)]
  transfers between devices with their start and end apart: 26 -> 26, of which waited for: 11 -> 14; matrix products, arithmetic and copies ran while one was open for 2% -> 2% of each run, Pallas kernels for 19% -> 19%
where the time goes in v10:
time: 106 us; the launch traced here: 105 us
  starting transfers between devices  54.6 us (52%)
  waiting for transfers between devices  25.4 us (24%)
  Pallas kernels  20.1 us (19%)
  other arithmetic  4.07 us (4%)
    ppermute x8, starting transfers between devices, with_sibling(): return lax.ppermute(v, 'col', [(i, i ^ 1) for i in range(COLS)])  20.1 us
    ppermute x5, starting transfers between devices, with_row_partner(): return lax.ppermute(v, 'row', [(i, i ^ k) for i in range(ROWS)])  14.9 us
    ppermute x5, waiting for transfers between devices, with_row_partner(): return lax.ppermute(v, 'row', [(i, i ^ k) for i in range(ROWS)])  12 us
    ppermute x8, starting transfers between devices, with_col_partner(): return lax.ppermute(v, 'col', perm)  10.9 us
    pallas_call x1, Pallas kernels, solve(): pl.pallas_call(solve_kernel, out_shape=[shape((B, 2048)), shape((16, 2048...  8.18 us
    pallas_call x1, Pallas kernels, trailing_update(): pl.pallas_call(trailing_kernel, grid=(2048 // tile,), out_shape=shape((20...  7.02 us
    ppermute x8, waiting for transfers between devices, with_col_partner(): return lax.ppermute(v, 'col', perm)  6.63 us
    pallas_call x1, Pallas kernels, prepare(): pl.pallas_call(prepare_kernel, out_shape=[shape((256, 1536), BF16), shape...  4.87 us
  transfers between devices with their start and end apart: 26, of which 14 were waited for; matrix products, arithmetic and copies ran while one was open for 2% of the time, Pallas kernels for 19%

profile of v10, /device:TPU:1, one launch (start us, length us, event | category | flops | bytes accessed | tf_op | source)
XLA Modules:
  0.0 105.3 jit_solution(10213557695547520848)
XLA Ops:
  1.4 3.2 %collective-permute-start = (f32[8,64]{1,0:T(8,128)S(1)}, f32[8,64]{1,0:T(8,128)S(1)}, u32[]{:S(2)}, u32[]{:S(2)}) collective-permute-start(f32[8,64]{1,0:T(8,128)S(1)} %get-tuple-element.55), channel_id=1, source_target_pairs={{0,1},{1,0},{2,3},{3,2},{4,5},{5,4},{6,7},{7,6},{8,9},{9,8},{10,11... | collective-permute-start | bytes 6152 | tf_op jit(solution)/shard_map/ppermute | solution.py:29
  4.6 0.9 slice_select_fusion.1
  5.7 1.2 %collective-permute-done.1 = f32[16,1024]{1,0:T(8,128)S(1)} collective-permute-done((f32[16,1024]{1,0:T(8,128)S(1)}, f32[16,1024]{1,0:T(8,128)S(1)}, u32[]{:S(2)}, u32[]{:S(2)}) %collective-permute-start.1) | collective-permute-done | bytes 65568 | tf_op jit(solution)/shard_map/ppermute | solution.py:29
  6.9 2.2 %collective-permute-start.3 = (f32[40,1024]{1,0:T(8,128)S(1)}, f32[40,1024]{1,0:T(8,128)S(1)}, u32[]{:S(2)}, u32[]{:S(2)}) collective-permute-start(f32[40,1024]{1,0:T(8,128)S(1)} %pad_maximum_fusion.3), channel_id=1, source_target_pairs={{0,4},{1,17},{2,6},{3,19},{4,0},{5,21},{6,2},{7,23},{8,12},{9,25},... | collective-permute-start | bytes 491528 | tf_op jit(solution)/shard_map/ppermute | solution.py:44
  9.1 1.7 %collective-permute-start.4 = (f32[40,1024]{1,0:T(8,128)S(1)}, f32[40,1024]{1,0:T(8,128)S(1)}, u32[]{:S(2)}, u32[]{:S(2)}) collective-permute-start(f32[40,1024]{1,0:T(8,128)S(1)} %pad_maximum_fusion.3), channel_id=1, source_target_pairs={{0,6},{1,25},{2,4},{3,27},{4,2},{5,29},{6,0},{7,31},{8,14},{9,17},... | collective-permute-start | bytes 491528 | tf_op jit(solution)/shard_map/ppermute | solution.py:44
  11.4 2.5 %collective-permute-done.3 = f32[40,1024]{1,0:T(8,128)S(1)} collective-permute-done((f32[40,1024]{1,0:T(8,128)S(1)}, f32[40,1024]{1,0:T(8,128)S(1)}, u32[]{:S(2)}, u32[]{:S(2)}) %collective-permute-start.3) | collective-permute-done | bytes 163872 | tf_op jit(solution)/shard_map/ppermute | solution.py:44
  13.9 1.8 %collective-permute-done.4 = f32[40,1024]{1,0:T(8,128)S(1)} collective-permute-done((f32[40,1024]{1,0:T(8,128)S(1)}, f32[40,1024]{1,0:T(8,128)S(1)}, u32[]{:S(2)}, u32[]{:S(2)}) %collective-permute-start.4) | collective-permute-done | bytes 163872 | tf_op jit(solution)/shard_map/ppermute | solution.py:44
  15.7 0.9 collective-permute-start.5
  16.6 1.7 %collective-permute-done.5 = f32[8,512]{1,0:T(8,128)S(1)} collective-permute-done((f32[8,512]{1,0:T(8,128)S(1)}, f32[8,512]{1,0:T(8,128)S(1)}, u32[]{:S(2)}, u32[]{:S(2)}) %collective-permute-start.5) | collective-permute-done | bytes 16416 | tf_op jit(solution)/shard_map/ppermute | solution.py:44
  18.3 2.6 %collective-permute-start.6 = (f32[16,512]{1,0:T(8,128)S(1)}, f32[16,512]{1,0:T(8,128)S(1)}, u32[]{:S(2)}, u32[]{:S(2)}) collective-permute-start(f32[16,512]{1,0:T(8,128)S(1)} %pad_maximum_fusion.6), channel_id=1, source_target_pairs={{0,16},{1,5},{2,18},{3,7},{4,20},{5,1},{6,22},{7,3},{8,24},{9,13},... | collective-permute-start | bytes 98312 | tf_op jit(solution)/shard_map/ppermute | solution.py:44
  21.0 6.7 %collective-permute-start.8 = (f32[64,384]{1,0:T(8,128)}, f32[64,384]{1,0:T(8,128)S(1)}, u32[]{:S(2)}, u32[]{:S(2)}) collective-permute-start(f32[64,384]{1,0:T(8,128)} %param.10), channel_id=1, source_target_pairs={{0,128},{32,160},{64,192},{96,224},{128,0},{160,32},{192,64},{224,... | collective-permute-start | bytes 294920 | tf_op jit(solution)/shard_map/ppermute | solution.py:17
  27.7 0.9 collective-permute-start.7
  28.6 1.4 %collective-permute-done.8 = f32[64,384]{1,0:T(8,128)S(1)} collective-permute-done((f32[64,384]{1,0:T(8,128)}, f32[64,384]{1,0:T(8,128)S(1)}, u32[]{:S(2)}, u32[]{:S(2)}) %collective-permute-start.8) | collective-permute-done | bytes 98336 | tf_op jit(solution)/shard_map/ppermute | solution.py:17
  30.0 0.9 pad_maximum_fusion.2
  30.9 3.3 %collective-permute-done.7 = f32[32,512]{1,0:T(8,128)S(1)} collective-permute-done((f32[32,512]{1,0:T(8,128)S(1)}, f32[32,512]{1,0:T(8,128)S(1)}, u32[]{:S(2)}, u32[]{:S(2)}) %collective-permute-start.7) | collective-permute-done | bytes 65568 | tf_op jit(solution)/shard_map/ppermute | solution.py:25
  34.2 2.5 %collective-permute-start.9 = (f32[64,512]{1,0:T(8,128)S(1)}, f32[64,512]{1,0:T(8,128)S(1)}, u32[]{:S(2)}, u32[]{:S(2)}) collective-permute-start(f32[64,512]{1,0:T(8,128)S(1)} %pad_maximum_fusion.4), channel_id=1, source_target_pairs={{0,128},{32,160},{64,192},{96,224},{128,0},{160,32},{192,64},{224,... | collective-permute-start | bytes 393224 | tf_op jit(solution)/shard_map/ppermute | solution.py:17
  37.8 2.3 %collective-permute-start.13 = (f32[128,1024]{1,0:T(8,128)S(1)}, f32[128,1024]{1,0:T(8,128)S(1)}, u32[]{:S(2)}, u32[]{:S(2)}) collective-permute-start(f32[128,1024]{1,0:T(8,128)S(1)} %pad_maximum_fusion.refs_0_), channel_id=1, source_target_pairs={{0,16},{1,5},{2,18},{3,7},{4,20},{5,1},{6,22},{7,3},{8,24},{9,13},... | collective-permute-start | bytes 1572872 | tf_op jit(solution)/shard_map/ppermute | solution.py:44
  40.2 2.0 %collective-permute-done.9 = f32[64,512]{1,0:T(8,128)S(1)} collective-permute-done((f32[64,512]{1,0:T(8,128)S(1)}, f32[64,512]{1,0:T(8,128)S(1)}, u32[]{:S(2)}, u32[]{:S(2)}) %collective-permute-start.9) | collective-permute-done | bytes 131104 | tf_op jit(solution)/shard_map/ppermute | solution.py:17
  42.2 0.8 collective-permute-start.10
  43.0 5.6 %collective-permute-start.18 = (f32[128,512]{1,0:T(8,128)S(1)}, f32[128,512]{1,0:T(8,128)S(1)}, u32[]{:S(2)}, u32[]{:S(2)}) collective-permute-start(f32[128,512]{1,0:T(8,128)S(1)} %pad_maximum_fusion.1.refs_0_), channel_id=1, source_target_pairs={{0,1},{1,0},{2,3},{3,2},{4,5},{5,4},{6,7},{7,6},{8,9},{9,8},{10,11... | collective-permute-start | bytes 786440 | tf_op jit(solution)/shard_map/ppermute | solution.py:29
  49.4 3.1 %collective-permute-start.21 = (f32[128,384]{1,0:T(8,128)S(1)}, f32[128,384]{1,0:T(8,128)S(1)}, u32[]{:S(2)}, u32[]{:S(2)}) collective-permute-start(f32[128,384]{1,0:T(8,128)S(1)} %pad_maximum_fusion.2), channel_id=1, source_target_pairs={{0,64},{1,193},{2,66},{3,195},{4,68},{5,197},{6,70},{7,199},{8,72}... | collective-permute-start | bytes 589832 | tf_op jit(solution)/shard_map/ppermute | solution.py:25
  52.6 5.2 %collective-permute-start.19 = (f32[128,512]{1,0:T(8,128)S(1)}, f32[128,512]{1,0:T(8,128)S(1)}, u32[]{:S(2)}, u32[]{:S(2)}) collective-permute-start(f32[128,512]{1,0:T(8,128)S(1)} %collective-permute-done.10.refs_1_), channel_id=1, source_target_pairs={{0,1},{1,0},{2,3},{3,2},{4,5},{5,4},{6,7},{7,6},{8,9},{9,8},{10,11... | collective-permute-start | bytes 786440 | tf_op jit(solution)/shard_map/ppermute | solution.py:29
  58.1 5.4 %collective-permute-start.15 = (f32[128,1024]{1,0:T(8,128)S(1)}, f32[128,1024]{1,0:T(8,128)S(1)}, u32[]{:S(2)}, u32[]{:S(2)}) collective-permute-start(f32[128,1024]{1,0:T(8,128)S(1)} %collective-permute-done.11.refs_1_), channel_id=1, source_target_pairs={{0,1},{1,0},{2,3},{3,2},{4,5},{5,4},{6,7},{7,6},{8,9},{9,8},{10,11... | collective-permute-start | bytes 1572872 | tf_op jit(solution)/shard_map/ppermute | solution.py:29
  64.1 3.9 %collective-permute-start.22 = (f32[256,384]{1,0:T(8,128)S(1)}, f32[256,384]{1,0:T(8,128)S(1)}, u32[]{:S(2)}, u32[]{:S(2)}) collective-permute-start(f32[256,384]{1,0:T(8,128)S(1)} %constant_dynamic-update-slice_fusion.refs_0_), channel_id=1, source_target_pairs={{0,32},{1,225},{2,34},{3,227},{4,36},{5,229},{6,38},{7,231},{8,40}... | collective-permute-start | bytes 1179656 | tf_op jit(solution)/shard_map/ppermute | solution.py:38
  68.0 4.9 %prepare.1 = (bf16[256,1536]{1,0:T(8,128)(2,1)S(1)}, bf16[256,768]{1,0:T(8,128)(2,1)S(1)}) custom-call(s32[7]{0:T(128)S(1)} %stack.31.ids, f32[128,512]{1,0:T(8,128)S(1)} %pad_maximum_fusion.1.refs_0_, f32[128,512]{1,0:T(8,128)S(1)} %collective-permute-done.10.refs_1_, f32[128,512]{1,0:T(8,128)S(1)} %collective-permute-done.18.refs_2_, ...), custom_call_target="tpu_custom_call" | custom-call | flops 4000000000 | bytes 2097152 | tf_op jit(solution)/shard_map/prepare/pallas_call | solution.py:246
  72.9 8.2 %solve.1 = (f32[512,2048]{1,0:T(8,128)S(1)}, f32[16,2048]{1,0:T(8,128)}, f32[288,384]{1,0:T(8,128)S(1)}, f32[72,384]{1,0:T(8,128)S(1)}, f32[72,384]{1,0:T(8,128)...) custom-call(s32[7]{0:T(128)S(1)} %stack.31.ids, f32[128,1024]{1,0:T(8,128)S(1)} %pad_maximum_fusion.refs_0_, ...), custom_call_target="tpu_custom_call" | custom-call | flops 6000000000 | bytes 12582912 | tf_op jit(solution)/shard_map/solve/pallas_call | solution.py:259
  81.2 7.0 %trailing.1 = f32[2048,384]{1,0:T(8,128)} custom-call(s32[7]{0:T(128)S(1)} %stack.31.ids, f32[256,384]{1,0:T(8,128)S(1)} %constant_dynamic-update-slice_fusion.refs_0_, f32[256,384]{1,0:T(8,128)S(1)} %collective-permute-done.22.refs_1_, f32[512,2048]{1,0:T(8,128)S(1)} %get-tuple-element.41.refs_2_, f32[2048,384]{1,0:T(8,128)S(1)} %copy-done.1), custom_call_target="tpu_custom_call" | custom-call | flops 4000000000 | bytes 11534336 | tf_op jit(solution)/shard_map/trailing/pallas_call | solution.py:279
  88.2 1.3 %collective-permute-done.20 = f32[288,384]{1,0:T(8,128)S(1)} collective-permute-done((f32[288,384]{1,0:T(8,128)S(1)}, f32[288,384]{1,0:T(8,128)S(1)}, u32[]{:S(2)}, u32[]{:S(2)}) %collective-permute-start.20) | collective-permute-done | bytes 442400 | tf_op jit(solution)/shard_map/ppermute | solution.py:38
  89.6 2.2 %collective-permute-start.24 = (f32[72,384]{1,0:T(8,128)S(1)}, f32[72,384]{1,0:T(8,128)S(1)}, u32[]{:S(2)}, u32[]{:S(2)}) collective-permute-start(f32[72,384]{1,0:T(8,128)S(1)} %get-tuple-element.48), channel_id=1, source_target_pairs={{0,128},{32,160},{64,192},{96,224},{128,0},{160,32},{192,64},{224,... | collective-permute-start | bytes 331784 | tf_op jit(solution)/shard_map/ppermute | solution.py:17
  91.9 3.4 %collective-permute-start.25 = (f32[72,384]{1,0:T(8,128)S(1)}, f32[72,384]{1,0:T(8,128)S(1)}, u32[]{:S(2)}, u32[]{:S(2)}) collective-permute-start(f32[72,384]{1,0:T(8,128)S(1)} %get-tuple-element.49), channel_id=1, source_target_pairs={{0,192},{32,224},{64,128},{96,160},{128,64},{160,96},{192,0},{224,... | collective-permute-start | bytes 331784 | tf_op jit(solution)/shard_map/ppermute | solution.py:17
  95.3 3.4 %collective-permute-done.23 = f32[72,384]{1,0:T(8,128)S(1)} collective-permute-done((f32[72,384]{1,0:T(8,128)S(1)}, f32[72,384]{1,0:T(8,128)S(1)}, u32[]{:S(2)}, u32[]{:S(2)}) %collective-permute-start.23) | collective-permute-done | bytes 110624 | tf_op jit(solution)/shard_map/ppermute | solution.py:17
  98.7 5.2 %collective-permute-done.25 = f32[72,384]{1,0:T(8,128)S(1)} collective-permute-done((f32[72,384]{1,0:T(8,128)S(1)}, f32[72,384]{1,0:T(8,128)S(1)}, u32[]{:S(2)}, u32[]{:S(2)}) %collective-permute-start.25) | collective-permute-done | bytes 110624 | tf_op jit(solution)/shard_map/ppermute | solution.py:17
  (61 shorter events, 6.2 us)
Async XLA Ops:
  1.4 4.2 %collective-permute-start = (f32[8,64]{1,0:T(8,128)S(1)}, f32[8,64]{1,0:T(8,128)S(1)}, u32[]{:S(2)}, u32[]{:S(2)}) collective-permute-start(f32[8,64]{1,0:T(8,128)S(1)} %get-tuple-element.55), channel_id=1, source_target_pairs={{0,1},{1,0},{2,3},{3,2},{4,5},{5,4},{6,7},{7,6},{8,9},{9,8},{10,11... | collective-permute-start | bytes 6152 | tf_op jit(solution)/shard_map/ppermute | solution.py:29
  5.5 1.3 %collective-permute-start.1 = (f32[16,1024]{1,0:T(8,128)S(1)}, f32[16,1024]{1,0:T(8,128)S(1)}, u32[]{:S(2)}, u32[]{:S(2)}) collective-permute-start(f32[16,1024]{1,0:T(8,128)S(1)} %get-tuple-element.52), channel_id=1, source_target_pairs={{0,1},{1,0},{2,3},{3,2},{4,5},{5,4},{6,7},{7,6},{8,9},{9,8},{10,11... | collective-permute-start | bytes 196616 | tf_op jit(solution)/shard_map/ppermute | solution.py:29
  6.8 4.6 %collective-permute-start.2 = (f32[40,1024]{1,0:T(8,128)S(1)}, f32[40,1024]{1,0:T(8,128)S(1)}, u32[]{:S(2)}, u32[]{:S(2)}) collective-permute-start(f32[40,1024]{1,0:T(8,128)S(1)} %pad_maximum_fusion.3), channel_id=1, source_target_pairs={{0,2},{1,9},{2,0},{3,11},{4,6},{5,13},{6,4},{7,15},{8,10},{9,1},{1... | collective-permute-start | bytes 491528 | tf_op jit(solution)/shard_map/ppermute | solution.py:44
  6.9 6.9 %collective-permute-start.3 = (f32[40,1024]{1,0:T(8,128)S(1)}, f32[40,1024]{1,0:T(8,128)S(1)}, u32[]{:S(2)}, u32[]{:S(2)}) collective-permute-start(f32[40,1024]{1,0:T(8,128)S(1)} %pad_maximum_fusion.3), channel_id=1, source_target_pairs={{0,4},{1,17},{2,6},{3,19},{4,0},{5,21},{6,2},{7,23},{8,12},{9,25},... | collective-permute-start | bytes 491528 | tf_op jit(solution)/shard_map/ppermute | solution.py:44
  9.1 6.5 %collective-permute-start.4 = (f32[40,1024]{1,0:T(8,128)S(1)}, f32[40,1024]{1,0:T(8,128)S(1)}, u32[]{:S(2)}, u32[]{:S(2)}) collective-permute-start(f32[40,1024]{1,0:T(8,128)S(1)} %pad_maximum_fusion.3), channel_id=1, source_target_pairs={{0,6},{1,25},{2,4},{3,27},{4,2},{5,29},{6,0},{7,31},{8,14},{9,17},... | collective-permute-start | bytes 491528 | tf_op jit(solution)/shard_map/ppermute | solution.py:44
  15.7 2.6 %collective-permute-start.5 = (f32[8,512]{1,0:T(8,128)S(1)}, f32[8,512]{1,0:T(8,128)S(1)}, u32[]{:S(2)}, u32[]{:S(2)}) collective-permute-start(f32[8,512]{1,0:T(8,128)S(1)} %concatenate.38), channel_id=1, source_target_pairs={{0,8},{1,3},{2,10},{3,1},{4,12},{5,7},{6,14},{7,5},{8,0},{9,11},{1... | collective-permute-start | bytes 49160 | tf_op jit(solution)/shard_map/ppermute | solution.py:44
  18.3 9.4 %collective-permute-start.6 = (f32[16,512]{1,0:T(8,128)S(1)}, f32[16,512]{1,0:T(8,128)S(1)}, u32[]{:S(2)}, u32[]{:S(2)}) collective-permute-start(f32[16,512]{1,0:T(8,128)S(1)} %pad_maximum_fusion.6), channel_id=1, source_target_pairs={{0,16},{1,5},{2,18},{3,7},{4,20},{5,1},{6,22},{7,3},{8,24},{9,13},... | collective-permute-start | bytes 98312 | tf_op jit(solution)/shard_map/ppermute | solution.py:44
  21.0 9.0 %collective-permute-start.8 = (f32[64,384]{1,0:T(8,128)}, f32[64,384]{1,0:T(8,128)S(1)}, u32[]{:S(2)}, u32[]{:S(2)}) collective-permute-start(f32[64,384]{1,0:T(8,128)} %param.10), channel_id=1, source_target_pairs={{0,128},{32,160},{64,192},{96,224},{128,0},{160,32},{192,64},{224,... | collective-permute-start | bytes 294920 | tf_op jit(solution)/shard_map/ppermute | solution.py:17
  27.7 6.5 %collective-permute-start.7 = (f32[32,512]{1,0:T(8,128)S(1)}, f32[32,512]{1,0:T(8,128)S(1)}, u32[]{:S(2)}, u32[]{:S(2)}) collective-permute-start(f32[32,512]{1,0:T(8,128)S(1)} %pad_maximum_fusion.5), channel_id=1, source_target_pairs={{0,64},{1,193},{2,66},{3,195},{4,68},{5,197},{6,70},{7,199},{8,72}... | collective-permute-start | bytes 196616 | tf_op jit(solution)/shard_map/ppermute | solution.py:25
  34.2 7.9 %collective-permute-start.9 = (f32[64,512]{1,0:T(8,128)S(1)}, f32[64,512]{1,0:T(8,128)S(1)}, u32[]{:S(2)}, u32[]{:S(2)}) collective-permute-start(f32[64,512]{1,0:T(8,128)S(1)} %pad_maximum_fusion.4), channel_id=1, source_target_pairs={{0,128},{32,160},{64,192},{96,224},{128,0},{160,32},{192,64},{224,... | collective-permute-start | bytes 393224 | tf_op jit(solution)/shard_map/ppermute | solution.py:17
  36.8 15.7 %collective-permute-start.11 = (f32[128,1024]{1,0:T(8,128)S(1)}, f32[128,1024]{1,0:T(8,128)S(1)}, u32[]{:S(2)}, u32[]{:S(2)}) collective-permute-start(f32[128,1024]{1,0:T(8,128)S(1)} %pad_maximum_fusion.refs_0_), channel_id=1, source_target_pairs={{0,8},{1,3},{2,10},{3,1},{4,12},{5,7},{6,14},{7,5},{8,0},{9,11},{1... | collective-permute-start | bytes 1572872 | tf_op jit(solution)/shard_map/ppermute | solution.py:44
  37.4 15.2 %collective-permute-start.12 = (f32[128,1024]{1,0:T(8,128)S(1)}, f32[128,1024]{1,0:T(8,128)S(1)}, u32[]{:S(2)}, u32[]{:S(2)}) collective-permute-start(f32[128,1024]{1,0:T(8,128)S(1)} %pad_maximum_fusion.refs_0_), channel_id=1, source_target_pairs={{0,24},{1,7},{2,26},{3,5},{4,28},{5,3},{6,30},{7,1},{8,16},{9,15},... | collective-permute-start | bytes 1572872 | tf_op jit(solution)/shard_map/ppermute | solution.py:44
  37.8 25.7 %collective-permute-start.13 = (f32[128,1024]{1,0:T(8,128)S(1)}, f32[128,1024]{1,0:T(8,128)S(1)}, u32[]{:S(2)}, u32[]{:S(2)}) collective-permute-start(f32[128,1024]{1,0:T(8,128)S(1)} %pad_maximum_fusion.refs_0_), channel_id=1, source_target_pairs={{0,16},{1,5},{2,18},{3,7},{4,20},{5,1},{6,22},{7,3},{8,24},{9,13},... | collective-permute-start | bytes 1572872 | tf_op jit(solution)/shard_map/ppermute | solution.py:44
  42.2 7.2 %collective-permute-start.10 = (f32[128,512]{1,0:T(8,128)S(1)}, f32[128,512]{1,0:T(8,128)S(1)}, u32[]{:S(2)}, u32[]{:S(2)}) collective-permute-start(f32[128,512]{1,0:T(8,128)S(1)} %pad_maximum_fusion.1.refs_0_), channel_id=1, source_target_pairs={{0,32},{1,225},{2,34},{3,227},{4,36},{5,229},{6,38},{7,231},{8,40}... | collective-permute-start | bytes 786440 | tf_op jit(solution)/shard_map/ppermute | solution.py:38
  43.0 20.5 %collective-permute-start.18 = (f32[128,512]{1,0:T(8,128)S(1)}, f32[128,512]{1,0:T(8,128)S(1)}, u32[]{:S(2)}, u32[]{:S(2)}) collective-permute-start(f32[128,512]{1,0:T(8,128)S(1)} %pad_maximum_fusion.1.refs_0_), channel_id=1, source_target_pairs={{0,1},{1,0},{2,3},{3,2},{4,5},{5,4},{6,7},{7,6},{8,9},{9,8},{10,11... | collective-permute-start | bytes 786440 | tf_op jit(solution)/shard_map/ppermute | solution.py:29
  49.4 8.7 %collective-permute-start.21 = (f32[128,384]{1,0:T(8,128)S(1)}, f32[128,384]{1,0:T(8,128)S(1)}, u32[]{:S(2)}, u32[]{:S(2)}) collective-permute-start(f32[128,384]{1,0:T(8,128)S(1)} %pad_maximum_fusion.2), channel_id=1, source_target_pairs={{0,64},{1,193},{2,66},{3,195},{4,68},{5,197},{6,70},{7,199},{8,72}... | collective-permute-start | bytes 589832 | tf_op jit(solution)/shard_map/ppermute | solution.py:25
  52.6 11.5 %collective-permute-start.19 = (f32[128,512]{1,0:T(8,128)S(1)}, f32[128,512]{1,0:T(8,128)S(1)}, u32[]{:S(2)}, u32[]{:S(2)}) collective-permute-start(f32[128,512]{1,0:T(8,128)S(1)} %collective-permute-done.10.refs_1_), channel_id=1, source_target_pairs={{0,1},{1,0},{2,3},{3,2},{4,5},{5,4},{6,7},{7,6},{8,9},{9,8},{10,11... | collective-permute-start | bytes 786440 | tf_op jit(solution)/shard_map/ppermute | solution.py:29
  57.9 15.0 %collective-permute-start.14 = (f32[128,1024]{1,0:T(8,128)S(1)}, f32[128,1024]{1,0:T(8,128)S(1)}, u32[]{:S(2)}, u32[]{:S(2)}) collective-permute-start(f32[128,1024]{1,0:T(8,128)S(1)} %pad_maximum_fusion.refs_0_), channel_id=1, source_target_pairs={{0,1},{1,0},{2,3},{3,2},{4,5},{5,4},{6,7},{7,6},{8,9},{9,8},{10,11... | collective-permute-start | bytes 1572872 | tf_op jit(solution)/shard_map/ppermute | solution.py:29
  58.1 14.8 %collective-permute-start.15 = (f32[128,1024]{1,0:T(8,128)S(1)}, f32[128,1024]{1,0:T(8,128)S(1)}, u32[]{:S(2)}, u32[]{:S(2)}) collective-permute-start(f32[128,1024]{1,0:T(8,128)S(1)} %collective-permute-done.11.refs_1_), channel_id=1, source_target_pairs={{0,1},{1,0},{2,3},{3,2},{4,5},{5,4},{6,7},{7,6},{8,9},{9,8},{10,11... | collective-permute-start | bytes 1572872 | tf_op jit(solution)/shard_map/ppermute | solution.py:29
  63.5 9.4 %collective-permute-start.17 = (f32[128,1024]{1,0:T(8,128)S(1)}, f32[128,1024]{1,0:T(8,128)S(1)}, u32[]{:S(2)}, u32[]{:S(2)}) collective-permute-start(f32[128,1024]{1,0:T(8,128)S(1)} %collective-permute-done.12.refs_3_), channel_id=1, source_target_pairs={{0,1},{1,0},{2,3},{3,2},{4,5},{5,4},{6,7},{7,6},{8,9},{9,8},{10,11... | collective-permute-start | bytes 1572872 | tf_op jit(solution)/shard_map/ppermute | solution.py:29
  63.5 9.4 %collective-permute-start.16 = (f32[128,1024]{1,0:T(8,128)S(1)}, f32[128,1024]{1,0:T(8,128)S(1)}, u32[]{:S(2)}, u32[]{:S(2)}) collective-permute-start(f32[128,1024]{1,0:T(8,128)S(1)} %collective-permute-done.13.refs_2_), channel_id=1, source_target_pairs={{0,1},{1,0},{2,3},{3,2},{4,5},{5,4},{6,7},{7,6},{8,9},{9,8},{10,11... | collective-permute-start | bytes 1572872 | tf_op jit(solution)/shard_map/ppermute | solution.py:29
  64.1 8.8 %copy-start = (f32[2048,384]{1,0:T(8,128)S(1)}, f32[2048,384]{1,0:T(8,128)}, u32[]{:S(2)}) copy-start(f32[2048,384]{1,0:T(8,128)} %refs_10_.1) | copy-start | bytes 9437188
  64.1 8.8 %copy-start.2 = (f32[2048,16]{0,1:T(8,128)S(1)}, f32[2048,16]{0,1:T(8,128)}, u32[]{:S(2)}) copy-start(f32[2048,16]{0,1:T(8,128)} %param.9) | copy-start | bytes 393220
  64.1 17.0 %collective-permute-start.22 = (f32[256,384]{1,0:T(8,128)S(1)}, f32[256,384]{1,0:T(8,128)S(1)}, u32[]{:S(2)}, u32[]{:S(2)}) collective-permute-start(f32[256,384]{1,0:T(8,128)S(1)} %constant_dynamic-update-slice_fusion.refs_0_), channel_id=1, source_target_pairs={{0,32},{1,225},{2,34},{3,227},{4,36},{5,229},{6,38},{7,231},{8,40}... | collective-permute-start | bytes 1179656 | tf_op jit(solution)/shard_map/ppermute | solution.py:38
  72.9 8.2 %copy-start.1 = (f32[2048,384]{1,0:T(8,128)S(1)}, f32[2048,384]{1,0:T(8,128)}, u32[]{:S(2)}) copy-start(f32[2048,384]{1,0:T(8,128)} %refs_3_.1) | copy-start | bytes 9437188
  81.1 8.4 %collective-permute-start.20 = (f32[288,384]{1,0:T(8,128)S(1)}, f32[288,384]{1,0:T(8,128)S(1)}, u32[]{:S(2)}, u32[]{:S(2)}) collective-permute-start(f32[288,384]{1,0:T(8,128)S(1)} %get-tuple-element.39), channel_id=1, source_target_pairs={{0,32},{1,225},{2,34},{3,227},{4,36},{5,229},{6,38},{7,231},{8,40}... | collective-permute-start | bytes 1327112 | tf_op jit(solution)/shard_map/ppermute | solution.py:38
  81.2 22.8 %copy-start.3 = (f32[64,384]{1,0:T(8,128)S(1)}, f32[64,384]{1,0:T(8,128)}, u32[]{:S(2)}) copy-start(f32[64,384]{1,0:T(8,128)} %param.14) | copy-start | bytes 294916
  81.2 23.5 %copy-start.4 = (f32[64,16]{0,1:T(8,128)S(1)}, f32[64,16]{0,1:T(8,128)}, u32[]{:S(2)}) copy-start(f32[64,16]{0,1:T(8,128)} %param.13) | copy-start | bytes 12292
  89.5 9.1 %collective-permute-start.23 = (f32[72,384]{1,0:T(8,128)S(1)}, f32[72,384]{1,0:T(8,128)S(1)}, u32[]{:S(2)}, u32[]{:S(2)}) collective-permute-start(f32[72,384]{1,0:T(8,128)S(1)} %get-tuple-element.50), channel_id=1, source_target_pairs={{0,64},{32,96},{64,0},{96,32},{128,192},{160,224},{192,128},{224,1... | collective-permute-start | bytes 331784 | tf_op jit(solution)/shard_map/ppermute | solution.py:17
  89.6 9.0 %collective-permute-start.24 = (f32[72,384]{1,0:T(8,128)S(1)}, f32[72,384]{1,0:T(8,128)S(1)}, u32[]{:S(2)}, u32[]{:S(2)}) collective-permute-start(f32[72,384]{1,0:T(8,128)S(1)} %get-tuple-element.48), channel_id=1, source_target_pairs={{0,128},{32,160},{64,192},{96,224},{128,0},{160,32},{192,64},{224,... | collective-permute-start | bytes 331784 | tf_op jit(solution)/shard_map/ppermute | solution.py:17
  91.9 12.0 %collective-permute-start.25 = (f32[72,384]{1,0:T(8,128)S(1)}, f32[72,384]{1,0:T(8,128)S(1)}, u32[]{:S(2)}, u32[]{:S(2)}) collective-permute-start(f32[72,384]{1,0:T(8,128)S(1)} %get-tuple-element.49), channel_id=1, source_target_pairs={{0,192},{32,224},{64,128},{96,160},{128,64},{160,96},{192,0},{224,... | collective-permute-start | bytes 331784 | tf_op jit(solution)/shard_map/ppermute | solution.py:17
